TPU v7x, 256 devices: a whole 4x4x8 slice. The times are simulated.
256 devices in a mesh: aux: 16 (over y_lo, x, core), blk: 16 (over y_hi, z).
Axes of the slice: x: 4, y: 4 (y_hi: 2, y_lo: 2; y = y_hi * 2 + y_lo), z: 8, core: 2. Of those that a mesh axis runs over, the one named last changes fastest.
Arguments:
- half_b: bfloat16 [32, 8192, 512], P('aux', 'blk'), may hold values from -1.25 to 1.25
Outputs:
- exchange: float32 [8192, 8192], P('blk', 'aux')
All inputs are finite; a program needn't handle non-finite values.
Results may differ from a plain program's by a relative error of at most 0.0003.
Values may be sent and summed in bfloat16 or wider, within the bound.
No kernel may reach another device: no remote copies, remote signals or barrier semaphores. Data moves between devices by JAX's collectives and lax.ppermute only.
A program may use at most 128 MiB of HBM per device.

v0:
```python
import jax
import jax.numpy as jnp
from jax import lax
from jax.sharding import PartitionSpec as P


def shifted(value, axis, steps):
    count = lax.axis_size(axis)
    pairs = [(source, (source + steps) % count) for source in range(count)]
    return lax.ppermute(value, axis, pairs)


def place_tile(partial_value, tile, column, width):
    start = column * width
    current = lax.dynamic_slice_in_dim(partial_value, start, width, 1)
    added = current + jnp.where(True, tile, jnp.float32(0.0))
    return lax.dynamic_update_slice_in_dim(partial_value, added, start, 1)


def per_device(half_b):
    aux_dev, width, occupied = half_b.shape
    local = jnp.transpose(half_b, (1, 0, 2)).reshape(width, aux_dev * occupied)
    count = lax.axis_size("blk")
    own = lax.axis_index("blk")

    def product(other):
        return lax.dot_general(
            local, other, (((1,), (1,)), ((), ())), preferred_element_type=jnp.float32
        )

    partial_value = jnp.zeros((width, count * width), jnp.float32)
    partial_value = place_tile(partial_value, product(local), own, width)

    def advance(index, carry):
        travel, summed = carry
        travel = shifted(travel, "blk", 1)
        column = (own - index) % count

        def compute(current):
            return place_tile(current, product(travel), column, width)

        def skip(current):
            return current

        summed = lax.cond(column > own, compute, skip, summed)
        return (travel, summed)

    _, partial_value = lax.fori_loop(1, count, advance, (local, partial_value))
    return lax.psum_scatter(partial_value, "aux", scatter_dimension=1, tiled=True)


def solution(mesh):
    placed = (P("aux", "blk", None),)
    return jax.shard_map(
        per_device, mesh=mesh, in_specs=placed, out_specs=P("blk", "aux"), check_vma=False
    )
```

profile of v0, /device:TPU:12, one launch (start us, length us, event | category | flops | bytes accessed | tf_op | source)
XLA Modules:
  0.0 513.5 jit_solution(16965271902845518620)
XLA Ops:
  10.9 5.7 %copy-done = f32[512,8192]{1,0:T(8,128)} copy-done((f32[512,8192]{1,0:T(8,128)}, f32[512,8192]{1,0:T(8,128)S(1)}, u32[]{:S(2)}) %copy-start) | copy-done | bytes 16777240
  16.6 397.5 %while.20 = (s32[]{:T(128)}, bf16[512,1024]{1,0:T(8,128)(2,1)S(1)}, f32[512,8192]{1,0:T(8,128)}, s32[]{:T(128)}, bf16[512,1024]{1,0:T(8,128)(2,1)S(1)}, /*index=5*/s32[]{:T(128)}, s32[]{:T(128)}, s32[]{:T(128)}, s32[]{:T(128)}) while((s32[]{:T(128)}, bf16[512,1024]{1,0:T(8,128)(2,1)S(1)}, f32[512,8192]{1,0:T(8,128)}, s32[]{:T(128)}, ...), condition=%wide.region_3.4_spmd, body=%wide.region_0.3_spmd.sunk | while | flops 537133056 | bytes 10486118 | solution.py:48
  18.5 28.8 %collective-permute-done = bf16[512,1024]{1,0:T(8,128)(2,1)S(1)} collective-permute-done((bf16[512,1024]{1,0:T(8,128)(2,1)S(1)}, bf16[512,1024]{1,0:T(8,128)(2,1)S(1)}, u32[]{:S(2)}, u32[]{:S(2)}) %collective-permute-start) | collective-permute-done | bytes 1048608 | tf_op jit(solution)/shard_map/while/body/eval_jaxpr/ppermute | solution.py:10
  47.3 3.0 conditional.2
  47.3 3.0 fusion
  50.5 27.9 %collective-permute-done = bf16[512,1024]{1,0:T(8,128)(2,1)S(1)} collective-permute-done((bf16[512,1024]{1,0:T(8,128)(2,1)S(1)}, bf16[512,1024]{1,0:T(8,128)(2,1)S(1)}, u32[]{:S(2)}, u32[]{:S(2)}) %collective-permute-start) | collective-permute-done | bytes 1048608 | tf_op jit(solution)/shard_map/while/body/eval_jaxpr/ppermute | solution.py:10
  81.6 27.0 %collective-permute-done = bf16[512,1024]{1,0:T(8,128)(2,1)S(1)} collective-permute-done((bf16[512,1024]{1,0:T(8,128)(2,1)S(1)}, bf16[512,1024]{1,0:T(8,128)(2,1)S(1)}, u32[]{:S(2)}, u32[]{:S(2)}) %collective-permute-start) | collective-permute-done | bytes 1048608 | tf_op jit(solution)/shard_map/while/body/eval_jaxpr/ppermute | solution.py:10
  111.7 26.1 %collective-permute-done = bf16[512,1024]{1,0:T(8,128)(2,1)S(1)} collective-permute-done((bf16[512,1024]{1,0:T(8,128)(2,1)S(1)}, bf16[512,1024]{1,0:T(8,128)(2,1)S(1)}, u32[]{:S(2)}, u32[]{:S(2)}) %collective-permute-start) | collective-permute-done | bytes 1048608 | tf_op jit(solution)/shard_map/while/body/eval_jaxpr/ppermute | solution.py:10
  137.8 3.0 conditional.2
  137.8 3.0 fusion
  140.9 25.2 %collective-permute-done = bf16[512,1024]{1,0:T(8,128)(2,1)S(1)} collective-permute-done((bf16[512,1024]{1,0:T(8,128)(2,1)S(1)}, bf16[512,1024]{1,0:T(8,128)(2,1)S(1)}, u32[]{:S(2)}, u32[]{:S(2)}) %collective-permute-start) | collective-permute-done | bytes 1048608 | tf_op jit(solution)/shard_map/while/body/eval_jaxpr/ppermute | solution.py:10
  169.2 24.2 %collective-permute-done = bf16[512,1024]{1,0:T(8,128)(2,1)S(1)} collective-permute-done((bf16[512,1024]{1,0:T(8,128)(2,1)S(1)}, bf16[512,1024]{1,0:T(8,128)(2,1)S(1)}, u32[]{:S(2)}, u32[]{:S(2)}) %collective-permute-start) | collective-permute-done | bytes 1048608 | tf_op jit(solution)/shard_map/while/body/eval_jaxpr/ppermute | solution.py:10
  193.5 3.0 conditional.2
  193.5 3.0 fusion
  196.6 23.3 %collective-permute-done = bf16[512,1024]{1,0:T(8,128)(2,1)S(1)} collective-permute-done((bf16[512,1024]{1,0:T(8,128)(2,1)S(1)}, bf16[512,1024]{1,0:T(8,128)(2,1)S(1)}, u32[]{:S(2)}, u32[]{:S(2)}) %collective-permute-start) | collective-permute-done | bytes 1048608 | tf_op jit(solution)/shard_map/while/body/eval_jaxpr/ppermute | solution.py:10
  219.9 3.0 conditional.2
  219.9 3.0 fusion
  223.1 22.4 %collective-permute-done = bf16[512,1024]{1,0:T(8,128)(2,1)S(1)} collective-permute-done((bf16[512,1024]{1,0:T(8,128)(2,1)S(1)}, bf16[512,1024]{1,0:T(8,128)(2,1)S(1)}, u32[]{:S(2)}, u32[]{:S(2)}) %collective-permute-start) | collective-permute-done | bytes 1048608 | tf_op jit(solution)/shard_map/while/body/eval_jaxpr/ppermute | solution.py:10
  245.5 3.0 conditional.2
  245.5 3.0 fusion
  248.7 21.5 %collective-permute-done = bf16[512,1024]{1,0:T(8,128)(2,1)S(1)} collective-permute-done((bf16[512,1024]{1,0:T(8,128)(2,1)S(1)}, bf16[512,1024]{1,0:T(8,128)(2,1)S(1)}, u32[]{:S(2)}, u32[]{:S(2)}) %collective-permute-start) | collective-permute-done | bytes 1048608 | tf_op jit(solution)/shard_map/while/body/eval_jaxpr/ppermute | solution.py:10
  273.3 20.5 %collective-permute-done = bf16[512,1024]{1,0:T(8,128)(2,1)S(1)} collective-permute-done((bf16[512,1024]{1,0:T(8,128)(2,1)S(1)}, bf16[512,1024]{1,0:T(8,128)(2,1)S(1)}, u32[]{:S(2)}, u32[]{:S(2)}) %collective-permute-start) | collective-permute-done | bytes 1048608 | tf_op jit(solution)/shard_map/while/body/eval_jaxpr/ppermute | solution.py:10
  297.0 20.2 %collective-permute-done = bf16[512,1024]{1,0:T(8,128)(2,1)S(1)} collective-permute-done((bf16[512,1024]{1,0:T(8,128)(2,1)S(1)}, bf16[512,1024]{1,0:T(8,128)(2,1)S(1)}, u32[]{:S(2)}, u32[]{:S(2)}) %collective-permute-start) | collective-permute-done | bytes 1048608 | tf_op jit(solution)/shard_map/while/body/eval_jaxpr/ppermute | solution.py:10
  320.3 20.2 %collective-permute-done = bf16[512,1024]{1,0:T(8,128)(2,1)S(1)} collective-permute-done((bf16[512,1024]{1,0:T(8,128)(2,1)S(1)}, bf16[512,1024]{1,0:T(8,128)(2,1)S(1)}, u32[]{:S(2)}, u32[]{:S(2)}) %collective-permute-start) | collective-permute-done | bytes 1048608 | tf_op jit(solution)/shard_map/while/body/eval_jaxpr/ppermute | solution.py:10
  343.6 20.9 %collective-permute-done = bf16[512,1024]{1,0:T(8,128)(2,1)S(1)} collective-permute-done((bf16[512,1024]{1,0:T(8,128)(2,1)S(1)}, bf16[512,1024]{1,0:T(8,128)(2,1)S(1)}, u32[]{:S(2)}, u32[]{:S(2)}) %collective-permute-start) | collective-permute-done | bytes 1048608 | tf_op jit(solution)/shard_map/while/body/eval_jaxpr/ppermute | solution.py:10
  364.5 3.0 conditional.2
  364.5 3.0 fusion
  367.6 21.9 %collective-permute-done = bf16[512,1024]{1,0:T(8,128)(2,1)S(1)} collective-permute-done((bf16[512,1024]{1,0:T(8,128)(2,1)S(1)}, bf16[512,1024]{1,0:T(8,128)(2,1)S(1)}, u32[]{:S(2)}, u32[]{:S(2)}) %collective-permute-start) | collective-permute-done | bytes 1048608 | tf_op jit(solution)/shard_map/while/body/eval_jaxpr/ppermute | solution.py:10
  392.7 18.4 %collective-permute-done = bf16[512,1024]{1,0:T(8,128)(2,1)S(1)} collective-permute-done((bf16[512,1024]{1,0:T(8,128)(2,1)S(1)}, bf16[512,1024]{1,0:T(8,128)(2,1)S(1)}, u32[]{:S(2)}, u32[]{:S(2)}) %collective-permute-start) | collective-permute-done | bytes 1048608 | tf_op jit(solution)/shard_map/while/body/eval_jaxpr/ppermute | solution.py:10
  411.1 3.0 conditional.2
  411.1 3.0 fusion
  414.1 92.5 %reduce-scatter.2.cloned.1.call-done = f32[512,512]{1,0:T(8,128)} async-done(((f32[512,8192]{1,0:T(8,128)}), f32[512,512]{1,0:T(8,128)}) %reduce-scatter.2.cloned.1.call-update) | async-done | bytes 1048592 | tf_op jit(solution)/shard_map/reduce_scatter | solution.py:49
  (55 shorter events, 55.4 us)
Async XLA Ops:
  6.5 3.6 copy-start.1
  6.5 500.1 %reduce-scatter.2.cloned.1.call-start = ((), (), s32[]{:S(2)}) async-start(), calls=%async_computation.1 | async-start | bytes 17825792 | tf_op jit(solution)/shard_map/reduce_scatter | solution.py:49
  10.9 5.7 %copy-start = (f32[512,8192]{1,0:T(8,128)}, f32[512,8192]{1,0:T(8,128)S(1)}, u32[]{:S(2)}) copy-start(f32[512,8192]{1,0:T(8,128)S(1)} %fusion.1) | copy-start | bytes 50331652
  16.6 30.7 %collective-permute-start = (bf16[512,1024]{1,0:T(8,128)(2,1)S(1)}, bf16[512,1024]{1,0:T(8,128)(2,1)S(1)}, u32[]{:S(2)}, u32[]{:S(2)}) collective-permute-start(bf16[512,1024]{1,0:T(8,128)(2,1)S(1)} %get-tuple-element.213), channel_id=1, source_target_pairs={{0,1},{1,2},{2,3},{3,4},{4,5},{5,6},{6,7},{7,8},{8,9},{9,10},{10,1... | collective-permute-start | bytes 3145736 | tf_op jit(solution)/shard_map/while/body/eval_jaxpr/ppermute | solution.py:10
  50.4 28.0 %collective-permute-start = (bf16[512,1024]{1,0:T(8,128)(2,1)S(1)}, bf16[512,1024]{1,0:T(8,128)(2,1)S(1)}, u32[]{:S(2)}, u32[]{:S(2)}) collective-permute-start(bf16[512,1024]{1,0:T(8,128)(2,1)S(1)} %get-tuple-element.213), channel_id=1, source_target_pairs={{0,1},{1,2},{2,3},{3,4},{4,5},{5,6},{6,7},{7,8},{8,9},{9,10},{10,1... | collective-permute-start | bytes 3145736 | tf_op jit(solution)/shard_map/while/body/eval_jaxpr/ppermute | solution.py:10
  81.5 27.1 %collective-permute-start = (bf16[512,1024]{1,0:T(8,128)(2,1)S(1)}, bf16[512,1024]{1,0:T(8,128)(2,1)S(1)}, u32[]{:S(2)}, u32[]{:S(2)}) collective-permute-start(bf16[512,1024]{1,0:T(8,128)(2,1)S(1)} %get-tuple-element.213), channel_id=1, source_target_pairs={{0,1},{1,2},{2,3},{3,4},{4,5},{5,6},{6,7},{7,8},{8,9},{9,10},{10,1... | collective-permute-start | bytes 3145736 | tf_op jit(solution)/shard_map/while/body/eval_jaxpr/ppermute | solution.py:10
  111.6 26.2 %collective-permute-start = (bf16[512,1024]{1,0:T(8,128)(2,1)S(1)}, bf16[512,1024]{1,0:T(8,128)(2,1)S(1)}, u32[]{:S(2)}, u32[]{:S(2)}) collective-permute-start(bf16[512,1024]{1,0:T(8,128)(2,1)S(1)} %get-tuple-element.213), channel_id=1, source_target_pairs={{0,1},{1,2},{2,3},{3,4},{4,5},{5,6},{6,7},{7,8},{8,9},{9,10},{10,1... | collective-permute-start | bytes 3145736 | tf_op jit(solution)/shard_map/while/body/eval_jaxpr/ppermute | solution.py:10
  140.8 25.3 %collective-permute-start = (bf16[512,1024]{1,0:T(8,128)(2,1)S(1)}, bf16[512,1024]{1,0:T(8,128)(2,1)S(1)}, u32[]{:S(2)}, u32[]{:S(2)}) collective-permute-start(bf16[512,1024]{1,0:T(8,128)(2,1)S(1)} %get-tuple-element.213), channel_id=1, source_target_pairs={{0,1},{1,2},{2,3},{3,4},{4,5},{5,6},{6,7},{7,8},{8,9},{9,10},{10,1... | collective-permute-start | bytes 3145736 | tf_op jit(solution)/shard_map/while/body/eval_jaxpr/ppermute | solution.py:10
  169.1 24.3 %collective-permute-start = (bf16[512,1024]{1,0:T(8,128)(2,1)S(1)}, bf16[512,1024]{1,0:T(8,128)(2,1)S(1)}, u32[]{:S(2)}, u32[]{:S(2)}) collective-permute-start(bf16[512,1024]{1,0:T(8,128)(2,1)S(1)} %get-tuple-element.213), channel_id=1, source_target_pairs={{0,1},{1,2},{2,3},{3,4},{4,5},{5,6},{6,7},{7,8},{8,9},{9,10},{10,1... | collective-permute-start | bytes 3145736 | tf_op jit(solution)/shard_map/while/body/eval_jaxpr/ppermute | solution.py:10
  196.5 23.4 %collective-permute-start = (bf16[512,1024]{1,0:T(8,128)(2,1)S(1)}, bf16[512,1024]{1,0:T(8,128)(2,1)S(1)}, u32[]{:S(2)}, u32[]{:S(2)}) collective-permute-start(bf16[512,1024]{1,0:T(8,128)(2,1)S(1)} %get-tuple-element.213), channel_id=1, source_target_pairs={{0,1},{1,2},{2,3},{3,4},{4,5},{5,6},{6,7},{7,8},{8,9},{9,10},{10,1... | collective-permute-start | bytes 3145736 | tf_op jit(solution)/shard_map/while/body/eval_jaxpr/ppermute | solution.py:10
  223.0 22.5 %collective-permute-start = (bf16[512,1024]{1,0:T(8,128)(2,1)S(1)}, bf16[512,1024]{1,0:T(8,128)(2,1)S(1)}, u32[]{:S(2)}, u32[]{:S(2)}) collective-permute-start(bf16[512,1024]{1,0:T(8,128)(2,1)S(1)} %get-tuple-element.213), channel_id=1, source_target_pairs={{0,1},{1,2},{2,3},{3,4},{4,5},{5,6},{6,7},{7,8},{8,9},{9,10},{10,1... | collective-permute-start | bytes 3145736 | tf_op jit(solution)/shard_map/while/body/eval_jaxpr/ppermute | solution.py:10
  248.5 21.6 %collective-permute-start = (bf16[512,1024]{1,0:T(8,128)(2,1)S(1)}, bf16[512,1024]{1,0:T(8,128)(2,1)S(1)}, u32[]{:S(2)}, u32[]{:S(2)}) collective-permute-start(bf16[512,1024]{1,0:T(8,128)(2,1)S(1)} %get-tuple-element.213), channel_id=1, source_target_pairs={{0,1},{1,2},{2,3},{3,4},{4,5},{5,6},{6,7},{7,8},{8,9},{9,10},{10,1... | collective-permute-start | bytes 3145736 | tf_op jit(solution)/shard_map/while/body/eval_jaxpr/ppermute | solution.py:10
  273.2 20.7 %collective-permute-start = (bf16[512,1024]{1,0:T(8,128)(2,1)S(1)}, bf16[512,1024]{1,0:T(8,128)(2,1)S(1)}, u32[]{:S(2)}, u32[]{:S(2)}) collective-permute-start(bf16[512,1024]{1,0:T(8,128)(2,1)S(1)} %get-tuple-element.213), channel_id=1, source_target_pairs={{0,1},{1,2},{2,3},{3,4},{4,5},{5,6},{6,7},{7,8},{8,9},{9,10},{10,1... | collective-permute-start | bytes 3145736 | tf_op jit(solution)/shard_map/while/body/eval_jaxpr/ppermute | solution.py:10
  296.8 20.3 %collective-permute-start = (bf16[512,1024]{1,0:T(8,128)(2,1)S(1)}, bf16[512,1024]{1,0:T(8,128)(2,1)S(1)}, u32[]{:S(2)}, u32[]{:S(2)}) collective-permute-start(bf16[512,1024]{1,0:T(8,128)(2,1)S(1)} %get-tuple-element.213), channel_id=1, source_target_pairs={{0,1},{1,2},{2,3},{3,4},{4,5},{5,6},{6,7},{7,8},{8,9},{9,10},{10,1... | collective-permute-start | bytes 3145736 | tf_op jit(solution)/shard_map/while/body/eval_jaxpr/ppermute | solution.py:10
  320.2 20.3 %collective-permute-start = (bf16[512,1024]{1,0:T(8,128)(2,1)S(1)}, bf16[512,1024]{1,0:T(8,128)(2,1)S(1)}, u32[]{:S(2)}, u32[]{:S(2)}) collective-permute-start(bf16[512,1024]{1,0:T(8,128)(2,1)S(1)} %get-tuple-element.213), channel_id=1, source_target_pairs={{0,1},{1,2},{2,3},{3,4},{4,5},{5,6},{6,7},{7,8},{8,9},{9,10},{10,1... | collective-permute-start | bytes 3145736 | tf_op jit(solution)/shard_map/while/body/eval_jaxpr/ppermute | solution.py:10
  343.5 21.0 %collective-permute-start = (bf16[512,1024]{1,0:T(8,128)(2,1)S(1)}, bf16[512,1024]{1,0:T(8,128)(2,1)S(1)}, u32[]{:S(2)}, u32[]{:S(2)}) collective-permute-start(bf16[512,1024]{1,0:T(8,128)(2,1)S(1)} %get-tuple-element.213), channel_id=1, source_target_pairs={{0,1},{1,2},{2,3},{3,4},{4,5},{5,6},{6,7},{7,8},{8,9},{9,10},{10,1... | collective-permute-start | bytes 3145736 | tf_op jit(solution)/shard_map/while/body/eval_jaxpr/ppermute | solution.py:10
  367.5 22.1 %collective-permute-start = (bf16[512,1024]{1,0:T(8,128)(2,1)S(1)}, bf16[512,1024]{1,0:T(8,128)(2,1)S(1)}, u32[]{:S(2)}, u32[]{:S(2)}) collective-permute-start(bf16[512,1024]{1,0:T(8,128)(2,1)S(1)} %get-tuple-element.213), channel_id=1, source_target_pairs={{0,1},{1,2},{2,3},{3,4},{4,5},{5,6},{6,7},{7,8},{8,9},{9,10},{10,1... | collective-permute-start | bytes 3145736 | tf_op jit(solution)/shard_map/while/body/eval_jaxpr/ppermute | solution.py:10
  392.6 18.5 %collective-permute-start = (bf16[512,1024]{1,0:T(8,128)(2,1)S(1)}, bf16[512,1024]{1,0:T(8,128)(2,1)S(1)}, u32[]{:S(2)}, u32[]{:S(2)}) collective-permute-start(bf16[512,1024]{1,0:T(8,128)(2,1)S(1)} %get-tuple-element.213), channel_id=1, source_target_pairs={{0,1},{1,2},{2,3},{3,4},{4,5},{5,6},{6,7},{7,8},{8,9},{9,10},{10,1... | collective-permute-start | bytes 3145736 | tf_op jit(solution)/shard_map/while/body/eval_jaxpr/ppermute | solution.py:10
Sparse Core Ops, SparseCore 0:
  414.3 92.3 reduce-scatter.1
where the time goes:
time: 517 us; the launch traced here: 513 us
  waiting for transfers between devices  441 us (85%)
  matrix products  45 us (9%)
  between operations  13.4 us (3%)
  local copies, waits for them, and re-layouts  10.3 us (2%)
    ppermute x15, waiting for transfers between devices, shifted(): return lax.ppermute(value, axis, pairs)  348 us
    reduce_scatter x1, waiting for transfers between devices, per_device(): lax.psum_scatter(partial_value, 'aux', scatter_dimension=1, tiled=True)  92.5 us
    dot_general x16, matrix products, product(): lax.dot_general(local, other, (((1,), (1,)), ((), ())), preferred_element...  45 us
  transfers between devices with their start and end apart: 16, of which 16 were waited for; matrix products, arithmetic and copies ran while one was open for 0% of the time, Pallas kernels for 0%

commit v1 on v0

v1 whole, which is shorter than its diff:
```python
import functools

import jax
import jax.numpy as jnp
import numpy as np
from jax import lax
from jax.experimental import pallas as pl
from jax.experimental.pallas import tpu as pltpu
from jax.sharding import PartitionSpec as P

ALL = ("aux", "blk")
NX, NZ, GROUPS = 4, 8, 16
EMPTY = 63
VMEM_LIMIT = 48 * 2**20


def device(y_lo, x, core, blk):
    return ((y_lo * NX + x % NX) * 2 + core) * GROUPS + blk


def block(h, z):
    return h % 2 * NZ + z % NZ


def every(move):
    return [
        (device(*move(y_lo, x, core, h, z)), device(y_lo, x, core, block(h, z)))
        for y_lo in range(2)
        for x in range(NX)
        for core in range(2)
        for h in range(2)
        for z in range(NZ)
    ]


def send(value, pairs):
    return lax.ppermute(value, ALL, pairs)


O, PZ, MZ, Y0 = (0, 0), (0, 1), (0, -1), (1, 0)
PP, MM, Y1, Y2 = (0, 2), (0, -2), (1, 1), (1, 2)
HELD_A = (O, PZ, MZ, Y0)
HELD_B = (MZ, PZ, PP, MM, Y1)
HELD_C = (MM, Y2)


def units_of(held, pairs, h, z):
    found = []
    for at, (first, second, halves) in enumerate(pairs):
        i, j = block(h + first[0], z + first[1]), block(h + second[0], z + second[1])
        for half in halves(h, z):
            found.append(((at * 2 + (i > j)) * 2 + half, min(i, j), max(i, j), half))
    return found


def both(h, z):
    return (0, 1)


def by_h(h, z):
    return (h,)


def by_z(h, z):
    return (0,) if 2 <= z < 6 else (1,)


PAIRS_A = ((O, PZ, both), (MZ, PZ, both), (O, Y0, by_h), (MZ, Y0, both))
PAIRS_B = ((MM, PZ, both), (MM, PP, by_z), (MZ, Y1, both), (MM, Y1, both))
PAIRS_C = ((MM, Y2, by_h),)


def ring(a, b, n):
    return min((a - b) % n, (b - a) % n)


def hops(y_lo, x, core, h, z, row, col):
    y_at, y_to = h * 2 + y_lo, row // NZ * 2 + col // 8
    return ring(x, col // 2 % NX, NX) + ring(y_at, y_to, 4) + ring(z, row % NZ, NZ) + 0.1 * (core != col % 2)


def assign(units, y_lo, h, z):
    best = {0: (0.0, ())}
    for _, row, col, _ in units:
        grown = {}
        for mask, (cost, taken) in best.items():
            for place in range(8):
                if mask >> place & 1:
                    continue
                total = cost + hops(y_lo, place // 2, place % 2, h, z, row, col) ** 2
                key = mask | 1 << place
                if key not in grown or total < grown[key][0]:
                    grown[key] = (total, taken + (place,))
        best = grown
    return min(best.values())[1]


@functools.cache
def plan():
    tables = np.full((2, GROUPS, 2, NX), EMPTY, np.int32)
    code_c = np.zeros((GROUPS,), np.int32)
    target_c = {}
    final = {(batch, half): [] for batch in range(2) for half in range(2)}
    for h in range(2):
        for z in range(NZ):
            own = block(h, z)
            for batch in range(2):
                units = units_of(None, PAIRS_B if batch else PAIRS_A, h, z)
                count = len(units)
                if batch:
                    units += units_of(None, PAIRS_C, h, z)
                places = assign(units, batch, h, z)
                for at, (unit, place) in enumerate(zip(units, places)):
                    code, row, col, half = unit
                    x, core = place // 2, place % 2
                    if at < count:
                        tables[batch, own, core, x] = code
                    else:
                        code_c[own] = code
                        target_c[own] = (batch, x, core)
                    final[batch, half].append((device(batch, x, core, own), col * GROUPS + row))
    local = np.zeros((2, 16, GROUPS, 2, NX), np.int32)
    for aux in range(16):
        x, core = aux // 2 % NX, aux % 2
        for j in range(NX):
            local[:, aux, :, 0, j] = tables[:, :, core, (x + j) % NX]
            local[:, aux, :, 1, j] = tables[:, :, 1 - core, (x + j) % NX]
    target_d = {b: (b // 8, b // 2 % NX, b % 2) for b in range(GROUPS)}
    return local, code_c, target_c, target_d, final


def dot_t(a, b):
    return lax.dot_general(a, b, (((1,), (1,)), ((), ())), preferred_element_type=jnp.float32)


def half_product(rows, cols, half):
    at = pl.ds(pl.multiple_of(half * 256, 256), 256)
    total = dot_t(rows[0, at, :], cols[0])
    for k in range(1, rows.shape[0]):
        total += dot_t(rows[k, at, :], cols[k])
    return total


def units_kernel(index_pairs, table, *refs):
    held, out = refs[:-1], refs[-1]

    def slot(j, carry):
        code = table[j]
        half = code % 2
        for at, (first, second) in enumerate(index_pairs):

            @pl.when(code // 2 == at * 2)
            def _():
                out[j] = half_product(held[first], held[second], half)

            @pl.when(code // 2 == at * 2 + 1)
            def _():
                out[j] = half_product(held[second], held[first], half)

        @pl.when(code == EMPTY)
        def _():
            out[j] = jnp.zeros(out.shape[1:], jnp.float32)

        return carry

    lax.fori_loop(0, out.shape[0], slot, 0)


def products(table, held, names, pairs):
    index_pairs = tuple((names.index(a), names.index(b)) for a, b, _ in pairs)
    return pl.pallas_call(
        functools.partial(units_kernel, index_pairs),
        out_shape=jax.ShapeDtypeStruct((table.shape[0], 256, 512), jnp.float32),
        in_specs=[pl.BlockSpec(memory_space=pltpu.SMEM)]
        + [pl.BlockSpec(memory_space=pltpu.VMEM)] * len(held),
        out_specs=pl.BlockSpec(memory_space=pltpu.VMEM),
        compiler_params=pltpu.CompilerParams(vmem_limit_bytes=VMEM_LIMIT),
    )(table, *held)


def square_kernel(own, out):
    total = dot_t(own[0], own[0])
    for k in range(1, own.shape[0]):
        total += dot_t(own[k], own[k])
    out[...] = total


def square(own):
    return pl.pallas_call(
        square_kernel,
        out_shape=jax.ShapeDtypeStruct((own.shape[1],) * 2, jnp.float32),
        in_specs=[pl.BlockSpec(memory_space=pltpu.VMEM)],
        out_specs=pl.BlockSpec(memory_space=pltpu.VMEM),
        compiler_params=pltpu.CompilerParams(vmem_limit_bytes=VMEM_LIMIT),
    )(own)


def to_one(value, targets):
    def pairs(source, only):
        return [
            (device(*source(y, x, c), b), device(*only(y, x, c), b))
            for b, (y, x, c) in targets.items()
        ]

    middle = value.shape[0] // 2
    steps = [(y, dx) for y in range(2) for dx in range(NX)]
    across = [
        (device(y, tx + dx, 1 - tc, b), device(y, tx + dx, tc, b))
        for b, (_, tx, tc) in targets.items()
        for y, dx in steps
    ]
    value = value + send(value, across)

    def along(offset_from, offset_to):
        return [
            (device(y, tx + offset_from, tc, b), device(y, tx + offset_to, tc, b))
            for b, (_, tx, tc) in targets.items()
            for y in range(2)
        ]

    top = send(value[:middle], along(2, 1))
    bottom = send(value[middle:], along(2, 3))
    value = value + jnp.concatenate([top, bottom], 0)
    value = value + send(value, along(1, 0)) + send(value, along(3, 0))
    last = [(device(1 - ty, tx, tc, b), device(ty, tx, tc, b)) for b, (ty, tx, tc) in targets.items()]
    return value + send(value, last)


CORE_SWAP = every(lambda y, x, c, h, z: (y, x, 1 - c, block(h, z)))
FROM_LEFT = every(lambda y, x, c, h, z: (y, x - 1, c, block(h, z)))
FROM_RIGHT = every(lambda y, x, c, h, z: (y, x + 1, c, block(h, z)))
FROM_UP = every(lambda y, x, c, h, z: (y, x, c, block(h, z + 1)))
FROM_DOWN = every(lambda y, x, c, h, z: (y, x, c, block(h, z - 1)))
FROM_OTHER = every(lambda y, x, c, h, z: (y, x, c, block(h + 1, z)))


def reduced(keep, given, y_to):
    got = send(given, CORE_SWAP)
    middle = keep.shape[1] // 2
    far_top = send(keep[2, :middle] + got[2, :middle], FROM_LEFT)
    far_bottom = send(keep[2, middle:] + got[2, middle:], FROM_RIGHT)
    right = keep[1] + got[1]
    right = jnp.concatenate([right[:middle] + far_top, right[middle:]], 0)
    left = keep[3] + got[3]
    left = jnp.concatenate([left[:middle], left[middle:] + far_bottom], 0)
    total = keep[0] + got[0] + send(right, FROM_LEFT) + send(left, FROM_RIGHT)
    over = [
        (device(1 - y_to, x, core, b), device(y_to, x, core, b))
        for x in range(NX)
        for core in range(2)
        for b in range(GROUPS)
    ]
    return total + send(total, over)


def per_device(half_b):
    local, code_c, target_c, target_d, final = plan()
    aux, blk = lax.axis_index("aux"), lax.axis_index("blk")
    tables = jnp.asarray(local.transpose(1, 2, 0, 3, 4).reshape(256, 4, NX))[aux * GROUPS + blk]
    table_c = jnp.asarray(code_c)[blk].reshape(1)

    held = {O: half_b}
    held[PZ] = send(half_b, FROM_UP)
    held[MZ] = send(half_b, FROM_DOWN)
    held[Y0] = send(half_b, FROM_OTHER)
    diagonal = to_one(square(half_b), target_d)

    held[PP] = send(held[PZ], FROM_UP)
    held[MM] = send(held[MZ], FROM_DOWN)
    held[Y1] = send(held[PZ], FROM_OTHER)

    names = HELD_A
    have = [held[n] for n in names]
    given = products(tables[1], have, names, PAIRS_A)
    keep = products(tables[0], have, names, PAIRS_A)
    done_a = reduced(keep, given, 0)
    top = send(done_a, final[0, 0])
    bottom = send(done_a, final[0, 1])

    held[Y2] = send(held[PP], FROM_OTHER)
    names = HELD_B
    have = [held[n] for n in names]
    given = products(tables[3], have, names, PAIRS_B)
    keep = products(tables[2], have, names, PAIRS_B)
    done_b = reduced(keep, given, 1)

    done_c = products(table_c, [held[n] for n in HELD_C], HELD_C, PAIRS_C)
    done_c = to_one(done_c[0], target_c)
    place_c = np.zeros((GROUPS,), np.int32)
    for b, (y, x, core) in target_c.items():
        place_c[b] = (y * NX + x) * 2 + core
    done_b = jnp.where(aux == jnp.asarray(place_c)[blk], done_c, done_b)
    top = top + send(done_b, final[1, 0])
    bottom = bottom + send(done_b, final[1, 1])
    other = jnp.concatenate([top, bottom], 0)
    return jnp.where(aux == blk, diagonal, other)


def solution(mesh):
    placed = (P("aux", "blk", None),)
    return jax.shard_map(
        per_device, mesh=mesh, in_specs=placed, out_specs=P("blk", "aux"), check_vma=False
    )
```

time: 517 us -> 200 us (0.39)
  the two profiles are of different devices: /device:TPU:12 before, /device:TPU:30 now
where the time goes in v1:
time: 200 us; the launch traced here: 199 us
  waiting for transfers between devices  88.2 us (44%)
  starting transfers between devices  64.8 us (32%)
  Pallas kernels  23.7 us (12%)
  other arithmetic  17.4 us (9%)
  local copies, waits for them, and re-layouts  4.27 us (2%)
    ppermute x35, waiting for transfers between devices, send(): return lax.ppermute(value, ALL, pairs)  88.2 us
    ppermute x35, starting transfers between devices, send(): return lax.ppermute(value, ALL, pairs)  64.8 us
    pallas_call x5, Pallas kernels, products(): pl.pallas_call(functools.partial(units_kernel, index_pairs), out_shape=ja...  22 us
  transfers between devices with their start and end apart: 35, of which 15 were waited for; matrix products, arithmetic and copies ran while one was open for 9% of the time, Pallas kernels for 12%

profile of v1, /device:TPU:30, one launch (start us, length us, event | category | flops | bytes accessed | tf_op | source)
XLA Modules:
  0.0 199.3 jit_solution(537419840756008834)
XLA Ops:
  0.0 5.9 %collective-permute-start.6 = (bf16[2,512,512]{2,1,0:T(8,128)(2,1)}, bf16[2,512,512]{2,1,0:T(8,128)(2,1)S(1)}, u32[]{:S(2)}, u32[]{:S(2)}) collective-permute-start(bf16[2,512,512]{2,1,0:T(8,128)(2,1)} %refs_0_.3), channel_id=1, source_target_pairs={{1,0},{2,1},{3,2},{4,3},{5,4},{6,5},{7,6},{0,7},{9,8},{10,9},{11,1... | collective-permute-start | bytes 3145736 | tf_op jit(solution)/shard_map/ppermute | solution.py:37
  8.4 1.7 shard_map.46
  12.1 16.5 %collective-permute-done.6.refs_1_ = bf16[2,512,512]{2,1,0:T(8,128)(2,1)S(1)} collective-permute-done((bf16[2,512,512]{2,1,0:T(8,128)(2,1)}, bf16[2,512,512]{2,1,0:T(8,128)(2,1)S(1)}, u32[]{:S(2)}, u32[]{:S(2)}) %collective-permute-start.6) | collective-permute-done | bytes 1048608 | tf_op jit(solution)/shard_map/ppermute | solution.py:37
  28.6 3.3 %collective-permute-done.7.refs_2_.refs_0_ = bf16[2,512,512]{2,1,0:T(8,128)(2,1)S(1)} collective-permute-done((bf16[2,512,512]{2,1,0:T(8,128)(2,1)}, bf16[2,512,512]{2,1,0:T(8,128)(2,1)S(1)}, u32[]{:S(2)}, u32[]{:S(2)}) %collective-permute-start.7) | collective-permute-done | bytes 1048608 | tf_op jit(solution)/shard_map/ppermute | solution.py:37
  32.3 4.7 %shard_map.48 = f32[4,256,512]{2,1,0:T(8,128)} custom-call(s32[4]{0:T(128)S(1)} %get-tuple-element.19.table, bf16[2,512,512]{2,1,0:T(8,128)(2,1)S(1)} %copy-done.1, bf16[2,512,512]{2,1,0:T(8,128)(2,1)S(1)} %collective-permute-done.6.refs_1_, bf16[2,512,512]{2,1,0:T(8,128)(2,1)S(1)} %collective-permute-done.7.refs_2_.refs_0_, ...), custom_call_target="tpu_custom_call" | custom-call | tf_op jit(solution)/shard_map/pallas_call | solution.py:171
  37.0 2.5 %collective-permute-start.17 = (bf16[2,512,512]{2,1,0:T(8,128)(2,1)S(1)}, bf16[2,512,512]{2,1,0:T(8,128)(2,1)}, u32[]{:S(2)}, u32[]{:S(2)}) collective-permute-start(bf16[2,512,512]{2,1,0:T(8,128)(2,1)S(1)} %collective-permute-done.6.refs_1_), channel_id=1, source_target_pairs={{1,0},{2,1},{3,2},{4,3},{5,4},{6,5},{7,6},{0,7},{9,8},{10,9},{11,1... | collective-permute-start | bytes 3145736 | tf_op jit(solution)/shard_map/ppermute | solution.py:37
  39.5 1.7 add.128
  43.6 1.7 collective-permute-start.25
  45.4 7.9 %collective-permute-done.2 = f32[256,512]{1,0:T(8,128)S(1)} collective-permute-done((f32[256,512]{1,0:T(8,128)S(1)}, f32[256,512]{1,0:T(8,128)S(1)}, u32[]{:S(2)}, u32[]{:S(2)}) %collective-permute-start.2) | collective-permute-done | bytes 524320 | tf_op jit(solution)/shard_map/ppermute | solution.py:37
  54.8 7.9 %collective-permute-done.17.refs_2_ = bf16[2,512,512]{2,1,0:T(8,128)(2,1)} collective-permute-done((bf16[2,512,512]{2,1,0:T(8,128)(2,1)S(1)}, bf16[2,512,512]{2,1,0:T(8,128)(2,1)}, u32[]{:S(2)}, u32[]{:S(2)}) %collective-permute-start.17) | collective-permute-done | bytes 1048608 | tf_op jit(solution)/shard_map/ppermute | solution.py:37
  64.9 4.4 %shard_map.47 = f32[4,256,512]{2,1,0:T(8,128)} custom-call(s32[4]{0:T(128)S(1)} %get-tuple-element.20.table, bf16[2,512,512]{2,1,0:T(8,128)(2,1)S(1)} %copy-done.1, bf16[2,512,512]{2,1,0:T(8,128)(2,1)S(1)} %collective-permute-done.6.refs_1_, bf16[2,512,512]{2,1,0:T(8,128)(2,1)S(1)} %collective-permute-done.7.refs_2_.refs_0_, ...), custom_call_target="tpu_custom_call" | custom-call | tf_op jit(solution)/shard_map/pallas_call | solution.py:171
  70.5 2.6 %collective-permute-start.4 = (f32[512,512]{1,0:T(8,128)S(1)}, f32[512,512]{1,0:T(8,128)S(1)}, u32[]{:S(2)}, u32[]{:S(2)}) collective-permute-start(f32[512,512]{1,0:T(8,128)S(1)} %maximum_add_fusion), channel_id=1, source_target_pairs={{96,0},{224,128},{113,17},{241,145},{2,34},{130,162},{19,51},{147,... | collective-permute-start | bytes 3145736 | tf_op jit(solution)/shard_map/ppermute | solution.py:37
  73.1 5.3 %shard_map.51 = f32[4,256,512]{2,1,0:T(8,128)} custom-call(s32[4]{0:T(128)S(1)} %get-tuple-element.18.table, bf16[2,512,512]{2,1,0:T(8,128)(2,1)S(1)} %collective-permute-done.7.refs_2_.refs_0_, bf16[2,512,512]{2,1,0:T(8,128)(2,1)S(1)} %collective-permute-done.6.refs_1_, bf16[2,512,512]{2,1,0:T(8,128)(2,1)} %collective-permute-done.17.refs_2_, ...), custom_call_target="tpu_custom_call" | custom-call | tf_op jit(solution)/shard_map/pallas_call | solution.py:171
  78.5 5.0 %shard_map.50 = f32[4,256,512]{2,1,0:T(8,128)} custom-call(s32[4]{0:T(128)S(1)} %get-tuple-element.17.table, bf16[2,512,512]{2,1,0:T(8,128)(2,1)S(1)} %collective-permute-done.7.refs_2_.refs_0_, bf16[2,512,512]{2,1,0:T(8,128)(2,1)S(1)} %collective-permute-done.6.refs_1_, bf16[2,512,512]{2,1,0:T(8,128)(2,1)} %collective-permute-done.17.refs_2_, ...), custom_call_target="tpu_custom_call" | custom-call | tf_op jit(solution)/shard_map/pallas_call | solution.py:171
  87.0 2.4 %collective-permute-start.10 = (f32[128,512]{1,0:T(8,128)S(1)}, f32[128,512]{1,0:T(8,128)S(1)}, u32[]{:S(2)}, u32[]{:S(2)}) collective-permute-start(f32[128,512]{1,0:T(8,128)S(1)} %get-tuple-element.9), channel_id=1, source_target_pairs={{96,0},{97,1},{98,2},{99,3},{100,4},{101,5},{102,6},{103,7},{104,8... | collective-permute-start | bytes 786440 | tf_op jit(solution)/shard_map/ppermute | solution.py:37
  89.4 3.1 %collective-permute-done.18.refs_1_ = bf16[2,512,512]{2,1,0:T(8,128)(2,1)} collective-permute-done((bf16[2,512,512]{2,1,0:T(8,128)(2,1)}, bf16[2,512,512]{2,1,0:T(8,128)(2,1)}, u32[]{:S(2)}, u32[]{:S(2)}) %collective-permute-start.18) | collective-permute-done | bytes 1048608 | tf_op jit(solution)/shard_map/ppermute | solution.py:37
  92.5 2.6 %shard_map.49 = f32[1,256,512]{2,1,0:T(8,128)S(1)} custom-call(s32[1]{0:T(128)} %dynamic_slice.11.table, bf16[2,512,512]{2,1,0:T(8,128)(2,1)} %collective-permute-done.16.refs_0_.refs_3_, bf16[2,512,512]{2,1,0:T(8,128)(2,1)} %collective-permute-done.18.refs_1_), custom_call_target="tpu_custom_call" | custom-call | tf_op jit(solution)/shard_map/pallas_call | solution.py:171
  96.5 2.2 %collective-permute-start.13 = (f32[256,512]{1,0:T(8,128)S(1)}, f32[256,512]{1,0:T(8,128)S(1)}, u32[]{:S(2)}, u32[]{:S(2)}) collective-permute-start(f32[256,512]{1,0:T(8,128)S(1)} %pad_maximum_fusion.1), channel_id=1, source_target_pairs={{32,0},{33,1},{34,2},{35,3},{36,4},{37,5},{38,6},{39,7},{40,8},{41... | collective-permute-start | bytes 1572872 | tf_op jit(solution)/shard_map/ppermute | solution.py:37
  102.5 10.2 %collective-permute-start.29 = (f32[128,512]{1,0:T(8,128)S(1)}, f32[128,512]{1,0:T(8,128)S(1)}, u32[]{:S(2)}, u32[]{:S(2)}) collective-permute-start(f32[128,512]{1,0:T(8,128)S(1)} %get-tuple-element.6), channel_id=1, source_target_pairs={{32,0},{33,1},{34,2},{35,3},{36,4},{37,5},{38,6},{39,7},{40,8},{41... | collective-permute-start | bytes 786440 | tf_op jit(solution)/shard_map/ppermute | solution.py:37
  112.9 5.0 %collective-permute-start.27 = (f32[128,512]{1,0:T(8,128)S(1)}, f32[128,512]{1,0:T(8,128)S(1)}, u32[]{:S(2)}, u32[]{:S(2)}) collective-permute-start(f32[128,512]{1,0:T(8,128)S(1)} %get-tuple-element.5), channel_id=1, source_target_pairs={{96,0},{97,1},{98,2},{99,3},{100,4},{101,5},{102,6},{103,7},{104,8... | collective-permute-start | bytes 786440 | tf_op jit(solution)/shard_map/ppermute | solution.py:37
  118.0 4.0 %collective-permute-done.29 = f32[128,512]{1,0:T(8,128)S(1)} collective-permute-done((f32[128,512]{1,0:T(8,128)S(1)}, f32[128,512]{1,0:T(8,128)S(1)}, u32[]{:S(2)}, u32[]{:S(2)}) %collective-permute-start.29) | collective-permute-done | bytes 262176 | tf_op jit(solution)/shard_map/ppermute | solution.py:37
  125.5 2.7 %collective-permute-start.30 = (f32[256,512]{1,0:T(8,128)S(1)}, f32[256,512]{1,0:T(8,128)S(1)}, u32[]{:S(2)}, u32[]{:S(2)}) collective-permute-start(f32[256,512]{1,0:T(8,128)S(1)} %pad_maximum_fusion.3), channel_id=1, source_target_pairs={{32,0},{33,1},{34,2},{35,3},{36,4},{37,5},{38,6},{39,7},{40,8},{41... | collective-permute-start | bytes 1572872 | tf_op jit(solution)/shard_map/ppermute | solution.py:37
  128.2 5.4 %collective-permute-done.23 = f32[256,512]{1,0:T(8,128)S(1)} collective-permute-done((f32[256,512]{1,0:T(8,128)S(1)}, f32[256,512]{1,0:T(8,128)S(1)}, u32[]{:S(2)}, u32[]{:S(2)}) %collective-permute-start.23) | collective-permute-done | bytes 524320 | tf_op jit(solution)/shard_map/ppermute | solution.py:37
  136.4 3.5 %collective-permute-start.14 = (f32[256,512]{1,0:T(8,128)S(1)}, f32[256,512]{1,0:T(8,128)}, u32[]{:S(2)}, u32[]{:S(2)}) collective-permute-start(f32[256,512]{1,0:T(8,128)S(1)} %fusion.5), channel_id=1, source_target_pairs={{128,0},{129,1},{130,2},{131,3},{132,4},{133,5},{134,6},{135,7},{1... | collective-permute-start | bytes 1572872 | tf_op jit(solution)/shard_map/ppermute | solution.py:37
  145.2 1.7 collective-permute-start.5
  150.5 2.9 %collective-permute-done.24 = f32[256,512]{1,0:T(8,128)} collective-permute-done((f32[256,512]{1,0:T(8,128)}, f32[256,512]{1,0:T(8,128)}, u32[]{:S(2)}, u32[]{:S(2)}) %collective-permute-start.24) | collective-permute-done | bytes 524320 | tf_op jit(solution)/shard_map/ppermute | solution.py:37
  153.4 22.5 %collective-permute-done.31 = f32[256,512]{1,0:T(8,128)} collective-permute-done((f32[256,512]{1,0:T(8,128)S(1)}, f32[256,512]{1,0:T(8,128)}, u32[]{:S(2)}, u32[]{:S(2)}) %collective-permute-start.31) | collective-permute-done | bytes 524320 | tf_op jit(solution)/shard_map/ppermute | solution.py:37
  175.9 2.4 %add_select_fusion = f32[256,512]{1,0:T(8,128)} fusion(f32[256,512]{1,0:T(8,128)S(1)} %fusion.2, f32[256,512]{1,0:T(8,128)} %collective-permute-done.31, f32[256,512]{1,0:T(8,128)} %add_add_fusion.1, f32[256,512]{1,0:T(8,128)} %collective-permute-done.24, pred[]{:T(512)S(6)} %eq.7), kind=kLoop, calls=%fused_computation.20 | loop fusion | flops 393216 | bytes 2621441 | tf_op jit(solution)/shard_map/jit(_where)/select_n | solution.py:292
  178.2 2.1 %collective-permute-start.34 = (f32[256,512]{1,0:T(8,128)}, f32[256,512]{1,0:T(8,128)}, u32[]{:S(2)}, u32[]{:S(2)}) collective-permute-start(f32[256,512]{1,0:T(8,128)} %add_select_fusion), channel_id=1, source_target_pairs={{240,97},{224,98},{208,151},{144,150},{225,114},{241,115},{193,160... | collective-permute-start | bytes 1572872 | tf_op jit(solution)/shard_map/ppermute | solution.py:37
  183.1 3.4 %collective-permute-done.34 = f32[256,512]{1,0:T(8,128)} collective-permute-done((f32[256,512]{1,0:T(8,128)}, f32[256,512]{1,0:T(8,128)}, u32[]{:S(2)}, u32[]{:S(2)}) %collective-permute-start.34) | collective-permute-done | bytes 524320 | tf_op jit(solution)/shard_map/ppermute | solution.py:37
  187.6 8.0 %collective-permute-done.15 = f32[256,512]{1,0:T(8,128)S(1)} collective-permute-done((f32[256,512]{1,0:T(8,128)S(1)}, f32[256,512]{1,0:T(8,128)S(1)}, u32[]{:S(2)}, u32[]{:S(2)}) %collective-permute-start.15) | collective-permute-done | bytes 524320 | tf_op jit(solution)/shard_map/ppermute | solution.py:37
  196.8 2.5 %maximum_select_fusion = f32[512,512]{1,0:T(8,128)} fusion(f32[256,512]{1,0:T(8,128)S(1)} %add.168, f32[256,512]{1,0:T(8,128)S(1)} %add.167, f32[512,512]{1,0:T(8,128)S(1)} %add_add_fusion, f32[512,512]{1,0:T(8,128)} %collective-permute-done.5, pred[]{:T(512)S(6)} %eq.6), kind=kLoop, calls=%fused_computation.1 | loop fusion | flops 786432 | bytes 4194305 | tf_op jit(solution)/shard_map/jit(_where)/select_n | solution.py:296
  (99 shorter events, 40.7 us)
Async XLA Ops:
  0.0 28.6 %collective-permute-start.6 = (bf16[2,512,512]{2,1,0:T(8,128)(2,1)}, bf16[2,512,512]{2,1,0:T(8,128)(2,1)S(1)}, u32[]{:S(2)}, u32[]{:S(2)}) collective-permute-start(bf16[2,512,512]{2,1,0:T(8,128)(2,1)} %refs_0_.3), channel_id=1, source_target_pairs={{1,0},{2,1},{3,2},{4,3},{5,4},{6,5},{7,6},{0,7},{9,8},{10,9},{11,1... | collective-permute-start | bytes 3145736 | tf_op jit(solution)/shard_map/ppermute | solution.py:37
  5.9 26.0 %collective-permute-start.7 = (bf16[2,512,512]{2,1,0:T(8,128)(2,1)}, bf16[2,512,512]{2,1,0:T(8,128)(2,1)S(1)}, u32[]{:S(2)}, u32[]{:S(2)}) collective-permute-start(bf16[2,512,512]{2,1,0:T(8,128)(2,1)} %refs_0_.3), channel_id=1, source_target_pairs={{7,0},{0,1},{1,2},{2,3},{3,4},{4,5},{5,6},{6,7},{15,8},{8,9},{9,10... | collective-permute-start | bytes 3145736 | tf_op jit(solution)/shard_map/ppermute | solution.py:37
  5.9 26.4 %collective-permute-start.8 = (bf16[2,512,512]{2,1,0:T(8,128)(2,1)}, bf16[2,512,512]{2,1,0:T(8,128)(2,1)}, u32[]{:S(2)}, u32[]{:S(2)}) collective-permute-start(bf16[2,512,512]{2,1,0:T(8,128)(2,1)} %refs_0_.3), channel_id=1, source_target_pairs={{8,0},{9,1},{10,2},{11,3},{12,4},{13,5},{14,6},{15,7},{0,8},{1,9},... | collective-permute-start | bytes 3145736 | tf_op jit(solution)/shard_map/ppermute | solution.py:37
  10.1 29.4 %collective-permute-start = (f32[512,512]{1,0:T(8,128)}, f32[512,512]{1,0:T(8,128)}, u32[]{:S(2)}, u32[]{:S(2)}) collective-permute-start(f32[512,512]{1,0:T(8,128)} %shard_map.46), channel_id=1, source_target_pairs={{16,0},{48,32},{80,64},{112,96},{144,128},{176,160},{208,192},{240... | collective-permute-start | bytes 3145736 | tf_op jit(solution)/shard_map/ppermute | solution.py:37
  37.0 46.5 %collective-permute-start.9 = (f32[4,256,512]{2,1,0:T(8,128)}, f32[4,256,512]{2,1,0:T(8,128)}, u32[]{:S(2)}, u32[]{:S(2)}) collective-permute-start(f32[4,256,512]{2,1,0:T(8,128)} %shard_map.48), channel_id=1, source_target_pairs={{16,0},{17,1},{18,2},{19,3},{20,4},{21,5},{22,6},{23,7},{24,8},{25... | collective-permute-start | bytes 6291464 | tf_op jit(solution)/shard_map/ppermute | solution.py:37
  37.0 25.7 %collective-permute-start.17 = (bf16[2,512,512]{2,1,0:T(8,128)(2,1)S(1)}, bf16[2,512,512]{2,1,0:T(8,128)(2,1)}, u32[]{:S(2)}, u32[]{:S(2)}) collective-permute-start(bf16[2,512,512]{2,1,0:T(8,128)(2,1)S(1)} %collective-permute-done.6.refs_1_), channel_id=1, source_target_pairs={{1,0},{2,1},{3,2},{4,3},{5,4},{6,5},{7,6},{0,7},{9,8},{10,9},{11,1... | collective-permute-start | bytes 3145736 | tf_op jit(solution)/shard_map/ppermute | solution.py:37
  42.2 11.1 %collective-permute-start.2 = (f32[256,512]{1,0:T(8,128)S(1)}, f32[256,512]{1,0:T(8,128)S(1)}, u32[]{:S(2)}, u32[]{:S(2)}) collective-permute-start(f32[256,512]{1,0:T(8,128)S(1)} %get-tuple-element.14), channel_id=1, source_target_pairs={{64,96},{192,224},{81,113},{209,241},{98,2},{226,130},{115,19},{24... | collective-permute-start | bytes 1572872 | tf_op jit(solution)/shard_map/ppermute | solution.py:37
  43.5 29.6 %collective-permute-start.16 = (bf16[2,512,512]{2,1,0:T(8,128)(2,1)S(1)}, bf16[2,512,512]{2,1,0:T(8,128)(2,1)}, u32[]{:S(2)}, u32[]{:S(2)}) collective-permute-start(bf16[2,512,512]{2,1,0:T(8,128)(2,1)S(1)} %collective-permute-done.7.refs_2_.refs_0_), channel_id=1, source_target_pairs={{7,0},{0,1},{1,2},{2,3},{3,4},{4,5},{5,6},{6,7},{15,8},{8,9},{9,10... | collective-permute-start | bytes 3145736 | tf_op jit(solution)/shard_map/ppermute | solution.py:37
  43.6 29.5 %collective-permute-start.25 = (bf16[2,512,512]{2,1,0:T(8,128)(2,1)S(1)}, bf16[2,512,512]{2,1,0:T(8,128)(2,1)}, u32[]{:S(2)}, u32[]{:S(2)}) collective-permute-start(bf16[2,512,512]{2,1,0:T(8,128)(2,1)S(1)} %collective-permute-done.6.refs_1_), channel_id=1, source_target_pairs={{8,0},{9,1},{10,2},{11,3},{12,4},{13,5},{14,6},{15,7},{0,8},{1,9},... | collective-permute-start | bytes 3145736 | tf_op jit(solution)/shard_map/ppermute | solution.py:37
  53.3 15.9 %collective-permute-start.1 = (f32[256,512]{1,0:T(8,128)}, f32[256,512]{1,0:T(8,128)}, u32[]{:S(2)}, u32[]{:S(2)}) collective-permute-start(f32[256,512]{1,0:T(8,128)} %get-tuple-element.13), channel_id=1, source_target_pairs={{64,32},{192,160},{81,49},{209,177},{98,66},{226,194},{115,83},{24... | collective-permute-start | bytes 1572872 | tf_op jit(solution)/shard_map/ppermute | solution.py:37
  62.6 29.8 %collective-permute-start.18 = (bf16[2,512,512]{2,1,0:T(8,128)(2,1)}, bf16[2,512,512]{2,1,0:T(8,128)(2,1)}, u32[]{:S(2)}, u32[]{:S(2)}) collective-permute-start(bf16[2,512,512]{2,1,0:T(8,128)(2,1)} %collective-permute-done.17.refs_2_), channel_id=1, source_target_pairs={{8,0},{9,1},{10,2},{11,3},{12,4},{13,5},{14,6},{15,7},{0,8},{1,9},... | collective-permute-start | bytes 3145736 | tf_op jit(solution)/shard_map/ppermute | solution.py:37
  70.5 74.4 %collective-permute-start.4 = (f32[512,512]{1,0:T(8,128)S(1)}, f32[512,512]{1,0:T(8,128)S(1)}, u32[]{:S(2)}, u32[]{:S(2)}) collective-permute-start(f32[512,512]{1,0:T(8,128)S(1)} %maximum_add_fusion), channel_id=1, source_target_pairs={{96,0},{224,128},{113,17},{241,145},{2,34},{130,162},{19,51},{147,... | collective-permute-start | bytes 3145736 | tf_op jit(solution)/shard_map/ppermute | solution.py:37
  78.5 24.0 %collective-permute-start.26 = (f32[4,256,512]{2,1,0:T(8,128)}, f32[4,256,512]{2,1,0:T(8,128)S(1)}, u32[]{:S(2)}, u32[]{:S(2)}) collective-permute-start(f32[4,256,512]{2,1,0:T(8,128)} %shard_map.51), channel_id=1, source_target_pairs={{16,0},{17,1},{18,2},{19,3},{20,4},{21,5},{22,6},{23,7},{24,8},{25... | collective-permute-start | bytes 6291464 | tf_op jit(solution)/shard_map/ppermute | solution.py:37
  84.6 11.9 %collective-permute-start.12 = (f32[128,512]{1,0:T(8,128)S(1)}, f32[128,512]{1,0:T(8,128)S(1)}, u32[]{:S(2)}, u32[]{:S(2)}) collective-permute-start(f32[128,512]{1,0:T(8,128)S(1)} %get-tuple-element.10), channel_id=1, source_target_pairs={{32,0},{33,1},{34,2},{35,3},{36,4},{37,5},{38,6},{39,7},{40,8},{41... | collective-permute-start | bytes 786440 | tf_op jit(solution)/shard_map/ppermute | solution.py:37
  87.0 12.9 %collective-permute-start.10 = (f32[128,512]{1,0:T(8,128)S(1)}, f32[128,512]{1,0:T(8,128)S(1)}, u32[]{:S(2)}, u32[]{:S(2)}) collective-permute-start(f32[128,512]{1,0:T(8,128)S(1)} %get-tuple-element.9), channel_id=1, source_target_pairs={{96,0},{97,1},{98,2},{99,3},{100,4},{101,5},{102,6},{103,7},{104,8... | collective-permute-start | bytes 786440 | tf_op jit(solution)/shard_map/ppermute | solution.py:37
  96.5 27.6 %collective-permute-start.13 = (f32[256,512]{1,0:T(8,128)S(1)}, f32[256,512]{1,0:T(8,128)S(1)}, u32[]{:S(2)}, u32[]{:S(2)}) collective-permute-start(f32[256,512]{1,0:T(8,128)S(1)} %pad_maximum_fusion.1), channel_id=1, source_target_pairs={{32,0},{33,1},{34,2},{35,3},{36,4},{37,5},{38,6},{39,7},{40,8},{41... | collective-permute-start | bytes 1572872 | tf_op jit(solution)/shard_map/ppermute | solution.py:37
  100.7 24.8 %collective-permute-start.11 = (f32[256,512]{1,0:T(8,128)S(1)}, f32[256,512]{1,0:T(8,128)S(1)}, u32[]{:S(2)}, u32[]{:S(2)}) collective-permute-start(f32[256,512]{1,0:T(8,128)S(1)} %pad_maximum_fusion), channel_id=1, source_target_pairs={{96,0},{97,1},{98,2},{99,3},{100,4},{101,5},{102,6},{103,7},{104,8... | collective-permute-start | bytes 1572872 | tf_op jit(solution)/shard_map/ppermute | solution.py:37
  102.5 19.4 %collective-permute-start.29 = (f32[128,512]{1,0:T(8,128)S(1)}, f32[128,512]{1,0:T(8,128)S(1)}, u32[]{:S(2)}, u32[]{:S(2)}) collective-permute-start(f32[128,512]{1,0:T(8,128)S(1)} %get-tuple-element.6), channel_id=1, source_target_pairs={{32,0},{33,1},{34,2},{35,3},{36,4},{37,5},{38,6},{39,7},{40,8},{41... | collective-permute-start | bytes 786440 | tf_op jit(solution)/shard_map/ppermute | solution.py:37
  112.9 10.4 %collective-permute-start.27 = (f32[128,512]{1,0:T(8,128)S(1)}, f32[128,512]{1,0:T(8,128)S(1)}, u32[]{:S(2)}, u32[]{:S(2)}) collective-permute-start(f32[128,512]{1,0:T(8,128)S(1)} %get-tuple-element.5), channel_id=1, source_target_pairs={{96,0},{97,1},{98,2},{99,3},{100,4},{101,5},{102,6},{103,7},{104,8... | collective-permute-start | bytes 786440 | tf_op jit(solution)/shard_map/ppermute | solution.py:37
  122.0 11.6 %collective-permute-start.23 = (f32[256,512]{1,0:T(8,128)S(1)}, f32[256,512]{1,0:T(8,128)S(1)}, u32[]{:S(2)}, u32[]{:S(2)}) collective-permute-start(f32[256,512]{1,0:T(8,128)S(1)} %maximum_add_fusion.1), channel_id=1, source_target_pairs={{0,32},{128,160},{49,81},{177,209},{66,98},{194,226},{83,115},{211... | collective-permute-start | bytes 1572872 | tf_op jit(solution)/shard_map/ppermute | solution.py:37
  123.3 21.5 %collective-permute-start.3 = (f32[512,512]{1,0:T(8,128)S(1)}, f32[512,512]{1,0:T(8,128)S(1)}, u32[]{:S(2)}, u32[]{:S(2)}) collective-permute-start(f32[512,512]{1,0:T(8,128)S(1)} %maximum_add_fusion), channel_id=1, source_target_pairs={{32,0},{160,128},{49,17},{177,145},{66,34},{194,162},{83,51},{211,... | collective-permute-start | bytes 3145736 | tf_op jit(solution)/shard_map/ppermute | solution.py:37
  124.1 12.3 %collective-permute-start.22 = (f32[256,512]{1,0:T(8,128)S(1)}, f32[256,512]{1,0:T(8,128)S(1)}, u32[]{:S(2)}, u32[]{:S(2)}) collective-permute-start(f32[256,512]{1,0:T(8,128)S(1)} %maximum_add_fusion.1), channel_id=1, source_target_pairs={{64,32},{192,160},{113,81},{241,209},{2,98},{130,226},{19,115},{14... | collective-permute-start | bytes 1572872 | tf_op jit(solution)/shard_map/ppermute | solution.py:37
  125.5 16.5 %collective-permute-start.30 = (f32[256,512]{1,0:T(8,128)S(1)}, f32[256,512]{1,0:T(8,128)S(1)}, u32[]{:S(2)}, u32[]{:S(2)}) collective-permute-start(f32[256,512]{1,0:T(8,128)S(1)} %pad_maximum_fusion.3), channel_id=1, source_target_pairs={{32,0},{33,1},{34,2},{35,3},{36,4},{37,5},{38,6},{39,7},{40,8},{41... | collective-permute-start | bytes 1572872 | tf_op jit(solution)/shard_map/ppermute | solution.py:37
  133.6 9.7 %collective-permute-start.28 = (f32[256,512]{1,0:T(8,128)S(1)}, f32[256,512]{1,0:T(8,128)S(1)}, u32[]{:S(2)}, u32[]{:S(2)}) collective-permute-start(f32[256,512]{1,0:T(8,128)S(1)} %pad_maximum_fusion.2), channel_id=1, source_target_pairs={{96,0},{97,1},{98,2},{99,3},{100,4},{101,5},{102,6},{103,7},{104,8... | collective-permute-start | bytes 1572872 | tf_op jit(solution)/shard_map/ppermute | solution.py:37
  136.4 11.7 %collective-permute-start.14 = (f32[256,512]{1,0:T(8,128)S(1)}, f32[256,512]{1,0:T(8,128)}, u32[]{:S(2)}, u32[]{:S(2)}) collective-permute-start(f32[256,512]{1,0:T(8,128)S(1)} %fusion.5), channel_id=1, source_target_pairs={{128,0},{129,1},{130,2},{131,3},{132,4},{133,5},{134,6},{135,7},{1... | collective-permute-start | bytes 1572872 | tf_op jit(solution)/shard_map/ppermute | solution.py:37
  142.0 11.4 %collective-permute-start.24 = (f32[256,512]{1,0:T(8,128)}, f32[256,512]{1,0:T(8,128)}, u32[]{:S(2)}, u32[]{:S(2)}) collective-permute-start(f32[256,512]{1,0:T(8,128)} %add_add_fusion.1), channel_id=1, source_target_pairs={{32,160},{81,209},{98,226},{115,243},{4,132},{85,213},{38,166},{11... | collective-permute-start | bytes 1572872 | tf_op jit(solution)/shard_map/ppermute | solution.py:37
  143.6 32.3 %collective-permute-start.31 = (f32[256,512]{1,0:T(8,128)S(1)}, f32[256,512]{1,0:T(8,128)}, u32[]{:S(2)}, u32[]{:S(2)}) collective-permute-start(f32[256,512]{1,0:T(8,128)S(1)} %fusion.2), channel_id=1, source_target_pairs={{0,128},{1,129},{2,130},{3,131},{4,132},{5,133},{6,134},{7,135},{8... | collective-permute-start | bytes 1572872 | tf_op jit(solution)/shard_map/ppermute | solution.py:37
  145.2 51.5 %collective-permute-start.5 = (f32[512,512]{1,0:T(8,128)S(1)}, f32[512,512]{1,0:T(8,128)}, u32[]{:S(2)}, u32[]{:S(2)}) collective-permute-start(f32[512,512]{1,0:T(8,128)S(1)} %add_add_fusion), channel_id=1, source_target_pairs={{128,0},{145,17},{162,34},{179,51},{196,68},{213,85},{230,102},{24... | collective-permute-start | bytes 3145736 | tf_op jit(solution)/shard_map/ppermute | solution.py:37
  149.2 33.9 %collective-permute-start.33 = (f32[256,512]{1,0:T(8,128)S(1)}, f32[256,512]{1,0:T(8,128)S(1)}, u32[]{:S(2)}, u32[]{:S(2)}) collective-permute-start(f32[256,512]{1,0:T(8,128)S(1)} %add.147), channel_id=1, source_target_pairs={{48,16},{112,113},{16,135},{81,33},{49,32},{17,144},{114,50},{82,4... | collective-permute-start | bytes 1572872 | tf_op jit(solution)/shard_map/ppermute | solution.py:37
  178.2 8.3 %collective-permute-start.34 = (f32[256,512]{1,0:T(8,128)}, f32[256,512]{1,0:T(8,128)}, u32[]{:S(2)}, u32[]{:S(2)}) collective-permute-start(f32[256,512]{1,0:T(8,128)} %add_select_fusion), channel_id=1, source_target_pairs={{240,97},{224,98},{208,151},{144,150},{225,114},{241,115},{193,160... | collective-permute-start | bytes 1572872 | tf_op jit(solution)/shard_map/ppermute | solution.py:37
  180.4 15.3 %collective-permute-start.15 = (f32[256,512]{1,0:T(8,128)S(1)}, f32[256,512]{1,0:T(8,128)S(1)}, u32[]{:S(2)}, u32[]{:S(2)}) collective-permute-start(f32[256,512]{1,0:T(8,128)S(1)} %add.147), channel_id=1, source_target_pairs={{32,16},{80,113},{96,128},{0,135},{65,33},{33,32},{113,145},{1,144... | collective-permute-start | bytes 1572872 | tf_op jit(solution)/shard_map/ppermute | solution.py:37
  181.6 14.0 %collective-permute-start.32 = (f32[256,512]{1,0:T(8,128)}, f32[256,512]{1,0:T(8,128)}, u32[]{:S(2)}, u32[]{:S(2)}) collective-permute-start(f32[256,512]{1,0:T(8,128)} %add_select_fusion), channel_id=1, source_target_pairs={{192,97},{176,151},{128,150},{160,166},{145,114},{129,160},{161,16... | collective-permute-start | bytes 1572872 | tf_op jit(solution)/shard_map/ppermute | solution.py:37
  (13 other events, 111.6 us)

commit v2 on v1

v2 whole, which is shorter than its diff:
```python
import functools

import jax
import jax.numpy as jnp
import numpy as np
from jax import lax
from jax.experimental import pallas as pl
from jax.experimental.pallas import tpu as pltpu
from jax.sharding import PartitionSpec as P

ALL = ("aux", "blk")
NX, NZ, GROUPS = 4, 8, 16
VMEM_LIMIT = 16 * 2**20


def device(y_lo, x, core, blk):
    return ((y_lo * NX + x % NX) * 2 + core) * GROUPS + blk


def block(h, z):
    return h % 2 * NZ + z % NZ


def every(move):
    return [
        (device(*move(y_lo, x, core, h, z)), device(y_lo, x, core, block(h, z)))
        for y_lo in range(2)
        for x in range(NX)
        for core in range(2)
        for h in range(2)
        for z in range(NZ)
    ]


def send(value, pairs):
    return lax.ppermute(value, ALL, pairs)


O, PZ, MZ, Y0 = (0, 0), (0, 1), (0, -1), (1, 0)
PP, MM, Y1, Y2 = (0, 2), (0, -2), (1, 1), (1, 2)
HELD_A = (O, PZ, MZ, Y0)
HELD_B = (O, MZ, PZ, PP, MM, Y1)
HELD_C = (MM, Y2)


def units_of(pairs, h, z):
    found = []
    for at, (first, second, halves) in enumerate(pairs):
        i, j = block(h + first[0], z + first[1]), block(h + second[0], z + second[1])
        for half in halves(h, z):
            found.append(((at * 2 + (i > j)) * 2 + half, min(i, j), max(i, j), half))
    return found


def both(h, z):
    return (0, 1)


def by_h(h, z):
    return (h,)


def by_z(h, z):
    return (0,) if 2 <= z < 6 else (1,)


def upper(h, z):
    return (0,)


def lower(h, z):
    return (1,)


PAIRS_A = ((O, PZ, both), (MZ, PZ, both), (O, Y0, by_h), (MZ, Y0, both), (O, O, upper))
PAIRS_B = ((MM, PZ, both), (MM, PP, by_z), (MZ, Y1, both), (MM, Y1, both), (O, O, lower))
PAIRS_C = ((MM, Y2, by_h),)


def ring(a, b, n):
    return min((a - b) % n, (b - a) % n)


def hops(y_lo, x, core, h, z, row, col):
    y_at, y_to = h * 2 + y_lo, row // NZ * 2 + col // 8
    return ring(x, col // 2 % NX, NX) + ring(y_at, y_to, 4) + ring(z, row % NZ, NZ) + 0.1 * (core != col % 2)


def assign(units, y_lo, h, z):
    best = {0: (0.0, ())}
    for _, row, col, _ in units:
        grown = {}
        for mask, (cost, taken) in best.items():
            for place in range(8):
                if mask >> place & 1:
                    continue
                total = cost + hops(y_lo, place // 2, place % 2, h, z, row, col) ** 2
                key = mask | 1 << place
                if key not in grown or total < grown[key][0]:
                    grown[key] = (total, taken + (place,))
        best = grown
    return min(best.values())[1]


@functools.cache
def plan():
    tables = np.zeros((2, GROUPS, 2, NX), np.int32)
    code_c = np.zeros((GROUPS,), np.int32)
    target_c = {}
    final = {(batch, half): [] for batch in range(3) for half in range(2)}
    for h in range(2):
        for z in range(NZ):
            own = block(h, z)
            for batch in range(2):
                units = units_of(PAIRS_B if batch else PAIRS_A, h, z)
                for (code, row, col, half), place in zip(units, assign(units, batch, h, z)):
                    x, core = place // 2, place % 2
                    tables[batch, own, core, x] = code
                    final[batch, half].append((device(batch, x, core, own), col * GROUPS + row))
            ((code, row, col, half),) = units_of(PAIRS_C, h, z)
            code_c[own] = code
            target_c[own] = (col // 8, col // 2 % NX, col % 2)
            final[2, half].append((device(*target_c[own], own), col * GROUPS + row))
    local = np.zeros((2, 16, GROUPS, 2, NX), np.int32)
    for aux in range(16):
        x, core = aux // 2 % NX, aux % 2
        for j in range(NX):
            local[:, aux, :, 0, j] = tables[:, :, core, (x + j) % NX]
            local[:, aux, :, 1, j] = tables[:, :, 1 - core, (x + j) % NX]
    return local.reshape(2, 16 * GROUPS, 2 * NX), code_c, target_c, final


def dot_t(a, b):
    return lax.dot_general(a, b, (((1,), (1,)), ((), ())), preferred_element_type=jnp.float32)


def half_product(rows, cols, half):
    at = pl.ds(pl.multiple_of(half * 256, 256), 256)
    total = dot_t(rows[0, at, :], cols[0])
    for k in range(1, rows.shape[0]):
        total += dot_t(rows[k, at, :], cols[k])
    return total


def units_kernel(index_pairs, spare, table, *refs):
    held, outs = refs[: len(refs) - spare], refs[len(refs) - spare :]

    def slot(base, out, j, carry):
        code = table[base + j]
        half = code % 2
        for at, (first, second) in enumerate(index_pairs):

            @pl.when(code // 2 == at * 2)
            def _():
                out[j] = half_product(held[first], held[second], half)

            if first != second:

                @pl.when(code // 2 == at * 2 + 1)
                def _():
                    out[j] = half_product(held[second], held[first], half)

        return carry

    base = 0
    for out in outs:
        lax.fori_loop(0, out.shape[0], functools.partial(slot, base, out), 0)
        base += out.shape[0]


def products(table, held, names, pairs, counts):
    index_pairs = tuple((names.index(a), names.index(b)) for a, b, _ in pairs)
    return pl.pallas_call(
        functools.partial(units_kernel, index_pairs, len(counts)),
        out_shape=[pltpu.VMEM((count, 256, 512), jnp.float32) for count in counts],
        in_specs=[pl.BlockSpec(memory_space=pltpu.SMEM)]
        + [pl.BlockSpec(memory_space=pltpu.VMEM)] * len(held),
        out_specs=[pl.BlockSpec(memory_space=pltpu.VMEM)] * len(counts),
        compiler_params=pltpu.CompilerParams(vmem_limit_bytes=VMEM_LIMIT),
    )(table, *held)


def to_one(value, targets):
    def pairs(source, only):
        return [
            (device(*source(y, x, c), b), device(*only(y, x, c), b))
            for b, (y, x, c) in targets.items()
        ]

    middle = value.shape[0] // 2
    steps = [(y, dx) for y in range(2) for dx in range(NX)]
    across = [
        (device(y, tx + dx, 1 - tc, b), device(y, tx + dx, tc, b))
        for b, (_, tx, tc) in targets.items()
        for y, dx in steps
    ]
    value = value + send(value, across)

    def along(offset_from, offset_to):
        return [
            (device(y, tx + offset_from, tc, b), device(y, tx + offset_to, tc, b))
            for b, (_, tx, tc) in targets.items()
            for y in range(2)
        ]

    top = send(value[:middle], along(2, 1))
    bottom = send(value[middle:], along(2, 3))
    value = value + jnp.concatenate([top, bottom], 0)
    value = value + send(value, along(1, 0)) + send(value, along(3, 0))
    last = [(device(1 - ty, tx, tc, b), device(ty, tx, tc, b)) for b, (ty, tx, tc) in targets.items()]
    return value + send(value, last)


CORE_SWAP = every(lambda y, x, c, h, z: (y, x, 1 - c, block(h, z)))
FROM_LEFT = every(lambda y, x, c, h, z: (y, x - 1, c, block(h, z)))
FROM_RIGHT = every(lambda y, x, c, h, z: (y, x + 1, c, block(h, z)))
FROM_UP = every(lambda y, x, c, h, z: (y, x, c, block(h, z + 1)))
FROM_DOWN = every(lambda y, x, c, h, z: (y, x, c, block(h, z - 1)))
FROM_OTHER = every(lambda y, x, c, h, z: (y, x, c, block(h + 1, z)))


def near(keep, got):
    middle = keep.shape[1] // 2
    far_top = send(keep[2, :middle] + got[2, :middle], FROM_LEFT)
    far_bottom = send(keep[2, middle:] + got[2, middle:], FROM_RIGHT)
    right = keep[1] + got[1]
    right = jnp.concatenate([right[:middle] + far_top, right[middle:]], 0)
    left = keep[3] + got[3]
    left = jnp.concatenate([left[:middle], left[middle:] + far_bottom], 0)
    return keep[0] + got[0], right, left


def over_y(total, y_to):
    pairs = [
        (device(1 - y_to, x, core, b), device(y_to, x, core, b))
        for x in range(NX)
        for core in range(2)
        for b in range(GROUPS)
    ]
    return total + send(total, pairs)


def together(*values):
    return lax.optimization_barrier(values)


def per_device(half_b):
    local, code_c, target_c, final = plan()
    aux, blk = lax.axis_index("aux"), lax.axis_index("blk")
    place = aux * GROUPS + blk
    table_a, table_b = jnp.asarray(local[0])[place], jnp.asarray(local[1])[place]
    table_c = jnp.asarray(code_c)[blk].reshape(1)

    held = {O: half_b}
    held[PZ] = send(half_b, FROM_UP)
    held[MZ] = send(half_b, FROM_DOWN)
    held[Y0] = send(half_b, FROM_OTHER)

    held[PP] = send(held[PZ], FROM_UP)
    held[MM] = send(held[MZ], FROM_DOWN)
    held[Y1] = send(held[PZ], FROM_OTHER)

    have = [held[n] for n in HELD_A]
    keep, given = products(table_a, have, HELD_A, PAIRS_A, (NX, NX))
    own_a, right_a, left_a = near(keep, send(given, CORE_SWAP))
    from_left, from_right = send(right_a, FROM_LEFT), send(left_a, FROM_RIGHT)
    held[PP], held[MM], held[Y1], _, _ = together(held[PP], held[MM], held[Y1], right_a, left_a)

    held[Y2] = send(held[PP], FROM_OTHER)
    have = [held[n] for n in HELD_B]
    keep, given = products(table_b, have, HELD_B, PAIRS_B, (NX, NX))
    own_b, right_b, left_b = near(keep, send(given, CORE_SWAP))
    done_a = over_y(own_a + from_left + from_right, 0)
    right_b, left_b, _ = together(right_b, left_b, done_a)
    top = send(done_a, final[0, 0])
    bottom = send(done_a, final[0, 1])
    total_b = own_b + send(right_b, FROM_LEFT) + send(left_b, FROM_RIGHT)

    held[Y2], _, _ = together(held[Y2], right_b, left_b)
    (part_c,) = products(table_c, [held[n] for n in HELD_C], HELD_C, PAIRS_C, (1,))
    done_c = to_one(part_c[0], target_c)
    total_b, top, bottom = together(total_b, top, bottom)
    done_b = over_y(total_b, 1)
    top = top + send(done_b, final[1, 0]) + send(done_c, final[2, 0])
    bottom = bottom + send(done_b, final[1, 1]) + send(done_c, final[2, 1])
    return jnp.concatenate([top, bottom], 0)


def solution(mesh):
    placed = (P("aux", "blk", None),)
    return jax.shard_map(
        per_device, mesh=mesh, in_specs=placed, out_specs=P("blk", "aux"), check_vma=False
    )
```

time: 200 us -> 210 us (1.050)
  the two profiles are of different devices: /device:TPU:30 before, /device:TPU:12 now
where the time goes in v2:
time: 210 us; the launch traced here: 209 us
  waiting for transfers between devices  142 us (68%)
  starting transfers between devices  41.2 us (20%)
  Pallas kernels  11.9 us (6%)
  other arithmetic  8.51 us (4%)
  local copies, waits for them, and re-layouts  4.78 us (2%)
    ppermute x31, waiting for transfers between devices, send(): return lax.ppermute(value, ALL, pairs)  142 us
    ppermute x31, starting transfers between devices, send(): return lax.ppermute(value, ALL, pairs)  41.2 us
    pallas_call x3, Pallas kernels, products(): pl.pallas_call(functools.partial(units_kernel, index_pairs, len(counts)),...  11.9 us
  transfers between devices with their start and end apart: 31, of which 19 were waited for; matrix products, arithmetic and copies ran while one was open for 5% of the time, Pallas kernels for 0%

profile of v2, /device:TPU:12, one launch (start us, length us, event | category | flops | bytes accessed | tf_op | source)
XLA Modules:
  0.0 208.7 jit_solution(5365138099607446951)
XLA Ops:
  0.0 5.9 %collective-permute-start.1 = (bf16[2,512,512]{2,1,0:T(8,128)(2,1)}, bf16[2,512,512]{2,1,0:T(8,128)(2,1)S(1)}, u32[]{:S(2)}, u32[]{:S(2)}) collective-permute-start(bf16[2,512,512]{2,1,0:T(8,128)(2,1)} %refs_0_.3), channel_id=1, source_target_pairs={{1,0},{2,1},{3,2},{4,3},{5,4},{6,5},{7,6},{0,7},{9,8},{10,9},{11,1... | collective-permute-start | bytes 3145736 | tf_op jit(solution)/shard_map/ppermute | solution.py:36
  5.9 2.3 %collective-permute-start.5 = (bf16[2,512,512]{2,1,0:T(8,128)(2,1)}, bf16[2,512,512]{2,1,0:T(8,128)(2,1)S(1)}, u32[]{:S(2)}, u32[]{:S(2)}) collective-permute-start(bf16[2,512,512]{2,1,0:T(8,128)(2,1)} %refs_0_.3), channel_id=1, source_target_pairs={{8,0},{9,1},{10,2},{11,3},{12,4},{13,5},{14,6},{15,7},{0,8},{1,9},... | collective-permute-start | bytes 3145736 | tf_op jit(solution)/shard_map/ppermute | solution.py:36
  8.8 19.7 %collective-permute-done.1.refs_1_.refs_2_ = bf16[2,512,512]{2,1,0:T(8,128)(2,1)S(1)} collective-permute-done((bf16[2,512,512]{2,1,0:T(8,128)(2,1)}, bf16[2,512,512]{2,1,0:T(8,128)(2,1)S(1)}, u32[]{:S(2)}, u32[]{:S(2)}) %collective-permute-start.1) | collective-permute-done | bytes 1048608 | tf_op jit(solution)/shard_map/ppermute | solution.py:36
  28.6 3.3 %collective-permute-done.refs_2_.refs_1_ = bf16[2,512,512]{2,1,0:T(8,128)(2,1)S(1)} collective-permute-done((bf16[2,512,512]{2,1,0:T(8,128)(2,1)}, bf16[2,512,512]{2,1,0:T(8,128)(2,1)S(1)}, u32[]{:S(2)}, u32[]{:S(2)}) %collective-permute-start) | collective-permute-done | bytes 1048608 | tf_op jit(solution)/shard_map/ppermute | solution.py:36
  33.4 4.7 %shard_map.46 = (f32[4,256,512]{2,1,0:T(8,128)S(1)}, f32[4,256,512]{2,1,0:T(8,128)S(1)}) custom-call(s32[8]{0:T(128)S(1)} %dynamic-slice_bitcast_fusion.table, bf16[2,512,512]{2,1,0:T(8,128)(2,1)S(1)} %copy-done, bf16[2,512,512]{2,1,0:T(8,128)(2,1)S(1)} %collective-permute-done.1.refs_1_.refs_2_, ...), custom_call_target="tpu_custom_call" | custom-call | tf_op jit(solution)/shard_map/pallas_call | solution.py:173
  38.9 3.0 %collective-permute-start.2 = (bf16[2,512,512]{2,1,0:T(8,128)(2,1)S(1)}, bf16[2,512,512]{2,1,0:T(8,128)(2,1)S(1)}, u32[]{:S(2)}, u32[]{:S(2)}) collective-permute-start(bf16[2,512,512]{2,1,0:T(8,128)(2,1)S(1)} %collective-permute-done.1.refs_1_.refs_2_), channel_id=1, source_target_pairs={{1,0},{2,1},{3,2},{4,3},{5,4},{6,5},{7,6},{0,7},{9,8},{10,9},{11,1... | collective-permute-start | bytes 3145736 | tf_op jit(solution)/shard_map/ppermute | solution.py:36
  41.9 2.3 %collective-permute-start.4 = (bf16[2,512,512]{2,1,0:T(8,128)(2,1)S(1)}, bf16[2,512,512]{2,1,0:T(8,128)(2,1)S(1)}, u32[]{:S(2)}, u32[]{:S(2)}) collective-permute-start(bf16[2,512,512]{2,1,0:T(8,128)(2,1)S(1)} %collective-permute-done.1.refs_1_.refs_2_), channel_id=1, source_target_pairs={{8,0},{9,1},{10,2},{11,3},{12,4},{13,5},{14,6},{15,7},{0,8},{1,9},... | collective-permute-start | bytes 3145736 | tf_op jit(solution)/shard_map/ppermute | solution.py:36
  45.1 1.8 collective-permute-start.7
  46.9 5.6 %collective-permute-done.8 = f32[128,512]{1,0:T(8,128)S(1)} collective-permute-done((f32[128,512]{1,0:T(8,128)S(1)}, f32[128,512]{1,0:T(8,128)S(1)}, u32[]{:S(2)}, u32[]{:S(2)}) %collective-permute-start.8) | collective-permute-done | bytes 262176 | tf_op jit(solution)/shard_map/ppermute | solution.py:36
  53.3 11.6 %collective-permute-done.2.refs_3_ = bf16[2,512,512]{2,1,0:T(8,128)(2,1)S(1)} collective-permute-done((bf16[2,512,512]{2,1,0:T(8,128)(2,1)S(1)}, bf16[2,512,512]{2,1,0:T(8,128)(2,1)S(1)}, u32[]{:S(2)}, u32[]{:S(2)}) %collective-permute-start.2) | collective-permute-done | bytes 1048608 | tf_op jit(solution)/shard_map/ppermute | solution.py:36
  64.9 3.7 %collective-permute-done.4.refs_5_ = bf16[2,512,512]{2,1,0:T(8,128)(2,1)S(1)} collective-permute-done((bf16[2,512,512]{2,1,0:T(8,128)(2,1)S(1)}, bf16[2,512,512]{2,1,0:T(8,128)(2,1)S(1)}, u32[]{:S(2)}, u32[]{:S(2)}) %collective-permute-start.4) | collective-permute-done | bytes 1048608 | tf_op jit(solution)/shard_map/ppermute | solution.py:36
  68.6 1.7 collective-permute-done.3.refs_4_.refs_0_
  70.4 6.0 %shard_map.47 = (f32[4,256,512]{2,1,0:T(8,128)S(1)}, f32[4,256,512]{2,1,0:T(8,128)}) custom-call(s32[8]{0:T(128)S(1)} %dynamic-slice_bitcast_fusion.1.table, bf16[2,512,512]{2,1,0:T(8,128)(2,1)S(1)} %copy-done.1, bf16[2,512,512]{2,1,0:T(8,128)(2,1)S(1)} %collective-permute-done.refs_2_.refs_1_, ...), custom_call_target="tpu_custom_call" | custom-call | tf_op jit(solution)/shard_map/pallas_call | solution.py:173
  76.4 1.4 copy-done.2
  78.3 1.5 collective-permute-start.12
  79.8 12.3 %collective-permute-done.13 = f32[256,512]{1,0:T(8,128)S(1)} collective-permute-done((f32[256,512]{1,0:T(8,128)S(1)}, f32[256,512]{1,0:T(8,128)S(1)}, u32[]{:S(2)}, u32[]{:S(2)}) %collective-permute-start.13) | collective-permute-done | bytes 524320 | tf_op jit(solution)/shard_map/ppermute | solution.py:36
  93.4 4.0 %collective-permute-start.14 = (f32[256,512]{1,0:T(8,128)}, f32[256,512]{1,0:T(8,128)}, u32[]{:S(2)}, u32[]{:S(2)}) collective-permute-start(f32[256,512]{1,0:T(8,128)} %fusion.2), channel_id=1, source_target_pairs={{128,0},{129,1},{130,2},{131,3},{132,4},{133,5},{134,6},{135,7},{1... | collective-permute-start | bytes 1572872 | tf_op jit(solution)/shard_map/ppermute | solution.py:36
  98.1 11.2 %collective-permute-done.14 = f32[256,512]{1,0:T(8,128)} collective-permute-done((f32[256,512]{1,0:T(8,128)}, f32[256,512]{1,0:T(8,128)}, u32[]{:S(2)}, u32[]{:S(2)}) %collective-permute-start.14) | collective-permute-done | bytes 524320 | tf_op jit(solution)/shard_map/ppermute | solution.py:36
  111.7 1.6 collective-permute-start.11
  114.0 1.4 slice_add_fusion.1
  115.5 2.8 %collective-permute-done.11 = f32[128,512]{1,0:T(8,128)S(1)} collective-permute-done((f32[128,512]{1,0:T(8,128)S(1)}, f32[128,512]{1,0:T(8,128)S(1)}, u32[]{:S(2)}, u32[]{:S(2)}) %collective-permute-start.11) | collective-permute-done | bytes 262176 | tf_op jit(solution)/shard_map/ppermute | solution.py:36
  118.4 2.3 %collective-permute-done.10 = f32[128,512]{1,0:T(8,128)S(1)} collective-permute-done((f32[128,512]{1,0:T(8,128)S(1)}, f32[128,512]{1,0:T(8,128)S(1)}, u32[]{:S(2)}, u32[]{:S(2)}) %collective-permute-start.10) | collective-permute-done | bytes 262176 | tf_op jit(solution)/shard_map/ppermute | solution.py:36
  120.7 9.8 %collective-permute-done.21.refs_1_ = bf16[2,512,512]{2,1,0:T(8,128)(2,1)S(1)} collective-permute-done((bf16[2,512,512]{2,1,0:T(8,128)(2,1)}, bf16[2,512,512]{2,1,0:T(8,128)(2,1)S(1)}, u32[]{:S(2)}, u32[]{:S(2)}) %collective-permute-start.21) | collective-permute-done | bytes 1048608 | tf_op jit(solution)/shard_map/ppermute | solution.py:36
  133.0 2.5 %collective-permute-start.15 = (f32[256,512]{1,0:T(8,128)S(1)}, f32[256,512]{1,0:T(8,128)S(1)}, u32[]{:S(2)}, u32[]{:S(2)}) collective-permute-start(f32[256,512]{1,0:T(8,128)S(1)} %pad_maximum_fusion.3), channel_id=1, source_target_pairs={{96,0},{97,1},{98,2},{99,3},{100,4},{101,5},{102,6},{103,7},{104,8... | collective-permute-start | bytes 1572872 | tf_op jit(solution)/shard_map/ppermute | solution.py:36
  135.7 1.3 collective-permute-start.23
  139.6 6.8 %collective-permute-done.23 = f32[128,512]{1,0:T(8,128)S(1)} collective-permute-done((f32[128,512]{1,0:T(8,128)S(1)}, f32[128,512]{1,0:T(8,128)S(1)}, u32[]{:S(2)}, u32[]{:S(2)}) %collective-permute-start.23) | collective-permute-done | bytes 262176 | tf_op jit(solution)/shard_map/ppermute | solution.py:36
  147.2 1.3 collective-permute-start.25
  149.2 5.9 %collective-permute-done.16 = f32[256,512]{1,0:T(8,128)S(1)} collective-permute-done((f32[256,512]{1,0:T(8,128)S(1)}, f32[256,512]{1,0:T(8,128)S(1)}, u32[]{:S(2)}, u32[]{:S(2)}) %collective-permute-start.16) | collective-permute-done | bytes 524320 | tf_op jit(solution)/shard_map/ppermute | solution.py:36
  158.6 11.2 %collective-permute-done.19 = f32[256,512]{1,0:T(8,128)S(1)} collective-permute-done((f32[256,512]{1,0:T(8,128)S(1)}, f32[256,512]{1,0:T(8,128)S(1)}, u32[]{:S(2)}, u32[]{:S(2)}) %collective-permute-start.19) | collective-permute-done | bytes 524320 | tf_op jit(solution)/shard_map/ppermute | solution.py:36
  169.9 1.3 collective-permute-start.20
  174.6 5.5 %collective-permute-done.20 = f32[256,512]{1,0:T(8,128)S(1)} collective-permute-done((f32[256,512]{1,0:T(8,128)S(1)}, f32[256,512]{1,0:T(8,128)S(1)}, u32[]{:S(2)}, u32[]{:S(2)}) %collective-permute-start.20) | collective-permute-done | bytes 524320 | tf_op jit(solution)/shard_map/ppermute | solution.py:36
  180.1 27.2 %collective-permute-done.28 = f32[256,512]{1,0:T(8,128)S(1)} collective-permute-done((f32[256,512]{1,0:T(8,128)S(1)}, f32[256,512]{1,0:T(8,128)S(1)}, u32[]{:S(2)}, u32[]{:S(2)}) %collective-permute-start.28) | collective-permute-done | bytes 524320 | tf_op jit(solution)/shard_map/ppermute | solution.py:36
  (75 shorter events, 25.4 us)
Async XLA Ops:
  0.0 28.6 %collective-permute-start.1 = (bf16[2,512,512]{2,1,0:T(8,128)(2,1)}, bf16[2,512,512]{2,1,0:T(8,128)(2,1)S(1)}, u32[]{:S(2)}, u32[]{:S(2)}) collective-permute-start(bf16[2,512,512]{2,1,0:T(8,128)(2,1)} %refs_0_.3), channel_id=1, source_target_pairs={{1,0},{2,1},{3,2},{4,3},{5,4},{6,5},{7,6},{0,7},{9,8},{10,9},{11,1... | collective-permute-start | bytes 3145736 | tf_op jit(solution)/shard_map/ppermute | solution.py:36
  5.9 26.0 %collective-permute-start = (bf16[2,512,512]{2,1,0:T(8,128)(2,1)}, bf16[2,512,512]{2,1,0:T(8,128)(2,1)S(1)}, u32[]{:S(2)}, u32[]{:S(2)}) collective-permute-start(bf16[2,512,512]{2,1,0:T(8,128)(2,1)} %refs_0_.3), channel_id=1, source_target_pairs={{7,0},{0,1},{1,2},{2,3},{3,4},{4,5},{5,6},{6,7},{15,8},{8,9},{9,10... | collective-permute-start | bytes 3145736 | tf_op jit(solution)/shard_map/ppermute | solution.py:36
  5.9 26.3 %collective-permute-start.5 = (bf16[2,512,512]{2,1,0:T(8,128)(2,1)}, bf16[2,512,512]{2,1,0:T(8,128)(2,1)S(1)}, u32[]{:S(2)}, u32[]{:S(2)}) collective-permute-start(bf16[2,512,512]{2,1,0:T(8,128)(2,1)} %refs_0_.3), channel_id=1, source_target_pairs={{8,0},{9,1},{10,2},{11,3},{12,4},{13,5},{14,6},{15,7},{0,8},{1,9},... | collective-permute-start | bytes 3145736 | tf_op jit(solution)/shard_map/ppermute | solution.py:36
  38.1 6.1 %collective-permute-start.6 = (f32[4,256,512]{2,1,0:T(8,128)S(1)}, f32[4,256,512]{2,1,0:T(8,128)S(1)}, u32[]{:S(2)}, u32[]{:S(2)}) collective-permute-start(f32[4,256,512]{2,1,0:T(8,128)S(1)} %get-tuple-element.19), channel_id=1, source_target_pairs={{16,0},{17,1},{18,2},{19,3},{20,4},{21,5},{22,6},{23,7},{24,8},{25... | collective-permute-start | bytes 6291464 | tf_op jit(solution)/shard_map/ppermute | solution.py:36
  38.9 26.0 %collective-permute-start.2 = (bf16[2,512,512]{2,1,0:T(8,128)(2,1)S(1)}, bf16[2,512,512]{2,1,0:T(8,128)(2,1)S(1)}, u32[]{:S(2)}, u32[]{:S(2)}) collective-permute-start(bf16[2,512,512]{2,1,0:T(8,128)(2,1)S(1)} %collective-permute-done.1.refs_1_.refs_2_), channel_id=1, source_target_pairs={{1,0},{2,1},{3,2},{4,3},{5,4},{6,5},{7,6},{0,7},{9,8},{10,9},{11,1... | collective-permute-start | bytes 3145736 | tf_op jit(solution)/shard_map/ppermute | solution.py:36
  41.9 26.8 %collective-permute-start.4 = (bf16[2,512,512]{2,1,0:T(8,128)(2,1)S(1)}, bf16[2,512,512]{2,1,0:T(8,128)(2,1)S(1)}, u32[]{:S(2)}, u32[]{:S(2)}) collective-permute-start(bf16[2,512,512]{2,1,0:T(8,128)(2,1)S(1)} %collective-permute-done.1.refs_1_.refs_2_), channel_id=1, source_target_pairs={{8,0},{9,1},{10,2},{11,3},{12,4},{13,5},{14,6},{15,7},{0,8},{1,9},... | collective-permute-start | bytes 3145736 | tf_op jit(solution)/shard_map/ppermute | solution.py:36
  44.2 26.2 %collective-permute-start.3 = (bf16[2,512,512]{2,1,0:T(8,128)(2,1)S(1)}, bf16[2,512,512]{2,1,0:T(8,128)(2,1)S(1)}, u32[]{:S(2)}, u32[]{:S(2)}) collective-permute-start(bf16[2,512,512]{2,1,0:T(8,128)(2,1)S(1)} %collective-permute-done.refs_2_.refs_1_), channel_id=1, source_target_pairs={{7,0},{0,1},{1,2},{2,3},{3,4},{4,5},{5,6},{6,7},{15,8},{8,9},{9,10... | collective-permute-start | bytes 3145736 | tf_op jit(solution)/shard_map/ppermute | solution.py:36
  44.3 8.2 %collective-permute-start.8 = (f32[128,512]{1,0:T(8,128)S(1)}, f32[128,512]{1,0:T(8,128)S(1)}, u32[]{:S(2)}, u32[]{:S(2)}) collective-permute-start(f32[128,512]{1,0:T(8,128)S(1)} %get-tuple-element.37), channel_id=1, source_target_pairs={{32,0},{33,1},{34,2},{35,3},{36,4},{37,5},{38,6},{39,7},{40,8},{41... | collective-permute-start | bytes 786440 | tf_op jit(solution)/shard_map/ppermute | solution.py:36
  45.1 8.1 %collective-permute-start.7 = (f32[128,512]{1,0:T(8,128)S(1)}, f32[128,512]{1,0:T(8,128)S(1)}, u32[]{:S(2)}, u32[]{:S(2)}) collective-permute-start(f32[128,512]{1,0:T(8,128)S(1)} %get-tuple-element.38), channel_id=1, source_target_pairs={{96,0},{97,1},{98,2},{99,3},{100,4},{101,5},{102,6},{103,7},{104,8... | collective-permute-start | bytes 786440 | tf_op jit(solution)/shard_map/ppermute | solution.py:36
  77.8 32.8 %copy-start.3 = (f32[4,256,512]{2,1,0:T(8,128)S(1)}, f32[4,256,512]{2,1,0:T(8,128)}, u32[]{:S(2)}) copy-start(f32[4,256,512]{2,1,0:T(8,128)} %copy-done.2) | copy-start | bytes 6291460
  77.8 32.8 %collective-permute-start.9 = (f32[4,256,512]{2,1,0:T(8,128)}, f32[4,256,512]{2,1,0:T(8,128)}, u32[]{:S(2)}, u32[]{:S(2)}) collective-permute-start(f32[4,256,512]{2,1,0:T(8,128)} %get-tuple-element.24), channel_id=1, source_target_pairs={{16,0},{17,1},{18,2},{19,3},{20,4},{21,5},{22,6},{23,7},{24,8},{25... | collective-permute-start | bytes 6291464 | tf_op jit(solution)/shard_map/ppermute | solution.py:36
  77.8 14.3 %collective-permute-start.13 = (f32[256,512]{1,0:T(8,128)S(1)}, f32[256,512]{1,0:T(8,128)S(1)}, u32[]{:S(2)}, u32[]{:S(2)}) collective-permute-start(f32[256,512]{1,0:T(8,128)S(1)} %pad_maximum_fusion.2), channel_id=1, source_target_pairs={{32,0},{33,1},{34,2},{35,3},{36,4},{37,5},{38,6},{39,7},{40,8},{41... | collective-permute-start | bytes 1572872 | tf_op jit(solution)/shard_map/ppermute | solution.py:36
  78.3 14.1 %collective-permute-start.12 = (f32[256,512]{1,0:T(8,128)S(1)}, f32[256,512]{1,0:T(8,128)S(1)}, u32[]{:S(2)}, u32[]{:S(2)}) collective-permute-start(f32[256,512]{1,0:T(8,128)S(1)} %pad_maximum_fusion.1), channel_id=1, source_target_pairs={{96,0},{97,1},{98,2},{99,3},{100,4},{101,5},{102,6},{103,7},{104,8... | collective-permute-start | bytes 1572872 | tf_op jit(solution)/shard_map/ppermute | solution.py:36
  93.4 15.9 %collective-permute-start.14 = (f32[256,512]{1,0:T(8,128)}, f32[256,512]{1,0:T(8,128)}, u32[]{:S(2)}, u32[]{:S(2)}) collective-permute-start(f32[256,512]{1,0:T(8,128)} %fusion.2), channel_id=1, source_target_pairs={{128,0},{129,1},{130,2},{131,3},{132,4},{133,5},{134,6},{135,7},{1... | collective-permute-start | bytes 1572872 | tf_op jit(solution)/shard_map/ppermute | solution.py:36
  98.1 32.5 %collective-permute-start.21 = (bf16[2,512,512]{2,1,0:T(8,128)(2,1)}, bf16[2,512,512]{2,1,0:T(8,128)(2,1)S(1)}, u32[]{:S(2)}, u32[]{:S(2)}) collective-permute-start(bf16[2,512,512]{2,1,0:T(8,128)(2,1)} %copy-done.4), channel_id=1, source_target_pairs={{8,0},{9,1},{10,2},{11,3},{12,4},{13,5},{14,6},{15,7},{0,8},{1,9},... | collective-permute-start | bytes 3145736 | tf_op jit(solution)/shard_map/ppermute | solution.py:36
  111.7 6.5 %collective-permute-start.11 = (f32[128,512]{1,0:T(8,128)S(1)}, f32[128,512]{1,0:T(8,128)S(1)}, u32[]{:S(2)}, u32[]{:S(2)}) collective-permute-start(f32[128,512]{1,0:T(8,128)S(1)} %get-tuple-element.33), channel_id=1, source_target_pairs={{32,0},{33,1},{34,2},{35,3},{36,4},{37,5},{38,6},{39,7},{40,8},{41... | collective-permute-start | bytes 786440 | tf_op jit(solution)/shard_map/ppermute | solution.py:36
  113.3 7.3 %collective-permute-start.10 = (f32[128,512]{1,0:T(8,128)S(1)}, f32[128,512]{1,0:T(8,128)S(1)}, u32[]{:S(2)}, u32[]{:S(2)}) collective-permute-start(f32[128,512]{1,0:T(8,128)S(1)} %get-tuple-element.34), channel_id=1, source_target_pairs={{96,0},{97,1},{98,2},{99,3},{100,4},{101,5},{102,6},{103,7},{104,8... | collective-permute-start | bytes 786440 | tf_op jit(solution)/shard_map/ppermute | solution.py:36
  131.7 3.8 %collective-permute-start.22 = (f32[256,512]{1,0:T(8,128)S(1)}, f32[256,512]{1,0:T(8,128)S(1)}, u32[]{:S(2)}, u32[]{:S(2)}) collective-permute-start(f32[256,512]{1,0:T(8,128)S(1)} %bitcast.50), channel_id=1, source_target_pairs={{48,32},{80,64},{112,96},{16,0},{176,160},{208,192},{240,224},{144... | collective-permute-start | bytes 1572872 | tf_op jit(solution)/shard_map/ppermute | solution.py:36
  133.0 15.5 %collective-permute-start.15 = (f32[256,512]{1,0:T(8,128)S(1)}, f32[256,512]{1,0:T(8,128)S(1)}, u32[]{:S(2)}, u32[]{:S(2)}) collective-permute-start(f32[256,512]{1,0:T(8,128)S(1)} %pad_maximum_fusion.3), channel_id=1, source_target_pairs={{96,0},{97,1},{98,2},{99,3},{100,4},{101,5},{102,6},{103,7},{104,8... | collective-permute-start | bytes 1572872 | tf_op jit(solution)/shard_map/ppermute | solution.py:36
  135.7 10.8 %collective-permute-start.23 = (f32[128,512]{1,0:T(8,128)S(1)}, f32[128,512]{1,0:T(8,128)S(1)}, u32[]{:S(2)}, u32[]{:S(2)}) collective-permute-start(f32[128,512]{1,0:T(8,128)S(1)} %get-tuple-element.39), channel_id=1, source_target_pairs={{96,64},{224,192},{113,81},{241,209},{2,98},{130,226},{19,115},{14... | collective-permute-start | bytes 786440 | tf_op jit(solution)/shard_map/ppermute | solution.py:36
  137.0 10.1 %collective-permute-start.24 = (f32[128,512]{1,0:T(8,128)S(1)}, f32[128,512]{1,0:T(8,128)S(1)}, u32[]{:S(2)}, u32[]{:S(2)}) collective-permute-start(f32[128,512]{1,0:T(8,128)S(1)} %get-tuple-element.40), channel_id=1, source_target_pairs={{96,0},{224,128},{113,17},{241,145},{2,34},{130,162},{19,51},{147,... | collective-permute-start | bytes 786440 | tf_op jit(solution)/shard_map/ppermute | solution.py:36
  137.6 17.5 %collective-permute-start.16 = (f32[256,512]{1,0:T(8,128)S(1)}, f32[256,512]{1,0:T(8,128)S(1)}, u32[]{:S(2)}, u32[]{:S(2)}) collective-permute-start(f32[256,512]{1,0:T(8,128)S(1)} %pad_maximum_fusion.4), channel_id=1, source_target_pairs={{32,0},{33,1},{34,2},{35,3},{36,4},{37,5},{38,6},{39,7},{40,8},{41... | collective-permute-start | bytes 1572872 | tf_op jit(solution)/shard_map/ppermute | solution.py:36
  138.9 17.5 %collective-permute-start.17 = (f32[256,512]{1,0:T(8,128)S(1)}, f32[256,512]{1,0:T(8,128)S(1)}, u32[]{:S(2)}, u32[]{:S(2)}) collective-permute-start(f32[256,512]{1,0:T(8,128)S(1)} %add.143), channel_id=1, source_target_pairs={{32,16},{80,113},{96,128},{0,135},{64,0},{65,33},{33,32},{113,145}... | collective-permute-start | bytes 1572872 | tf_op jit(solution)/shard_map/ppermute | solution.py:36
  146.4 10.0 %collective-permute-start.18 = (f32[256,512]{1,0:T(8,128)S(1)}, f32[256,512]{1,0:T(8,128)S(1)}, u32[]{:S(2)}, u32[]{:S(2)}) collective-permute-start(f32[256,512]{1,0:T(8,128)S(1)} %add.143), channel_id=1, source_target_pairs={{48,16},{112,113},{16,135},{81,33},{49,32},{17,144},{114,50},{82,4... | collective-permute-start | bytes 1572872 | tf_op jit(solution)/shard_map/ppermute | solution.py:36
  147.2 10.5 %collective-permute-start.25 = (f32[256,512]{1,0:T(8,128)S(1)}, f32[256,512]{1,0:T(8,128)S(1)}, u32[]{:S(2)}, u32[]{:S(2)}) collective-permute-start(f32[256,512]{1,0:T(8,128)S(1)} %maximum_add_fusion), channel_id=1, source_target_pairs={{64,32},{192,160},{81,49},{209,177},{98,66},{226,194},{115,83},{24... | collective-permute-start | bytes 1572872 | tf_op jit(solution)/shard_map/ppermute | solution.py:36
  148.5 9.2 %collective-permute-start.26 = (f32[256,512]{1,0:T(8,128)S(1)}, f32[256,512]{1,0:T(8,128)S(1)}, u32[]{:S(2)}, u32[]{:S(2)}) collective-permute-start(f32[256,512]{1,0:T(8,128)S(1)} %maximum_add_fusion), channel_id=1, source_target_pairs={{0,32},{128,160},{17,49},{145,177},{34,66},{162,194},{51,83},{179,... | collective-permute-start | bytes 1572872 | tf_op jit(solution)/shard_map/ppermute | solution.py:36
  156.4 13.3 %collective-permute-start.19 = (f32[256,512]{1,0:T(8,128)S(1)}, f32[256,512]{1,0:T(8,128)S(1)}, u32[]{:S(2)}, u32[]{:S(2)}) collective-permute-start(f32[256,512]{1,0:T(8,128)S(1)} %fusion.5), channel_id=1, source_target_pairs={{0,128},{1,129},{2,130},{3,131},{4,132},{5,133},{6,134},{7,135},{8... | collective-permute-start | bytes 1572872 | tf_op jit(solution)/shard_map/ppermute | solution.py:36
  157.9 13.3 %collective-permute-start.27 = (f32[256,512]{1,0:T(8,128)S(1)}, f32[256,512]{1,0:T(8,128)S(1)}, u32[]{:S(2)}, u32[]{:S(2)}) collective-permute-start(f32[256,512]{1,0:T(8,128)S(1)} %add_add_fusion.1), channel_id=1, source_target_pairs={{32,160},{49,177},{66,194},{83,211},{100,228},{117,245},{6,134},{2... | collective-permute-start | bytes 1572872 | tf_op jit(solution)/shard_map/ppermute | solution.py:36
  169.9 10.2 %collective-permute-start.20 = (f32[256,512]{1,0:T(8,128)S(1)}, f32[256,512]{1,0:T(8,128)S(1)}, u32[]{:S(2)}, u32[]{:S(2)}) collective-permute-start(f32[256,512]{1,0:T(8,128)S(1)} %add.146), channel_id=1, source_target_pairs={{192,97},{176,151},{128,150},{209,114},{129,160},{161,167},{162,48... | collective-permute-start | bytes 1572872 | tf_op jit(solution)/shard_map/ppermute | solution.py:36
  171.3 36.0 %collective-permute-start.28 = (f32[256,512]{1,0:T(8,128)S(1)}, f32[256,512]{1,0:T(8,128)S(1)}, u32[]{:S(2)}, u32[]{:S(2)}) collective-permute-start(f32[256,512]{1,0:T(8,128)S(1)} %add.153), channel_id=1, source_target_pairs={{160,166},{177,183},{194,192},{211,209},{228,226},{245,243},{134,1... | collective-permute-start | bytes 1572872 | tf_op jit(solution)/shard_map/ppermute | solution.py:36
  172.6 34.9 %collective-permute-start.29 = (f32[256,512]{1,0:T(8,128)S(1)}, f32[256,512]{1,0:T(8,128)S(1)}, u32[]{:S(2)}, u32[]{:S(2)}) collective-permute-start(f32[256,512]{1,0:T(8,128)S(1)} %add.146), channel_id=1, source_target_pairs={{240,97},{224,98},{208,151},{144,150},{160,0},{225,114},{241,115},... | collective-permute-start | bytes 1572872 | tf_op jit(solution)/shard_map/ppermute | solution.py:36
  173.3 34.2 %collective-permute-start.30 = (f32[256,512]{1,0:T(8,128)S(1)}, f32[256,512]{1,0:T(8,128)S(1)}, u32[]{:S(2)}, u32[]{:S(2)}) collective-permute-start(f32[256,512]{1,0:T(8,128)S(1)} %add.153), channel_id=1, source_target_pairs={{232,226},{249,243},{138,132},{155,149},{172,166},{189,183},{206,1... | collective-permute-start | bytes 1572872 | tf_op jit(solution)/shard_map/ppermute | solution.py:36
  (5 other events, 57.2 us)

commit v3 on v2

--- a/solution.py
+++ b/solution.py
@@ -180,35 +180,42 @@
     )(table, *held)
 
 
-def to_one(value, targets):
-    def pairs(source, only):
-        return [
-            (device(*source(y, x, c), b), device(*only(y, x, c), b))
-            for b, (y, x, c) in targets.items()
-        ]
-
+def toward(targets, source, only):
+    return [
+        (device(*source(y, x, c, step), b), device(*only(y, x, c, step), b))
+        for b, (y, x, c) in targets.items()
+        for step in range(8)
+    ]
+
+
+def one_core(value, targets):
+    def at(core_of):
+        return lambda y, x, c, step: (step // NX, x + step % NX, core_of(c))
+
+    return value + send(value, toward(targets, at(lambda c: 1 - c), at(lambda c: c)))
+
+
+def along(targets, offset_from, offset_to):
+    def at(offset):
+        return lambda y, x, c, step: (step % 2, x + offset, c)
+
+    return sorted(set(toward(targets, at(offset_from), at(offset_to))))
+
+
+def one_far(value, targets):
     middle = value.shape[0] // 2
-    steps = [(y, dx) for y in range(2) for dx in range(NX)]
-    across = [
-        (device(y, tx + dx, 1 - tc, b), device(y, tx + dx, tc, b))
-        for b, (_, tx, tc) in targets.items()
-        for y, dx in steps
-    ]
-    value = value + send(value, across)
-
-    def along(offset_from, offset_to):
-        return [
-            (device(y, tx + offset_from, tc, b), device(y, tx + offset_to, tc, b))
-            for b, (_, tx, tc) in targets.items()
-            for y in range(2)
-        ]
-
-    top = send(value[:middle], along(2, 1))
-    bottom = send(value[middle:], along(2, 3))
-    value = value + jnp.concatenate([top, bottom], 0)
-    value = value + send(value, along(1, 0)) + send(value, along(3, 0))
-    last = [(device(1 - ty, tx, tc, b), device(ty, tx, tc, b)) for b, (ty, tx, tc) in targets.items()]
-    return value + send(value, last)
+    top = send(value[:middle], along(targets, 2, 1))
+    bottom = send(value[middle:], along(targets, 2, 3))
+    return value + jnp.concatenate([top, bottom], 0)
+
+
+def one_near(value, targets):
+    return value + send(value, along(targets, 1, 0)) + send(value, along(targets, 3, 0))
+
+
+def one_y(value, targets):
+    pairs = [(device(1 - y, x, c, b), device(y, x, c, b)) for b, (y, x, c) in targets.items()]
+    return value + send(value, pairs)
 
 
 CORE_SWAP = every(lambda y, x, c, h, z: (y, x, 1 - c, block(h, z)))
@@ -255,32 +262,35 @@
     held[PZ] = send(half_b, FROM_UP)
     held[MZ] = send(half_b, FROM_DOWN)
     held[Y0] = send(half_b, FROM_OTHER)
+    held[PZ], held[MZ], held[Y0] = together(held[PZ], held[MZ], held[Y0])
 
     held[PP] = send(held[PZ], FROM_UP)
     held[MM] = send(held[MZ], FROM_DOWN)
     held[Y1] = send(held[PZ], FROM_OTHER)
-
-    have = [held[n] for n in HELD_A]
-    keep, given = products(table_a, have, HELD_A, PAIRS_A, (NX, NX))
+    keep, given = products(table_a, [held[n] for n in HELD_A], HELD_A, PAIRS_A, (NX, NX))
     own_a, right_a, left_a = near(keep, send(given, CORE_SWAP))
-    from_left, from_right = send(right_a, FROM_LEFT), send(left_a, FROM_RIGHT)
-    held[PP], held[MM], held[Y1], _, _ = together(held[PP], held[MM], held[Y1], right_a, left_a)
+    own_a, right_a, left_a, held[PP], held[MM], held[Y1] = together(
+        own_a, right_a, left_a, held[PP], held[MM], held[Y1]
+    )
 
     held[Y2] = send(held[PP], FROM_OTHER)
-    have = [held[n] for n in HELD_B]
-    keep, given = products(table_b, have, HELD_B, PAIRS_B, (NX, NX))
+    total_a = own_a + send(right_a, FROM_LEFT) + send(left_a, FROM_RIGHT)
+    keep, given = products(table_b, [held[n] for n in HELD_B], HELD_B, PAIRS_B, (NX, NX))
     own_b, right_b, left_b = near(keep, send(given, CORE_SWAP))
-    done_a = over_y(own_a + from_left + from_right, 0)
-    right_b, left_b, _ = together(right_b, left_b, done_a)
+    total_a, own_b, right_b, left_b, held[Y2] = together(total_a, own_b, right_b, left_b, held[Y2])
+
+    done_a = over_y(total_a, 0)
+    total_b = own_b + send(right_b, FROM_LEFT) + send(left_b, FROM_RIGHT)
+    (part_c,) = products(table_c, [held[n] for n in HELD_C], HELD_C, PAIRS_C, (1,))
+    part_c = one_far(one_core(part_c[0], target_c), target_c)
+    done_a, total_b, part_c = together(done_a, total_b, part_c)
+
     top = send(done_a, final[0, 0])
     bottom = send(done_a, final[0, 1])
-    total_b = own_b + send(right_b, FROM_LEFT) + send(left_b, FROM_RIGHT)
-
-    held[Y2], _, _ = together(held[Y2], right_b, left_b)
-    (part_c,) = products(table_c, [held[n] for n in HELD_C], HELD_C, PAIRS_C, (1,))
-    done_c = to_one(part_c[0], target_c)
-    total_b, top, bottom = together(total_b, top, bottom)
     done_b = over_y(total_b, 1)
+    done_c = one_y(one_near(part_c, target_c), target_c)
+    top, bottom, done_b, done_c = together(top, bottom, done_b, done_c)
+
     top = top + send(done_b, final[1, 0]) + send(done_c, final[2, 0])
     bottom = bottom + send(done_b, final[1, 1]) + send(done_c, final[2, 1])
     return jnp.concatenate([top, bottom], 0)

time: 210 us -> 194 us (0.924)
  the two profiles are of different devices: /device:TPU:12 before, /device:TPU:70 now
where the time goes in v3:
time: 194 us
  waiting for transfers between devices  122 us (63%)
  starting transfers between devices  46.1 us (24%)
  Pallas kernels  11.8 us (6%)
  other arithmetic  9.49 us (5%)
  local copies, waits for them, and re-layouts  4.04 us (2%)
    ppermute x31, waiting for transfers between devices, send(): return lax.ppermute(value, ALL, pairs)  122 us
    ppermute x31, starting transfers between devices, send(): return lax.ppermute(value, ALL, pairs)  46.1 us
    pallas_call x3, Pallas kernels, products(): pl.pallas_call(functools.partial(units_kernel, index_pairs, len(counts)),...  11.8 us
  transfers between devices with their start and end apart: 31, of which 18 were waited for; matrix products, arithmetic and copies ran while one was open for 5% of the time, Pallas kernels for 0%

profile of v3, /device:TPU:70, one launch (start us, length us, event | category | flops | bytes accessed | tf_op | source)
XLA Modules:
  0.0 193.8 jit_solution(3517503443730423088)
XLA Ops:
  0.1 1.9 collective-permute-start.1
  2.0 3.2 %collective-permute-start.2 = (bf16[2,512,512]{2,1,0:T(8,128)(2,1)}, bf16[2,512,512]{2,1,0:T(8,128)(2,1)S(1)}, u32[]{:S(2)}, u32[]{:S(2)}) collective-permute-start(bf16[2,512,512]{2,1,0:T(8,128)(2,1)} %refs_0_.3), channel_id=1, source_target_pairs={{8,0},{9,1},{10,2},{11,3},{12,4},{13,5},{14,6},{15,7},{0,8},{1,9},... | collective-permute-start | bytes 3145736 | tf_op jit(solution)/shard_map/ppermute | solution.py:36
  5.9 19.4 %collective-permute-done.refs_1_.refs_2_ = bf16[2,512,512]{2,1,0:T(8,128)(2,1)S(1)} collective-permute-done((bf16[2,512,512]{2,1,0:T(8,128)(2,1)}, bf16[2,512,512]{2,1,0:T(8,128)(2,1)S(1)}, u32[]{:S(2)}, u32[]{:S(2)}) %collective-permute-start) | collective-permute-done | bytes 1048608 | tf_op jit(solution)/shard_map/ppermute | solution.py:36
  25.3 3.0 %collective-permute-done.2.refs_3_ = bf16[2,512,512]{2,1,0:T(8,128)(2,1)S(1)} collective-permute-done((bf16[2,512,512]{2,1,0:T(8,128)(2,1)}, bf16[2,512,512]{2,1,0:T(8,128)(2,1)S(1)}, u32[]{:S(2)}, u32[]{:S(2)}) %collective-permute-start.2) | collective-permute-done | bytes 1048608 | tf_op jit(solution)/shard_map/ppermute | solution.py:36
  29.5 4.7 %shard_map.46 = (f32[4,256,512]{2,1,0:T(8,128)S(1)}, f32[4,256,512]{2,1,0:T(8,128)S(1)}) custom-call(s32[8]{0:T(128)S(1)} %get-tuple-element.68.table, bf16[2,512,512]{2,1,0:T(8,128)(2,1)S(1)} %copy-done, bf16[2,512,512]{2,1,0:T(8,128)(2,1)S(1)} %collective-permute-done.refs_1_.refs_2_, bf16[2,512,512]{2,1,0:T(8,128)(2,1)S(1)} %collective-permute-done.1.refs_2_.refs_1_, ...), custom_call_target="tpu_custom_call" | custom-call | tf_op jit(solution)/shard_map/pallas_call | solution.py:173
  35.3 2.3 %collective-permute-start.7 = (bf16[2,512,512]{2,1,0:T(8,128)(2,1)S(1)}, bf16[2,512,512]{2,1,0:T(8,128)(2,1)S(1)}, u32[]{:S(2)}, u32[]{:S(2)}) collective-permute-start(bf16[2,512,512]{2,1,0:T(8,128)(2,1)S(1)} %collective-permute-done.1.refs_2_.refs_1_), channel_id=1, source_target_pairs={{7,0},{0,1},{1,2},{2,3},{3,4},{4,5},{5,6},{6,7},{15,8},{8,9},{9,10... | collective-permute-start | bytes 3145736 | tf_op jit(solution)/shard_map/ppermute | solution.py:36
  37.6 3.2 %collective-permute-start.8 = (bf16[2,512,512]{2,1,0:T(8,128)(2,1)S(1)}, bf16[2,512,512]{2,1,0:T(8,128)(2,1)S(1)}, u32[]{:S(2)}, u32[]{:S(2)}) collective-permute-start(bf16[2,512,512]{2,1,0:T(8,128)(2,1)S(1)} %collective-permute-done.refs_1_.refs_2_), channel_id=1, source_target_pairs={{8,0},{9,1},{10,2},{11,3},{12,4},{13,5},{14,6},{15,7},{0,8},{1,9},... | collective-permute-start | bytes 3145736 | tf_op jit(solution)/shard_map/ppermute | solution.py:36
  42.6 1.8 collective-permute-start.5
  44.4 4.5 %collective-permute-done.4 = f32[128,512]{1,0:T(8,128)S(1)} collective-permute-done((f32[128,512]{1,0:T(8,128)S(1)}, f32[128,512]{1,0:T(8,128)S(1)}, u32[]{:S(2)}, u32[]{:S(2)}) %collective-permute-start.4) | collective-permute-done | bytes 262176 | tf_op jit(solution)/shard_map/ppermute | solution.py:36
  49.8 2.0 %collective-permute-done.5 = f32[128,512]{1,0:T(8,128)S(1)} collective-permute-done((f32[128,512]{1,0:T(8,128)S(1)}, f32[128,512]{1,0:T(8,128)S(1)}, u32[]{:S(2)}, u32[]{:S(2)}) %collective-permute-start.5) | collective-permute-done | bytes 262176 | tf_op jit(solution)/shard_map/ppermute | solution.py:36
  52.7 8.6 %collective-permute-done.6.refs_3_ = bf16[2,512,512]{2,1,0:T(8,128)(2,1)S(1)} collective-permute-done((bf16[2,512,512]{2,1,0:T(8,128)(2,1)S(1)}, bf16[2,512,512]{2,1,0:T(8,128)(2,1)S(1)}, u32[]{:S(2)}, u32[]{:S(2)}) %collective-permute-start.6) | collective-permute-done | bytes 1048608 | tf_op jit(solution)/shard_map/ppermute | solution.py:36
  62.0 2.2 %collective-permute-done.8.refs_5_ = bf16[2,512,512]{2,1,0:T(8,128)(2,1)S(1)} collective-permute-done((bf16[2,512,512]{2,1,0:T(8,128)(2,1)S(1)}, bf16[2,512,512]{2,1,0:T(8,128)(2,1)S(1)}, u32[]{:S(2)}, u32[]{:S(2)}) %collective-permute-start.8) | collective-permute-done | bytes 1048608 | tf_op jit(solution)/shard_map/ppermute | solution.py:36
  64.2 6.0 %shard_map.47 = (f32[4,256,512]{2,1,0:T(8,128)S(1)}, f32[4,256,512]{2,1,0:T(8,128)}) custom-call(s32[8]{0:T(128)S(1)} %get-tuple-element.67.table, bf16[2,512,512]{2,1,0:T(8,128)(2,1)S(1)} %copy-done.1, bf16[2,512,512]{2,1,0:T(8,128)(2,1)S(1)} %collective-permute-done.1.refs_2_.refs_1_, bf16[2,512,512]{2,1,0:T(8,128)(2,1)S(1)} %collective-permute-done.refs_1_.refs_2_, ...), custom_call_target="tpu_custom_call" | custom-call | tf_op jit(solution)/shard_map/pallas_call | solution.py:173
  70.3 1.4 copy-done.2
  72.5 2.4 %collective-permute-start.9 = (f32[256,512]{1,0:T(8,128)}, f32[256,512]{1,0:T(8,128)}, u32[]{:S(2)}, u32[]{:S(2)}) collective-permute-start(f32[256,512]{1,0:T(8,128)} %pad_maximum_fusion.1), channel_id=1, source_target_pairs={{96,0},{97,1},{98,2},{99,3},{100,4},{101,5},{102,6},{103,7},{104,8... | collective-permute-start | bytes 1572872 | tf_op jit(solution)/shard_map/ppermute | solution.py:36
  75.5 3.2 %collective-permute-start.14 = (bf16[2,512,512]{2,1,0:T(8,128)(2,1)}, bf16[2,512,512]{2,1,0:T(8,128)(2,1)S(1)}, u32[]{:S(2)}, u32[]{:S(2)}) collective-permute-start(bf16[2,512,512]{2,1,0:T(8,128)(2,1)} %copy-done.4), channel_id=1, source_target_pairs={{8,0},{9,1},{10,2},{11,3},{12,4},{13,5},{14,6},{15,7},{0,8},{1,9},... | collective-permute-start | bytes 3145736 | tf_op jit(solution)/shard_map/ppermute | solution.py:36
  78.7 8.8 %collective-permute-done.10 = f32[256,512]{1,0:T(8,128)} collective-permute-done((f32[256,512]{1,0:T(8,128)}, f32[256,512]{1,0:T(8,128)}, u32[]{:S(2)}, u32[]{:S(2)}) %collective-permute-start.10) | collective-permute-done | bytes 524320 | tf_op jit(solution)/shard_map/ppermute | solution.py:36
  87.5 1.5 add_add_fusion.4
  90.2 3.0 %collective-permute-start.12 = (f32[128,512]{1,0:T(8,128)S(1)}, f32[128,512]{1,0:T(8,128)S(1)}, u32[]{:S(2)}, u32[]{:S(2)}) collective-permute-start(f32[128,512]{1,0:T(8,128)S(1)} %get-tuple-element.59), channel_id=1, source_target_pairs={{96,0},{97,1},{98,2},{99,3},{100,4},{101,5},{102,6},{103,7},{104,8... | collective-permute-start | bytes 786440 | tf_op jit(solution)/shard_map/ppermute | solution.py:36
  93.2 1.7 slice_add_fusion
  95.0 3.3 %collective-permute-done.12 = f32[128,512]{1,0:T(8,128)S(1)} collective-permute-done((f32[128,512]{1,0:T(8,128)S(1)}, f32[128,512]{1,0:T(8,128)S(1)}, u32[]{:S(2)}, u32[]{:S(2)}) %collective-permute-start.12) | collective-permute-done | bytes 262176 | tf_op jit(solution)/shard_map/ppermute | solution.py:36
  98.4 5.1 %collective-permute-done.13 = f32[128,512]{1,0:T(8,128)S(1)} collective-permute-done((f32[128,512]{1,0:T(8,128)S(1)}, f32[128,512]{1,0:T(8,128)S(1)}, u32[]{:S(2)}, u32[]{:S(2)}) %collective-permute-start.13) | collective-permute-done | bytes 262176 | tf_op jit(solution)/shard_map/ppermute | solution.py:36
  107.4 3.2 %collective-permute-start.16 = (f32[256,512]{1,0:T(8,128)S(1)}, f32[256,512]{1,0:T(8,128)S(1)}, u32[]{:S(2)}, u32[]{:S(2)}) collective-permute-start(f32[256,512]{1,0:T(8,128)S(1)} %pad_maximum_fusion.3), channel_id=1, source_target_pairs={{96,0},{97,1},{98,2},{99,3},{100,4},{101,5},{102,6},{103,7},{104,8... | collective-permute-start | bytes 1572872 | tf_op jit(solution)/shard_map/ppermute | solution.py:36
  112.8 9.8 %collective-permute-done.15 = f32[256,512]{1,0:T(8,128)S(1)} collective-permute-done((f32[256,512]{1,0:T(8,128)S(1)}, f32[256,512]{1,0:T(8,128)S(1)}, u32[]{:S(2)}, u32[]{:S(2)}) %collective-permute-start.15) | collective-permute-done | bytes 524320 | tf_op jit(solution)/shard_map/ppermute | solution.py:36
  123.4 2.8 %collective-permute-done.19 = f32[128,512]{1,0:T(8,128)S(1)} collective-permute-done((f32[128,512]{1,0:T(8,128)S(1)}, f32[128,512]{1,0:T(8,128)S(1)}, u32[]{:S(2)}, u32[]{:S(2)}) %collective-permute-start.19) | collective-permute-done | bytes 262176 | tf_op jit(solution)/shard_map/ppermute | solution.py:36
  128.4 4.5 %collective-permute-start.23 = (f32[256,512]{1,0:T(8,128)S(1)}, f32[256,512]{1,0:T(8,128)S(1)}, u32[]{:S(2)}, u32[]{:S(2)}) collective-permute-start(f32[256,512]{1,0:T(8,128)S(1)} %add_add_fusion.3), channel_id=1, source_target_pairs={{0,128},{1,129},{2,130},{3,131},{4,132},{5,133},{6,134},{7,135},{8... | collective-permute-start | bytes 1572872 | tf_op jit(solution)/shard_map/ppermute | solution.py:36
  132.9 2.1 %collective-permute-done.24 = f32[256,512]{1,0:T(8,128)S(1)} collective-permute-done((f32[256,512]{1,0:T(8,128)S(1)}, f32[256,512]{1,0:T(8,128)S(1)}, u32[]{:S(2)}, u32[]{:S(2)}) %collective-permute-start.24) | collective-permute-done | bytes 524320 | tf_op jit(solution)/shard_map/ppermute | solution.py:36
  135.9 2.7 %collective-permute-start.21 = (f32[256,512]{1,0:T(8,128)S(1)}, f32[256,512]{1,0:T(8,128)S(1)}, u32[]{:S(2)}, u32[]{:S(2)}) collective-permute-start(f32[256,512]{1,0:T(8,128)S(1)} %add.143), channel_id=1, source_target_pairs={{32,16},{80,113},{96,128},{0,135},{64,0},{65,33},{33,32},{113,145}... | collective-permute-start | bytes 1572872 | tf_op jit(solution)/shard_map/ppermute | solution.py:36
  139.3 1.7 collective-permute-done.23
  141.1 5.2 %collective-permute-done.21 = f32[256,512]{1,0:T(8,128)S(1)} collective-permute-done((f32[256,512]{1,0:T(8,128)S(1)}, f32[256,512]{1,0:T(8,128)S(1)}, u32[]{:S(2)}, u32[]{:S(2)}) %collective-permute-start.21) | collective-permute-done | bytes 524320 | tf_op jit(solution)/shard_map/ppermute | solution.py:36
  150.3 15.4 %collective-permute-done.29 = f32[256,512]{1,0:T(8,128)S(1)} collective-permute-done((f32[256,512]{1,0:T(8,128)S(1)}, f32[256,512]{1,0:T(8,128)S(1)}, u32[]{:S(2)}, u32[]{:S(2)}) %collective-permute-start.29) | collective-permute-done | bytes 524320 | tf_op jit(solution)/shard_map/ppermute | solution.py:36
  165.8 26.8 %collective-permute-done.27 = f32[256,512]{1,0:T(8,128)S(1)} collective-permute-done((f32[256,512]{1,0:T(8,128)S(1)}, f32[256,512]{1,0:T(8,128)S(1)}, u32[]{:S(2)}, u32[]{:S(2)}) %collective-permute-start.27) | collective-permute-done | bytes 524320 | tf_op jit(solution)/shard_map/ppermute | solution.py:36
  (75 shorter events, 26.1 us)
Async XLA Ops:
  0.0 25.3 %collective-permute-start = (bf16[2,512,512]{2,1,0:T(8,128)(2,1)}, bf16[2,512,512]{2,1,0:T(8,128)(2,1)S(1)}, u32[]{:S(2)}, u32[]{:S(2)}) collective-permute-start(bf16[2,512,512]{2,1,0:T(8,128)(2,1)} %refs_0_.3), channel_id=1, source_target_pairs={{1,0},{2,1},{3,2},{4,3},{5,4},{6,5},{7,6},{0,7},{9,8},{10,9},{11,1... | collective-permute-start | bytes 3145736 | tf_op jit(solution)/shard_map/ppermute | solution.py:36
  0.1 25.2 %collective-permute-start.1 = (bf16[2,512,512]{2,1,0:T(8,128)(2,1)}, bf16[2,512,512]{2,1,0:T(8,128)(2,1)S(1)}, u32[]{:S(2)}, u32[]{:S(2)}) collective-permute-start(bf16[2,512,512]{2,1,0:T(8,128)(2,1)} %refs_0_.3), channel_id=1, source_target_pairs={{7,0},{0,1},{1,2},{2,3},{3,4},{4,5},{5,6},{6,7},{15,8},{8,9},{9,10... | collective-permute-start | bytes 3145736 | tf_op jit(solution)/shard_map/ppermute | solution.py:36
  2.0 26.2 %collective-permute-start.2 = (bf16[2,512,512]{2,1,0:T(8,128)(2,1)}, bf16[2,512,512]{2,1,0:T(8,128)(2,1)S(1)}, u32[]{:S(2)}, u32[]{:S(2)}) collective-permute-start(bf16[2,512,512]{2,1,0:T(8,128)(2,1)} %refs_0_.3), channel_id=1, source_target_pairs={{8,0},{9,1},{10,2},{11,3},{12,4},{13,5},{14,6},{15,7},{0,8},{1,9},... | collective-permute-start | bytes 3145736 | tf_op jit(solution)/shard_map/ppermute | solution.py:36
  34.2 6.6 %collective-permute-start.3 = (f32[4,256,512]{2,1,0:T(8,128)S(1)}, f32[4,256,512]{2,1,0:T(8,128)S(1)}, u32[]{:S(2)}, u32[]{:S(2)}) collective-permute-start(f32[4,256,512]{2,1,0:T(8,128)S(1)} %get-tuple-element.34), channel_id=1, source_target_pairs={{16,0},{17,1},{18,2},{19,3},{20,4},{21,5},{22,6},{23,7},{24,8},{25... | collective-permute-start | bytes 6291464 | tf_op jit(solution)/shard_map/ppermute | solution.py:36
  34.3 26.9 %collective-permute-start.6 = (bf16[2,512,512]{2,1,0:T(8,128)(2,1)S(1)}, bf16[2,512,512]{2,1,0:T(8,128)(2,1)S(1)}, u32[]{:S(2)}, u32[]{:S(2)}) collective-permute-start(bf16[2,512,512]{2,1,0:T(8,128)(2,1)S(1)} %collective-permute-done.refs_1_.refs_2_), channel_id=1, source_target_pairs={{1,0},{2,1},{3,2},{4,3},{5,4},{6,5},{7,6},{0,7},{9,8},{10,9},{11,1... | collective-permute-start | bytes 3145736 | tf_op jit(solution)/shard_map/ppermute | solution.py:36
  35.3 26.7 %collective-permute-start.7 = (bf16[2,512,512]{2,1,0:T(8,128)(2,1)S(1)}, bf16[2,512,512]{2,1,0:T(8,128)(2,1)S(1)}, u32[]{:S(2)}, u32[]{:S(2)}) collective-permute-start(bf16[2,512,512]{2,1,0:T(8,128)(2,1)S(1)} %collective-permute-done.1.refs_2_.refs_1_), channel_id=1, source_target_pairs={{7,0},{0,1},{1,2},{2,3},{3,4},{4,5},{5,6},{6,7},{15,8},{8,9},{9,10... | collective-permute-start | bytes 3145736 | tf_op jit(solution)/shard_map/ppermute | solution.py:36
  37.6 26.6 %collective-permute-start.8 = (bf16[2,512,512]{2,1,0:T(8,128)(2,1)S(1)}, bf16[2,512,512]{2,1,0:T(8,128)(2,1)S(1)}, u32[]{:S(2)}, u32[]{:S(2)}) collective-permute-start(bf16[2,512,512]{2,1,0:T(8,128)(2,1)S(1)} %collective-permute-done.refs_1_.refs_2_), channel_id=1, source_target_pairs={{8,0},{9,1},{10,2},{11,3},{12,4},{13,5},{14,6},{15,7},{0,8},{1,9},... | collective-permute-start | bytes 3145736 | tf_op jit(solution)/shard_map/ppermute | solution.py:36
  40.8 8.1 %collective-permute-start.4 = (f32[128,512]{1,0:T(8,128)S(1)}, f32[128,512]{1,0:T(8,128)S(1)}, u32[]{:S(2)}, u32[]{:S(2)}) collective-permute-start(f32[128,512]{1,0:T(8,128)S(1)} %get-tuple-element.64), channel_id=1, source_target_pairs={{96,0},{97,1},{98,2},{99,3},{100,4},{101,5},{102,6},{103,7},{104,8... | collective-permute-start | bytes 786440 | tf_op jit(solution)/shard_map/ppermute | solution.py:36
  42.6 9.2 %collective-permute-start.5 = (f32[128,512]{1,0:T(8,128)S(1)}, f32[128,512]{1,0:T(8,128)S(1)}, u32[]{:S(2)}, u32[]{:S(2)}) collective-permute-start(f32[128,512]{1,0:T(8,128)S(1)} %get-tuple-element.63), channel_id=1, source_target_pairs={{32,0},{33,1},{34,2},{35,3},{36,4},{37,5},{38,6},{39,7},{40,8},{41... | collective-permute-start | bytes 786440 | tf_op jit(solution)/shard_map/ppermute | solution.py:36
  44.4 19.9 %copy-start.1 = (bf16[2,512,512]{2,1,0:T(8,128)(2,1)S(1)}, bf16[2,512,512]{2,1,0:T(8,128)(2,1)}, u32[]{:S(2)}) copy-start(bf16[2,512,512]{2,1,0:T(8,128)(2,1)} %refs_0_.3) | copy-start | bytes 3145732
  71.7 17.4 %collective-permute-start.11 = (f32[4,256,512]{2,1,0:T(8,128)}, f32[4,256,512]{2,1,0:T(8,128)}, u32[]{:S(2)}, u32[]{:S(2)}) collective-permute-start(f32[4,256,512]{2,1,0:T(8,128)} %get-tuple-element.42), channel_id=1, source_target_pairs={{16,0},{17,1},{18,2},{19,3},{20,4},{21,5},{22,6},{23,7},{24,8},{25... | collective-permute-start | bytes 6291464 | tf_op jit(solution)/shard_map/ppermute | solution.py:36
  71.7 15.9 %collective-permute-start.10 = (f32[256,512]{1,0:T(8,128)}, f32[256,512]{1,0:T(8,128)}, u32[]{:S(2)}, u32[]{:S(2)}) collective-permute-start(f32[256,512]{1,0:T(8,128)} %pad_maximum_fusion.2), channel_id=1, source_target_pairs={{32,0},{33,1},{34,2},{35,3},{36,4},{37,5},{38,6},{39,7},{40,8},{41... | collective-permute-start | bytes 1572872 | tf_op jit(solution)/shard_map/ppermute | solution.py:36
  72.5 15.1 %collective-permute-start.9 = (f32[256,512]{1,0:T(8,128)}, f32[256,512]{1,0:T(8,128)}, u32[]{:S(2)}, u32[]{:S(2)}) collective-permute-start(f32[256,512]{1,0:T(8,128)} %pad_maximum_fusion.1), channel_id=1, source_target_pairs={{96,0},{97,1},{98,2},{99,3},{100,4},{101,5},{102,6},{103,7},{104,8... | collective-permute-start | bytes 1572872 | tf_op jit(solution)/shard_map/ppermute | solution.py:36
  75.5 28.1 %collective-permute-start.14 = (bf16[2,512,512]{2,1,0:T(8,128)(2,1)}, bf16[2,512,512]{2,1,0:T(8,128)(2,1)S(1)}, u32[]{:S(2)}, u32[]{:S(2)}) collective-permute-start(bf16[2,512,512]{2,1,0:T(8,128)(2,1)} %copy-done.4), channel_id=1, source_target_pairs={{8,0},{9,1},{10,2},{11,3},{12,4},{13,5},{14,6},{15,7},{0,8},{1,9},... | collective-permute-start | bytes 3145736 | tf_op jit(solution)/shard_map/ppermute | solution.py:36
  90.2 8.2 %collective-permute-start.12 = (f32[128,512]{1,0:T(8,128)S(1)}, f32[128,512]{1,0:T(8,128)S(1)}, u32[]{:S(2)}, u32[]{:S(2)}) collective-permute-start(f32[128,512]{1,0:T(8,128)S(1)} %get-tuple-element.59), channel_id=1, source_target_pairs={{96,0},{97,1},{98,2},{99,3},{100,4},{101,5},{102,6},{103,7},{104,8... | collective-permute-start | bytes 786440 | tf_op jit(solution)/shard_map/ppermute | solution.py:36
  94.9 8.6 %collective-permute-start.13 = (f32[128,512]{1,0:T(8,128)S(1)}, f32[128,512]{1,0:T(8,128)S(1)}, u32[]{:S(2)}, u32[]{:S(2)}) collective-permute-start(f32[128,512]{1,0:T(8,128)S(1)} %get-tuple-element.58), channel_id=1, source_target_pairs={{32,0},{33,1},{34,2},{35,3},{36,4},{37,5},{38,6},{39,7},{40,8},{41... | collective-permute-start | bytes 786440 | tf_op jit(solution)/shard_map/ppermute | solution.py:36
  104.7 5.9 %collective-permute-start.18 = (f32[256,512]{1,0:T(8,128)S(1)}, f32[256,512]{1,0:T(8,128)S(1)}, u32[]{:S(2)}, u32[]{:S(2)}) collective-permute-start(f32[256,512]{1,0:T(8,128)S(1)} %bitcast.42), channel_id=1, source_target_pairs={{48,32},{80,64},{112,96},{16,0},{176,160},{208,192},{240,224},{144... | collective-permute-start | bytes 1572872 | tf_op jit(solution)/shard_map/ppermute | solution.py:36
  106.0 16.5 %collective-permute-start.15 = (f32[256,512]{1,0:T(8,128)S(1)}, f32[256,512]{1,0:T(8,128)S(1)}, u32[]{:S(2)}, u32[]{:S(2)}) collective-permute-start(f32[256,512]{1,0:T(8,128)S(1)} %add_add_fusion.4), channel_id=1, source_target_pairs={{128,0},{129,1},{130,2},{131,3},{132,4},{133,5},{134,6},{135,7},{1... | collective-permute-start | bytes 1572872 | tf_op jit(solution)/shard_map/ppermute | solution.py:36
  107.3 15.9 %collective-permute-start.17 = (f32[256,512]{1,0:T(8,128)S(1)}, f32[256,512]{1,0:T(8,128)S(1)}, u32[]{:S(2)}, u32[]{:S(2)}) collective-permute-start(f32[256,512]{1,0:T(8,128)S(1)} %pad_maximum_fusion.4), channel_id=1, source_target_pairs={{32,0},{33,1},{34,2},{35,3},{36,4},{37,5},{38,6},{39,7},{40,8},{41... | collective-permute-start | bytes 1572872 | tf_op jit(solution)/shard_map/ppermute | solution.py:36
  107.4 15.8 %collective-permute-start.16 = (f32[256,512]{1,0:T(8,128)S(1)}, f32[256,512]{1,0:T(8,128)S(1)}, u32[]{:S(2)}, u32[]{:S(2)}) collective-permute-start(f32[256,512]{1,0:T(8,128)S(1)} %pad_maximum_fusion.3), channel_id=1, source_target_pairs={{96,0},{97,1},{98,2},{99,3},{100,4},{101,5},{102,6},{103,7},{104,8... | collective-permute-start | bytes 1572872 | tf_op jit(solution)/shard_map/ppermute | solution.py:36
  110.8 12.6 %collective-permute-start.20 = (f32[128,512]{1,0:T(8,128)S(1)}, f32[128,512]{1,0:T(8,128)S(1)}, u32[]{:S(2)}, u32[]{:S(2)}) collective-permute-start(f32[128,512]{1,0:T(8,128)S(1)} %get-tuple-element.66), channel_id=1, source_target_pairs={{2,34},{14,46},{19,51},{31,63},{36,68},{40,72},{53,85},{57,89},{70... | collective-permute-start | bytes 786440 | tf_op jit(solution)/shard_map/ppermute | solution.py:36
  111.5 14.8 %collective-permute-start.19 = (f32[128,512]{1,0:T(8,128)S(1)}, f32[128,512]{1,0:T(8,128)S(1)}, u32[]{:S(2)}, u32[]{:S(2)}) collective-permute-start(f32[128,512]{1,0:T(8,128)S(1)} %get-tuple-element.65), channel_id=1, source_target_pairs={{2,98},{14,110},{19,115},{31,127},{36,4},{40,8},{53,21},{57,25},{7... | collective-permute-start | bytes 786440 | tf_op jit(solution)/shard_map/ppermute | solution.py:36
  126.3 6.6 %collective-permute-start.25 = (f32[256,512]{1,0:T(8,128)S(1)}, f32[256,512]{1,0:T(8,128)S(1)}, u32[]{:S(2)}, u32[]{:S(2)}) collective-permute-start(f32[256,512]{1,0:T(8,128)S(1)} %maximum_add_fusion), channel_id=1, source_target_pairs={{0,32},{12,44},{17,49},{29,61},{34,66},{46,78},{51,83},{63,95},{68... | collective-permute-start | bytes 1572872 | tf_op jit(solution)/shard_map/ppermute | solution.py:36
  127.0 8.0 %collective-permute-start.24 = (f32[256,512]{1,0:T(8,128)S(1)}, f32[256,512]{1,0:T(8,128)S(1)}, u32[]{:S(2)}, u32[]{:S(2)}) collective-permute-start(f32[256,512]{1,0:T(8,128)S(1)} %maximum_add_fusion), channel_id=1, source_target_pairs={{4,100},{8,104},{21,117},{25,121},{38,6},{42,10},{55,23},{59,27},{... | collective-permute-start | bytes 1572872 | tf_op jit(solution)/shard_map/ppermute | solution.py:36
  128.4 12.6 %collective-permute-start.23 = (f32[256,512]{1,0:T(8,128)S(1)}, f32[256,512]{1,0:T(8,128)S(1)}, u32[]{:S(2)}, u32[]{:S(2)}) collective-permute-start(f32[256,512]{1,0:T(8,128)S(1)} %add_add_fusion.3), channel_id=1, source_target_pairs={{0,128},{1,129},{2,130},{3,131},{4,132},{5,133},{6,134},{7,135},{8... | collective-permute-start | bytes 1572872 | tf_op jit(solution)/shard_map/ppermute | solution.py:36
  135.2 5.9 %collective-permute-start.26 = (f32[256,512]{1,0:T(8,128)S(1)}, f32[256,512]{1,0:T(8,128)S(1)}, u32[]{:S(2)}, u32[]{:S(2)}) collective-permute-start(f32[256,512]{1,0:T(8,128)S(1)} %add_add_fusion.2), channel_id=1, source_target_pairs={{32,160},{49,177},{66,194},{83,211},{100,228},{117,245},{6,134},{2... | collective-permute-start | bytes 1572872 | tf_op jit(solution)/shard_map/ppermute | solution.py:36
  135.9 10.4 %collective-permute-start.21 = (f32[256,512]{1,0:T(8,128)S(1)}, f32[256,512]{1,0:T(8,128)S(1)}, u32[]{:S(2)}, u32[]{:S(2)}) collective-permute-start(f32[256,512]{1,0:T(8,128)S(1)} %add.143), channel_id=1, source_target_pairs={{32,16},{80,113},{96,128},{0,135},{64,0},{65,33},{33,32},{113,145}... | collective-permute-start | bytes 1572872 | tf_op jit(solution)/shard_map/ppermute | solution.py:36
  138.6 7.7 %collective-permute-start.22 = (f32[256,512]{1,0:T(8,128)S(1)}, f32[256,512]{1,0:T(8,128)S(1)}, u32[]{:S(2)}, u32[]{:S(2)}) collective-permute-start(f32[256,512]{1,0:T(8,128)S(1)} %add.143), channel_id=1, source_target_pairs={{48,16},{112,113},{16,135},{81,33},{49,32},{17,144},{114,50},{82,4... | collective-permute-start | bytes 1572872 | tf_op jit(solution)/shard_map/ppermute | solution.py:36
  146.3 4.0 %collective-permute-start.30 = (f32[256,512]{1,0:T(8,128)S(1)}, f32[256,512]{1,0:T(8,128)S(1)}, u32[]{:S(2)}, u32[]{:S(2)}) collective-permute-start(f32[256,512]{1,0:T(8,128)S(1)} %add.152), channel_id=1, source_target_pairs={{232,226},{249,243},{138,132},{155,149},{172,166},{189,183},{206,1... | collective-permute-start | bytes 1572872 | tf_op jit(solution)/shard_map/ppermute | solution.py:36
  147.0 18.7 %collective-permute-start.29 = (f32[256,512]{1,0:T(8,128)S(1)}, f32[256,512]{1,0:T(8,128)S(1)}, u32[]{:S(2)}, u32[]{:S(2)}) collective-permute-start(f32[256,512]{1,0:T(8,128)S(1)} %add.149), channel_id=1, source_target_pairs={{240,97},{224,98},{208,151},{144,150},{160,0},{225,114},{241,115},... | collective-permute-start | bytes 1572872 | tf_op jit(solution)/shard_map/ppermute | solution.py:36
  148.3 17.6 %collective-permute-start.28 = (f32[256,512]{1,0:T(8,128)S(1)}, f32[256,512]{1,0:T(8,128)S(1)}, u32[]{:S(2)}, u32[]{:S(2)}) collective-permute-start(f32[256,512]{1,0:T(8,128)S(1)} %add.152), channel_id=1, source_target_pairs={{160,166},{177,183},{194,192},{211,209},{228,226},{245,243},{134,1... | collective-permute-start | bytes 1572872 | tf_op jit(solution)/shard_map/ppermute | solution.py:36
  149.0 43.6 %collective-permute-start.27 = (f32[256,512]{1,0:T(8,128)S(1)}, f32[256,512]{1,0:T(8,128)S(1)}, u32[]{:S(2)}, u32[]{:S(2)}) collective-permute-start(f32[256,512]{1,0:T(8,128)S(1)} %add.149), channel_id=1, source_target_pairs={{192,97},{176,151},{128,150},{209,114},{129,160},{161,167},{162,48... | collective-permute-start | bytes 1572872 | tf_op jit(solution)/shard_map/ppermute | solution.py:36
  (5 other events, 39.7 us)

commit v4 on v3

--- a/solution.py
+++ b/solution.py
@@ -81,20 +81,15 @@
     return min((a - b) % n, (b - a) % n)
 
 
-def hops(y_lo, x, core, h, z, row, col):
-    y_at, y_to = h * 2 + y_lo, row // NZ * 2 + col // 8
-    return ring(x, col // 2 % NX, NX) + ring(y_at, y_to, 4) + ring(z, row % NZ, NZ) + 0.1 * (core != col % 2)
-
-
-def assign(units, y_lo, h, z):
+def assign(units):
     best = {0: (0.0, ())}
-    for _, row, col, _ in units:
+    for _, _, col, _ in units:
         grown = {}
         for mask, (cost, taken) in best.items():
             for place in range(8):
                 if mask >> place & 1:
                     continue
-                total = cost + hops(y_lo, place // 2, place % 2, h, z, row, col) ** 2
+                total = cost + ring(place // 2, col // 2 % NX, NX) ** 2 + 0.1 * (place % 2 != col % 2)
                 key = mask | 1 << place
                 if key not in grown or total < grown[key][0]:
                     grown[key] = (total, taken + (place,))
@@ -102,24 +97,30 @@
     return min(best.values())[1]
 
 
+def plane(h, row, col):
+    return h if row // NZ == col // NZ else 1 - h
+
+
 @functools.cache
 def plan():
     tables = np.zeros((2, GROUPS, 2, NX), np.int32)
     code_c = np.zeros((GROUPS,), np.int32)
     target_c = {}
+    over = {0: [], 1: []}
     final = {(batch, half): [] for batch in range(3) for half in range(2)}
     for h in range(2):
         for z in range(NZ):
             own = block(h, z)
             for batch in range(2):
                 units = units_of(PAIRS_B if batch else PAIRS_A, h, z)
-                for (code, row, col, half), place in zip(units, assign(units, batch, h, z)):
-                    x, core = place // 2, place % 2
+                for (code, row, col, half), place in zip(units, assign(units)):
+                    x, core, y = place // 2, place % 2, plane(h, row, col)
                     tables[batch, own, core, x] = code
-                    final[batch, half].append((device(batch, x, core, own), col * GROUPS + row))
+                    over[batch].append((device(1 - y, x, core, own), device(y, x, core, own)))
+                    final[batch, half].append((device(y, x, core, own), col * GROUPS + row))
             ((code, row, col, half),) = units_of(PAIRS_C, h, z)
             code_c[own] = code
-            target_c[own] = (col // 8, col // 2 % NX, col % 2)
+            target_c[own] = (1 - h, col // 2 % NX, col % 2)
             final[2, half].append((device(*target_c[own], own), col * GROUPS + row))
     local = np.zeros((2, 16, GROUPS, 2, NX), np.int32)
     for aux in range(16):
@@ -127,7 +128,7 @@
         for j in range(NX):
             local[:, aux, :, 0, j] = tables[:, :, core, (x + j) % NX]
             local[:, aux, :, 1, j] = tables[:, :, 1 - core, (x + j) % NX]
-    return local.reshape(2, 16 * GROUPS, 2 * NX), code_c, target_c, final
+    return local.reshape(2, 16 * GROUPS, 2 * NX), code_c, target_c, over, final
 
 
 def dot_t(a, b):
@@ -188,6 +189,20 @@
     ]
 
 
+def copy_kernel(source, out):
+    out[...] = source[...]
+
+
+def placed(value):
+    return pl.pallas_call(
+        copy_kernel,
+        out_shape=pltpu.VMEM(value.shape, value.dtype),
+        in_specs=[pl.BlockSpec(memory_space=pltpu.VMEM)],
+        out_specs=pl.BlockSpec(memory_space=pltpu.VMEM),
+        compiler_params=pltpu.CompilerParams(vmem_limit_bytes=VMEM_LIMIT),
+    )(value)
+
+
 def one_core(value, targets):
     def at(core_of):
         return lambda y, x, c, step: (step // NX, x + step % NX, core_of(c))
@@ -237,49 +252,37 @@
     return keep[0] + got[0], right, left
 
 
-def over_y(total, y_to):
-    pairs = [
-        (device(1 - y_to, x, core, b), device(y_to, x, core, b))
-        for x in range(NX)
-        for core in range(2)
-        for b in range(GROUPS)
-    ]
-    return total + send(total, pairs)
-
-
 def together(*values):
     return lax.optimization_barrier(values)
 
 
 def per_device(half_b):
-    local, code_c, target_c, final = plan()
+    local, code_c, target_c, over, final = plan()
     aux, blk = lax.axis_index("aux"), lax.axis_index("blk")
     place = aux * GROUPS + blk
     table_a, table_b = jnp.asarray(local[0])[place], jnp.asarray(local[1])[place]
     table_c = jnp.asarray(code_c)[blk].reshape(1)
 
-    held = {O: half_b}
+    held = {O: placed(half_b)}
     held[PZ] = send(half_b, FROM_UP)
     held[MZ] = send(half_b, FROM_DOWN)
     held[Y0] = send(half_b, FROM_OTHER)
-    held[PZ], held[MZ], held[Y0] = together(held[PZ], held[MZ], held[Y0])
+    held[O], held[PZ], held[MZ], held[Y0] = together(held[O], held[PZ], held[MZ], held[Y0])
 
     held[PP] = send(held[PZ], FROM_UP)
     held[MM] = send(held[MZ], FROM_DOWN)
     held[Y1] = send(held[PZ], FROM_OTHER)
     keep, given = products(table_a, [held[n] for n in HELD_A], HELD_A, PAIRS_A, (NX, NX))
     own_a, right_a, left_a = near(keep, send(given, CORE_SWAP))
-    own_a, right_a, left_a, held[PP], held[MM], held[Y1] = together(
-        own_a, right_a, left_a, held[PP], held[MM], held[Y1]
-    )
+    total_a = own_a + send(right_a, FROM_LEFT) + send(left_a, FROM_RIGHT)
+    total_a, held[PP], held[MM], held[Y1] = together(total_a, held[PP], held[MM], held[Y1])
 
     held[Y2] = send(held[PP], FROM_OTHER)
-    total_a = own_a + send(right_a, FROM_LEFT) + send(left_a, FROM_RIGHT)
     keep, given = products(table_b, [held[n] for n in HELD_B], HELD_B, PAIRS_B, (NX, NX))
     own_b, right_b, left_b = near(keep, send(given, CORE_SWAP))
-    total_a, own_b, right_b, left_b, held[Y2] = together(total_a, own_b, right_b, left_b, held[Y2])
-
-    done_a = over_y(total_a, 0)
+    own_b, right_b, left_b, held[Y2] = together(own_b, right_b, left_b, held[Y2])
+
+    done_a = total_a + send(total_a, over[0])
     total_b = own_b + send(right_b, FROM_LEFT) + send(left_b, FROM_RIGHT)
     (part_c,) = products(table_c, [held[n] for n in HELD_C], HELD_C, PAIRS_C, (1,))
     part_c = one_far(one_core(part_c[0], target_c), target_c)
@@ -287,7 +290,7 @@
 
     top = send(done_a, final[0, 0])
     bottom = send(done_a, final[0, 1])
-    done_b = over_y(total_b, 1)
+    done_b = total_b + send(total_b, over[1])
     done_c = one_y(one_near(part_c, target_c), target_c)
     top, bottom, done_b, done_c = together(top, bottom, done_b, done_c)
 

time: 194 us -> 185 us (0.954)
  the two profiles are of different devices: /device:TPU:70 before, /device:TPU:29 now
where the time goes in v4:
time: 185 us; the launch traced here: 184 us
  waiting for transfers between devices  114 us (62%)
  starting transfers between devices  47.1 us (25%)
  Pallas kernels  12.6 us (7%)
  other arithmetic  6.47 us (3%)
  local copies, waits for them, and re-layouts  4.1 us (2%)
    ppermute x31, waiting for transfers between devices, send(): return lax.ppermute(value, ALL, pairs)  114 us
    ppermute x31, starting transfers between devices, send(): return lax.ppermute(value, ALL, pairs)  47.1 us
    pallas_call x3, Pallas kernels, products(): pl.pallas_call(functools.partial(units_kernel, index_pairs, len(counts)),...  12.6 us
  transfers between devices with their start and end apart: 31, of which 18 were waited for; matrix products, arithmetic and copies ran while one was open for 4% of the time, Pallas kernels for 1%

profile of v4, /device:TPU:29, one launch (start us, length us, event | category | flops | bytes accessed | tf_op | source)
XLA Modules:
  0.0 184.4 jit_solution(7226683786555580497)
XLA Ops:
  0.0 5.6 %collective-permute-start = (bf16[2,512,512]{2,1,0:T(8,128)(2,1)}, bf16[2,512,512]{2,1,0:T(8,128)(2,1)S(1)}, u32[]{:S(2)}, u32[]{:S(2)}) collective-permute-start(bf16[2,512,512]{2,1,0:T(8,128)(2,1)} %source.1), channel_id=1, source_target_pairs={{1,0},{2,1},{3,2},{4,3},{5,4},{6,5},{7,6},{0,7},{9,8},{10,9},{11,1... | collective-permute-start | bytes 3145736 | tf_op jit(solution)/shard_map/ppermute | solution.py:36
  6.5 1.3 copy-done.4
  8.6 19.1 %collective-permute-done.refs_1_.refs_2_ = bf16[2,512,512]{2,1,0:T(8,128)(2,1)S(1)} collective-permute-done((bf16[2,512,512]{2,1,0:T(8,128)(2,1)}, bf16[2,512,512]{2,1,0:T(8,128)(2,1)S(1)}, u32[]{:S(2)}, u32[]{:S(2)}) %collective-permute-start) | collective-permute-done | bytes 1048608 | tf_op jit(solution)/shard_map/ppermute | solution.py:36
  27.7 3.1 %collective-permute-done.1.refs_2_.refs_1_ = bf16[2,512,512]{2,1,0:T(8,128)(2,1)S(1)} collective-permute-done((bf16[2,512,512]{2,1,0:T(8,128)(2,1)}, bf16[2,512,512]{2,1,0:T(8,128)(2,1)S(1)}, u32[]{:S(2)}, u32[]{:S(2)}) %collective-permute-start.1) | collective-permute-done | bytes 1048608 | tf_op jit(solution)/shard_map/ppermute | solution.py:36
  31.1 5.4 %shard_map.47 = (f32[4,256,512]{2,1,0:T(8,128)S(1)}, f32[4,256,512]{2,1,0:T(8,128)S(1)}) custom-call(s32[8]{0:T(128)S(1)} %get-tuple-element.63.table, bf16[2,512,512]{2,1,0:T(8,128)(2,1)S(1)} %shard_map.46.refs_0_, bf16[2,512,512]{2,1,0:T(8,128)(2,1)S(1)} %collective-permute-done.refs_1_.refs_2_, ...), custom_call_target="tpu_custom_call" | custom-call | tf_op jit(solution)/shard_map/pallas_call | solution.py:174
  36.5 2.0 %collective-permute-start.3 = (f32[4,256,512]{2,1,0:T(8,128)S(1)}, f32[4,256,512]{2,1,0:T(8,128)S(1)}, u32[]{:S(2)}, u32[]{:S(2)}) collective-permute-start(f32[4,256,512]{2,1,0:T(8,128)S(1)} %get-tuple-element.33), channel_id=1, source_target_pairs={{16,0},{17,1},{18,2},{19,3},{20,4},{21,5},{22,6},{23,7},{24,8},{25... | collective-permute-start | bytes 6291464 | tf_op jit(solution)/shard_map/ppermute | solution.py:36
  38.5 2.7 %collective-permute-start.8 = (bf16[2,512,512]{2,1,0:T(8,128)(2,1)S(1)}, bf16[2,512,512]{2,1,0:T(8,128)(2,1)S(1)}, u32[]{:S(2)}, u32[]{:S(2)}) collective-permute-start(bf16[2,512,512]{2,1,0:T(8,128)(2,1)S(1)} %collective-permute-done.refs_1_.refs_2_), channel_id=1, source_target_pairs={{1,0},{2,1},{3,2},{4,3},{5,4},{6,5},{7,6},{0,7},{9,8},{10,9},{11,1... | collective-permute-start | bytes 3145736 | tf_op jit(solution)/shard_map/ppermute | solution.py:36
  42.9 1.3 collective-permute-start.4
  44.2 5.6 %collective-permute-done.6 = f32[128,512]{1,0:T(8,128)S(1)} collective-permute-done((f32[128,512]{1,0:T(8,128)S(1)}, f32[128,512]{1,0:T(8,128)S(1)}, u32[]{:S(2)}, u32[]{:S(2)}) %collective-permute-start.6) | collective-permute-done | bytes 262176 | tf_op jit(solution)/shard_map/ppermute | solution.py:36
  50.5 2.0 %collective-permute-start.5 = (f32[256,512]{1,0:T(8,128)S(1)}, f32[256,512]{1,0:T(8,128)S(1)}, u32[]{:S(2)}, u32[]{:S(2)}) collective-permute-start(f32[256,512]{1,0:T(8,128)S(1)} %pad_maximum_fusion.1), channel_id=1, source_target_pairs={{96,0},{97,1},{98,2},{99,3},{100,4},{101,5},{102,6},{103,7},{104,8... | collective-permute-start | bytes 1572872 | tf_op jit(solution)/shard_map/ppermute | solution.py:36
  52.4 10.7 %collective-permute-done.7 = f32[256,512]{1,0:T(8,128)S(1)} collective-permute-done((f32[256,512]{1,0:T(8,128)S(1)}, f32[256,512]{1,0:T(8,128)S(1)}, u32[]{:S(2)}, u32[]{:S(2)}) %collective-permute-start.7) | collective-permute-done | bytes 524320 | tf_op jit(solution)/shard_map/ppermute | solution.py:36
  64.2 2.6 %collective-permute-done.9.refs_4_.refs_0_ = bf16[2,512,512]{2,1,0:T(8,128)(2,1)S(1)} collective-permute-done((bf16[2,512,512]{2,1,0:T(8,128)(2,1)S(1)}, bf16[2,512,512]{2,1,0:T(8,128)(2,1)S(1)}, u32[]{:S(2)}, u32[]{:S(2)}) %collective-permute-start.9) | collective-permute-done | bytes 1048608 | tf_op jit(solution)/shard_map/ppermute | solution.py:36
  67.0 6.0 %shard_map.48 = (f32[4,256,512]{2,1,0:T(8,128)S(1)}, f32[4,256,512]{2,1,0:T(8,128)}) custom-call(s32[8]{0:T(128)S(1)} %get-tuple-element.62.table, bf16[2,512,512]{2,1,0:T(8,128)(2,1)S(1)} %shard_map.46.refs_0_, bf16[2,512,512]{2,1,0:T(8,128)(2,1)S(1)} %collective-permute-done.1.refs_2_.refs_1_, ...), custom_call_target="tpu_custom_call" | custom-call | tf_op jit(solution)/shard_map/pallas_call | solution.py:174
  73.1 1.3 copy-done.2
  77.2 1.3 collective-permute-start.11
  80.7 1.5 collective-permute-start.13
  82.2 1.7 slice_add_fusion
  84.1 4.2 %collective-permute-done.13 = f32[128,512]{1,0:T(8,128)S(1)} collective-permute-done((f32[128,512]{1,0:T(8,128)S(1)}, f32[128,512]{1,0:T(8,128)S(1)}, u32[]{:S(2)}, u32[]{:S(2)}) %collective-permute-start.13) | collective-permute-done | bytes 262176 | tf_op jit(solution)/shard_map/ppermute | solution.py:36
  88.4 3.7 %collective-permute-done.14 = f32[128,512]{1,0:T(8,128)S(1)} collective-permute-done((f32[128,512]{1,0:T(8,128)S(1)}, f32[128,512]{1,0:T(8,128)S(1)}, u32[]{:S(2)}, u32[]{:S(2)}) %collective-permute-start.14) | collective-permute-done | bytes 262176 | tf_op jit(solution)/shard_map/ppermute | solution.py:36
  92.2 10.6 %collective-permute-done.15.refs_1_ = bf16[2,512,512]{2,1,0:T(8,128)(2,1)S(1)} collective-permute-done((bf16[2,512,512]{2,1,0:T(8,128)(2,1)}, bf16[2,512,512]{2,1,0:T(8,128)(2,1)S(1)}, u32[]{:S(2)}, u32[]{:S(2)}) %collective-permute-start.15) | collective-permute-done | bytes 1048608 | tf_op jit(solution)/shard_map/ppermute | solution.py:36
  104.0 3.1 %collective-permute-start.18 = (f32[256,512]{1,0:T(8,128)S(1)}, f32[256,512]{1,0:T(8,128)S(1)}, u32[]{:S(2)}, u32[]{:S(2)}) collective-permute-start(f32[256,512]{1,0:T(8,128)S(1)} %bitcast.46), channel_id=1, source_target_pairs={{48,32},{80,64},{112,96},{16,0},{176,160},{208,192},{240,224},{144... | collective-permute-start | bytes 1572872 | tf_op jit(solution)/shard_map/ppermute | solution.py:36
  107.4 1.2 collective-permute-start.16
  108.6 3.0 %collective-permute-done.11 = f32[256,512]{1,0:T(8,128)S(1)} collective-permute-done((f32[256,512]{1,0:T(8,128)}, f32[256,512]{1,0:T(8,128)S(1)}, u32[]{:S(2)}, u32[]{:S(2)}) %collective-permute-start.11) | collective-permute-done | bytes 524320 | tf_op jit(solution)/shard_map/ppermute | solution.py:36
  113.2 7.7 %collective-permute-done.17 = f32[256,512]{1,0:T(8,128)S(1)} collective-permute-done((f32[256,512]{1,0:T(8,128)S(1)}, f32[256,512]{1,0:T(8,128)S(1)}, u32[]{:S(2)}, u32[]{:S(2)}) %collective-permute-start.17) | collective-permute-done | bytes 524320 | tf_op jit(solution)/shard_map/ppermute | solution.py:36
  120.9 1.6 collective-permute-done.16
  124.2 2.2 %collective-permute-start.23 = (f32[256,512]{1,0:T(8,128)S(1)}, f32[256,512]{1,0:T(8,128)S(1)}, u32[]{:S(2)}, u32[]{:S(2)}) collective-permute-start(f32[256,512]{1,0:T(8,128)S(1)} %add_add_fusion.3), channel_id=1, source_target_pairs={{192,64},{208,80},{224,96},{48,176},{112,240},{0,128},{16,144},{16... | collective-permute-start | bytes 1572872 | tf_op jit(solution)/shard_map/ppermute | solution.py:36
  127.9 10.9 %collective-permute-start.22 = (f32[256,512]{1,0:T(8,128)S(1)}, f32[256,512]{1,0:T(8,128)S(1)}, u32[]{:S(2)}, u32[]{:S(2)}) collective-permute-start(f32[256,512]{1,0:T(8,128)S(1)} %add.133), channel_id=1, source_target_pairs={{48,16},{80,113},{224,135},{49,33},{81,32},{129,144},{50,50},{114,... | collective-permute-start | bytes 1572872 | tf_op jit(solution)/shard_map/ppermute | solution.py:36
  139.1 10.1 %collective-permute-done.22 = f32[256,512]{1,0:T(8,128)S(1)} collective-permute-done((f32[256,512]{1,0:T(8,128)S(1)}, f32[256,512]{1,0:T(8,128)S(1)}, u32[]{:S(2)}, u32[]{:S(2)}) %collective-permute-start.22) | collective-permute-done | bytes 524320 | tf_op jit(solution)/shard_map/ppermute | solution.py:36
  149.9 1.3 collective-permute-start.29
  151.9 1.3 collective-permute-start.27
  153.2 19.4 %collective-permute-done.29 = f32[256,512]{1,0:T(8,128)S(1)} collective-permute-done((f32[256,512]{1,0:T(8,128)S(1)}, f32[256,512]{1,0:T(8,128)S(1)}, u32[]{:S(2)}, u32[]{:S(2)}) %collective-permute-start.29) | collective-permute-done | bytes 524320 | tf_op jit(solution)/shard_map/ppermute | solution.py:36
  172.8 10.4 %collective-permute-done.27 = f32[256,512]{1,0:T(8,128)S(1)} collective-permute-done((f32[256,512]{1,0:T(8,128)S(1)}, f32[256,512]{1,0:T(8,128)S(1)}, u32[]{:S(2)}, u32[]{:S(2)}) %collective-permute-start.27) | collective-permute-done | bytes 524320 | tf_op jit(solution)/shard_map/ppermute | solution.py:36
  (78 shorter events, 20.2 us)
Async XLA Ops:
  0.0 27.7 %collective-permute-start = (bf16[2,512,512]{2,1,0:T(8,128)(2,1)}, bf16[2,512,512]{2,1,0:T(8,128)(2,1)S(1)}, u32[]{:S(2)}, u32[]{:S(2)}) collective-permute-start(bf16[2,512,512]{2,1,0:T(8,128)(2,1)} %source.1), channel_id=1, source_target_pairs={{1,0},{2,1},{3,2},{4,3},{5,4},{6,5},{7,6},{0,7},{9,8},{10,9},{11,1... | collective-permute-start | bytes 3145736 | tf_op jit(solution)/shard_map/ppermute | solution.py:36
  5.6 25.2 %collective-permute-start.1 = (bf16[2,512,512]{2,1,0:T(8,128)(2,1)}, bf16[2,512,512]{2,1,0:T(8,128)(2,1)S(1)}, u32[]{:S(2)}, u32[]{:S(2)}) collective-permute-start(bf16[2,512,512]{2,1,0:T(8,128)(2,1)} %source.1), channel_id=1, source_target_pairs={{7,0},{0,1},{1,2},{2,3},{3,4},{4,5},{5,6},{6,7},{15,8},{8,9},{9,10... | collective-permute-start | bytes 3145736 | tf_op jit(solution)/shard_map/ppermute | solution.py:36
  5.6 25.5 %collective-permute-start.2 = (bf16[2,512,512]{2,1,0:T(8,128)(2,1)}, bf16[2,512,512]{2,1,0:T(8,128)(2,1)}, u32[]{:S(2)}, u32[]{:S(2)}) collective-permute-start(bf16[2,512,512]{2,1,0:T(8,128)(2,1)} %source.1), channel_id=1, source_target_pairs={{8,0},{9,1},{10,2},{11,3},{12,4},{13,5},{14,6},{15,7},{0,8},{1,9},... | collective-permute-start | bytes 3145736 | tf_op jit(solution)/shard_map/ppermute | solution.py:36
  36.5 5.7 %collective-permute-start.3 = (f32[4,256,512]{2,1,0:T(8,128)S(1)}, f32[4,256,512]{2,1,0:T(8,128)S(1)}, u32[]{:S(2)}, u32[]{:S(2)}) collective-permute-start(f32[4,256,512]{2,1,0:T(8,128)S(1)} %get-tuple-element.33), channel_id=1, source_target_pairs={{16,0},{17,1},{18,2},{19,3},{20,4},{21,5},{22,6},{23,7},{24,8},{25... | collective-permute-start | bytes 6291464 | tf_op jit(solution)/shard_map/ppermute | solution.py:36
  38.5 25.7 %collective-permute-start.8 = (bf16[2,512,512]{2,1,0:T(8,128)(2,1)S(1)}, bf16[2,512,512]{2,1,0:T(8,128)(2,1)S(1)}, u32[]{:S(2)}, u32[]{:S(2)}) collective-permute-start(bf16[2,512,512]{2,1,0:T(8,128)(2,1)S(1)} %collective-permute-done.refs_1_.refs_2_), channel_id=1, source_target_pairs={{1,0},{2,1},{3,2},{4,3},{5,4},{6,5},{7,6},{0,7},{9,8},{10,9},{11,1... | collective-permute-start | bytes 3145736 | tf_op jit(solution)/shard_map/ppermute | solution.py:36
  41.1 25.6 %collective-permute-start.9 = (bf16[2,512,512]{2,1,0:T(8,128)(2,1)S(1)}, bf16[2,512,512]{2,1,0:T(8,128)(2,1)S(1)}, u32[]{:S(2)}, u32[]{:S(2)}) collective-permute-start(bf16[2,512,512]{2,1,0:T(8,128)(2,1)S(1)} %collective-permute-done.1.refs_2_.refs_1_), channel_id=1, source_target_pairs={{7,0},{0,1},{1,2},{2,3},{3,4},{4,5},{5,6},{6,7},{15,8},{8,9},{9,10... | collective-permute-start | bytes 3145736 | tf_op jit(solution)/shard_map/ppermute | solution.py:36
  41.1 25.9 %collective-permute-start.10 = (bf16[2,512,512]{2,1,0:T(8,128)(2,1)S(1)}, bf16[2,512,512]{2,1,0:T(8,128)(2,1)S(1)}, u32[]{:S(2)}, u32[]{:S(2)}) collective-permute-start(bf16[2,512,512]{2,1,0:T(8,128)(2,1)S(1)} %collective-permute-done.refs_1_.refs_2_), channel_id=1, source_target_pairs={{8,0},{9,1},{10,2},{11,3},{12,4},{13,5},{14,6},{15,7},{0,8},{1,9},... | collective-permute-start | bytes 3145736 | tf_op jit(solution)/shard_map/ppermute | solution.py:36
  42.3 7.4 %collective-permute-start.6 = (f32[128,512]{1,0:T(8,128)S(1)}, f32[128,512]{1,0:T(8,128)S(1)}, u32[]{:S(2)}, u32[]{:S(2)}) collective-permute-start(f32[128,512]{1,0:T(8,128)S(1)} %get-tuple-element.57), channel_id=1, source_target_pairs={{32,0},{33,1},{34,2},{35,3},{36,4},{37,5},{38,6},{39,7},{40,8},{41... | collective-permute-start | bytes 786440 | tf_op jit(solution)/shard_map/ppermute | solution.py:36
  42.9 7.5 %collective-permute-start.4 = (f32[128,512]{1,0:T(8,128)S(1)}, f32[128,512]{1,0:T(8,128)S(1)}, u32[]{:S(2)}, u32[]{:S(2)}) collective-permute-start(f32[128,512]{1,0:T(8,128)S(1)} %get-tuple-element.56), channel_id=1, source_target_pairs={{96,0},{97,1},{98,2},{99,3},{100,4},{101,5},{102,6},{103,7},{104,8... | collective-permute-start | bytes 786440 | tf_op jit(solution)/shard_map/ppermute | solution.py:36
  49.8 13.3 %collective-permute-start.7 = (f32[256,512]{1,0:T(8,128)S(1)}, f32[256,512]{1,0:T(8,128)S(1)}, u32[]{:S(2)}, u32[]{:S(2)}) collective-permute-start(f32[256,512]{1,0:T(8,128)S(1)} %pad_maximum_fusion.2), channel_id=1, source_target_pairs={{32,0},{33,1},{34,2},{35,3},{36,4},{37,5},{38,6},{39,7},{40,8},{41... | collective-permute-start | bytes 1572872 | tf_op jit(solution)/shard_map/ppermute | solution.py:36
  50.5 12.7 %collective-permute-start.5 = (f32[256,512]{1,0:T(8,128)S(1)}, f32[256,512]{1,0:T(8,128)S(1)}, u32[]{:S(2)}, u32[]{:S(2)}) collective-permute-start(f32[256,512]{1,0:T(8,128)S(1)} %pad_maximum_fusion.1), channel_id=1, source_target_pairs={{96,0},{97,1},{98,2},{99,3},{100,4},{101,5},{102,6},{103,7},{104,8... | collective-permute-start | bytes 1572872 | tf_op jit(solution)/shard_map/ppermute | solution.py:36
  74.4 5.2 %collective-permute-start.12 = (f32[4,256,512]{2,1,0:T(8,128)}, f32[4,256,512]{2,1,0:T(8,128)S(1)}, u32[]{:S(2)}, u32[]{:S(2)}) collective-permute-start(f32[4,256,512]{2,1,0:T(8,128)} %get-tuple-element.39), channel_id=1, source_target_pairs={{16,0},{17,1},{18,2},{19,3},{20,4},{21,5},{22,6},{23,7},{24,8},{25... | collective-permute-start | bytes 6291464 | tf_op jit(solution)/shard_map/ppermute | solution.py:36
  76.3 26.5 %collective-permute-start.15 = (bf16[2,512,512]{2,1,0:T(8,128)(2,1)}, bf16[2,512,512]{2,1,0:T(8,128)(2,1)S(1)}, u32[]{:S(2)}, u32[]{:S(2)}) collective-permute-start(bf16[2,512,512]{2,1,0:T(8,128)(2,1)} %copy-done.3), channel_id=1, source_target_pairs={{8,0},{9,1},{10,2},{11,3},{12,4},{13,5},{14,6},{15,7},{0,8},{1,9},... | collective-permute-start | bytes 3145736 | tf_op jit(solution)/shard_map/ppermute | solution.py:36
  77.2 34.4 %collective-permute-start.11 = (f32[256,512]{1,0:T(8,128)}, f32[256,512]{1,0:T(8,128)S(1)}, u32[]{:S(2)}, u32[]{:S(2)}) collective-permute-start(f32[256,512]{1,0:T(8,128)} %fusion.3), channel_id=1, source_target_pairs={{144,16},{176,48},{192,64},{208,80},{0,128},{32,160},{96,224},{240... | collective-permute-start | bytes 1572872 | tf_op jit(solution)/shard_map/ppermute | solution.py:36
  80.7 7.6 %collective-permute-start.13 = (f32[128,512]{1,0:T(8,128)S(1)}, f32[128,512]{1,0:T(8,128)S(1)}, u32[]{:S(2)}, u32[]{:S(2)}) collective-permute-start(f32[128,512]{1,0:T(8,128)S(1)} %get-tuple-element.55), channel_id=1, source_target_pairs={{96,0},{97,1},{98,2},{99,3},{100,4},{101,5},{102,6},{103,7},{104,8... | collective-permute-start | bytes 786440 | tf_op jit(solution)/shard_map/ppermute | solution.py:36
  84.0 8.2 %collective-permute-start.14 = (f32[128,512]{1,0:T(8,128)S(1)}, f32[128,512]{1,0:T(8,128)S(1)}, u32[]{:S(2)}, u32[]{:S(2)}) collective-permute-start(f32[128,512]{1,0:T(8,128)S(1)} %get-tuple-element.54), channel_id=1, source_target_pairs={{32,0},{33,1},{34,2},{35,3},{36,4},{37,5},{38,6},{39,7},{40,8},{41... | collective-permute-start | bytes 786440 | tf_op jit(solution)/shard_map/ppermute | solution.py:36
  88.4 23.2 %copy-start.5 = (f32[256,512]{1,0:T(8,128)S(1)}, f32[256,512]{1,0:T(8,128)}, u32[]{:S(2)}) copy-start(f32[256,512]{1,0:T(8,128)} %fusion.3) | copy-start | bytes 1572868
  104.0 7.7 %collective-permute-start.18 = (f32[256,512]{1,0:T(8,128)S(1)}, f32[256,512]{1,0:T(8,128)S(1)}, u32[]{:S(2)}, u32[]{:S(2)}) collective-permute-start(f32[256,512]{1,0:T(8,128)S(1)} %bitcast.46), channel_id=1, source_target_pairs={{48,32},{80,64},{112,96},{16,0},{176,160},{208,192},{240,224},{144... | collective-permute-start | bytes 1572872 | tf_op jit(solution)/shard_map/ppermute | solution.py:36
  107.1 13.8 %collective-permute-start.17 = (f32[256,512]{1,0:T(8,128)S(1)}, f32[256,512]{1,0:T(8,128)S(1)}, u32[]{:S(2)}, u32[]{:S(2)}) collective-permute-start(f32[256,512]{1,0:T(8,128)S(1)} %pad_maximum_fusion.4), channel_id=1, source_target_pairs={{32,0},{33,1},{34,2},{35,3},{36,4},{37,5},{38,6},{39,7},{40,8},{41... | collective-permute-start | bytes 1572872 | tf_op jit(solution)/shard_map/ppermute | solution.py:36
  107.4 15.1 %collective-permute-start.16 = (f32[256,512]{1,0:T(8,128)S(1)}, f32[256,512]{1,0:T(8,128)S(1)}, u32[]{:S(2)}, u32[]{:S(2)}) collective-permute-start(f32[256,512]{1,0:T(8,128)S(1)} %pad_maximum_fusion.3), channel_id=1, source_target_pairs={{96,0},{97,1},{98,2},{99,3},{100,4},{101,5},{102,6},{103,7},{104,8... | collective-permute-start | bytes 1572872 | tf_op jit(solution)/shard_map/ppermute | solution.py:36
  111.8 10.8 %collective-permute-start.20 = (f32[128,512]{1,0:T(8,128)S(1)}, f32[128,512]{1,0:T(8,128)S(1)}, u32[]{:S(2)}, u32[]{:S(2)}) collective-permute-start(f32[128,512]{1,0:T(8,128)S(1)} %get-tuple-element.61), channel_id=1, source_target_pairs={{2,34},{14,46},{19,51},{31,63},{36,68},{40,72},{53,85},{57,89},{70... | collective-permute-start | bytes 786440 | tf_op jit(solution)/shard_map/ppermute | solution.py:36
  112.5 10.2 %collective-permute-start.19 = (f32[128,512]{1,0:T(8,128)S(1)}, f32[128,512]{1,0:T(8,128)S(1)}, u32[]{:S(2)}, u32[]{:S(2)}) collective-permute-start(f32[128,512]{1,0:T(8,128)S(1)} %get-tuple-element.60), channel_id=1, source_target_pairs={{2,98},{14,110},{19,115},{31,127},{36,4},{40,8},{53,21},{57,25},{7... | collective-permute-start | bytes 786440 | tf_op jit(solution)/shard_map/ppermute | solution.py:36
  122.8 3.6 %collective-permute-start.25 = (f32[256,512]{1,0:T(8,128)S(1)}, f32[256,512]{1,0:T(8,128)S(1)}, u32[]{:S(2)}, u32[]{:S(2)}) collective-permute-start(f32[256,512]{1,0:T(8,128)S(1)} %maximum_add_fusion), channel_id=1, source_target_pairs={{0,32},{12,44},{17,49},{29,61},{34,66},{46,78},{51,83},{63,95},{68... | collective-permute-start | bytes 1572872 | tf_op jit(solution)/shard_map/ppermute | solution.py:36
  123.5 2.9 %collective-permute-start.24 = (f32[256,512]{1,0:T(8,128)S(1)}, f32[256,512]{1,0:T(8,128)S(1)}, u32[]{:S(2)}, u32[]{:S(2)}) collective-permute-start(f32[256,512]{1,0:T(8,128)S(1)} %maximum_add_fusion), channel_id=1, source_target_pairs={{4,100},{8,104},{21,117},{25,121},{38,6},{42,10},{55,23},{59,27},{... | collective-permute-start | bytes 1572872 | tf_op jit(solution)/shard_map/ppermute | solution.py:36
  124.2 14.7 %collective-permute-start.23 = (f32[256,512]{1,0:T(8,128)S(1)}, f32[256,512]{1,0:T(8,128)S(1)}, u32[]{:S(2)}, u32[]{:S(2)}) collective-permute-start(f32[256,512]{1,0:T(8,128)S(1)} %add_add_fusion.3), channel_id=1, source_target_pairs={{192,64},{208,80},{224,96},{48,176},{112,240},{0,128},{16,144},{16... | collective-permute-start | bytes 1572872 | tf_op jit(solution)/shard_map/ppermute | solution.py:36
  126.5 12.4 %collective-permute-start.26 = (f32[256,512]{1,0:T(8,128)S(1)}, f32[256,512]{1,0:T(8,128)S(1)}, u32[]{:S(2)}, u32[]{:S(2)}) collective-permute-start(f32[256,512]{1,0:T(8,128)S(1)} %add_add_fusion.2), channel_id=1, source_target_pairs={{32,160},{49,177},{66,194},{83,211},{100,228},{117,245},{6,134},{2... | collective-permute-start | bytes 1572872 | tf_op jit(solution)/shard_map/ppermute | solution.py:36
  127.2 11.8 %collective-permute-start.21 = (f32[256,512]{1,0:T(8,128)S(1)}, f32[256,512]{1,0:T(8,128)S(1)}, u32[]{:S(2)}, u32[]{:S(2)}) collective-permute-start(f32[256,512]{1,0:T(8,128)S(1)} %add.133), channel_id=1, source_target_pairs={{16,16},{64,113},{128,128},{160,135},{112,0},{33,33},{65,32},{241,... | collective-permute-start | bytes 1572872 | tf_op jit(solution)/shard_map/ppermute | solution.py:36
  127.9 21.3 %collective-permute-start.22 = (f32[256,512]{1,0:T(8,128)S(1)}, f32[256,512]{1,0:T(8,128)S(1)}, u32[]{:S(2)}, u32[]{:S(2)}) collective-permute-start(f32[256,512]{1,0:T(8,128)S(1)} %add.133), channel_id=1, source_target_pairs={{48,16},{80,113},{224,135},{49,33},{81,32},{129,144},{50,50},{114,... | collective-permute-start | bytes 1572872 | tf_op jit(solution)/shard_map/ppermute | solution.py:36
  149.2 4.0 %collective-permute-start.30 = (f32[256,512]{1,0:T(8,128)S(1)}, f32[256,512]{1,0:T(8,128)S(1)}, u32[]{:S(2)}, u32[]{:S(2)}) collective-permute-start(f32[256,512]{1,0:T(8,128)S(1)} %add.152), channel_id=1, source_target_pairs={{104,226},{121,243},{10,132},{27,149},{44,166},{61,183},{78,192},{... | collective-permute-start | bytes 1572872 | tf_op jit(solution)/shard_map/ppermute | solution.py:36
  149.9 22.8 %collective-permute-start.29 = (f32[256,512]{1,0:T(8,128)S(1)}, f32[256,512]{1,0:T(8,128)S(1)}, u32[]{:S(2)}, u32[]{:S(2)}) collective-permute-start(f32[256,512]{1,0:T(8,128)S(1)} %add.149), channel_id=1, source_target_pairs={{80,97},{96,98},{240,151},{144,150},{32,0},{97,114},{113,115},{161... | collective-permute-start | bytes 1572872 | tf_op jit(solution)/shard_map/ppermute | solution.py:36
  151.2 21.6 %collective-permute-start.28 = (f32[256,512]{1,0:T(8,128)S(1)}, f32[256,512]{1,0:T(8,128)S(1)}, u32[]{:S(2)}, u32[]{:S(2)}) collective-permute-start(f32[256,512]{1,0:T(8,128)S(1)} %add.152), channel_id=1, source_target_pairs={{160,166},{177,183},{194,192},{211,209},{228,226},{245,243},{134,1... | collective-permute-start | bytes 1572872 | tf_op jit(solution)/shard_map/ppermute | solution.py:36
  151.9 31.3 %collective-permute-start.27 = (f32[256,512]{1,0:T(8,128)S(1)}, f32[256,512]{1,0:T(8,128)S(1)}, u32[]{:S(2)}, u32[]{:S(2)}) collective-permute-start(f32[256,512]{1,0:T(8,128)S(1)} %add.149), channel_id=1, source_target_pairs={{64,97},{176,151},{128,150},{81,114},{129,160},{177,167},{2,48},{9... | collective-permute-start | bytes 1572872 | tf_op jit(solution)/shard_map/ppermute | solution.py:36
  (6 other events, 45.2 us)

commit v5 on v4

--- a/solution.py
+++ b/solution.py
@@ -1,4 +1,6 @@
+import collections
 import functools
+import random
 
 import jax
 import jax.numpy as jnp
@@ -39,7 +41,7 @@
 O, PZ, MZ, Y0 = (0, 0), (0, 1), (0, -1), (1, 0)
 PP, MM, Y1, Y2 = (0, 2), (0, -2), (1, 1), (1, 2)
 HELD_A = (O, PZ, MZ, Y0)
-HELD_B = (O, MZ, PZ, PP, MM, Y1)
+HELD_B = (O, MZ, PP, MM, Y1)
 HELD_C = (MM, Y2)
 
 
@@ -73,32 +75,70 @@
 
 
 PAIRS_A = ((O, PZ, both), (MZ, PZ, both), (O, Y0, by_h), (MZ, Y0, both), (O, O, upper))
-PAIRS_B = ((MM, PZ, both), (MM, PP, by_z), (MZ, Y1, both), (MM, Y1, both), (O, O, lower))
+PAIRS_B = ((MZ, PP, both), (MM, PP, by_z), (MZ, Y1, both), (MM, Y1, both), (O, O, lower))
 PAIRS_C = ((MM, Y2, by_h),)
 
 
-def ring(a, b, n):
-    return min((a - b) % n, (b - a) % n)
-
-
-def assign(units):
-    best = {0: (0.0, ())}
-    for _, _, col, _ in units:
-        grown = {}
-        for mask, (cost, taken) in best.items():
-            for place in range(8):
-                if mask >> place & 1:
-                    continue
-                total = cost + ring(place // 2, col // 2 % NX, NX) ** 2 + 0.1 * (place % 2 != col % 2)
-                key = mask | 1 << place
-                if key not in grown or total < grown[key][0]:
-                    grown[key] = (total, taken + (place,))
-        best = grown
-    return min(best.values())[1]
-
-
-def plane(h, row, col):
-    return h if row // NZ == col // NZ else 1 - h
+def steps(a, b, n):
+    ahead, back = (b - a) % n, (a - b) % n
+    share = 0.5 if ahead == back else 1.0
+    found = []
+    if ahead and ahead <= back:
+        found += [((a + i) % n, 1, share) for i in range(ahead)]
+    if ahead and back <= ahead:
+        found += [((a - i) % n, -1, share) for i in range(back)]
+    return found
+
+
+@functools.cache
+def route(source, target):
+    found = []
+    for order in ((0, 1, 2), (2, 1, 0)):
+        at = list(source)
+        for axis in order:
+            for place, way, share in steps(at[axis], target[axis], (NX, 4, NZ)[axis]):
+                link = at[:axis] + [place] + at[axis + 1 :]
+                found.append(((order, axis, way, *link), share))
+            at[axis] = target[axis]
+    return found
+
+
+def links(own, place, y, row, col):
+    h, z = own // NZ, own % NZ
+    x = place // 2
+    return route((x, 2 * h + y, z), (col // 2 % NX, row // NZ * 2 + col // NZ, row % NZ)) + [((own, x, y), 1.0)]
+
+
+@functools.cache
+def spread(pairs, trials=20000):
+    draw = random.Random(0)
+    units = [units_of(pairs, own // NZ, own % NZ) for own in range(GROUPS)]
+    places = [list(range(8)) for _ in range(GROUPS)]
+    planes = [
+        [own // NZ if row // NZ == col // NZ else 1 - own // NZ for _, row, col, _ in units[own]]
+        for own in range(GROUPS)
+    ]
+    load = collections.Counter()
+    for own in range(GROUPS):
+        for (_, row, col, _), place, y in zip(units[own], places[own], planes[own]):
+            for link, share in links(own, place, y, row, col):
+                load[link] += share
+    for _ in range(trials):
+        own, u, v = draw.randrange(GROUPS), draw.randrange(8), draw.randrange(8)
+        place, y = places[own], planes[own]
+        moved = [(u, place[v], y[u]), (v, place[u], y[v])] if u != v else [(u, place[u], 1 - y[u])]
+        change = collections.Counter()
+        for w, new_place, new_y in moved:
+            _, row, col, _ = units[own][w]
+            for link, share in links(own, place[w], y[w], row, col):
+                change[link] -= share
+            for link, share in links(own, new_place, new_y, row, col):
+                change[link] += share
+        if sum((load[k] + d) ** 4 - load[k] ** 4 for k, d in change.items()) <= 0:
+            load.update(change)
+            for w, new_place, new_y in moved:
+                place[w], y[w] = new_place, new_y
+    return [list(zip(units[own], places[own], planes[own])) for own in range(GROUPS)]
 
 
 @functools.cache
@@ -107,28 +147,29 @@
     code_c = np.zeros((GROUPS,), np.int32)
     target_c = {}
     over = {0: [], 1: []}
-    final = {(batch, half): [] for batch in range(3) for half in range(2)}
+    final = {(batch, half): [] for batch in (0, 1) for half in (0, 1)}
+    final_c = {(y, half): [] for y in (0, 1) for half in (0, 1)}
     for h in range(2):
         for z in range(NZ):
             own = block(h, z)
             for batch in range(2):
-                units = units_of(PAIRS_B if batch else PAIRS_A, h, z)
-                for (code, row, col, half), place in zip(units, assign(units)):
-                    x, core, y = place // 2, place % 2, plane(h, row, col)
+                for (code, row, col, half), place, y in spread(PAIRS_B if batch else PAIRS_A)[own]:
+                    x, core = place // 2, place % 2
                     tables[batch, own, core, x] = code
                     over[batch].append((device(1 - y, x, core, own), device(y, x, core, own)))
                     final[batch, half].append((device(y, x, core, own), col * GROUPS + row))
             ((code, row, col, half),) = units_of(PAIRS_C, h, z)
             code_c[own] = code
             target_c[own] = (1 - h, col // 2 % NX, col % 2)
-            final[2, half].append((device(*target_c[own], own), col * GROUPS + row))
+            for y in (0, 1):
+                final_c[y, half].append((device(y, *target_c[own][1:], own), col * GROUPS + row))
     local = np.zeros((2, 16, GROUPS, 2, NX), np.int32)
     for aux in range(16):
         x, core = aux // 2 % NX, aux % 2
         for j in range(NX):
             local[:, aux, :, 0, j] = tables[:, :, core, (x + j) % NX]
             local[:, aux, :, 1, j] = tables[:, :, 1 - core, (x + j) % NX]
-    return local.reshape(2, 16 * GROUPS, 2 * NX), code_c, target_c, over, final
+    return local.reshape(2, 16 * GROUPS, 2 * NX), code_c, target_c, over, final, final_c
 
 
 def dot_t(a, b):
@@ -228,11 +269,6 @@
     return value + send(value, along(targets, 1, 0)) + send(value, along(targets, 3, 0))
 
 
-def one_y(value, targets):
-    pairs = [(device(1 - y, x, c, b), device(y, x, c, b)) for b, (y, x, c) in targets.items()]
-    return value + send(value, pairs)
-
-
 CORE_SWAP = every(lambda y, x, c, h, z: (y, x, 1 - c, block(h, z)))
 FROM_LEFT = every(lambda y, x, c, h, z: (y, x - 1, c, block(h, z)))
 FROM_RIGHT = every(lambda y, x, c, h, z: (y, x + 1, c, block(h, z)))
@@ -257,7 +293,7 @@
 
 
 def per_device(half_b):
-    local, code_c, target_c, over, final = plan()
+    local, code_c, target_c, over, final, final_c = plan()
     aux, blk = lax.axis_index("aux"), lax.axis_index("blk")
     place = aux * GROUPS + blk
     table_a, table_b = jnp.asarray(local[0])[place], jnp.asarray(local[1])[place]
@@ -280,22 +316,23 @@
     held[Y2] = send(held[PP], FROM_OTHER)
     keep, given = products(table_b, [held[n] for n in HELD_B], HELD_B, PAIRS_B, (NX, NX))
     own_b, right_b, left_b = near(keep, send(given, CORE_SWAP))
-    own_b, right_b, left_b, held[Y2] = together(own_b, right_b, left_b, held[Y2])
+    own_b, right_b, left_b = together(own_b, right_b, left_b)
 
     done_a = total_a + send(total_a, over[0])
     total_b = own_b + send(right_b, FROM_LEFT) + send(left_b, FROM_RIGHT)
-    (part_c,) = products(table_c, [held[n] for n in HELD_C], HELD_C, PAIRS_C, (1,))
-    part_c = one_far(one_core(part_c[0], target_c), target_c)
-    done_a, total_b, part_c = together(done_a, total_b, part_c)
+    done_a, total_b, held[Y2] = together(done_a, total_b, held[Y2])
 
     top = send(done_a, final[0, 0])
     bottom = send(done_a, final[0, 1])
     done_b = total_b + send(total_b, over[1])
-    done_c = one_y(one_near(part_c, target_c), target_c)
-    top, bottom, done_b, done_c = together(top, bottom, done_b, done_c)
-
-    top = top + send(done_b, final[1, 0]) + send(done_c, final[2, 0])
-    bottom = bottom + send(done_b, final[1, 1]) + send(done_c, final[2, 1])
+    (part_c,) = products(table_c, [held[n] for n in HELD_C], HELD_C, PAIRS_C, (1,))
+    part_c = one_far(one_core(part_c[0], target_c), target_c)
+    top, bottom, part_c = together(top, bottom, part_c)
+    part_c = one_near(part_c, target_c)
+    top, bottom, done_b, part_c = together(top, bottom, done_b, part_c)
+
+    top = top + send(done_b, final[1, 0]) + send(part_c, final_c[0, 0]) + send(part_c, final_c[1, 0])
+    bottom = bottom + send(done_b, final[1, 1]) + send(part_c, final_c[0, 1]) + send(part_c, final_c[1, 1])
     return jnp.concatenate([top, bottom], 0)
 
 

time: 185 us -> 172 us (0.930)
  the two profiles are of different devices: /device:TPU:29 before, /device:TPU:43 now
where the time goes in v5:
time: 172 us; the launch traced here: 171 us
  waiting for transfers between devices  107 us (62%)
  starting transfers between devices  41.2 us (24%)
  Pallas kernels  12 us (7%)
  other arithmetic  7.94 us (5%)
  local copies, waits for them, and re-layouts  2.75 us (2%)
    ppermute x32, waiting for transfers between devices, send(): return lax.ppermute(value, ALL, pairs)  107 us
    ppermute x32, starting transfers between devices, send(): return lax.ppermute(value, ALL, pairs)  41.2 us
    pallas_call x3, Pallas kernels, products(): pl.pallas_call(functools.partial(units_kernel, index_pairs, len(counts)),...  11.9 us
  transfers between devices with their start and end apart: 32, of which 15 were waited for; matrix products, arithmetic and copies ran while one was open for 5% of the time, Pallas kernels for 0%

profile of v5, /device:TPU:43, one launch (start us, length us, event | category | flops | bytes accessed | tf_op | source)
XLA Modules:
  0.0 171.4 jit_solution(6548806445551886043)
XLA Ops:
  0.0 1.6 collective-permute-start.1
  1.6 2.0 %collective-permute-start.2 = (bf16[2,512,512]{2,1,0:T(8,128)(2,1)}, bf16[2,512,512]{2,1,0:T(8,128)(2,1)S(1)}, u32[]{:S(2)}, u32[]{:S(2)}) collective-permute-start(bf16[2,512,512]{2,1,0:T(8,128)(2,1)} %source.1), channel_id=1, source_target_pairs={{8,0},{9,1},{10,2},{11,3},{12,4},{13,5},{14,6},{15,7},{0,8},{1,9},... | collective-permute-start | bytes 3145736 | tf_op jit(solution)/shard_map/ppermute | solution.py:38
  5.7 19.0 %collective-permute-done.refs_1_ = bf16[2,512,512]{2,1,0:T(8,128)(2,1)} collective-permute-done((bf16[2,512,512]{2,1,0:T(8,128)(2,1)}, bf16[2,512,512]{2,1,0:T(8,128)(2,1)}, u32[]{:S(2)}, u32[]{:S(2)}) %collective-permute-start) | collective-permute-done | bytes 1048608 | tf_op jit(solution)/shard_map/ppermute | solution.py:38
  24.7 3.5 %collective-permute-done.1.refs_2_.refs_1_ = bf16[2,512,512]{2,1,0:T(8,128)(2,1)S(1)} collective-permute-done((bf16[2,512,512]{2,1,0:T(8,128)(2,1)}, bf16[2,512,512]{2,1,0:T(8,128)(2,1)S(1)}, u32[]{:S(2)}, u32[]{:S(2)}) %collective-permute-start.1) | collective-permute-done | bytes 1048608 | tf_op jit(solution)/shard_map/ppermute | solution.py:38
  28.2 5.4 %shard_map.47 = (f32[4,256,512]{2,1,0:T(8,128)S(1)}, f32[4,256,512]{2,1,0:T(8,128)S(1)}) custom-call(s32[8]{0:T(128)S(1)} %get-tuple-element.67.table, bf16[2,512,512]{2,1,0:T(8,128)(2,1)S(1)} %shard_map.46.refs_0_, bf16[2,512,512]{2,1,0:T(8,128)(2,1)} %collective-permute-done.refs_1_, bf16[2,512,512]{2,1,0:T(8,128)(2,1)S(1)} %collective-permute-done.1.refs_2_.refs_1_, ...), custom_call_target="tpu_custom_call" | custom-call | tf_op jit(solution)/shard_map/pallas_call | solution.py:215
  33.6 1.6 collective-permute-start.3
  35.2 2.9 %collective-permute-start.8 = (bf16[2,512,512]{2,1,0:T(8,128)(2,1)}, bf16[2,512,512]{2,1,0:T(8,128)(2,1)}, u32[]{:S(2)}, u32[]{:S(2)}) collective-permute-start(bf16[2,512,512]{2,1,0:T(8,128)(2,1)} %collective-permute-done.refs_1_), channel_id=1, source_target_pairs={{1,0},{2,1},{3,2},{4,3},{5,4},{6,5},{7,6},{0,7},{9,8},{10,9},{11,1... | collective-permute-start | bytes 3145736 | tf_op jit(solution)/shard_map/ppermute | solution.py:38
  38.2 2.0 %collective-permute-start.10 = (bf16[2,512,512]{2,1,0:T(8,128)(2,1)}, bf16[2,512,512]{2,1,0:T(8,128)(2,1)S(1)}, u32[]{:S(2)}, u32[]{:S(2)}) collective-permute-start(bf16[2,512,512]{2,1,0:T(8,128)(2,1)} %collective-permute-done.refs_1_), channel_id=1, source_target_pairs={{8,0},{9,1},{10,2},{11,3},{12,4},{13,5},{14,6},{15,7},{0,8},{1,9},... | collective-permute-start | bytes 3145736 | tf_op jit(solution)/shard_map/ppermute | solution.py:38
  42.2 5.5 %collective-permute-done.6 = f32[128,512]{1,0:T(8,128)S(1)} collective-permute-done((f32[128,512]{1,0:T(8,128)S(1)}, f32[128,512]{1,0:T(8,128)S(1)}, u32[]{:S(2)}, u32[]{:S(2)}) %collective-permute-start.6) | collective-permute-done | bytes 262176 | tf_op jit(solution)/shard_map/ppermute | solution.py:38
  49.7 10.5 %collective-permute-done.7 = f32[256,512]{1,0:T(8,128)S(1)} collective-permute-done((f32[256,512]{1,0:T(8,128)S(1)}, f32[256,512]{1,0:T(8,128)S(1)}, u32[]{:S(2)}, u32[]{:S(2)}) %collective-permute-start.7) | collective-permute-done | bytes 524320 | tf_op jit(solution)/shard_map/ppermute | solution.py:38
  60.2 2.3 %collective-permute-done.5 = f32[256,512]{1,0:T(8,128)S(1)} collective-permute-done((f32[256,512]{1,0:T(8,128)S(1)}, f32[256,512]{1,0:T(8,128)S(1)}, u32[]{:S(2)}, u32[]{:S(2)}) %collective-permute-start.5) | collective-permute-done | bytes 524320 | tf_op jit(solution)/shard_map/ppermute | solution.py:38
  64.3 5.4 %shard_map.48 = (f32[4,256,512]{2,1,0:T(8,128)S(1)}, f32[4,256,512]{2,1,0:T(8,128)S(1)}) custom-call(s32[8]{0:T(128)S(1)} %get-tuple-element.66.table, bf16[2,512,512]{2,1,0:T(8,128)(2,1)S(1)} %shard_map.46.refs_0_, bf16[2,512,512]{2,1,0:T(8,128)(2,1)S(1)} %collective-permute-done.1.refs_2_.refs_1_, bf16[2,512,512]{2,1,0:T(8,128)(2,1)} %collective-permute-done.8.refs_2_, ...), custom_call_target="tpu_custom_call" | custom-call | tf_op jit(solution)/shard_map/pallas_call | solution.py:215
  69.7 1.8 %collective-permute-start.12 = (f32[4,256,512]{2,1,0:T(8,128)S(1)}, f32[4,256,512]{2,1,0:T(8,128)S(1)}, u32[]{:S(2)}, u32[]{:S(2)}) collective-permute-start(f32[4,256,512]{2,1,0:T(8,128)S(1)} %get-tuple-element.41), channel_id=1, source_target_pairs={{16,0},{17,1},{18,2},{19,3},{20,4},{21,5},{22,6},{23,7},{24,8},{25... | collective-permute-start | bytes 6291464 | tf_op jit(solution)/shard_map/ppermute | solution.py:38
  71.4 1.5 collective-permute-start.17
  73.0 3.0 %collective-permute-start.11 = (f32[256,512]{1,0:T(8,128)}, f32[256,512]{1,0:T(8,128)S(1)}, u32[]{:S(2)}, u32[]{:S(2)}) collective-permute-start(f32[256,512]{1,0:T(8,128)} %fusion.3), channel_id=1, source_target_pairs={{176,48},{144,16},{192,64},{96,224},{0,128},{32,160},{80,208},{240... | collective-permute-start | bytes 1572872 | tf_op jit(solution)/shard_map/ppermute | solution.py:38
  76.6 2.0 %collective-permute-start.14 = (f32[128,512]{1,0:T(8,128)S(1)}, f32[128,512]{1,0:T(8,128)S(1)}, u32[]{:S(2)}, u32[]{:S(2)}) collective-permute-start(f32[128,512]{1,0:T(8,128)S(1)} %get-tuple-element.58), channel_id=1, source_target_pairs={{32,0},{33,1},{34,2},{35,3},{36,4},{37,5},{38,6},{39,7},{40,8},{41... | collective-permute-start | bytes 786440 | tf_op jit(solution)/shard_map/ppermute | solution.py:38
  78.5 5.1 %collective-permute-done.13 = f32[128,512]{1,0:T(8,128)S(1)} collective-permute-done((f32[128,512]{1,0:T(8,128)S(1)}, f32[128,512]{1,0:T(8,128)S(1)}, u32[]{:S(2)}, u32[]{:S(2)}) %collective-permute-start.13) | collective-permute-done | bytes 262176 | tf_op jit(solution)/shard_map/ppermute | solution.py:38
  85.4 2.4 %collective-permute-start.16 = (f32[256,512]{1,0:T(8,128)}, f32[256,512]{1,0:T(8,128)}, u32[]{:S(2)}, u32[]{:S(2)}) collective-permute-start(f32[256,512]{1,0:T(8,128)} %pad_maximum_fusion.4), channel_id=1, source_target_pairs={{32,0},{33,1},{34,2},{35,3},{36,4},{37,5},{38,6},{39,7},{40,8},{41... | collective-permute-start | bytes 1572872 | tf_op jit(solution)/shard_map/ppermute | solution.py:38
  88.5 13.4 %collective-permute-done.11 = f32[256,512]{1,0:T(8,128)S(1)} collective-permute-done((f32[256,512]{1,0:T(8,128)}, f32[256,512]{1,0:T(8,128)S(1)}, u32[]{:S(2)}, u32[]{:S(2)}) %collective-permute-start.11) | collective-permute-done | bytes 524320 | tf_op jit(solution)/shard_map/ppermute | solution.py:38
  103.0 1.3 add_add_fusion.3
  105.6 1.3 collective-permute-start.20
  108.3 2.1 %collective-permute-done.20 = f32[256,512]{1,0:T(8,128)S(1)} collective-permute-done((f32[256,512]{1,0:T(8,128)S(1)}, f32[256,512]{1,0:T(8,128)S(1)}, u32[]{:S(2)}, u32[]{:S(2)}) %collective-permute-start.20) | collective-permute-done | bytes 524320 | tf_op jit(solution)/shard_map/ppermute | solution.py:38
  111.8 5.0 %collective-permute-start.23 = (f32[256,512]{1,0:T(8,128)S(1)}, f32[256,512]{1,0:T(8,128)S(1)}, u32[]{:S(2)}, u32[]{:S(2)}) collective-permute-start(f32[256,512]{1,0:T(8,128)S(1)} %add_add_fusion.3), channel_id=1, source_target_pairs={{112,240},{192,64},{224,96},{128,0},{32,160},{80,208},{16,144},{17... | collective-permute-start | bytes 1572872 | tf_op jit(solution)/shard_map/ppermute | solution.py:38
  117.0 1.3 collective-permute-start.25
  118.3 1.3 collective-permute-start.24
  119.6 3.3 %collective-permute-done.23 = f32[256,512]{1,0:T(8,128)S(1)} collective-permute-done((f32[256,512]{1,0:T(8,128)S(1)}, f32[256,512]{1,0:T(8,128)S(1)}, u32[]{:S(2)}, u32[]{:S(2)}) %collective-permute-start.23) | collective-permute-done | bytes 524320 | tf_op jit(solution)/shard_map/ppermute | solution.py:38
  123.1 20.2 %collective-permute-done.25 = f32[256,512]{1,0:T(8,128)S(1)} collective-permute-done((f32[256,512]{1,0:T(8,128)S(1)}, f32[256,512]{1,0:T(8,128)S(1)}, u32[]{:S(2)}, u32[]{:S(2)}) %collective-permute-start.25) | collective-permute-done | bytes 524320 | tf_op jit(solution)/shard_map/ppermute | solution.py:38
  144.8 1.3 collective-permute-start.29
  146.1 1.3 collective-permute-start.28
  148.2 1.3 collective-permute-start.26
  149.5 5.3 %collective-permute-done.29 = f32[256,512]{1,0:T(8,128)S(1)} collective-permute-done((f32[256,512]{1,0:T(8,128)S(1)}, f32[256,512]{1,0:T(8,128)S(1)}, u32[]{:S(2)}, u32[]{:S(2)}) %collective-permute-start.29) | collective-permute-done | bytes 524320 | tf_op jit(solution)/shard_map/ppermute | solution.py:38
  155.0 15.1 %collective-permute-done.26 = f32[256,512]{1,0:T(8,128)S(1)} collective-permute-done((f32[256,512]{1,0:T(8,128)S(1)}, f32[256,512]{1,0:T(8,128)S(1)}, u32[]{:S(2)}, u32[]{:S(2)}) %collective-permute-start.26) | collective-permute-done | bytes 524320 | tf_op jit(solution)/shard_map/ppermute | solution.py:38
  (69 shorter events, 19.7 us)
Async XLA Ops:
  0.0 24.7 %collective-permute-start = (bf16[2,512,512]{2,1,0:T(8,128)(2,1)}, bf16[2,512,512]{2,1,0:T(8,128)(2,1)}, u32[]{:S(2)}, u32[]{:S(2)}) collective-permute-start(bf16[2,512,512]{2,1,0:T(8,128)(2,1)} %source.1), channel_id=1, source_target_pairs={{1,0},{2,1},{3,2},{4,3},{5,4},{6,5},{7,6},{0,7},{9,8},{10,9},{11,1... | collective-permute-start | bytes 3145736 | tf_op jit(solution)/shard_map/ppermute | solution.py:38
  0.0 28.2 %collective-permute-start.1 = (bf16[2,512,512]{2,1,0:T(8,128)(2,1)}, bf16[2,512,512]{2,1,0:T(8,128)(2,1)S(1)}, u32[]{:S(2)}, u32[]{:S(2)}) collective-permute-start(bf16[2,512,512]{2,1,0:T(8,128)(2,1)} %source.1), channel_id=1, source_target_pairs={{7,0},{0,1},{1,2},{2,3},{3,4},{4,5},{5,6},{6,7},{15,8},{8,9},{9,10... | collective-permute-start | bytes 3145736 | tf_op jit(solution)/shard_map/ppermute | solution.py:38
  1.6 26.6 %collective-permute-start.2 = (bf16[2,512,512]{2,1,0:T(8,128)(2,1)}, bf16[2,512,512]{2,1,0:T(8,128)(2,1)S(1)}, u32[]{:S(2)}, u32[]{:S(2)}) collective-permute-start(bf16[2,512,512]{2,1,0:T(8,128)(2,1)} %source.1), channel_id=1, source_target_pairs={{8,0},{9,1},{10,2},{11,3},{12,4},{13,5},{14,6},{15,7},{0,8},{1,9},... | collective-permute-start | bytes 3145736 | tf_op jit(solution)/shard_map/ppermute | solution.py:38
  33.6 6.6 %collective-permute-start.3 = (f32[4,256,512]{2,1,0:T(8,128)S(1)}, f32[4,256,512]{2,1,0:T(8,128)S(1)}, u32[]{:S(2)}, u32[]{:S(2)}) collective-permute-start(f32[4,256,512]{2,1,0:T(8,128)S(1)} %get-tuple-element.35), channel_id=1, source_target_pairs={{16,0},{17,1},{18,2},{19,3},{20,4},{21,5},{22,6},{23,7},{24,8},{25... | collective-permute-start | bytes 6291464 | tf_op jit(solution)/shard_map/ppermute | solution.py:38
  35.2 28.3 %collective-permute-start.8 = (bf16[2,512,512]{2,1,0:T(8,128)(2,1)}, bf16[2,512,512]{2,1,0:T(8,128)(2,1)}, u32[]{:S(2)}, u32[]{:S(2)}) collective-permute-start(bf16[2,512,512]{2,1,0:T(8,128)(2,1)} %collective-permute-done.refs_1_), channel_id=1, source_target_pairs={{1,0},{2,1},{3,2},{4,3},{5,4},{6,5},{7,6},{0,7},{9,8},{10,9},{11,1... | collective-permute-start | bytes 3145736 | tf_op jit(solution)/shard_map/ppermute | solution.py:38
  38.2 25.9 %collective-permute-start.9 = (bf16[2,512,512]{2,1,0:T(8,128)(2,1)S(1)}, bf16[2,512,512]{2,1,0:T(8,128)(2,1)S(1)}, u32[]{:S(2)}, u32[]{:S(2)}) collective-permute-start(bf16[2,512,512]{2,1,0:T(8,128)(2,1)S(1)} %collective-permute-done.1.refs_2_.refs_1_), channel_id=1, source_target_pairs={{7,0},{0,1},{1,2},{2,3},{3,4},{4,5},{5,6},{6,7},{15,8},{8,9},{9,10... | collective-permute-start | bytes 3145736 | tf_op jit(solution)/shard_map/ppermute | solution.py:38
  38.2 26.1 %collective-permute-start.10 = (bf16[2,512,512]{2,1,0:T(8,128)(2,1)}, bf16[2,512,512]{2,1,0:T(8,128)(2,1)S(1)}, u32[]{:S(2)}, u32[]{:S(2)}) collective-permute-start(bf16[2,512,512]{2,1,0:T(8,128)(2,1)} %collective-permute-done.refs_1_), channel_id=1, source_target_pairs={{8,0},{9,1},{10,2},{11,3},{12,4},{13,5},{14,6},{15,7},{0,8},{1,9},... | collective-permute-start | bytes 3145736 | tf_op jit(solution)/shard_map/ppermute | solution.py:38
  40.3 7.4 %collective-permute-start.6 = (f32[128,512]{1,0:T(8,128)S(1)}, f32[128,512]{1,0:T(8,128)S(1)}, u32[]{:S(2)}, u32[]{:S(2)}) collective-permute-start(f32[128,512]{1,0:T(8,128)S(1)} %get-tuple-element.61), channel_id=1, source_target_pairs={{32,0},{33,1},{34,2},{35,3},{36,4},{37,5},{38,6},{39,7},{40,8},{41... | collective-permute-start | bytes 786440 | tf_op jit(solution)/shard_map/ppermute | solution.py:38
  40.9 8.4 %collective-permute-start.4 = (f32[128,512]{1,0:T(8,128)S(1)}, f32[128,512]{1,0:T(8,128)S(1)}, u32[]{:S(2)}, u32[]{:S(2)}) collective-permute-start(f32[128,512]{1,0:T(8,128)S(1)} %get-tuple-element.60), channel_id=1, source_target_pairs={{96,0},{97,1},{98,2},{99,3},{100,4},{101,5},{102,6},{103,7},{104,8... | collective-permute-start | bytes 786440 | tf_op jit(solution)/shard_map/ppermute | solution.py:38
  47.8 12.4 %collective-permute-start.7 = (f32[256,512]{1,0:T(8,128)S(1)}, f32[256,512]{1,0:T(8,128)S(1)}, u32[]{:S(2)}, u32[]{:S(2)}) collective-permute-start(f32[256,512]{1,0:T(8,128)S(1)} %pad_maximum_fusion.2), channel_id=1, source_target_pairs={{32,0},{33,1},{34,2},{35,3},{36,4},{37,5},{38,6},{39,7},{40,8},{41... | collective-permute-start | bytes 1572872 | tf_op jit(solution)/shard_map/ppermute | solution.py:38
  49.4 13.1 %collective-permute-start.5 = (f32[256,512]{1,0:T(8,128)S(1)}, f32[256,512]{1,0:T(8,128)S(1)}, u32[]{:S(2)}, u32[]{:S(2)}) collective-permute-start(f32[256,512]{1,0:T(8,128)S(1)} %pad_maximum_fusion.1), channel_id=1, source_target_pairs={{96,0},{97,1},{98,2},{99,3},{100,4},{101,5},{102,6},{103,7},{104,8... | collective-permute-start | bytes 1572872 | tf_op jit(solution)/shard_map/ppermute | solution.py:38
  69.7 6.3 %collective-permute-start.12 = (f32[4,256,512]{2,1,0:T(8,128)S(1)}, f32[4,256,512]{2,1,0:T(8,128)S(1)}, u32[]{:S(2)}, u32[]{:S(2)}) collective-permute-start(f32[4,256,512]{2,1,0:T(8,128)S(1)} %get-tuple-element.41), channel_id=1, source_target_pairs={{16,0},{17,1},{18,2},{19,3},{20,4},{21,5},{22,6},{23,7},{24,8},{25... | collective-permute-start | bytes 6291464 | tf_op jit(solution)/shard_map/ppermute | solution.py:38
  71.4 33.0 %collective-permute-start.17 = (bf16[2,512,512]{2,1,0:T(8,128)(2,1)}, bf16[2,512,512]{2,1,0:T(8,128)(2,1)S(1)}, u32[]{:S(2)}, u32[]{:S(2)}) collective-permute-start(bf16[2,512,512]{2,1,0:T(8,128)(2,1)} %collective-permute-done.8.refs_2_), channel_id=1, source_target_pairs={{8,0},{9,1},{10,2},{11,3},{12,4},{13,5},{14,6},{15,7},{0,8},{1,9},... | collective-permute-start | bytes 3145736 | tf_op jit(solution)/shard_map/ppermute | solution.py:38
  73.0 28.9 %collective-permute-start.11 = (f32[256,512]{1,0:T(8,128)}, f32[256,512]{1,0:T(8,128)S(1)}, u32[]{:S(2)}, u32[]{:S(2)}) collective-permute-start(f32[256,512]{1,0:T(8,128)} %fusion.3), channel_id=1, source_target_pairs={{176,48},{144,16},{192,64},{96,224},{0,128},{32,160},{80,208},{240... | collective-permute-start | bytes 1572872 | tf_op jit(solution)/shard_map/ppermute | solution.py:38
  76.1 7.6 %collective-permute-start.13 = (f32[128,512]{1,0:T(8,128)S(1)}, f32[128,512]{1,0:T(8,128)S(1)}, u32[]{:S(2)}, u32[]{:S(2)}) collective-permute-start(f32[128,512]{1,0:T(8,128)S(1)} %get-tuple-element.59), channel_id=1, source_target_pairs={{96,0},{97,1},{98,2},{99,3},{100,4},{101,5},{102,6},{103,7},{104,8... | collective-permute-start | bytes 786440 | tf_op jit(solution)/shard_map/ppermute | solution.py:38
  76.6 7.2 %collective-permute-start.14 = (f32[128,512]{1,0:T(8,128)S(1)}, f32[128,512]{1,0:T(8,128)S(1)}, u32[]{:S(2)}, u32[]{:S(2)}) collective-permute-start(f32[128,512]{1,0:T(8,128)S(1)} %get-tuple-element.58), channel_id=1, source_target_pairs={{32,0},{33,1},{34,2},{35,3},{36,4},{37,5},{38,6},{39,7},{40,8},{41... | collective-permute-start | bytes 786440 | tf_op jit(solution)/shard_map/ppermute | solution.py:38
  85.4 17.6 %collective-permute-start.16 = (f32[256,512]{1,0:T(8,128)}, f32[256,512]{1,0:T(8,128)}, u32[]{:S(2)}, u32[]{:S(2)}) collective-permute-start(f32[256,512]{1,0:T(8,128)} %pad_maximum_fusion.4), channel_id=1, source_target_pairs={{32,0},{33,1},{34,2},{35,3},{36,4},{37,5},{38,6},{39,7},{40,8},{41... | collective-permute-start | bytes 1572872 | tf_op jit(solution)/shard_map/ppermute | solution.py:38
  87.8 15.3 %collective-permute-start.15 = (f32[256,512]{1,0:T(8,128)}, f32[256,512]{1,0:T(8,128)}, u32[]{:S(2)}, u32[]{:S(2)}) collective-permute-start(f32[256,512]{1,0:T(8,128)} %pad_maximum_fusion.3), channel_id=1, source_target_pairs={{96,0},{97,1},{98,2},{99,3},{100,4},{101,5},{102,6},{103,7},{104,8... | collective-permute-start | bytes 1572872 | tf_op jit(solution)/shard_map/ppermute | solution.py:38
  105.6 4.8 %collective-permute-start.20 = (f32[256,512]{1,0:T(8,128)S(1)}, f32[256,512]{1,0:T(8,128)S(1)}, u32[]{:S(2)}, u32[]{:S(2)}) collective-permute-start(f32[256,512]{1,0:T(8,128)S(1)} %bitcast.46), channel_id=1, source_target_pairs={{48,32},{80,64},{112,96},{16,0},{176,160},{208,192},{240,224},{144... | collective-permute-start | bytes 1572872 | tf_op jit(solution)/shard_map/ppermute | solution.py:38
  106.9 10.1 %collective-permute-start.18 = (f32[256,512]{1,0:T(8,128)S(1)}, f32[256,512]{1,0:T(8,128)S(1)}, u32[]{:S(2)}, u32[]{:S(2)}) collective-permute-start(f32[256,512]{1,0:T(8,128)S(1)} %add.136), channel_id=1, source_target_pairs={{48,16},{64,113},{128,128},{160,135},{112,0},{49,33},{209,32},{161... | collective-permute-start | bytes 1572872 | tf_op jit(solution)/shard_map/ppermute | solution.py:38
  107.6 9.4 %collective-permute-start.19 = (f32[256,512]{1,0:T(8,128)S(1)}, f32[256,512]{1,0:T(8,128)S(1)}, u32[]{:S(2)}, u32[]{:S(2)}) collective-permute-start(f32[256,512]{1,0:T(8,128)S(1)} %add.136), channel_id=1, source_target_pairs={{16,16},{224,113},{208,135},{65,33},{1,32},{145,144},{178,50},{34,... | collective-permute-start | bytes 1572872 | tf_op jit(solution)/shard_map/ppermute | solution.py:38
  110.5 6.4 %collective-permute-start.22 = (f32[128,512]{1,0:T(8,128)S(1)}, f32[128,512]{1,0:T(8,128)S(1)}, u32[]{:S(2)}, u32[]{:S(2)}) collective-permute-start(f32[128,512]{1,0:T(8,128)S(1)} %get-tuple-element.65), channel_id=1, source_target_pairs={{2,34},{14,46},{19,51},{31,63},{36,68},{40,72},{53,85},{57,89},{70... | collective-permute-start | bytes 786440 | tf_op jit(solution)/shard_map/ppermute | solution.py:38
  111.2 5.8 %collective-permute-start.21 = (f32[128,512]{1,0:T(8,128)S(1)}, f32[128,512]{1,0:T(8,128)S(1)}, u32[]{:S(2)}, u32[]{:S(2)}) collective-permute-start(f32[128,512]{1,0:T(8,128)S(1)} %get-tuple-element.64), channel_id=1, source_target_pairs={{2,98},{14,110},{19,115},{31,127},{36,4},{40,8},{53,21},{57,25},{7... | collective-permute-start | bytes 786440 | tf_op jit(solution)/shard_map/ppermute | solution.py:38
  111.8 11.1 %collective-permute-start.23 = (f32[256,512]{1,0:T(8,128)S(1)}, f32[256,512]{1,0:T(8,128)S(1)}, u32[]{:S(2)}, u32[]{:S(2)}) collective-permute-start(f32[256,512]{1,0:T(8,128)S(1)} %add_add_fusion.3), channel_id=1, source_target_pairs={{112,240},{192,64},{224,96},{128,0},{32,160},{80,208},{16,144},{17... | collective-permute-start | bytes 1572872 | tf_op jit(solution)/shard_map/ppermute | solution.py:38
  117.0 26.2 %collective-permute-start.25 = (f32[256,512]{1,0:T(8,128)S(1)}, f32[256,512]{1,0:T(8,128)S(1)}, u32[]{:S(2)}, u32[]{:S(2)}) collective-permute-start(f32[256,512]{1,0:T(8,128)S(1)} %maximum_add_fusion), channel_id=1, source_target_pairs={{0,32},{12,44},{17,49},{29,61},{34,66},{46,78},{51,83},{63,95},{68... | collective-permute-start | bytes 1572872 | tf_op jit(solution)/shard_map/ppermute | solution.py:38
  118.3 25.0 %collective-permute-start.24 = (f32[256,512]{1,0:T(8,128)S(1)}, f32[256,512]{1,0:T(8,128)S(1)}, u32[]{:S(2)}, u32[]{:S(2)}) collective-permute-start(f32[256,512]{1,0:T(8,128)S(1)} %maximum_add_fusion), channel_id=1, source_target_pairs={{4,100},{8,104},{21,117},{25,121},{38,6},{42,10},{55,23},{59,27},{... | collective-permute-start | bytes 1572872 | tf_op jit(solution)/shard_map/ppermute | solution.py:38
  143.4 4.7 %collective-permute-start.31 = (f32[256,512]{1,0:T(8,128)S(1)}, f32[256,512]{1,0:T(8,128)S(1)}, u32[]{:S(2)}, u32[]{:S(2)}) collective-permute-start(f32[256,512]{1,0:T(8,128)S(1)} %add_add_fusion.2), channel_id=1, source_target_pairs={{232,226},{249,243},{138,132},{155,149},{172,166},{189,183},{206,1... | collective-permute-start | bytes 1572872 | tf_op jit(solution)/shard_map/ppermute | solution.py:38
  144.1 5.3 %collective-permute-start.30 = (f32[256,512]{1,0:T(8,128)S(1)}, f32[256,512]{1,0:T(8,128)S(1)}, u32[]{:S(2)}, u32[]{:S(2)}) collective-permute-start(f32[256,512]{1,0:T(8,128)S(1)} %add_add_fusion.2), channel_id=1, source_target_pairs={{104,226},{121,243},{10,132},{27,149},{44,166},{61,183},{78,192},{... | collective-permute-start | bytes 1572872 | tf_op jit(solution)/shard_map/ppermute | solution.py:38
  144.8 9.9 %collective-permute-start.29 = (f32[256,512]{1,0:T(8,128)S(1)}, f32[256,512]{1,0:T(8,128)S(1)}, u32[]{:S(2)}, u32[]{:S(2)}) collective-permute-start(f32[256,512]{1,0:T(8,128)S(1)} %add.152), channel_id=1, source_target_pairs={{64,114},{96,98},{160,151},{144,150},{48,0},{113,48},{145,115},{16... | collective-permute-start | bytes 1572872 | tf_op jit(solution)/shard_map/ppermute | solution.py:38
  146.1 8.8 %collective-permute-start.28 = (f32[256,512]{1,0:T(8,128)S(1)}, f32[256,512]{1,0:T(8,128)S(1)}, u32[]{:S(2)}, u32[]{:S(2)}) collective-permute-start(f32[256,512]{1,0:T(8,128)S(1)} %add_add_fusion.2), channel_id=1, source_target_pairs={{160,166},{177,183},{194,192},{211,209},{228,226},{245,243},{134,1... | collective-permute-start | bytes 1572872 | tf_op jit(solution)/shard_map/ppermute | solution.py:38
  147.5 7.5 %collective-permute-start.27 = (f32[256,512]{1,0:T(8,128)S(1)}, f32[256,512]{1,0:T(8,128)S(1)}, u32[]{:S(2)}, u32[]{:S(2)}) collective-permute-start(f32[256,512]{1,0:T(8,128)S(1)} %add_add_fusion.2), channel_id=1, source_target_pairs={{32,166},{49,183},{66,192},{83,209},{100,226},{117,243},{6,132},{2... | collective-permute-start | bytes 1572872 | tf_op jit(solution)/shard_map/ppermute | solution.py:38
  148.2 21.9 %collective-permute-start.26 = (f32[256,512]{1,0:T(8,128)S(1)}, f32[256,512]{1,0:T(8,128)S(1)}, u32[]{:S(2)}, u32[]{:S(2)}) collective-permute-start(f32[256,512]{1,0:T(8,128)S(1)} %add.152), channel_id=1, source_target_pairs={{240,114},{0,151},{208,150},{1,48},{49,160},{193,167},{114,65},{82... | collective-permute-start | bytes 1572872 | tf_op jit(solution)/shard_map/ppermute | solution.py:38
  (2 other events, 10.5 us)

commit v6 on v5

--- a/solution.py
+++ b/solution.py
@@ -93,52 +93,65 @@
 @functools.cache
 def route(source, target):
     found = []
-    for order in ((0, 1, 2), (2, 1, 0)):
+    for weight, order in ((0.05, (0, 1, 2)), (1.0, (2, 1, 0))):
         at = list(source)
         for axis in order:
             for place, way, share in steps(at[axis], target[axis], (NX, 4, NZ)[axis]):
                 link = at[:axis] + [place] + at[axis + 1 :]
-                found.append(((order, axis, way, *link), share))
+                found.append(((weight, axis, way, *link), share))
             at[axis] = target[axis]
     return found
 
 
-def links(own, place, y, row, col):
+def links(own, place, y, unit):
     h, z = own // NZ, own % NZ
-    x = place // 2
-    return route((x, 2 * h + y, z), (col // 2 % NX, row // NZ * 2 + col // NZ, row % NZ)) + [((own, x, y), 1.0)]
+    _, row, col, _ = unit
+    return route((place // 2, 2 * h + y, z), (col // 2 % NX, row // NZ * 2 + col // NZ, row % NZ))
 
 
 @functools.cache
-def spread(pairs, trials=20000):
+def spread(trials=40000):
     draw = random.Random(0)
-    units = [units_of(pairs, own // NZ, own % NZ) for own in range(GROUPS)]
-    places = [list(range(8)) for _ in range(GROUPS)]
-    planes = [
-        [own // NZ if row // NZ == col // NZ else 1 - own // NZ for _, row, col, _ in units[own]]
-        for own in range(GROUPS)
-    ]
+    where = [(own // NZ, own % NZ) for own in range(GROUPS)]
+    units = [[units_of(pairs, h, z) for pairs in (PAIRS_A, PAIRS_B)] for h, z in where]
+    at = [[list(range(8)), list(range(8))] for _ in where]
+    planes = [[h] * 8 for h, _ in where]
     load = collections.Counter()
-    for own in range(GROUPS):
-        for (_, row, col, _), place, y in zip(units[own], places[own], planes[own]):
-            for link, share in links(own, place, y, row, col):
-                load[link] += share
+
+    def on(own, batch, place, index, y):
+        return links(own, place, 1 - y if batch else y, units[own][batch][index])
+
+    for own, (h, z) in enumerate(where):
+        for batch in (0, 1):
+            for place in range(8):
+                for link, share in on(own, batch, place, at[own][batch][place], planes[own][place]):
+                    load[link] += share
+        for unit in units_of(PAIRS_C, h, z):
+            for y in (0, 1):
+                for link, share in links(own, unit[2] % 8, y, unit):
+                    load[link] += share
     for _ in range(trials):
-        own, u, v = draw.randrange(GROUPS), draw.randrange(8), draw.randrange(8)
-        place, y = places[own], planes[own]
-        moved = [(u, place[v], y[u]), (v, place[u], y[v])] if u != v else [(u, place[u], 1 - y[u])]
+        own, batch, u, v = draw.randrange(GROUPS), draw.randrange(2), draw.randrange(8), draw.randrange(8)
+        now, plane = at[own], planes[own]
         change = collections.Counter()
-        for w, new_place, new_y in moved:
-            _, row, col, _ = units[own][w]
-            for link, share in links(own, place[w], y[w], row, col):
-                change[link] -= share
-            for link, share in links(own, new_place, new_y, row, col):
-                change[link] += share
-        if sum((load[k] + d) ** 4 - load[k] ** 4 for k, d in change.items()) <= 0:
-            load.update(change)
-            for w, new_place, new_y in moved:
-                place[w], y[w] = new_place, new_y
-    return [list(zip(units[own], places[own], planes[own])) for own in range(GROUPS)]
+        if u == v:
+            for one in (0, 1):
+                for sign, y in ((-1, plane[u]), (1, 1 - plane[u])):
+                    for link, share in on(own, one, u, now[one][u], y):
+                        change[link] += sign * share
+        else:
+            i, j = now[batch][u], now[batch][v]
+            for sign, place, index in ((-1, u, i), (-1, v, j), (1, u, j), (1, v, i)):
+                for link, share in on(own, batch, place, index, plane[place]):
+                    change[link] += sign * share
+        if sum(link[0] * ((load[link] + d) ** 4 - load[link] ** 4) for link, d in change.items()) <= 0:
+            for link, d in change.items():
+                load[link] += d
+            if u == v:
+                plane[u] = 1 - plane[u]
+            else:
+                now[batch][u], now[batch][v] = j, i
+    return units, at, planes
 
 
 @functools.cache
@@ -146,18 +159,21 @@
     tables = np.zeros((2, GROUPS, 2, NX), np.int32)
     code_c = np.zeros((GROUPS,), np.int32)
     target_c = {}
-    over = {0: [], 1: []}
-    final = {(batch, half): [] for batch in (0, 1) for half in (0, 1)}
+    final = {half: [] for half in (0, 1)}
     final_c = {(y, half): [] for y in (0, 1) for half in (0, 1)}
+    first = np.zeros((16, GROUPS), np.bool_)
+    units, at, planes = spread()
     for h in range(2):
         for z in range(NZ):
             own = block(h, z)
-            for batch in range(2):
-                for (code, row, col, half), place, y in spread(PAIRS_B if batch else PAIRS_A)[own]:
-                    x, core = place // 2, place % 2
+            for place in range(8):
+                x, core = place // 2, place % 2
+                for batch in range(2):
+                    code, row, col, half = units[own][batch][at[own][batch][place]]
+                    y = 1 - planes[own][place] if batch else planes[own][place]
                     tables[batch, own, core, x] = code
-                    over[batch].append((device(1 - y, x, core, own), device(y, x, core, own)))
-                    final[batch, half].append((device(y, x, core, own), col * GROUPS + row))
+                    final[half].append((device(y, x, core, own), col * GROUPS + row))
+                    first[(y * NX + x) * 2 + core, own] = not batch
             ((code, row, col, half),) = units_of(PAIRS_C, h, z)
             code_c[own] = code
             target_c[own] = (1 - h, col // 2 % NX, col % 2)
@@ -169,7 +185,7 @@
         for j in range(NX):
             local[:, aux, :, 0, j] = tables[:, :, core, (x + j) % NX]
             local[:, aux, :, 1, j] = tables[:, :, 1 - core, (x + j) % NX]
-    return local.reshape(2, 16 * GROUPS, 2 * NX), code_c, target_c, over, final, final_c
+    return local.reshape(2, 16 * GROUPS, 2 * NX), code_c, target_c, first, final, final_c
 
 
 def dot_t(a, b):
@@ -269,6 +285,7 @@
     return value + send(value, along(targets, 1, 0)) + send(value, along(targets, 3, 0))
 
 
+Y_SWAP = every(lambda y, x, c, h, z: (1 - y, x, c, block(h, z)))
 CORE_SWAP = every(lambda y, x, c, h, z: (y, x, 1 - c, block(h, z)))
 FROM_LEFT = every(lambda y, x, c, h, z: (y, x - 1, c, block(h, z)))
 FROM_RIGHT = every(lambda y, x, c, h, z: (y, x + 1, c, block(h, z)))
@@ -293,7 +310,7 @@
 
 
 def per_device(half_b):
-    local, code_c, target_c, over, final, final_c = plan()
+    local, code_c, target_c, first, final, final_c = plan()
     aux, blk = lax.axis_index("aux"), lax.axis_index("blk")
     place = aux * GROUPS + blk
     table_a, table_b = jnp.asarray(local[0])[place], jnp.asarray(local[1])[place]
@@ -318,21 +335,17 @@
     own_b, right_b, left_b = near(keep, send(given, CORE_SWAP))
     own_b, right_b, left_b = together(own_b, right_b, left_b)
 
-    done_a = total_a + send(total_a, over[0])
     total_b = own_b + send(right_b, FROM_LEFT) + send(left_b, FROM_RIGHT)
-    done_a, total_b, held[Y2] = together(done_a, total_b, held[Y2])
-
-    top = send(done_a, final[0, 0])
-    bottom = send(done_a, final[0, 1])
-    done_b = total_b + send(total_b, over[1])
+    total_b, held[Y2] = together(total_b, held[Y2])
+
+    has_first = jnp.asarray(first)[aux, blk]
+    done = jnp.where(has_first, total_a, total_b) + send(jnp.where(has_first, total_b, total_a), Y_SWAP)
     (part_c,) = products(table_c, [held[n] for n in HELD_C], HELD_C, PAIRS_C, (1,))
-    part_c = one_far(one_core(part_c[0], target_c), target_c)
-    top, bottom, part_c = together(top, bottom, part_c)
-    part_c = one_near(part_c, target_c)
-    top, bottom, done_b, part_c = together(top, bottom, done_b, part_c)
-
-    top = top + send(done_b, final[1, 0]) + send(part_c, final_c[0, 0]) + send(part_c, final_c[1, 0])
-    bottom = bottom + send(done_b, final[1, 1]) + send(part_c, final_c[0, 1]) + send(part_c, final_c[1, 1])
+    part_c = one_near(one_far(one_core(part_c[0], target_c), target_c), target_c)
+    done, part_c = together(done, part_c)
+
+    top = send(done, final[0]) + send(part_c, final_c[0, 0]) + send(part_c, final_c[1, 0])
+    bottom = send(done, final[1]) + send(part_c, final_c[0, 1]) + send(part_c, final_c[1, 1])
     return jnp.concatenate([top, bottom], 0)
 
 

time: 172 us -> 168 us (0.977)
  the two profiles are of different devices: /device:TPU:43 before, /device:TPU:12 now
where the time goes in v6:
time: 168 us; the launch traced here: 167 us
  waiting for transfers between devices  99.1 us (59%)
  starting transfers between devices  43.9 us (26%)
  Pallas kernels  12 us (7%)
  other arithmetic  8.07 us (5%)
  local copies, waits for them, and re-layouts  4.03 us (2%)
    ppermute x29, waiting for transfers between devices, send(): return lax.ppermute(value, ALL, pairs)  99.1 us
    ppermute x29, starting transfers between devices, send(): return lax.ppermute(value, ALL, pairs)  43.9 us
    pallas_call x3, Pallas kernels, products(): pl.pallas_call(functools.partial(units_kernel, index_pairs, len(counts)),...  11.9 us
  transfers between devices with their start and end apart: 29, of which 19 were waited for; matrix products, arithmetic and copies ran while one was open for 6% of the time, Pallas kernels for 0%

profile of v6, /device:TPU:12, one launch (start us, length us, event | category | flops | bytes accessed | tf_op | source)
XLA Modules:
  0.0 167.5 jit_solution(7100191596771423979)
XLA Ops:
  0.0 5.9 %collective-permute-start = (bf16[2,512,512]{2,1,0:T(8,128)(2,1)}, bf16[2,512,512]{2,1,0:T(8,128)(2,1)}, u32[]{:S(2)}, u32[]{:S(2)}) collective-permute-start(bf16[2,512,512]{2,1,0:T(8,128)(2,1)} %source.1), channel_id=1, source_target_pairs={{1,0},{2,1},{3,2},{4,3},{5,4},{6,5},{7,6},{0,7},{9,8},{10,9},{11,1... | collective-permute-start | bytes 3145736 | tf_op jit(solution)/shard_map/ppermute | solution.py:38
  5.9 2.3 %collective-permute-start.2 = (bf16[2,512,512]{2,1,0:T(8,128)(2,1)}, bf16[2,512,512]{2,1,0:T(8,128)(2,1)S(1)}, u32[]{:S(2)}, u32[]{:S(2)}) collective-permute-start(bf16[2,512,512]{2,1,0:T(8,128)(2,1)} %source.1), channel_id=1, source_target_pairs={{8,0},{9,1},{10,2},{11,3},{12,4},{13,5},{14,6},{15,7},{0,8},{1,9},... | collective-permute-start | bytes 3145736 | tf_op jit(solution)/shard_map/ppermute | solution.py:38
  10.2 18.4 %collective-permute-done.refs_1_ = bf16[2,512,512]{2,1,0:T(8,128)(2,1)} collective-permute-done((bf16[2,512,512]{2,1,0:T(8,128)(2,1)}, bf16[2,512,512]{2,1,0:T(8,128)(2,1)}, u32[]{:S(2)}, u32[]{:S(2)}) %collective-permute-start) | collective-permute-done | bytes 1048608 | tf_op jit(solution)/shard_map/ppermute | solution.py:38
  28.6 3.3 %collective-permute-done.1.refs_2_.refs_1_ = bf16[2,512,512]{2,1,0:T(8,128)(2,1)S(1)} collective-permute-done((bf16[2,512,512]{2,1,0:T(8,128)(2,1)}, bf16[2,512,512]{2,1,0:T(8,128)(2,1)S(1)}, u32[]{:S(2)}, u32[]{:S(2)}) %collective-permute-start.1) | collective-permute-done | bytes 1048608 | tf_op jit(solution)/shard_map/ppermute | solution.py:38
  32.2 5.4 %shard_map.56 = (f32[4,256,512]{2,1,0:T(8,128)S(1)}, f32[4,256,512]{2,1,0:T(8,128)S(1)}) custom-call(s32[8]{0:T(128)S(1)} %get-tuple-element.55.table, bf16[2,512,512]{2,1,0:T(8,128)(2,1)S(1)} %shard_map.55.refs_0_, bf16[2,512,512]{2,1,0:T(8,128)(2,1)} %collective-permute-done.refs_1_, bf16[2,512,512]{2,1,0:T(8,128)(2,1)S(1)} %collective-permute-done.1.refs_2_.refs_1_, ...), custom_call_target="tpu_custom_call" | custom-call | tf_op jit(solution)/shard_map/pallas_call | solution.py:231
  37.7 2.4 %collective-permute-start.10 = (bf16[2,512,512]{2,1,0:T(8,128)(2,1)}, bf16[2,512,512]{2,1,0:T(8,128)(2,1)S(1)}, u32[]{:S(2)}, u32[]{:S(2)}) collective-permute-start(bf16[2,512,512]{2,1,0:T(8,128)(2,1)} %collective-permute-done.refs_1_), channel_id=1, source_target_pairs={{8,0},{9,1},{10,2},{11,3},{12,4},{13,5},{14,6},{15,7},{0,8},{1,9},... | collective-permute-start | bytes 3145736 | tf_op jit(solution)/shard_map/ppermute | solution.py:38
  40.1 2.9 %collective-permute-start.8 = (bf16[2,512,512]{2,1,0:T(8,128)(2,1)}, bf16[2,512,512]{2,1,0:T(8,128)(2,1)}, u32[]{:S(2)}, u32[]{:S(2)}) collective-permute-start(bf16[2,512,512]{2,1,0:T(8,128)(2,1)} %collective-permute-done.refs_1_), channel_id=1, source_target_pairs={{1,0},{2,1},{3,2},{4,3},{5,4},{6,5},{7,6},{0,7},{9,8},{10,9},{11,1... | collective-permute-start | bytes 3145736 | tf_op jit(solution)/shard_map/ppermute | solution.py:38
  45.6 5.7 %collective-permute-done.4 = f32[128,512]{1,0:T(8,128)S(1)} collective-permute-done((f32[128,512]{1,0:T(8,128)S(1)}, f32[128,512]{1,0:T(8,128)S(1)}, u32[]{:S(2)}, u32[]{:S(2)}) %collective-permute-start.4) | collective-permute-done | bytes 262176 | tf_op jit(solution)/shard_map/ppermute | solution.py:38
  51.4 1.5 collective-permute-start.5
  53.8 10.7 %collective-permute-done.5 = f32[256,512]{1,0:T(8,128)S(1)} collective-permute-done((f32[256,512]{1,0:T(8,128)S(1)}, f32[256,512]{1,0:T(8,128)S(1)}, u32[]{:S(2)}, u32[]{:S(2)}) %collective-permute-start.5) | collective-permute-done | bytes 524320 | tf_op jit(solution)/shard_map/ppermute | solution.py:38
  66.7 2.5 %collective-permute-done.9.refs_3_.refs_0_ = bf16[2,512,512]{2,1,0:T(8,128)(2,1)S(1)} collective-permute-done((bf16[2,512,512]{2,1,0:T(8,128)(2,1)S(1)}, bf16[2,512,512]{2,1,0:T(8,128)(2,1)S(1)}, u32[]{:S(2)}, u32[]{:S(2)}) %collective-permute-start.9) | collective-permute-done | bytes 1048608 | tf_op jit(solution)/shard_map/ppermute | solution.py:38
  69.2 5.4 %shard_map.57 = (f32[4,256,512]{2,1,0:T(8,128)S(1)}, f32[4,256,512]{2,1,0:T(8,128)S(1)}) custom-call(s32[8]{0:T(128)S(1)} %get-tuple-element.54.table, bf16[2,512,512]{2,1,0:T(8,128)(2,1)S(1)} %shard_map.55.refs_0_, bf16[2,512,512]{2,1,0:T(8,128)(2,1)S(1)} %collective-permute-done.1.refs_2_.refs_1_, bf16[2,512,512]{2,1,0:T(8,128)(2,1)} %collective-permute-done.8.refs_2_, ...), custom_call_target="tpu_custom_call" | custom-call | tf_op jit(solution)/shard_map/pallas_call | solution.py:231
  74.6 1.3 collective-permute-start.16
  76.0 2.8 %collective-permute-done.11 = f32[4,256,512]{2,1,0:T(8,128)S(1)} collective-permute-done((f32[4,256,512]{2,1,0:T(8,128)S(1)}, f32[4,256,512]{2,1,0:T(8,128)S(1)}, u32[]{:S(2)}, u32[]{:S(2)}) %collective-permute-start.11) | collective-permute-done | bytes 2097184 | tf_op jit(solution)/shard_map/ppermute | solution.py:38
  79.9 1.6 collective-permute-start.12
  81.5 5.8 %collective-permute-done.13 = f32[128,512]{1,0:T(8,128)S(1)} collective-permute-done((f32[128,512]{1,0:T(8,128)S(1)}, f32[128,512]{1,0:T(8,128)S(1)}, u32[]{:S(2)}, u32[]{:S(2)}) %collective-permute-start.13) | collective-permute-done | bytes 262176 | tf_op jit(solution)/shard_map/ppermute | solution.py:38
  88.9 1.8 %collective-permute-start.14 = (f32[256,512]{1,0:T(8,128)}, f32[256,512]{1,0:T(8,128)}, u32[]{:S(2)}, u32[]{:S(2)}) collective-permute-start(f32[256,512]{1,0:T(8,128)} %pad_maximum_fusion.3), channel_id=1, source_target_pairs={{96,0},{97,1},{98,2},{99,3},{100,4},{101,5},{102,6},{103,7},{104,8... | collective-permute-start | bytes 1572872 | tf_op jit(solution)/shard_map/ppermute | solution.py:38
  91.6 10.6 %collective-permute-done.14 = f32[256,512]{1,0:T(8,128)} collective-permute-done((f32[256,512]{1,0:T(8,128)}, f32[256,512]{1,0:T(8,128)}, u32[]{:S(2)}, u32[]{:S(2)}) %collective-permute-start.14) | collective-permute-done | bytes 524320 | tf_op jit(solution)/shard_map/ppermute | solution.py:38
  102.2 2.7 %collective-permute-done.15 = f32[256,512]{1,0:T(8,128)} collective-permute-done((f32[256,512]{1,0:T(8,128)S(1)}, f32[256,512]{1,0:T(8,128)}, u32[]{:S(2)}, u32[]{:S(2)}) %collective-permute-start.15) | collective-permute-done | bytes 524320 | tf_op jit(solution)/shard_map/ppermute | solution.py:38
  104.9 2.1 %add_add_fusion.3 = f32[256,512]{1,0:T(8,128)} fusion(f32[256,512]{1,0:T(8,128)} %collective-permute-done.15, f32[256,512]{1,0:T(8,128)S(1)} %get-tuple-element.36, f32[256,512]{1,0:T(8,128)} %collective-permute-done.14), kind=kLoop, calls=%fused_computation.20 | loop fusion | flops 262144 | bytes 2097152 | tf_op jit(solution)/shard_map/add | solution.py:338
  108.3 1.4 collective-permute-start.18
  109.7 1.3 dynamic_slice.12
  112.3 1.3 collective-permute-start.19
  115.0 1.4 collective-permute-start.17
  116.5 4.4 %collective-permute-done.19 = f32[128,512]{1,0:T(8,128)S(1)} collective-permute-done((f32[128,512]{1,0:T(8,128)S(1)}, f32[128,512]{1,0:T(8,128)S(1)}, u32[]{:S(2)}, u32[]{:S(2)}) %collective-permute-start.19) | collective-permute-done | bytes 262176 | tf_op jit(solution)/shard_map/ppermute | solution.py:38
  121.0 1.3 collective-permute-start.21
  123.0 5.4 %collective-permute-done.17 = f32[256,512]{1,0:T(8,128)S(1)} collective-permute-done((f32[256,512]{1,0:T(8,128)S(1)}, f32[256,512]{1,0:T(8,128)S(1)}, u32[]{:S(2)}, u32[]{:S(2)}) %collective-permute-start.17) | collective-permute-done | bytes 524320 | tf_op jit(solution)/shard_map/ppermute | solution.py:38
  132.7 7.5 %collective-permute-start.26 = (f32[256,512]{1,0:T(8,128)S(1)}, f32[256,512]{1,0:T(8,128)S(1)}, u32[]{:S(2)}, u32[]{:S(2)}) collective-permute-start(f32[256,512]{1,0:T(8,128)S(1)} %select_add_fusion), channel_id=1, source_target_pairs={{128,0},{16,151},{32,16},{48,98},{64,113},{192,150},{208,135},{80,... | collective-permute-start | bytes 1572872 | tf_op jit(solution)/shard_map/ppermute | solution.py:38
  140.2 1.3 collective-permute-start.27
  144.1 11.4 %collective-permute-done.25 = f32[256,512]{1,0:T(8,128)S(1)} collective-permute-done((f32[256,512]{1,0:T(8,128)S(1)}, f32[256,512]{1,0:T(8,128)S(1)}, u32[]{:S(2)}, u32[]{:S(2)}) %collective-permute-start.25) | collective-permute-done | bytes 524320 | tf_op jit(solution)/shard_map/ppermute | solution.py:38
  155.7 5.2 %collective-permute-done.27 = f32[256,512]{1,0:T(8,128)S(1)} collective-permute-done((f32[256,512]{1,0:T(8,128)S(1)}, f32[256,512]{1,0:T(8,128)S(1)}, u32[]{:S(2)}, u32[]{:S(2)}) %collective-permute-start.27) | collective-permute-done | bytes 524320 | tf_op jit(solution)/shard_map/ppermute | solution.py:38
  160.8 5.4 %collective-permute-done.28 = f32[256,512]{1,0:T(8,128)S(1)} collective-permute-done((f32[256,512]{1,0:T(8,128)S(1)}, f32[256,512]{1,0:T(8,128)S(1)}, u32[]{:S(2)}, u32[]{:S(2)}) %collective-permute-start.28) | collective-permute-done | bytes 524320 | tf_op jit(solution)/shard_map/ppermute | solution.py:38
  (68 shorter events, 24.5 us)
Async XLA Ops:
  0.0 28.6 %collective-permute-start = (bf16[2,512,512]{2,1,0:T(8,128)(2,1)}, bf16[2,512,512]{2,1,0:T(8,128)(2,1)}, u32[]{:S(2)}, u32[]{:S(2)}) collective-permute-start(bf16[2,512,512]{2,1,0:T(8,128)(2,1)} %source.1), channel_id=1, source_target_pairs={{1,0},{2,1},{3,2},{4,3},{5,4},{6,5},{7,6},{0,7},{9,8},{10,9},{11,1... | collective-permute-start | bytes 3145736 | tf_op jit(solution)/shard_map/ppermute | solution.py:38
  5.9 26.0 %collective-permute-start.1 = (bf16[2,512,512]{2,1,0:T(8,128)(2,1)}, bf16[2,512,512]{2,1,0:T(8,128)(2,1)S(1)}, u32[]{:S(2)}, u32[]{:S(2)}) collective-permute-start(bf16[2,512,512]{2,1,0:T(8,128)(2,1)} %source.1), channel_id=1, source_target_pairs={{7,0},{0,1},{1,2},{2,3},{3,4},{4,5},{5,6},{6,7},{15,8},{8,9},{9,10... | collective-permute-start | bytes 3145736 | tf_op jit(solution)/shard_map/ppermute | solution.py:38
  5.9 26.3 %collective-permute-start.2 = (bf16[2,512,512]{2,1,0:T(8,128)(2,1)}, bf16[2,512,512]{2,1,0:T(8,128)(2,1)S(1)}, u32[]{:S(2)}, u32[]{:S(2)}) collective-permute-start(bf16[2,512,512]{2,1,0:T(8,128)(2,1)} %source.1), channel_id=1, source_target_pairs={{8,0},{9,1},{10,2},{11,3},{12,4},{13,5},{14,6},{15,7},{0,8},{1,9},... | collective-permute-start | bytes 3145736 | tf_op jit(solution)/shard_map/ppermute | solution.py:38
  37.6 5.4 %collective-permute-start.3 = (f32[4,256,512]{2,1,0:T(8,128)S(1)}, f32[4,256,512]{2,1,0:T(8,128)S(1)}, u32[]{:S(2)}, u32[]{:S(2)}) collective-permute-start(f32[4,256,512]{2,1,0:T(8,128)S(1)} %get-tuple-element.29), channel_id=1, source_target_pairs={{16,0},{17,1},{18,2},{19,3},{20,4},{21,5},{22,6},{23,7},{24,8},{25... | collective-permute-start | bytes 6291464 | tf_op jit(solution)/shard_map/ppermute | solution.py:38
  37.7 29.0 %collective-permute-start.10 = (bf16[2,512,512]{2,1,0:T(8,128)(2,1)}, bf16[2,512,512]{2,1,0:T(8,128)(2,1)S(1)}, u32[]{:S(2)}, u32[]{:S(2)}) collective-permute-start(bf16[2,512,512]{2,1,0:T(8,128)(2,1)} %collective-permute-done.refs_1_), channel_id=1, source_target_pairs={{8,0},{9,1},{10,2},{11,3},{12,4},{13,5},{14,6},{15,7},{0,8},{1,9},... | collective-permute-start | bytes 3145736 | tf_op jit(solution)/shard_map/ppermute | solution.py:38
  40.1 26.6 %collective-permute-start.8 = (bf16[2,512,512]{2,1,0:T(8,128)(2,1)}, bf16[2,512,512]{2,1,0:T(8,128)(2,1)}, u32[]{:S(2)}, u32[]{:S(2)}) collective-permute-start(bf16[2,512,512]{2,1,0:T(8,128)(2,1)} %collective-permute-done.refs_1_), channel_id=1, source_target_pairs={{1,0},{2,1},{3,2},{4,3},{5,4},{6,5},{7,6},{0,7},{9,8},{10,9},{11,1... | collective-permute-start | bytes 3145736 | tf_op jit(solution)/shard_map/ppermute | solution.py:38
  43.0 26.1 %collective-permute-start.9 = (bf16[2,512,512]{2,1,0:T(8,128)(2,1)S(1)}, bf16[2,512,512]{2,1,0:T(8,128)(2,1)S(1)}, u32[]{:S(2)}, u32[]{:S(2)}) collective-permute-start(bf16[2,512,512]{2,1,0:T(8,128)(2,1)S(1)} %collective-permute-done.1.refs_2_.refs_1_), channel_id=1, source_target_pairs={{7,0},{0,1},{1,2},{2,3},{3,4},{4,5},{5,6},{6,7},{15,8},{8,9},{9,10... | collective-permute-start | bytes 3145736 | tf_op jit(solution)/shard_map/ppermute | solution.py:38
  43.1 8.2 %collective-permute-start.4 = (f32[128,512]{1,0:T(8,128)S(1)}, f32[128,512]{1,0:T(8,128)S(1)}, u32[]{:S(2)}, u32[]{:S(2)}) collective-permute-start(f32[128,512]{1,0:T(8,128)S(1)} %get-tuple-element.48), channel_id=1, source_target_pairs={{96,0},{97,1},{98,2},{99,3},{100,4},{101,5},{102,6},{103,7},{104,8... | collective-permute-start | bytes 786440 | tf_op jit(solution)/shard_map/ppermute | solution.py:38
  44.6 8.2 %collective-permute-start.6 = (f32[128,512]{1,0:T(8,128)S(1)}, f32[128,512]{1,0:T(8,128)S(1)}, u32[]{:S(2)}, u32[]{:S(2)}) collective-permute-start(f32[128,512]{1,0:T(8,128)S(1)} %get-tuple-element.49), channel_id=1, source_target_pairs={{32,0},{33,1},{34,2},{35,3},{36,4},{37,5},{38,6},{39,7},{40,8},{41... | collective-permute-start | bytes 786440 | tf_op jit(solution)/shard_map/ppermute | solution.py:38
  51.4 13.2 %collective-permute-start.5 = (f32[256,512]{1,0:T(8,128)S(1)}, f32[256,512]{1,0:T(8,128)S(1)}, u32[]{:S(2)}, u32[]{:S(2)}) collective-permute-start(f32[256,512]{1,0:T(8,128)S(1)} %pad_maximum_fusion.1), channel_id=1, source_target_pairs={{96,0},{97,1},{98,2},{99,3},{100,4},{101,5},{102,6},{103,7},{104,8... | collective-permute-start | bytes 1572872 | tf_op jit(solution)/shard_map/ppermute | solution.py:38
  52.9 12.7 %collective-permute-start.7 = (f32[256,512]{1,0:T(8,128)S(1)}, f32[256,512]{1,0:T(8,128)S(1)}, u32[]{:S(2)}, u32[]{:S(2)}) collective-permute-start(f32[256,512]{1,0:T(8,128)S(1)} %pad_maximum_fusion.2), channel_id=1, source_target_pairs={{32,0},{33,1},{34,2},{35,3},{36,4},{37,5},{38,6},{39,7},{40,8},{41... | collective-permute-start | bytes 1572872 | tf_op jit(solution)/shard_map/ppermute | solution.py:38
  74.5 4.2 %collective-permute-start.11 = (f32[4,256,512]{2,1,0:T(8,128)S(1)}, f32[4,256,512]{2,1,0:T(8,128)S(1)}, u32[]{:S(2)}, u32[]{:S(2)}) collective-permute-start(f32[4,256,512]{2,1,0:T(8,128)S(1)} %get-tuple-element.35), channel_id=1, source_target_pairs={{16,0},{17,1},{18,2},{19,3},{20,4},{21,5},{22,6},{23,7},{24,8},{25... | collective-permute-start | bytes 6291464 | tf_op jit(solution)/shard_map/ppermute | solution.py:38
  74.6 32.4 %collective-permute-start.16 = (bf16[2,512,512]{2,1,0:T(8,128)(2,1)}, bf16[2,512,512]{2,1,0:T(8,128)(2,1)S(1)}, u32[]{:S(2)}, u32[]{:S(2)}) collective-permute-start(bf16[2,512,512]{2,1,0:T(8,128)(2,1)} %collective-permute-done.8.refs_2_), channel_id=1, source_target_pairs={{8,0},{9,1},{10,2},{11,3},{12,4},{13,5},{14,6},{15,7},{0,8},{1,9},... | collective-permute-start | bytes 3145736 | tf_op jit(solution)/shard_map/ppermute | solution.py:38
  78.9 8.4 %collective-permute-start.13 = (f32[128,512]{1,0:T(8,128)S(1)}, f32[128,512]{1,0:T(8,128)S(1)}, u32[]{:S(2)}, u32[]{:S(2)}) collective-permute-start(f32[128,512]{1,0:T(8,128)S(1)} %get-tuple-element.46), channel_id=1, source_target_pairs={{32,0},{33,1},{34,2},{35,3},{36,4},{37,5},{38,6},{39,7},{40,8},{41... | collective-permute-start | bytes 786440 | tf_op jit(solution)/shard_map/ppermute | solution.py:38
  79.9 8.1 %collective-permute-start.12 = (f32[128,512]{1,0:T(8,128)S(1)}, f32[128,512]{1,0:T(8,128)S(1)}, u32[]{:S(2)}, u32[]{:S(2)}) collective-permute-start(f32[128,512]{1,0:T(8,128)S(1)} %get-tuple-element.47), channel_id=1, source_target_pairs={{96,0},{97,1},{98,2},{99,3},{100,4},{101,5},{102,6},{103,7},{104,8... | collective-permute-start | bytes 786440 | tf_op jit(solution)/shard_map/ppermute | solution.py:38
  81.4 9.5 %copy-start.3 = (s32[16]{0:T(128)S(1)}, s32[16]{0:T(128)}, u32[]{:S(2)}) copy-start(s32[16]{0:T(128)} %constant.23.clone) | copy-start | bytes 196
  88.9 13.3 %collective-permute-start.14 = (f32[256,512]{1,0:T(8,128)}, f32[256,512]{1,0:T(8,128)}, u32[]{:S(2)}, u32[]{:S(2)}) collective-permute-start(f32[256,512]{1,0:T(8,128)} %pad_maximum_fusion.3), channel_id=1, source_target_pairs={{96,0},{97,1},{98,2},{99,3},{100,4},{101,5},{102,6},{103,7},{104,8... | collective-permute-start | bytes 1572872 | tf_op jit(solution)/shard_map/ppermute | solution.py:38
  90.7 14.3 %collective-permute-start.15 = (f32[256,512]{1,0:T(8,128)S(1)}, f32[256,512]{1,0:T(8,128)}, u32[]{:S(2)}, u32[]{:S(2)}) collective-permute-start(f32[256,512]{1,0:T(8,128)S(1)} %pad_maximum_fusion.4), channel_id=1, source_target_pairs={{32,0},{33,1},{34,2},{35,3},{36,4},{37,5},{38,6},{39,7},{40,8},{41... | collective-permute-start | bytes 1572872 | tf_op jit(solution)/shard_map/ppermute | solution.py:38
  107.1 7.2 %copy-start.1 = (f32[256,512]{1,0:T(8,128)S(1)}, f32[256,512]{1,0:T(8,128)}, u32[]{:S(2)}) copy-start(f32[256,512]{1,0:T(8,128)} %fusion.3) | copy-start | bytes 1572868
  108.3 6.1 %copy-start.2 = (f32[256,512]{1,0:T(8,128)S(1)}, f32[256,512]{1,0:T(8,128)}, u32[]{:S(2)}) copy-start(f32[256,512]{1,0:T(8,128)} %add_add_fusion.3) | copy-start | bytes 1572868
  108.3 3.9 %collective-permute-start.18 = (f32[256,512]{1,0:T(8,128)S(1)}, f32[256,512]{1,0:T(8,128)S(1)}, u32[]{:S(2)}, u32[]{:S(2)}) collective-permute-start(f32[256,512]{1,0:T(8,128)S(1)} %bitcast.47), channel_id=1, source_target_pairs={{48,32},{80,64},{112,96},{16,0},{176,160},{208,192},{240,224},{144... | collective-permute-start | bytes 1572872 | tf_op jit(solution)/shard_map/ppermute | solution.py:38
  112.3 8.6 %collective-permute-start.19 = (f32[128,512]{1,0:T(8,128)S(1)}, f32[128,512]{1,0:T(8,128)S(1)}, u32[]{:S(2)}, u32[]{:S(2)}) collective-permute-start(f32[128,512]{1,0:T(8,128)S(1)} %get-tuple-element.52), channel_id=1, source_target_pairs={{2,98},{14,110},{19,115},{31,127},{36,4},{40,8},{53,21},{57,25},{7... | collective-permute-start | bytes 786440 | tf_op jit(solution)/shard_map/ppermute | solution.py:38
  113.6 7.3 %collective-permute-start.20 = (f32[128,512]{1,0:T(8,128)S(1)}, f32[128,512]{1,0:T(8,128)S(1)}, u32[]{:S(2)}, u32[]{:S(2)}) collective-permute-start(f32[128,512]{1,0:T(8,128)S(1)} %get-tuple-element.53), channel_id=1, source_target_pairs={{2,34},{14,46},{19,51},{31,63},{36,68},{40,72},{53,85},{57,89},{70... | collective-permute-start | bytes 786440 | tf_op jit(solution)/shard_map/ppermute | solution.py:38
  115.0 13.4 %collective-permute-start.17 = (f32[256,512]{1,0:T(8,128)S(1)}, f32[256,512]{1,0:T(8,128)S(1)}, u32[]{:S(2)}, u32[]{:S(2)}) collective-permute-start(f32[256,512]{1,0:T(8,128)S(1)} %broadcast_select_fusion), channel_id=1, source_target_pairs={{128,0},{129,1},{130,2},{131,3},{132,4},{133,5},{134,6},{135,7},{1... | collective-permute-start | bytes 1572872 | tf_op jit(solution)/shard_map/ppermute | solution.py:38
  121.0 8.3 %collective-permute-start.21 = (f32[256,512]{1,0:T(8,128)S(1)}, f32[256,512]{1,0:T(8,128)S(1)}, u32[]{:S(2)}, u32[]{:S(2)}) collective-permute-start(f32[256,512]{1,0:T(8,128)S(1)} %maximum_add_fusion), channel_id=1, source_target_pairs={{4,100},{8,104},{21,117},{25,121},{38,6},{42,10},{55,23},{59,27},{... | collective-permute-start | bytes 1572872 | tf_op jit(solution)/shard_map/ppermute | solution.py:38
  122.3 6.9 %collective-permute-start.22 = (f32[256,512]{1,0:T(8,128)S(1)}, f32[256,512]{1,0:T(8,128)S(1)}, u32[]{:S(2)}, u32[]{:S(2)}) collective-permute-start(f32[256,512]{1,0:T(8,128)S(1)} %maximum_add_fusion), channel_id=1, source_target_pairs={{0,32},{12,44},{17,49},{29,61},{34,66},{46,78},{51,83},{63,95},{68... | collective-permute-start | bytes 1572872 | tf_op jit(solution)/shard_map/ppermute | solution.py:38
  129.4 12.1 %collective-permute-start.23 = (f32[256,512]{1,0:T(8,128)S(1)}, f32[256,512]{1,0:T(8,128)S(1)}, u32[]{:S(2)}, u32[]{:S(2)}) collective-permute-start(f32[256,512]{1,0:T(8,128)S(1)} %select_add_fusion), channel_id=1, source_target_pairs={{0,16},{144,135},{160,114},{176,128},{96,113},{224,151},{112,0},{2... | collective-permute-start | bytes 1572872 | tf_op jit(solution)/shard_map/ppermute | solution.py:38
  130.1 13.9 %collective-permute-start.24 = (f32[256,512]{1,0:T(8,128)S(1)}, f32[256,512]{1,0:T(8,128)S(1)}, u32[]{:S(2)}, u32[]{:S(2)}) collective-permute-start(f32[256,512]{1,0:T(8,128)S(1)} %add_add_fusion.2), channel_id=1, source_target_pairs={{32,166},{49,183},{66,192},{83,209},{100,226},{117,243},{6,132},{2... | collective-permute-start | bytes 1572872 | tf_op jit(solution)/shard_map/ppermute | solution.py:38
  131.4 24.1 %collective-permute-start.25 = (f32[256,512]{1,0:T(8,128)S(1)}, f32[256,512]{1,0:T(8,128)S(1)}, u32[]{:S(2)}, u32[]{:S(2)}) collective-permute-start(f32[256,512]{1,0:T(8,128)S(1)} %add_add_fusion.2), channel_id=1, source_target_pairs={{160,166},{177,183},{194,192},{211,209},{228,226},{245,243},{134,1... | collective-permute-start | bytes 1572872 | tf_op jit(solution)/shard_map/ppermute | solution.py:38
  132.7 22.9 %collective-permute-start.26 = (f32[256,512]{1,0:T(8,128)S(1)}, f32[256,512]{1,0:T(8,128)S(1)}, u32[]{:S(2)}, u32[]{:S(2)}) collective-permute-start(f32[256,512]{1,0:T(8,128)S(1)} %select_add_fusion), channel_id=1, source_target_pairs={{128,0},{16,151},{32,16},{48,98},{64,113},{192,150},{208,135},{80,... | collective-permute-start | bytes 1572872 | tf_op jit(solution)/shard_map/ppermute | solution.py:38
  140.2 20.6 %collective-permute-start.27 = (f32[256,512]{1,0:T(8,128)S(1)}, f32[256,512]{1,0:T(8,128)S(1)}, u32[]{:S(2)}, u32[]{:S(2)}) collective-permute-start(f32[256,512]{1,0:T(8,128)S(1)} %add_add_fusion.2), channel_id=1, source_target_pairs={{104,226},{121,243},{10,132},{27,149},{44,166},{61,183},{78,192},{... | collective-permute-start | bytes 1572872 | tf_op jit(solution)/shard_map/ppermute | solution.py:38
  141.5 24.8 %collective-permute-start.28 = (f32[256,512]{1,0:T(8,128)S(1)}, f32[256,512]{1,0:T(8,128)S(1)}, u32[]{:S(2)}, u32[]{:S(2)}) collective-permute-start(f32[256,512]{1,0:T(8,128)S(1)} %add_add_fusion.2), channel_id=1, source_target_pairs={{232,226},{249,243},{138,132},{155,149},{172,166},{189,183},{206,1... | collective-permute-start | bytes 1572872 | tf_op jit(solution)/shard_map/ppermute | solution.py:38
  (1 other events, 1.3 us)

commit v7 on v6

--- a/solution.py
+++ b/solution.py
@@ -50,7 +50,8 @@
     for at, (first, second, halves) in enumerate(pairs):
         i, j = block(h + first[0], z + first[1]), block(h + second[0], z + second[1])
         for half in halves(h, z):
-            found.append(((at * 2 + (i > j)) * 2 + half, min(i, j), max(i, j), half))
+            core = half if halves is both else int(first == second)
+            found.append(((at, int(i > j), core), min(i, j), max(i, j), half))
     return found
 
 
@@ -109,12 +110,17 @@
     return route((place // 2, 2 * h + y, z), (col // 2 % NX, row // NZ * 2 + col // NZ, row % NZ))
 
 
+def by_core(units):
+    cores = [[index for index, unit in enumerate(units) if unit[0][2] == core] for core in (0, 1)]
+    return [cores[place % 2][place // 2] for place in range(8)]
+
+
 @functools.cache
 def spread(trials=40000):
     draw = random.Random(0)
     where = [(own // NZ, own % NZ) for own in range(GROUPS)]
     units = [[units_of(pairs, h, z) for pairs in (PAIRS_A, PAIRS_B)] for h, z in where]
-    at = [[list(range(8)), list(range(8))] for _ in where]
+    at = [[by_core(batch) for batch in both_batches] for both_batches in units]
     planes = [[h] * 8 for h, _ in where]
     load = collections.Counter()
 
@@ -132,6 +138,8 @@
                     load[link] += share
     for _ in range(trials):
         own, batch, u, v = draw.randrange(GROUPS), draw.randrange(2), draw.randrange(8), draw.randrange(8)
+        if (u - v) % 2:
+            continue
         now, plane = at[own], planes[own]
         change = collections.Counter()
         if u == v:
@@ -156,8 +164,8 @@
 
 @functools.cache
 def plan():
-    tables = np.zeros((2, GROUPS, 2, NX), np.int32)
-    code_c = np.zeros((GROUPS,), np.int32)
+    tables = np.zeros((2, 16, GROUPS, 5, 4), np.int32)
+    table_c = np.zeros((GROUPS, 4), np.int32)
     target_c = {}
     final = {half: [] for half in (0, 1)}
     final_c = {(y, half): [] for y in (0, 1) for half in (0, 1)}
@@ -169,23 +177,25 @@
             for place in range(8):
                 x, core = place // 2, place % 2
                 for batch in range(2):
-                    code, row, col, half = units[own][batch][at[own][batch][place]]
+                    (pair, swap, _), row, col, half = units[own][batch][at[own][batch][place]]
                     y = 1 - planes[own][place] if batch else planes[own][place]
-                    tables[batch, own, core, x] = code
                     final[half].append((device(y, x, core, own), col * GROUPS + row))
                     first[(y * NX + x) * 2 + core, own] = not batch
-            ((code, row, col, half),) = units_of(PAIRS_C, h, z)
-            code_c[own] = code
+                    for aux in range(16):
+                        entry, offset = tables[batch, aux, own, pair], (x - aux // 2) % NX
+                        kept = aux % 2 == core
+                        entry[0] = swap
+                        if (PAIRS_A, PAIRS_B)[batch][pair][2] is both:
+                            entry[1 if kept else 2] = offset
+                            entry[3] = aux % 2
+                        else:
+                            entry[1:] = offset, kept, half
+            (((_, swap, _), row, col, half),) = units_of(PAIRS_C, h, z)
+            table_c[own] = swap, 0, 1, half
             target_c[own] = (1 - h, col // 2 % NX, col % 2)
             for y in (0, 1):
                 final_c[y, half].append((device(y, *target_c[own][1:], own), col * GROUPS + row))
-    local = np.zeros((2, 16, GROUPS, 2, NX), np.int32)
-    for aux in range(16):
-        x, core = aux // 2 % NX, aux % 2
-        for j in range(NX):
-            local[:, aux, :, 0, j] = tables[:, :, core, (x + j) % NX]
-            local[:, aux, :, 1, j] = tables[:, :, 1 - core, (x + j) % NX]
-    return local.reshape(2, 16 * GROUPS, 2 * NX), code_c, target_c, first, final, final_c
+    return tables.reshape(2, 16 * GROUPS, 20), table_c, target_c, first, final, final_c
 
 
 def dot_t(a, b):
@@ -200,36 +210,31 @@
     return total
 
 
-def units_kernel(index_pairs, spare, table, *refs):
+def units_kernel(pairs, index_pairs, spare, table, *refs):
     held, outs = refs[: len(refs) - spare], refs[len(refs) - spare :]
-
-    def slot(base, out, j, carry):
-        code = table[base + j]
-        half = code % 2
-        for at, (first, second) in enumerate(index_pairs):
-
-            @pl.when(code // 2 == at * 2)
-            def _():
-                out[j] = half_product(held[first], held[second], half)
-
-            if first != second:
-
-                @pl.when(code // 2 == at * 2 + 1)
+    for at, ((first, second), (_, _, halves)) in enumerate(zip(index_pairs, pairs)):
+        swap, one, two, half = (table[4 * at + i] for i in range(4))
+        for turned in range(1 if first == second else 2):
+            rows, cols = (held[second], held[first]) if turned else (held[first], held[second])
+            if halves is both:
+
+                @pl.when(swap == turned)
                 def _():
-                    out[j] = half_product(held[second], held[first], half)
-
-        return carry
-
-    base = 0
-    for out in outs:
-        lax.fori_loop(0, out.shape[0], functools.partial(slot, base, out), 0)
-        base += out.shape[0]
+                    outs[1][two] = half_product(rows, cols, 1 - half)
+                    outs[0][one] = half_product(rows, cols, half)
+
+            else:
+                for mine in range(2 - len(outs), 2):
+
+                    @pl.when((swap == turned) & (two == mine))
+                    def _():
+                        outs[1 - mine][one] = half_product(rows, cols, half)
 
 
 def products(table, held, names, pairs, counts):
     index_pairs = tuple((names.index(a), names.index(b)) for a, b, _ in pairs)
     return pl.pallas_call(
-        functools.partial(units_kernel, index_pairs, len(counts)),
+        functools.partial(units_kernel, pairs, index_pairs, len(counts)),
         out_shape=[pltpu.VMEM((count, 256, 512), jnp.float32) for count in counts],
         in_specs=[pl.BlockSpec(memory_space=pltpu.SMEM)]
         + [pl.BlockSpec(memory_space=pltpu.VMEM)] * len(held),
@@ -310,11 +315,11 @@
 
 
 def per_device(half_b):
-    local, code_c, target_c, first, final, final_c = plan()
+    local, codes_c, target_c, first, final, final_c = plan()
     aux, blk = lax.axis_index("aux"), lax.axis_index("blk")
     place = aux * GROUPS + blk
     table_a, table_b = jnp.asarray(local[0])[place], jnp.asarray(local[1])[place]
-    table_c = jnp.asarray(code_c)[blk].reshape(1)
+    table_c = jnp.asarray(codes_c)[blk]
 
     held = {O: placed(half_b)}
     held[PZ] = send(half_b, FROM_UP)
@@ -341,7 +346,9 @@
     has_first = jnp.asarray(first)[aux, blk]
     done = jnp.where(has_first, total_a, total_b) + send(jnp.where(has_first, total_b, total_a), Y_SWAP)
     (part_c,) = products(table_c, [held[n] for n in HELD_C], HELD_C, PAIRS_C, (1,))
-    part_c = one_near(one_far(one_core(part_c[0], target_c), target_c), target_c)
+    part_c = one_far(one_core(part_c[0], target_c), target_c)
+    done, part_c = together(done, part_c)
+    part_c = one_near(part_c, target_c)
     done, part_c = together(done, part_c)
 
     top = send(done, final[0]) + send(part_c, final_c[0, 0]) + send(part_c, final_c[1, 0])

time: 168 us -> 171 us (1.018)
  waiting for transfers between devices: 99.1 us -> 108 us
  starting transfers between devices: 43.9 us -> 39.8 us
  Pallas kernels: 12 us -> 9.91 us
    ppermute x29, waiting for transfers between devices: 99.1 us -> 108 us  [send(): return lax.ppermute(value, ALL, pairs)]
    ppermute x29, starting transfers between devices: 43.9 us -> 39.8 us  [send(): return lax.ppermute(value, ALL, pairs)]
    pallas_call x3, Pallas kernels: 11.9 us -> 9.84 us  [products(): pl.pallas_call(functools.partial(units_kernel, pairs, index_pairs, len(co...]
  transfers between devices with their start and end apart: 29 -> 29, of which waited for: 19 -> 18; matrix products, arithmetic and copies ran while one was open for 6% -> 6% of each run, Pallas kernels for 0% -> 0%
where the time goes in v7:
time: 171 us
  waiting for transfers between devices  108 us (63%)
  starting transfers between devices  39.8 us (23%)
  Pallas kernels  9.91 us (6%)
  other arithmetic  8.94 us (5%)
  local copies, waits for them, and re-layouts  4.06 us (2%)
    ppermute x29, waiting for transfers between devices, send(): return lax.ppermute(value, ALL, pairs)  108 us
    ppermute x29, starting transfers between devices, send(): return lax.ppermute(value, ALL, pairs)  39.8 us
    pallas_call x3, Pallas kernels, products(): pl.pallas_call(functools.partial(units_kernel, pairs, index_pairs, len(co...  9.84 us
  transfers between devices with their start and end apart: 29, of which 18 were waited for; matrix products, arithmetic and copies ran while one was open for 6% of the time, Pallas kernels for 0%

profile of v7, /device:TPU:12, one launch (start us, length us, event | category | flops | bytes accessed | tf_op | source)
XLA Modules:
  0.0 170.9 jit_solution(9708028960701021105)
XLA Ops:
  0.0 5.9 %collective-permute-start = (bf16[2,512,512]{2,1,0:T(8,128)(2,1)}, bf16[2,512,512]{2,1,0:T(8,128)(2,1)}, u32[]{:S(2)}, u32[]{:S(2)}) collective-permute-start(bf16[2,512,512]{2,1,0:T(8,128)(2,1)} %source.1), channel_id=1, source_target_pairs={{1,0},{2,1},{3,2},{4,3},{5,4},{6,5},{7,6},{0,7},{9,8},{10,9},{11,1... | collective-permute-start | bytes 3145736 | tf_op jit(solution)/shard_map/ppermute | solution.py:38
  5.9 2.3 %collective-permute-start.2 = (bf16[2,512,512]{2,1,0:T(8,128)(2,1)}, bf16[2,512,512]{2,1,0:T(8,128)(2,1)S(1)}, u32[]{:S(2)}, u32[]{:S(2)}) collective-permute-start(bf16[2,512,512]{2,1,0:T(8,128)(2,1)} %source.1), channel_id=1, source_target_pairs={{8,0},{9,1},{10,2},{11,3},{12,4},{13,5},{14,6},{15,7},{0,8},{1,9},... | collective-permute-start | bytes 3145736 | tf_op jit(solution)/shard_map/ppermute | solution.py:38
  10.2 18.4 %collective-permute-done.refs_1_ = bf16[2,512,512]{2,1,0:T(8,128)(2,1)} collective-permute-done((bf16[2,512,512]{2,1,0:T(8,128)(2,1)}, bf16[2,512,512]{2,1,0:T(8,128)(2,1)}, u32[]{:S(2)}, u32[]{:S(2)}) %collective-permute-start) | collective-permute-done | bytes 1048608 | tf_op jit(solution)/shard_map/ppermute | solution.py:38
  28.6 3.3 %collective-permute-done.1.refs_2_.refs_1_ = bf16[2,512,512]{2,1,0:T(8,128)(2,1)S(1)} collective-permute-done((bf16[2,512,512]{2,1,0:T(8,128)(2,1)}, bf16[2,512,512]{2,1,0:T(8,128)(2,1)S(1)}, u32[]{:S(2)}, u32[]{:S(2)}) %collective-permute-start.1) | collective-permute-done | bytes 1048608 | tf_op jit(solution)/shard_map/ppermute | solution.py:38
  32.2 4.4 %shard_map.56 = (f32[4,256,512]{2,1,0:T(8,128)S(1)}, f32[4,256,512]{2,1,0:T(8,128)S(1)}) custom-call(s32[20]{0:T(128)S(1)} %get-tuple-element.58.table, bf16[2,512,512]{2,1,0:T(8,128)(2,1)S(1)} %shard_map.55.refs_0_, bf16[2,512,512]{2,1,0:T(8,128)(2,1)} %collective-permute-done.refs_1_, bf16[2,512,512]{2,1,0:T(8,128)(2,1)S(1)} %collective-permute-done.1.refs_2_.refs_1_, ...), custom_call_target="tpu_custom_call" | custom-call | tf_op jit(solution)/shard_map/pallas_call | solution.py:236
  36.7 2.4 %collective-permute-start.10 = (bf16[2,512,512]{2,1,0:T(8,128)(2,1)}, bf16[2,512,512]{2,1,0:T(8,128)(2,1)S(1)}, u32[]{:S(2)}, u32[]{:S(2)}) collective-permute-start(bf16[2,512,512]{2,1,0:T(8,128)(2,1)} %collective-permute-done.refs_1_), channel_id=1, source_target_pairs={{8,0},{9,1},{10,2},{11,3},{12,4},{13,5},{14,6},{15,7},{0,8},{1,9},... | collective-permute-start | bytes 3145736 | tf_op jit(solution)/shard_map/ppermute | solution.py:38
  39.1 2.9 %collective-permute-start.8 = (bf16[2,512,512]{2,1,0:T(8,128)(2,1)}, bf16[2,512,512]{2,1,0:T(8,128)(2,1)}, u32[]{:S(2)}, u32[]{:S(2)}) collective-permute-start(bf16[2,512,512]{2,1,0:T(8,128)(2,1)} %collective-permute-done.refs_1_), channel_id=1, source_target_pairs={{1,0},{2,1},{3,2},{4,3},{5,4},{6,5},{7,6},{0,7},{9,8},{10,9},{11,1... | collective-permute-start | bytes 3145736 | tf_op jit(solution)/shard_map/ppermute | solution.py:38
  44.6 5.7 %collective-permute-done.4 = f32[128,512]{1,0:T(8,128)S(1)} collective-permute-done((f32[128,512]{1,0:T(8,128)S(1)}, f32[128,512]{1,0:T(8,128)S(1)}, u32[]{:S(2)}, u32[]{:S(2)}) %collective-permute-start.4) | collective-permute-done | bytes 262176 | tf_op jit(solution)/shard_map/ppermute | solution.py:38
  52.8 10.6 %collective-permute-done.5 = f32[256,512]{1,0:T(8,128)S(1)} collective-permute-done((f32[256,512]{1,0:T(8,128)S(1)}, f32[256,512]{1,0:T(8,128)S(1)}, u32[]{:S(2)}, u32[]{:S(2)}) %collective-permute-start.5) | collective-permute-done | bytes 524320 | tf_op jit(solution)/shard_map/ppermute | solution.py:38
  65.7 2.5 %collective-permute-done.9.refs_3_.refs_0_ = bf16[2,512,512]{2,1,0:T(8,128)(2,1)S(1)} collective-permute-done((bf16[2,512,512]{2,1,0:T(8,128)(2,1)S(1)}, bf16[2,512,512]{2,1,0:T(8,128)(2,1)S(1)}, u32[]{:S(2)}, u32[]{:S(2)}) %collective-permute-start.9) | collective-permute-done | bytes 1048608 | tf_op jit(solution)/shard_map/ppermute | solution.py:38
  68.2 4.4 %shard_map.57 = (f32[4,256,512]{2,1,0:T(8,128)S(1)}, f32[4,256,512]{2,1,0:T(8,128)S(1)}) custom-call(s32[20]{0:T(128)S(1)} %get-tuple-element.59.table, bf16[2,512,512]{2,1,0:T(8,128)(2,1)S(1)} %shard_map.55.refs_0_, bf16[2,512,512]{2,1,0:T(8,128)(2,1)S(1)} %collective-permute-done.1.refs_2_.refs_1_, bf16[2,512,512]{2,1,0:T(8,128)(2,1)} %collective-permute-done.8.refs_2_, ...), custom_call_target="tpu_custom_call" | custom-call | tf_op jit(solution)/shard_map/pallas_call | solution.py:236
  72.7 1.3 collective-permute-start.16
  74.0 2.8 %collective-permute-done.11 = f32[4,256,512]{2,1,0:T(8,128)S(1)} collective-permute-done((f32[4,256,512]{2,1,0:T(8,128)S(1)}, f32[4,256,512]{2,1,0:T(8,128)S(1)}, u32[]{:S(2)}, u32[]{:S(2)}) %collective-permute-start.11) | collective-permute-done | bytes 2097184 | tf_op jit(solution)/shard_map/ppermute | solution.py:38
  77.9 1.6 collective-permute-start.12
  79.5 5.8 %collective-permute-done.13 = f32[128,512]{1,0:T(8,128)S(1)} collective-permute-done((f32[128,512]{1,0:T(8,128)S(1)}, f32[128,512]{1,0:T(8,128)S(1)}, u32[]{:S(2)}, u32[]{:S(2)}) %collective-permute-start.13) | collective-permute-done | bytes 262176 | tf_op jit(solution)/shard_map/ppermute | solution.py:38
  87.8 1.8 %collective-permute-start.14 = (f32[256,512]{1,0:T(8,128)}, f32[256,512]{1,0:T(8,128)}, u32[]{:S(2)}, u32[]{:S(2)}) collective-permute-start(f32[256,512]{1,0:T(8,128)} %pad_maximum_fusion.3), channel_id=1, source_target_pairs={{96,0},{97,1},{98,2},{99,3},{100,4},{101,5},{102,6},{103,7},{104,8... | collective-permute-start | bytes 1572872 | tf_op jit(solution)/shard_map/ppermute | solution.py:38
  90.5 10.5 %collective-permute-done.14 = f32[256,512]{1,0:T(8,128)} collective-permute-done((f32[256,512]{1,0:T(8,128)}, f32[256,512]{1,0:T(8,128)}, u32[]{:S(2)}, u32[]{:S(2)}) %collective-permute-start.14) | collective-permute-done | bytes 524320 | tf_op jit(solution)/shard_map/ppermute | solution.py:38
  101.1 3.0 %collective-permute-done.15 = f32[256,512]{1,0:T(8,128)} collective-permute-done((f32[256,512]{1,0:T(8,128)}, f32[256,512]{1,0:T(8,128)}, u32[]{:S(2)}, u32[]{:S(2)}) %collective-permute-start.15) | collective-permute-done | bytes 524320 | tf_op jit(solution)/shard_map/ppermute | solution.py:38
  104.0 2.1 %add_add_fusion.3 = f32[256,512]{1,0:T(8,128)} fusion(f32[256,512]{1,0:T(8,128)} %collective-permute-done.15, f32[256,512]{1,0:T(8,128)S(1)} %get-tuple-element.38, f32[256,512]{1,0:T(8,128)} %collective-permute-done.14), kind=kLoop, calls=%fused_computation.20 | loop fusion | flops 262144 | bytes 2097152 | tf_op jit(solution)/shard_map/add | solution.py:343
  107.2 1.3 collective-permute-start.18
  110.5 2.5 %collective-permute-start.17 = (f32[256,512]{1,0:T(8,128)S(1)}, f32[256,512]{1,0:T(8,128)S(1)}, u32[]{:S(2)}, u32[]{:S(2)}) collective-permute-start(f32[256,512]{1,0:T(8,128)S(1)} %broadcast_select_fusion), channel_id=1, source_target_pairs={{128,0},{129,1},{130,2},{131,3},{132,4},{133,5},{134,6},{135,7},{1... | collective-permute-start | bytes 1572872 | tf_op jit(solution)/shard_map/ppermute | solution.py:38
  113.1 1.3 collective-permute-start.19
  115.1 10.3 %collective-permute-done.17 = f32[256,512]{1,0:T(8,128)S(1)} collective-permute-done((f32[256,512]{1,0:T(8,128)S(1)}, f32[256,512]{1,0:T(8,128)S(1)}, u32[]{:S(2)}, u32[]{:S(2)}) %collective-permute-start.17) | collective-permute-done | bytes 524320 | tf_op jit(solution)/shard_map/ppermute | solution.py:38
  126.3 2.5 %collective-permute-start.21 = (f32[256,512]{1,0:T(8,128)S(1)}, f32[256,512]{1,0:T(8,128)S(1)}, u32[]{:S(2)}, u32[]{:S(2)}) collective-permute-start(f32[256,512]{1,0:T(8,128)S(1)} %maximum_add_fusion), channel_id=1, source_target_pairs={{4,100},{8,104},{21,117},{25,121},{38,6},{42,10},{55,23},{59,27},{... | collective-permute-start | bytes 1572872 | tf_op jit(solution)/shard_map/ppermute | solution.py:38
  129.5 11.6 %collective-permute-done.21 = f32[256,512]{1,0:T(8,128)S(1)} collective-permute-done((f32[256,512]{1,0:T(8,128)S(1)}, f32[256,512]{1,0:T(8,128)S(1)}, u32[]{:S(2)}, u32[]{:S(2)}) %collective-permute-start.21) | collective-permute-done | bytes 524320 | tf_op jit(solution)/shard_map/ppermute | solution.py:38
  141.2 1.3 collective-permute-start.23
  142.5 1.3 collective-permute-start.24
  143.8 1.3 collective-permute-start.25
  145.8 1.3 collective-permute-start.27
  147.1 2.0 %collective-permute-done.23 = f32[256,512]{1,0:T(8,128)S(1)} collective-permute-done((f32[256,512]{1,0:T(8,128)S(1)}, f32[256,512]{1,0:T(8,128)S(1)}, u32[]{:S(2)}, u32[]{:S(2)}) %collective-permute-start.23) | collective-permute-done | bytes 524320 | tf_op jit(solution)/shard_map/ppermute | solution.py:38
  150.4 11.0 %collective-permute-done.24 = f32[256,512]{1,0:T(8,128)S(1)} collective-permute-done((f32[256,512]{1,0:T(8,128)S(1)}, f32[256,512]{1,0:T(8,128)S(1)}, u32[]{:S(2)}, u32[]{:S(2)}) %collective-permute-start.24) | collective-permute-done | bytes 524320 | tf_op jit(solution)/shard_map/ppermute | solution.py:38
  161.6 7.1 %collective-permute-done.27 = f32[256,512]{1,0:T(8,128)S(1)} collective-permute-done((f32[256,512]{1,0:T(8,128)S(1)}, f32[256,512]{1,0:T(8,128)S(1)}, u32[]{:S(2)}, u32[]{:S(2)}) %collective-permute-start.27) | collective-permute-done | bytes 524320 | tf_op jit(solution)/shard_map/ppermute | solution.py:38
  (66 shorter events, 24.1 us)
Async XLA Ops:
  0.0 28.6 %collective-permute-start = (bf16[2,512,512]{2,1,0:T(8,128)(2,1)}, bf16[2,512,512]{2,1,0:T(8,128)(2,1)}, u32[]{:S(2)}, u32[]{:S(2)}) collective-permute-start(bf16[2,512,512]{2,1,0:T(8,128)(2,1)} %source.1), channel_id=1, source_target_pairs={{1,0},{2,1},{3,2},{4,3},{5,4},{6,5},{7,6},{0,7},{9,8},{10,9},{11,1... | collective-permute-start | bytes 3145736 | tf_op jit(solution)/shard_map/ppermute | solution.py:38
  5.9 26.0 %collective-permute-start.1 = (bf16[2,512,512]{2,1,0:T(8,128)(2,1)}, bf16[2,512,512]{2,1,0:T(8,128)(2,1)S(1)}, u32[]{:S(2)}, u32[]{:S(2)}) collective-permute-start(bf16[2,512,512]{2,1,0:T(8,128)(2,1)} %source.1), channel_id=1, source_target_pairs={{7,0},{0,1},{1,2},{2,3},{3,4},{4,5},{5,6},{6,7},{15,8},{8,9},{9,10... | collective-permute-start | bytes 3145736 | tf_op jit(solution)/shard_map/ppermute | solution.py:38
  5.9 26.3 %collective-permute-start.2 = (bf16[2,512,512]{2,1,0:T(8,128)(2,1)}, bf16[2,512,512]{2,1,0:T(8,128)(2,1)S(1)}, u32[]{:S(2)}, u32[]{:S(2)}) collective-permute-start(bf16[2,512,512]{2,1,0:T(8,128)(2,1)} %source.1), channel_id=1, source_target_pairs={{8,0},{9,1},{10,2},{11,3},{12,4},{13,5},{14,6},{15,7},{0,8},{1,9},... | collective-permute-start | bytes 3145736 | tf_op jit(solution)/shard_map/ppermute | solution.py:38
  8.2 1.3 copy-start
  36.6 5.4 %collective-permute-start.3 = (f32[4,256,512]{2,1,0:T(8,128)S(1)}, f32[4,256,512]{2,1,0:T(8,128)S(1)}, u32[]{:S(2)}, u32[]{:S(2)}) collective-permute-start(f32[4,256,512]{2,1,0:T(8,128)S(1)} %get-tuple-element.31), channel_id=1, source_target_pairs={{16,0},{17,1},{18,2},{19,3},{20,4},{21,5},{22,6},{23,7},{24,8},{25... | collective-permute-start | bytes 6291464 | tf_op jit(solution)/shard_map/ppermute | solution.py:38
  36.7 29.0 %collective-permute-start.10 = (bf16[2,512,512]{2,1,0:T(8,128)(2,1)}, bf16[2,512,512]{2,1,0:T(8,128)(2,1)S(1)}, u32[]{:S(2)}, u32[]{:S(2)}) collective-permute-start(bf16[2,512,512]{2,1,0:T(8,128)(2,1)} %collective-permute-done.refs_1_), channel_id=1, source_target_pairs={{8,0},{9,1},{10,2},{11,3},{12,4},{13,5},{14,6},{15,7},{0,8},{1,9},... | collective-permute-start | bytes 3145736 | tf_op jit(solution)/shard_map/ppermute | solution.py:38
  39.1 26.6 %collective-permute-start.8 = (bf16[2,512,512]{2,1,0:T(8,128)(2,1)}, bf16[2,512,512]{2,1,0:T(8,128)(2,1)}, u32[]{:S(2)}, u32[]{:S(2)}) collective-permute-start(bf16[2,512,512]{2,1,0:T(8,128)(2,1)} %collective-permute-done.refs_1_), channel_id=1, source_target_pairs={{1,0},{2,1},{3,2},{4,3},{5,4},{6,5},{7,6},{0,7},{9,8},{10,9},{11,1... | collective-permute-start | bytes 3145736 | tf_op jit(solution)/shard_map/ppermute | solution.py:38
  42.1 26.1 %collective-permute-start.9 = (bf16[2,512,512]{2,1,0:T(8,128)(2,1)S(1)}, bf16[2,512,512]{2,1,0:T(8,128)(2,1)S(1)}, u32[]{:S(2)}, u32[]{:S(2)}) collective-permute-start(bf16[2,512,512]{2,1,0:T(8,128)(2,1)S(1)} %collective-permute-done.1.refs_2_.refs_1_), channel_id=1, source_target_pairs={{7,0},{0,1},{1,2},{2,3},{3,4},{4,5},{5,6},{6,7},{15,8},{8,9},{9,10... | collective-permute-start | bytes 3145736 | tf_op jit(solution)/shard_map/ppermute | solution.py:38
  42.1 8.2 %collective-permute-start.4 = (f32[128,512]{1,0:T(8,128)S(1)}, f32[128,512]{1,0:T(8,128)S(1)}, u32[]{:S(2)}, u32[]{:S(2)}) collective-permute-start(f32[128,512]{1,0:T(8,128)S(1)} %get-tuple-element.52), channel_id=1, source_target_pairs={{96,0},{97,1},{98,2},{99,3},{100,4},{101,5},{102,6},{103,7},{104,8... | collective-permute-start | bytes 786440 | tf_op jit(solution)/shard_map/ppermute | solution.py:38
  43.7 8.0 %collective-permute-start.6 = (f32[128,512]{1,0:T(8,128)S(1)}, f32[128,512]{1,0:T(8,128)S(1)}, u32[]{:S(2)}, u32[]{:S(2)}) collective-permute-start(f32[128,512]{1,0:T(8,128)S(1)} %get-tuple-element.53), channel_id=1, source_target_pairs={{32,0},{33,1},{34,2},{35,3},{36,4},{37,5},{38,6},{39,7},{40,8},{41... | collective-permute-start | bytes 786440 | tf_op jit(solution)/shard_map/ppermute | solution.py:38
  50.4 13.0 %collective-permute-start.5 = (f32[256,512]{1,0:T(8,128)S(1)}, f32[256,512]{1,0:T(8,128)S(1)}, u32[]{:S(2)}, u32[]{:S(2)}) collective-permute-start(f32[256,512]{1,0:T(8,128)S(1)} %pad_maximum_fusion.1), channel_id=1, source_target_pairs={{96,0},{97,1},{98,2},{99,3},{100,4},{101,5},{102,6},{103,7},{104,8... | collective-permute-start | bytes 1572872 | tf_op jit(solution)/shard_map/ppermute | solution.py:38
  51.7 12.9 %collective-permute-start.7 = (f32[256,512]{1,0:T(8,128)S(1)}, f32[256,512]{1,0:T(8,128)S(1)}, u32[]{:S(2)}, u32[]{:S(2)}) collective-permute-start(f32[256,512]{1,0:T(8,128)S(1)} %pad_maximum_fusion.2), channel_id=1, source_target_pairs={{32,0},{33,1},{34,2},{35,3},{36,4},{37,5},{38,6},{39,7},{40,8},{41... | collective-permute-start | bytes 1572872 | tf_op jit(solution)/shard_map/ppermute | solution.py:38
  72.6 4.2 %collective-permute-start.11 = (f32[4,256,512]{2,1,0:T(8,128)S(1)}, f32[4,256,512]{2,1,0:T(8,128)S(1)}, u32[]{:S(2)}, u32[]{:S(2)}) collective-permute-start(f32[4,256,512]{2,1,0:T(8,128)S(1)} %get-tuple-element.37), channel_id=1, source_target_pairs={{16,0},{17,1},{18,2},{19,3},{20,4},{21,5},{22,6},{23,7},{24,8},{25... | collective-permute-start | bytes 6291464 | tf_op jit(solution)/shard_map/ppermute | solution.py:38
  72.7 33.4 %collective-permute-start.16 = (bf16[2,512,512]{2,1,0:T(8,128)(2,1)}, bf16[2,512,512]{2,1,0:T(8,128)(2,1)S(1)}, u32[]{:S(2)}, u32[]{:S(2)}) collective-permute-start(bf16[2,512,512]{2,1,0:T(8,128)(2,1)} %collective-permute-done.8.refs_2_), channel_id=1, source_target_pairs={{8,0},{9,1},{10,2},{11,3},{12,4},{13,5},{14,6},{15,7},{0,8},{1,9},... | collective-permute-start | bytes 3145736 | tf_op jit(solution)/shard_map/ppermute | solution.py:38
  77.0 8.4 %collective-permute-start.13 = (f32[128,512]{1,0:T(8,128)S(1)}, f32[128,512]{1,0:T(8,128)S(1)}, u32[]{:S(2)}, u32[]{:S(2)}) collective-permute-start(f32[128,512]{1,0:T(8,128)S(1)} %get-tuple-element.50), channel_id=1, source_target_pairs={{32,0},{33,1},{34,2},{35,3},{36,4},{37,5},{38,6},{39,7},{40,8},{41... | collective-permute-start | bytes 786440 | tf_op jit(solution)/shard_map/ppermute | solution.py:38
  77.9 8.1 %collective-permute-start.12 = (f32[128,512]{1,0:T(8,128)S(1)}, f32[128,512]{1,0:T(8,128)S(1)}, u32[]{:S(2)}, u32[]{:S(2)}) collective-permute-start(f32[128,512]{1,0:T(8,128)S(1)} %get-tuple-element.51), channel_id=1, source_target_pairs={{96,0},{97,1},{98,2},{99,3},{100,4},{101,5},{102,6},{103,7},{104,8... | collective-permute-start | bytes 786440 | tf_op jit(solution)/shard_map/ppermute | solution.py:38
  87.8 13.3 %collective-permute-start.14 = (f32[256,512]{1,0:T(8,128)}, f32[256,512]{1,0:T(8,128)}, u32[]{:S(2)}, u32[]{:S(2)}) collective-permute-start(f32[256,512]{1,0:T(8,128)} %pad_maximum_fusion.3), channel_id=1, source_target_pairs={{96,0},{97,1},{98,2},{99,3},{100,4},{101,5},{102,6},{103,7},{104,8... | collective-permute-start | bytes 1572872 | tf_op jit(solution)/shard_map/ppermute | solution.py:38
  89.6 14.5 %collective-permute-start.15 = (f32[256,512]{1,0:T(8,128)}, f32[256,512]{1,0:T(8,128)}, u32[]{:S(2)}, u32[]{:S(2)}) collective-permute-start(f32[256,512]{1,0:T(8,128)} %pad_maximum_fusion.4), channel_id=1, source_target_pairs={{32,0},{33,1},{34,2},{35,3},{36,4},{37,5},{38,6},{39,7},{40,8},{41... | collective-permute-start | bytes 1572872 | tf_op jit(solution)/shard_map/ppermute | solution.py:38
  90.5 19.2 %copy-start.1 = (f32[256,512]{1,0:T(8,128)S(1)}, f32[256,512]{1,0:T(8,128)}, u32[]{:S(2)}) copy-start(f32[256,512]{1,0:T(8,128)} %fusion.3) | copy-start | bytes 1572868
  107.2 5.8 %collective-permute-start.18 = (f32[256,512]{1,0:T(8,128)S(1)}, f32[256,512]{1,0:T(8,128)S(1)}, u32[]{:S(2)}, u32[]{:S(2)}) collective-permute-start(f32[256,512]{1,0:T(8,128)S(1)} %bitcast.49), channel_id=1, source_target_pairs={{48,32},{80,64},{112,96},{16,0},{176,160},{208,192},{240,224},{144... | collective-permute-start | bytes 1572872 | tf_op jit(solution)/shard_map/ppermute | solution.py:38
  109.8 15.6 %copy-start.2 = (f32[256,512]{1,0:T(8,128)S(1)}, f32[256,512]{1,0:T(8,128)}, u32[]{:S(2)}) copy-start(f32[256,512]{1,0:T(8,128)} %add_add_fusion.3) | copy-start | bytes 1572868
  110.5 14.9 %collective-permute-start.17 = (f32[256,512]{1,0:T(8,128)S(1)}, f32[256,512]{1,0:T(8,128)S(1)}, u32[]{:S(2)}, u32[]{:S(2)}) collective-permute-start(f32[256,512]{1,0:T(8,128)S(1)} %broadcast_select_fusion), channel_id=1, source_target_pairs={{128,0},{129,1},{130,2},{131,3},{132,4},{133,5},{134,6},{135,7},{1... | collective-permute-start | bytes 1572872 | tf_op jit(solution)/shard_map/ppermute | solution.py:38
  113.1 13.0 %collective-permute-start.19 = (f32[128,512]{1,0:T(8,128)S(1)}, f32[128,512]{1,0:T(8,128)S(1)}, u32[]{:S(2)}, u32[]{:S(2)}) collective-permute-start(f32[128,512]{1,0:T(8,128)S(1)} %get-tuple-element.56), channel_id=1, source_target_pairs={{2,98},{14,110},{19,115},{31,127},{36,4},{40,8},{53,21},{57,25},{7... | collective-permute-start | bytes 786440 | tf_op jit(solution)/shard_map/ppermute | solution.py:38
  114.4 11.7 %collective-permute-start.20 = (f32[128,512]{1,0:T(8,128)S(1)}, f32[128,512]{1,0:T(8,128)S(1)}, u32[]{:S(2)}, u32[]{:S(2)}) collective-permute-start(f32[128,512]{1,0:T(8,128)S(1)} %get-tuple-element.57), channel_id=1, source_target_pairs={{2,34},{14,46},{19,51},{31,63},{36,68},{40,72},{53,85},{57,89},{70... | collective-permute-start | bytes 786440 | tf_op jit(solution)/shard_map/ppermute | solution.py:38
  126.3 14.7 %collective-permute-start.21 = (f32[256,512]{1,0:T(8,128)S(1)}, f32[256,512]{1,0:T(8,128)S(1)}, u32[]{:S(2)}, u32[]{:S(2)}) collective-permute-start(f32[256,512]{1,0:T(8,128)S(1)} %maximum_add_fusion), channel_id=1, source_target_pairs={{4,100},{8,104},{21,117},{25,121},{38,6},{42,10},{55,23},{59,27},{... | collective-permute-start | bytes 1572872 | tf_op jit(solution)/shard_map/ppermute | solution.py:38
  128.8 12.3 %collective-permute-start.22 = (f32[256,512]{1,0:T(8,128)S(1)}, f32[256,512]{1,0:T(8,128)S(1)}, u32[]{:S(2)}, u32[]{:S(2)}) collective-permute-start(f32[256,512]{1,0:T(8,128)S(1)} %maximum_add_fusion), channel_id=1, source_target_pairs={{0,32},{12,44},{17,49},{29,61},{34,66},{46,78},{51,83},{63,95},{68... | collective-permute-start | bytes 1572872 | tf_op jit(solution)/shard_map/ppermute | solution.py:38
  141.2 8.0 %collective-permute-start.23 = (f32[256,512]{1,0:T(8,128)S(1)}, f32[256,512]{1,0:T(8,128)S(1)}, u32[]{:S(2)}, u32[]{:S(2)}) collective-permute-start(f32[256,512]{1,0:T(8,128)S(1)} %select_add_fusion), channel_id=1, source_target_pairs={{128,135},{0,151},{144,0},{160,128},{32,114},{64,113},{192,150},{9... | collective-permute-start | bytes 1572872 | tf_op jit(solution)/shard_map/ppermute | solution.py:38
  142.5 18.9 %collective-permute-start.24 = (f32[256,512]{1,0:T(8,128)S(1)}, f32[256,512]{1,0:T(8,128)S(1)}, u32[]{:S(2)}, u32[]{:S(2)}) collective-permute-start(f32[256,512]{1,0:T(8,128)S(1)} %add_add_fusion.2), channel_id=1, source_target_pairs={{32,166},{49,183},{66,192},{83,209},{100,226},{117,243},{6,132},{2... | collective-permute-start | bytes 1572872 | tf_op jit(solution)/shard_map/ppermute | solution.py:38
  143.8 17.6 %collective-permute-start.25 = (f32[256,512]{1,0:T(8,128)S(1)}, f32[256,512]{1,0:T(8,128)S(1)}, u32[]{:S(2)}, u32[]{:S(2)}) collective-permute-start(f32[256,512]{1,0:T(8,128)S(1)} %add_add_fusion.2), channel_id=1, source_target_pairs={{160,166},{177,183},{194,192},{211,209},{228,226},{245,243},{134,1... | collective-permute-start | bytes 1572872 | tf_op jit(solution)/shard_map/ppermute | solution.py:38
  145.1 16.5 %collective-permute-start.26 = (f32[256,512]{1,0:T(8,128)S(1)}, f32[256,512]{1,0:T(8,128)S(1)}, u32[]{:S(2)}, u32[]{:S(2)}) collective-permute-start(f32[256,512]{1,0:T(8,128)S(1)} %select_add_fusion), channel_id=1, source_target_pairs={{16,0},{48,16},{176,151},{80,135},{208,150},{224,98},{240,113},{11... | collective-permute-start | bytes 1572872 | tf_op jit(solution)/shard_map/ppermute | solution.py:38
  145.8 22.9 %collective-permute-start.27 = (f32[256,512]{1,0:T(8,128)S(1)}, f32[256,512]{1,0:T(8,128)S(1)}, u32[]{:S(2)}, u32[]{:S(2)}) collective-permute-start(f32[256,512]{1,0:T(8,128)S(1)} %add_add_fusion.2), channel_id=1, source_target_pairs={{104,226},{121,243},{10,132},{27,149},{44,166},{61,183},{78,192},{... | collective-permute-start | bytes 1572872 | tf_op jit(solution)/shard_map/ppermute | solution.py:38
  149.2 20.5 %collective-permute-start.28 = (f32[256,512]{1,0:T(8,128)S(1)}, f32[256,512]{1,0:T(8,128)S(1)}, u32[]{:S(2)}, u32[]{:S(2)}) collective-permute-start(f32[256,512]{1,0:T(8,128)S(1)} %add_add_fusion.2), channel_id=1, source_target_pairs={{232,226},{249,243},{138,132},{155,149},{172,166},{189,183},{206,1... | collective-permute-start | bytes 1572872 | tf_op jit(solution)/shard_map/ppermute | solution.py:38

commit v8 on v7

--- a/solution.py
+++ b/solution.py
@@ -279,15 +279,9 @@
     return sorted(set(toward(targets, at(offset_from), at(offset_to))))
 
 
-def one_far(value, targets):
-    middle = value.shape[0] // 2
-    top = send(value[:middle], along(targets, 2, 1))
-    bottom = send(value[middle:], along(targets, 2, 3))
-    return value + jnp.concatenate([top, bottom], 0)
-
-
-def one_near(value, targets):
-    return value + send(value, along(targets, 1, 0)) + send(value, along(targets, 3, 0))
+def one_x(value, targets):
+    parts = [send(value, along(targets, offset, 0)) for offset in (2, 1, 3)]
+    return value + parts[0] + (parts[1] + parts[2])
 
 
 Y_SWAP = every(lambda y, x, c, h, z: (1 - y, x, c, block(h, z)))
@@ -346,9 +340,7 @@
     has_first = jnp.asarray(first)[aux, blk]
     done = jnp.where(has_first, total_a, total_b) + send(jnp.where(has_first, total_b, total_a), Y_SWAP)
     (part_c,) = products(table_c, [held[n] for n in HELD_C], HELD_C, PAIRS_C, (1,))
-    part_c = one_far(one_core(part_c[0], target_c), target_c)
-    done, part_c = together(done, part_c)
-    part_c = one_near(part_c, target_c)
+    part_c = one_x(one_core(part_c[0], target_c), target_c)
     done, part_c = together(done, part_c)
 
     top = send(done, final[0]) + send(part_c, final_c[0, 0]) + send(part_c, final_c[1, 0])

time: 171 us -> 165 us (0.965)
  waiting for transfers between devices: 108 us -> 101 us
    ppermute x29 -> x28, waiting for transfers between devices: 108 us -> 101 us  [send(): return lax.ppermute(value, ALL, pairs)]
    ppermute x29 -> x28, starting transfers between devices: 39.8 us -> 39.4 us  [send(): return lax.ppermute(value, ALL, pairs)]
  transfers between devices with their start and end apart: 29 -> 28, of which waited for: 18 -> 18; matrix products, arithmetic and copies ran while one was open for 6% -> 6% of each run, Pallas kernels for 0% -> 0%
where the time goes in v8:
time: 165 us; the launch traced here: 164 us
  waiting for transfers between devices  101 us (61%)
  starting transfers between devices  39.4 us (24%)
  Pallas kernels  9.91 us (6%)
  other arithmetic  8.98 us (5%)
  local copies, waits for them, and re-layouts  4.09 us (2%)
    ppermute x28, waiting for transfers between devices, send(): return lax.ppermute(value, ALL, pairs)  101 us
    ppermute x28, starting transfers between devices, send(): return lax.ppermute(value, ALL, pairs)  39.4 us
    pallas_call x3, Pallas kernels, products(): pl.pallas_call(functools.partial(units_kernel, pairs, index_pairs, len(co...  9.84 us
  transfers between devices with their start and end apart: 28, of which 18 were waited for; matrix products, arithmetic and copies ran while one was open for 6% of the time, Pallas kernels for 0%

profile of v8, /device:TPU:12, one launch (start us, length us, event | category | flops | bytes accessed | tf_op | source)
XLA Modules:
  0.0 163.5 jit_solution(4848405401396473174)
XLA Ops:
  0.0 5.9 %collective-permute-start = (bf16[2,512,512]{2,1,0:T(8,128)(2,1)}, bf16[2,512,512]{2,1,0:T(8,128)(2,1)}, u32[]{:S(2)}, u32[]{:S(2)}) collective-permute-start(bf16[2,512,512]{2,1,0:T(8,128)(2,1)} %source.1), channel_id=1, source_target_pairs={{1,0},{2,1},{3,2},{4,3},{5,4},{6,5},{7,6},{0,7},{9,8},{10,9},{11,1... | collective-permute-start | bytes 3145736 | tf_op jit(solution)/shard_map/ppermute | solution.py:38
  5.9 2.3 %collective-permute-start.2 = (bf16[2,512,512]{2,1,0:T(8,128)(2,1)}, bf16[2,512,512]{2,1,0:T(8,128)(2,1)S(1)}, u32[]{:S(2)}, u32[]{:S(2)}) collective-permute-start(bf16[2,512,512]{2,1,0:T(8,128)(2,1)} %source.1), channel_id=1, source_target_pairs={{8,0},{9,1},{10,2},{11,3},{12,4},{13,5},{14,6},{15,7},{0,8},{1,9},... | collective-permute-start | bytes 3145736 | tf_op jit(solution)/shard_map/ppermute | solution.py:38
  10.2 18.4 %collective-permute-done.refs_1_ = bf16[2,512,512]{2,1,0:T(8,128)(2,1)} collective-permute-done((bf16[2,512,512]{2,1,0:T(8,128)(2,1)}, bf16[2,512,512]{2,1,0:T(8,128)(2,1)}, u32[]{:S(2)}, u32[]{:S(2)}) %collective-permute-start) | collective-permute-done | bytes 1048608 | tf_op jit(solution)/shard_map/ppermute | solution.py:38
  28.6 3.3 %collective-permute-done.1.refs_2_.refs_1_ = bf16[2,512,512]{2,1,0:T(8,128)(2,1)S(1)} collective-permute-done((bf16[2,512,512]{2,1,0:T(8,128)(2,1)}, bf16[2,512,512]{2,1,0:T(8,128)(2,1)S(1)}, u32[]{:S(2)}, u32[]{:S(2)}) %collective-permute-start.1) | collective-permute-done | bytes 1048608 | tf_op jit(solution)/shard_map/ppermute | solution.py:38
  32.2 4.4 %shard_map.56 = (f32[4,256,512]{2,1,0:T(8,128)S(1)}, f32[4,256,512]{2,1,0:T(8,128)S(1)}) custom-call(s32[20]{0:T(128)S(1)} %get-tuple-element.52.table, bf16[2,512,512]{2,1,0:T(8,128)(2,1)S(1)} %shard_map.55.refs_0_, bf16[2,512,512]{2,1,0:T(8,128)(2,1)} %collective-permute-done.refs_1_, bf16[2,512,512]{2,1,0:T(8,128)(2,1)S(1)} %collective-permute-done.1.refs_2_.refs_1_, ...), custom_call_target="tpu_custom_call" | custom-call | tf_op jit(solution)/shard_map/pallas_call | solution.py:236
  36.7 2.4 %collective-permute-start.10 = (bf16[2,512,512]{2,1,0:T(8,128)(2,1)}, bf16[2,512,512]{2,1,0:T(8,128)(2,1)S(1)}, u32[]{:S(2)}, u32[]{:S(2)}) collective-permute-start(bf16[2,512,512]{2,1,0:T(8,128)(2,1)} %collective-permute-done.refs_1_), channel_id=1, source_target_pairs={{8,0},{9,1},{10,2},{11,3},{12,4},{13,5},{14,6},{15,7},{0,8},{1,9},... | collective-permute-start | bytes 3145736 | tf_op jit(solution)/shard_map/ppermute | solution.py:38
  39.1 2.9 %collective-permute-start.8 = (bf16[2,512,512]{2,1,0:T(8,128)(2,1)}, bf16[2,512,512]{2,1,0:T(8,128)(2,1)}, u32[]{:S(2)}, u32[]{:S(2)}) collective-permute-start(bf16[2,512,512]{2,1,0:T(8,128)(2,1)} %collective-permute-done.refs_1_), channel_id=1, source_target_pairs={{1,0},{2,1},{3,2},{4,3},{5,4},{6,5},{7,6},{0,7},{9,8},{10,9},{11,1... | collective-permute-start | bytes 3145736 | tf_op jit(solution)/shard_map/ppermute | solution.py:38
  44.6 5.7 %collective-permute-done.4 = f32[128,512]{1,0:T(8,128)S(1)} collective-permute-done((f32[128,512]{1,0:T(8,128)S(1)}, f32[128,512]{1,0:T(8,128)S(1)}, u32[]{:S(2)}, u32[]{:S(2)}) %collective-permute-start.4) | collective-permute-done | bytes 262176 | tf_op jit(solution)/shard_map/ppermute | solution.py:38
  52.8 10.6 %collective-permute-done.5 = f32[256,512]{1,0:T(8,128)S(1)} collective-permute-done((f32[256,512]{1,0:T(8,128)S(1)}, f32[256,512]{1,0:T(8,128)S(1)}, u32[]{:S(2)}, u32[]{:S(2)}) %collective-permute-start.5) | collective-permute-done | bytes 524320 | tf_op jit(solution)/shard_map/ppermute | solution.py:38
  65.7 2.5 %collective-permute-done.9.refs_3_.refs_0_ = bf16[2,512,512]{2,1,0:T(8,128)(2,1)S(1)} collective-permute-done((bf16[2,512,512]{2,1,0:T(8,128)(2,1)S(1)}, bf16[2,512,512]{2,1,0:T(8,128)(2,1)S(1)}, u32[]{:S(2)}, u32[]{:S(2)}) %collective-permute-start.9) | collective-permute-done | bytes 1048608 | tf_op jit(solution)/shard_map/ppermute | solution.py:38
  68.2 4.4 %shard_map.57 = (f32[4,256,512]{2,1,0:T(8,128)S(1)}, f32[4,256,512]{2,1,0:T(8,128)S(1)}) custom-call(s32[20]{0:T(128)S(1)} %get-tuple-element.53.table, bf16[2,512,512]{2,1,0:T(8,128)(2,1)S(1)} %shard_map.55.refs_0_, bf16[2,512,512]{2,1,0:T(8,128)(2,1)S(1)} %collective-permute-done.1.refs_2_.refs_1_, bf16[2,512,512]{2,1,0:T(8,128)(2,1)} %collective-permute-done.8.refs_2_, ...), custom_call_target="tpu_custom_call" | custom-call | tf_op jit(solution)/shard_map/pallas_call | solution.py:236
  72.7 1.3 collective-permute-start.16
  74.0 2.8 %collective-permute-done.11 = f32[4,256,512]{2,1,0:T(8,128)S(1)} collective-permute-done((f32[4,256,512]{2,1,0:T(8,128)S(1)}, f32[4,256,512]{2,1,0:T(8,128)S(1)}, u32[]{:S(2)}, u32[]{:S(2)}) %collective-permute-start.11) | collective-permute-done | bytes 2097184 | tf_op jit(solution)/shard_map/ppermute | solution.py:38
  77.9 1.6 collective-permute-start.12
  79.5 5.8 %collective-permute-done.13 = f32[128,512]{1,0:T(8,128)S(1)} collective-permute-done((f32[128,512]{1,0:T(8,128)S(1)}, f32[128,512]{1,0:T(8,128)S(1)}, u32[]{:S(2)}, u32[]{:S(2)}) %collective-permute-start.13) | collective-permute-done | bytes 262176 | tf_op jit(solution)/shard_map/ppermute | solution.py:38
  87.8 1.8 %collective-permute-start.14 = (f32[256,512]{1,0:T(8,128)}, f32[256,512]{1,0:T(8,128)}, u32[]{:S(2)}, u32[]{:S(2)}) collective-permute-start(f32[256,512]{1,0:T(8,128)} %pad_maximum_fusion.3), channel_id=1, source_target_pairs={{96,0},{97,1},{98,2},{99,3},{100,4},{101,5},{102,6},{103,7},{104,8... | collective-permute-start | bytes 1572872 | tf_op jit(solution)/shard_map/ppermute | solution.py:38
  90.5 10.5 %collective-permute-done.14 = f32[256,512]{1,0:T(8,128)} collective-permute-done((f32[256,512]{1,0:T(8,128)}, f32[256,512]{1,0:T(8,128)}, u32[]{:S(2)}, u32[]{:S(2)}) %collective-permute-start.14) | collective-permute-done | bytes 524320 | tf_op jit(solution)/shard_map/ppermute | solution.py:38
  101.0 3.0 %collective-permute-done.15 = f32[256,512]{1,0:T(8,128)} collective-permute-done((f32[256,512]{1,0:T(8,128)}, f32[256,512]{1,0:T(8,128)}, u32[]{:S(2)}, u32[]{:S(2)}) %collective-permute-start.15) | collective-permute-done | bytes 524320 | tf_op jit(solution)/shard_map/ppermute | solution.py:38
  104.0 2.1 %add_add_fusion.3 = f32[256,512]{1,0:T(8,128)} fusion(f32[256,512]{1,0:T(8,128)} %collective-permute-done.15, f32[256,512]{1,0:T(8,128)S(1)} %get-tuple-element.36, f32[256,512]{1,0:T(8,128)} %collective-permute-done.14), kind=kLoop, calls=%fused_computation.19 | loop fusion | flops 262144 | bytes 2097152 | tf_op jit(solution)/shard_map/add | solution.py:337
  107.2 1.4 collective-permute-start.18
  108.6 1.3 dynamic_slice.12
  110.7 2.5 %collective-permute-start.17 = (f32[256,512]{1,0:T(8,128)S(1)}, f32[256,512]{1,0:T(8,128)S(1)}, u32[]{:S(2)}, u32[]{:S(2)}) collective-permute-start(f32[256,512]{1,0:T(8,128)S(1)} %broadcast_select_fusion), channel_id=1, source_target_pairs={{128,0},{129,1},{130,2},{131,3},{132,4},{133,5},{134,6},{135,7},{1... | collective-permute-start | bytes 1572872 | tf_op jit(solution)/shard_map/ppermute | solution.py:38
  114.0 1.3 collective-permute-start.20
  116.0 9.6 %collective-permute-done.17 = f32[256,512]{1,0:T(8,128)S(1)} collective-permute-done((f32[256,512]{1,0:T(8,128)S(1)}, f32[256,512]{1,0:T(8,128)S(1)}, u32[]{:S(2)}, u32[]{:S(2)}) %collective-permute-start.17) | collective-permute-done | bytes 524320 | tf_op jit(solution)/shard_map/ppermute | solution.py:38
  127.8 3.2 %collective-permute-start.22 = (f32[256,512]{1,0:T(8,128)S(1)}, f32[256,512]{1,0:T(8,128)S(1)}, u32[]{:S(2)}, u32[]{:S(2)}) collective-permute-start(f32[256,512]{1,0:T(8,128)S(1)} %select_add_fusion), channel_id=1, source_target_pairs={{128,135},{0,151},{144,0},{160,128},{32,114},{64,113},{192,150},{9... | collective-permute-start | bytes 1572872 | tf_op jit(solution)/shard_map/ppermute | solution.py:38
  131.1 1.3 collective-permute-start.23
  132.4 1.3 collective-permute-start.24
  134.4 1.3 collective-permute-start.26
  135.7 5.5 %collective-permute-done.22 = f32[256,512]{1,0:T(8,128)S(1)} collective-permute-done((f32[256,512]{1,0:T(8,128)S(1)}, f32[256,512]{1,0:T(8,128)S(1)}, u32[]{:S(2)}, u32[]{:S(2)}) %collective-permute-start.22) | collective-permute-done | bytes 524320 | tf_op jit(solution)/shard_map/ppermute | solution.py:38
  142.4 7.3 %collective-permute-done.23 = f32[256,512]{1,0:T(8,128)S(1)} collective-permute-done((f32[256,512]{1,0:T(8,128)S(1)}, f32[256,512]{1,0:T(8,128)S(1)}, u32[]{:S(2)}, u32[]{:S(2)}) %collective-permute-start.23) | collective-permute-done | bytes 524320 | tf_op jit(solution)/shard_map/ppermute | solution.py:38
  149.7 2.3 %collective-permute-done.24 = f32[256,512]{1,0:T(8,128)S(1)} collective-permute-done((f32[256,512]{1,0:T(8,128)S(1)}, f32[256,512]{1,0:T(8,128)S(1)}, u32[]{:S(2)}, u32[]{:S(2)}) %collective-permute-start.24) | collective-permute-done | bytes 524320 | tf_op jit(solution)/shard_map/ppermute | solution.py:38
  152.2 10.1 %collective-permute-done.26 = f32[256,512]{1,0:T(8,128)S(1)} collective-permute-done((f32[256,512]{1,0:T(8,128)S(1)}, f32[256,512]{1,0:T(8,128)S(1)}, u32[]{:S(2)}, u32[]{:S(2)}) %collective-permute-start.26) | collective-permute-done | bytes 524320 | tf_op jit(solution)/shard_map/ppermute | solution.py:38
  (62 shorter events, 23.0 us)
Async XLA Ops:
  0.0 28.6 %collective-permute-start = (bf16[2,512,512]{2,1,0:T(8,128)(2,1)}, bf16[2,512,512]{2,1,0:T(8,128)(2,1)}, u32[]{:S(2)}, u32[]{:S(2)}) collective-permute-start(bf16[2,512,512]{2,1,0:T(8,128)(2,1)} %source.1), channel_id=1, source_target_pairs={{1,0},{2,1},{3,2},{4,3},{5,4},{6,5},{7,6},{0,7},{9,8},{10,9},{11,1... | collective-permute-start | bytes 3145736 | tf_op jit(solution)/shard_map/ppermute | solution.py:38
  5.9 26.0 %collective-permute-start.1 = (bf16[2,512,512]{2,1,0:T(8,128)(2,1)}, bf16[2,512,512]{2,1,0:T(8,128)(2,1)S(1)}, u32[]{:S(2)}, u32[]{:S(2)}) collective-permute-start(bf16[2,512,512]{2,1,0:T(8,128)(2,1)} %source.1), channel_id=1, source_target_pairs={{7,0},{0,1},{1,2},{2,3},{3,4},{4,5},{5,6},{6,7},{15,8},{8,9},{9,10... | collective-permute-start | bytes 3145736 | tf_op jit(solution)/shard_map/ppermute | solution.py:38
  5.9 26.3 %collective-permute-start.2 = (bf16[2,512,512]{2,1,0:T(8,128)(2,1)}, bf16[2,512,512]{2,1,0:T(8,128)(2,1)S(1)}, u32[]{:S(2)}, u32[]{:S(2)}) collective-permute-start(bf16[2,512,512]{2,1,0:T(8,128)(2,1)} %source.1), channel_id=1, source_target_pairs={{8,0},{9,1},{10,2},{11,3},{12,4},{13,5},{14,6},{15,7},{0,8},{1,9},... | collective-permute-start | bytes 3145736 | tf_op jit(solution)/shard_map/ppermute | solution.py:38
  8.2 1.3 copy-start
  36.6 5.4 %collective-permute-start.3 = (f32[4,256,512]{2,1,0:T(8,128)S(1)}, f32[4,256,512]{2,1,0:T(8,128)S(1)}, u32[]{:S(2)}, u32[]{:S(2)}) collective-permute-start(f32[4,256,512]{2,1,0:T(8,128)S(1)} %get-tuple-element.29), channel_id=1, source_target_pairs={{16,0},{17,1},{18,2},{19,3},{20,4},{21,5},{22,6},{23,7},{24,8},{25... | collective-permute-start | bytes 6291464 | tf_op jit(solution)/shard_map/ppermute | solution.py:38
  36.7 29.0 %collective-permute-start.10 = (bf16[2,512,512]{2,1,0:T(8,128)(2,1)}, bf16[2,512,512]{2,1,0:T(8,128)(2,1)S(1)}, u32[]{:S(2)}, u32[]{:S(2)}) collective-permute-start(bf16[2,512,512]{2,1,0:T(8,128)(2,1)} %collective-permute-done.refs_1_), channel_id=1, source_target_pairs={{8,0},{9,1},{10,2},{11,3},{12,4},{13,5},{14,6},{15,7},{0,8},{1,9},... | collective-permute-start | bytes 3145736 | tf_op jit(solution)/shard_map/ppermute | solution.py:38
  39.1 26.6 %collective-permute-start.8 = (bf16[2,512,512]{2,1,0:T(8,128)(2,1)}, bf16[2,512,512]{2,1,0:T(8,128)(2,1)}, u32[]{:S(2)}, u32[]{:S(2)}) collective-permute-start(bf16[2,512,512]{2,1,0:T(8,128)(2,1)} %collective-permute-done.refs_1_), channel_id=1, source_target_pairs={{1,0},{2,1},{3,2},{4,3},{5,4},{6,5},{7,6},{0,7},{9,8},{10,9},{11,1... | collective-permute-start | bytes 3145736 | tf_op jit(solution)/shard_map/ppermute | solution.py:38
  42.1 26.1 %collective-permute-start.9 = (bf16[2,512,512]{2,1,0:T(8,128)(2,1)S(1)}, bf16[2,512,512]{2,1,0:T(8,128)(2,1)S(1)}, u32[]{:S(2)}, u32[]{:S(2)}) collective-permute-start(bf16[2,512,512]{2,1,0:T(8,128)(2,1)S(1)} %collective-permute-done.1.refs_2_.refs_1_), channel_id=1, source_target_pairs={{7,0},{0,1},{1,2},{2,3},{3,4},{4,5},{5,6},{6,7},{15,8},{8,9},{9,10... | collective-permute-start | bytes 3145736 | tf_op jit(solution)/shard_map/ppermute | solution.py:38
  42.1 8.2 %collective-permute-start.4 = (f32[128,512]{1,0:T(8,128)S(1)}, f32[128,512]{1,0:T(8,128)S(1)}, u32[]{:S(2)}, u32[]{:S(2)}) collective-permute-start(f32[128,512]{1,0:T(8,128)S(1)} %get-tuple-element.48), channel_id=1, source_target_pairs={{96,0},{97,1},{98,2},{99,3},{100,4},{101,5},{102,6},{103,7},{104,8... | collective-permute-start | bytes 786440 | tf_op jit(solution)/shard_map/ppermute | solution.py:38
  43.7 8.0 %collective-permute-start.6 = (f32[128,512]{1,0:T(8,128)S(1)}, f32[128,512]{1,0:T(8,128)S(1)}, u32[]{:S(2)}, u32[]{:S(2)}) collective-permute-start(f32[128,512]{1,0:T(8,128)S(1)} %get-tuple-element.49), channel_id=1, source_target_pairs={{32,0},{33,1},{34,2},{35,3},{36,4},{37,5},{38,6},{39,7},{40,8},{41... | collective-permute-start | bytes 786440 | tf_op jit(solution)/shard_map/ppermute | solution.py:38
  50.4 13.0 %collective-permute-start.5 = (f32[256,512]{1,0:T(8,128)S(1)}, f32[256,512]{1,0:T(8,128)S(1)}, u32[]{:S(2)}, u32[]{:S(2)}) collective-permute-start(f32[256,512]{1,0:T(8,128)S(1)} %pad_maximum_fusion.1), channel_id=1, source_target_pairs={{96,0},{97,1},{98,2},{99,3},{100,4},{101,5},{102,6},{103,7},{104,8... | collective-permute-start | bytes 1572872 | tf_op jit(solution)/shard_map/ppermute | solution.py:38
  51.7 12.9 %collective-permute-start.7 = (f32[256,512]{1,0:T(8,128)S(1)}, f32[256,512]{1,0:T(8,128)S(1)}, u32[]{:S(2)}, u32[]{:S(2)}) collective-permute-start(f32[256,512]{1,0:T(8,128)S(1)} %pad_maximum_fusion.2), channel_id=1, source_target_pairs={{32,0},{33,1},{34,2},{35,3},{36,4},{37,5},{38,6},{39,7},{40,8},{41... | collective-permute-start | bytes 1572872 | tf_op jit(solution)/shard_map/ppermute | solution.py:38
  72.6 4.2 %collective-permute-start.11 = (f32[4,256,512]{2,1,0:T(8,128)S(1)}, f32[4,256,512]{2,1,0:T(8,128)S(1)}, u32[]{:S(2)}, u32[]{:S(2)}) collective-permute-start(f32[4,256,512]{2,1,0:T(8,128)S(1)} %get-tuple-element.35), channel_id=1, source_target_pairs={{16,0},{17,1},{18,2},{19,3},{20,4},{21,5},{22,6},{23,7},{24,8},{25... | collective-permute-start | bytes 6291464 | tf_op jit(solution)/shard_map/ppermute | solution.py:38
  72.7 33.4 %collective-permute-start.16 = (bf16[2,512,512]{2,1,0:T(8,128)(2,1)}, bf16[2,512,512]{2,1,0:T(8,128)(2,1)S(1)}, u32[]{:S(2)}, u32[]{:S(2)}) collective-permute-start(bf16[2,512,512]{2,1,0:T(8,128)(2,1)} %collective-permute-done.8.refs_2_), channel_id=1, source_target_pairs={{8,0},{9,1},{10,2},{11,3},{12,4},{13,5},{14,6},{15,7},{0,8},{1,9},... | collective-permute-start | bytes 3145736 | tf_op jit(solution)/shard_map/ppermute | solution.py:38
  77.0 8.4 %collective-permute-start.13 = (f32[128,512]{1,0:T(8,128)S(1)}, f32[128,512]{1,0:T(8,128)S(1)}, u32[]{:S(2)}, u32[]{:S(2)}) collective-permute-start(f32[128,512]{1,0:T(8,128)S(1)} %get-tuple-element.46), channel_id=1, source_target_pairs={{32,0},{33,1},{34,2},{35,3},{36,4},{37,5},{38,6},{39,7},{40,8},{41... | collective-permute-start | bytes 786440 | tf_op jit(solution)/shard_map/ppermute | solution.py:38
  77.9 8.1 %collective-permute-start.12 = (f32[128,512]{1,0:T(8,128)S(1)}, f32[128,512]{1,0:T(8,128)S(1)}, u32[]{:S(2)}, u32[]{:S(2)}) collective-permute-start(f32[128,512]{1,0:T(8,128)S(1)} %get-tuple-element.47), channel_id=1, source_target_pairs={{96,0},{97,1},{98,2},{99,3},{100,4},{101,5},{102,6},{103,7},{104,8... | collective-permute-start | bytes 786440 | tf_op jit(solution)/shard_map/ppermute | solution.py:38
  87.8 13.3 %collective-permute-start.14 = (f32[256,512]{1,0:T(8,128)}, f32[256,512]{1,0:T(8,128)}, u32[]{:S(2)}, u32[]{:S(2)}) collective-permute-start(f32[256,512]{1,0:T(8,128)} %pad_maximum_fusion.3), channel_id=1, source_target_pairs={{96,0},{97,1},{98,2},{99,3},{100,4},{101,5},{102,6},{103,7},{104,8... | collective-permute-start | bytes 1572872 | tf_op jit(solution)/shard_map/ppermute | solution.py:38
  89.5 14.5 %collective-permute-start.15 = (f32[256,512]{1,0:T(8,128)}, f32[256,512]{1,0:T(8,128)}, u32[]{:S(2)}, u32[]{:S(2)}) collective-permute-start(f32[256,512]{1,0:T(8,128)} %pad_maximum_fusion.4), channel_id=1, source_target_pairs={{32,0},{33,1},{34,2},{35,3},{36,4},{37,5},{38,6},{39,7},{40,8},{41... | collective-permute-start | bytes 1572872 | tf_op jit(solution)/shard_map/ppermute | solution.py:38
  90.5 19.4 %copy-start.1 = (f32[256,512]{1,0:T(8,128)S(1)}, f32[256,512]{1,0:T(8,128)}, u32[]{:S(2)}) copy-start(f32[256,512]{1,0:T(8,128)} %fusion.3) | copy-start | bytes 1572868
  107.2 18.4 %copy-start.2 = (f32[256,512]{1,0:T(8,128)S(1)}, f32[256,512]{1,0:T(8,128)}, u32[]{:S(2)}) copy-start(f32[256,512]{1,0:T(8,128)} %add_add_fusion.3) | copy-start | bytes 1572868
  107.2 6.0 %collective-permute-start.18 = (f32[256,512]{1,0:T(8,128)S(1)}, f32[256,512]{1,0:T(8,128)S(1)}, u32[]{:S(2)}, u32[]{:S(2)}) collective-permute-start(f32[256,512]{1,0:T(8,128)S(1)} %bitcast.49), channel_id=1, source_target_pairs={{48,32},{80,64},{112,96},{16,0},{176,160},{208,192},{240,224},{144... | collective-permute-start | bytes 1572872 | tf_op jit(solution)/shard_map/ppermute | solution.py:38
  110.7 14.9 %collective-permute-start.17 = (f32[256,512]{1,0:T(8,128)S(1)}, f32[256,512]{1,0:T(8,128)S(1)}, u32[]{:S(2)}, u32[]{:S(2)}) collective-permute-start(f32[256,512]{1,0:T(8,128)S(1)} %broadcast_select_fusion), channel_id=1, source_target_pairs={{128,0},{129,1},{130,2},{131,3},{132,4},{133,5},{134,6},{135,7},{1... | collective-permute-start | bytes 1572872 | tf_op jit(solution)/shard_map/ppermute | solution.py:38
  113.3 13.1 %collective-permute-start.19 = (f32[256,512]{1,0:T(8,128)S(1)}, f32[256,512]{1,0:T(8,128)S(1)}, u32[]{:S(2)}, u32[]{:S(2)}) collective-permute-start(f32[256,512]{1,0:T(8,128)S(1)} %bitcast_add_fusion), channel_id=1, source_target_pairs={{2,66},{14,78},{19,83},{31,95},{36,100},{40,104},{53,117},{57,121}... | collective-permute-start | bytes 1572872 | tf_op jit(solution)/shard_map/ppermute | solution.py:38
  114.0 13.6 %collective-permute-start.20 = (f32[256,512]{1,0:T(8,128)S(1)}, f32[256,512]{1,0:T(8,128)S(1)}, u32[]{:S(2)}, u32[]{:S(2)}) collective-permute-start(f32[256,512]{1,0:T(8,128)S(1)} %bitcast_add_fusion), channel_id=1, source_target_pairs={{4,100},{8,104},{21,117},{25,121},{38,6},{42,10},{55,23},{59,27},{... | collective-permute-start | bytes 1572872 | tf_op jit(solution)/shard_map/ppermute | solution.py:38
  115.3 12.3 %collective-permute-start.21 = (f32[256,512]{1,0:T(8,128)S(1)}, f32[256,512]{1,0:T(8,128)S(1)}, u32[]{:S(2)}, u32[]{:S(2)}) collective-permute-start(f32[256,512]{1,0:T(8,128)S(1)} %bitcast_add_fusion), channel_id=1, source_target_pairs={{0,32},{12,44},{17,49},{29,61},{34,66},{46,78},{51,83},{63,95},{68... | collective-permute-start | bytes 1572872 | tf_op jit(solution)/shard_map/ppermute | solution.py:38
  127.8 13.3 %collective-permute-start.22 = (f32[256,512]{1,0:T(8,128)S(1)}, f32[256,512]{1,0:T(8,128)S(1)}, u32[]{:S(2)}, u32[]{:S(2)}) collective-permute-start(f32[256,512]{1,0:T(8,128)S(1)} %select_add_fusion), channel_id=1, source_target_pairs={{128,135},{0,151},{144,0},{160,128},{32,114},{64,113},{192,150},{9... | collective-permute-start | bytes 1572872 | tf_op jit(solution)/shard_map/ppermute | solution.py:38
  131.1 18.6 %collective-permute-start.23 = (f32[256,512]{1,0:T(8,128)S(1)}, f32[256,512]{1,0:T(8,128)S(1)}, u32[]{:S(2)}, u32[]{:S(2)}) collective-permute-start(f32[256,512]{1,0:T(8,128)S(1)} %add_add_fusion.2), channel_id=1, source_target_pairs={{32,166},{49,183},{66,192},{83,209},{100,226},{117,243},{6,132},{2... | collective-permute-start | bytes 1572872 | tf_op jit(solution)/shard_map/ppermute | solution.py:38
  132.4 19.7 %collective-permute-start.24 = (f32[256,512]{1,0:T(8,128)S(1)}, f32[256,512]{1,0:T(8,128)S(1)}, u32[]{:S(2)}, u32[]{:S(2)}) collective-permute-start(f32[256,512]{1,0:T(8,128)S(1)} %add_add_fusion.2), channel_id=1, source_target_pairs={{160,166},{177,183},{194,192},{211,209},{228,226},{245,243},{134,1... | collective-permute-start | bytes 1572872 | tf_op jit(solution)/shard_map/ppermute | solution.py:38
  133.7 18.5 %collective-permute-start.25 = (f32[256,512]{1,0:T(8,128)S(1)}, f32[256,512]{1,0:T(8,128)S(1)}, u32[]{:S(2)}, u32[]{:S(2)}) collective-permute-start(f32[256,512]{1,0:T(8,128)S(1)} %select_add_fusion), channel_id=1, source_target_pairs={{16,0},{48,16},{176,151},{80,135},{208,150},{224,98},{240,113},{11... | collective-permute-start | bytes 1572872 | tf_op jit(solution)/shard_map/ppermute | solution.py:38
  134.4 28.0 %collective-permute-start.26 = (f32[256,512]{1,0:T(8,128)S(1)}, f32[256,512]{1,0:T(8,128)S(1)}, u32[]{:S(2)}, u32[]{:S(2)}) collective-permute-start(f32[256,512]{1,0:T(8,128)S(1)} %add_add_fusion.2), channel_id=1, source_target_pairs={{104,226},{121,243},{10,132},{27,149},{44,166},{61,183},{78,192},{... | collective-permute-start | bytes 1572872 | tf_op jit(solution)/shard_map/ppermute | solution.py:38
  141.1 21.2 %collective-permute-start.27 = (f32[256,512]{1,0:T(8,128)S(1)}, f32[256,512]{1,0:T(8,128)S(1)}, u32[]{:S(2)}, u32[]{:S(2)}) collective-permute-start(f32[256,512]{1,0:T(8,128)S(1)} %add_add_fusion.2), channel_id=1, source_target_pairs={{232,226},{249,243},{138,132},{155,149},{172,166},{189,183},{206,1... | collective-permute-start | bytes 1572872 | tf_op jit(solution)/shard_map/ppermute | solution.py:38

commit v9 on v8

--- a/solution.py
+++ b/solution.py
@@ -94,7 +94,7 @@
 @functools.cache
 def route(source, target):
     found = []
-    for weight, order in ((0.05, (0, 1, 2)), (1.0, (2, 1, 0))):
+    for weight, order in ((1.0, (2, 0, 1)), (0.01, (2, 1, 0))):
         at = list(source)
         for axis in order:
             for place, way, share in steps(at[axis], target[axis], (NX, 4, NZ)[axis]):
@@ -116,7 +116,7 @@
 
 
 @functools.cache
-def spread(trials=40000):
+def spread(trials=120000):
     draw = random.Random(0)
     where = [(own // NZ, own % NZ) for own in range(GROUPS)]
     units = [[units_of(pairs, h, z) for pairs in (PAIRS_A, PAIRS_B)] for h, z in where]
@@ -152,7 +152,7 @@
             for sign, place, index in ((-1, u, i), (-1, v, j), (1, u, j), (1, v, i)):
                 for link, share in on(own, batch, place, index, plane[place]):
                     change[link] += sign * share
-        if sum(link[0] * ((load[link] + d) ** 4 - load[link] ** 4) for link, d in change.items()) <= 0:
+        if sum(link[0] * ((load[link] + d) ** 6 - load[link] ** 6) for link, d in change.items()) <= 0:
             for link, d in change.items():
                 load[link] += d
             if u == v:

time: 165 us -> 167 us (1.012); the launches traced: 164 us -> 164 us
  no operation moved by 1% of the time
where the time goes in v9:
time: 167 us; the launch traced here: 164 us
  waiting for transfers between devices  101 us (60%)
  starting transfers between devices  39.2 us (23%)
  Pallas kernels  9.91 us (6%)
  other arithmetic  8.98 us (5%)
  local copies, waits for them, and re-layouts  4.09 us (2%)
    ppermute x28, waiting for transfers between devices, send(): return lax.ppermute(value, ALL, pairs)  101 us
    ppermute x28, starting transfers between devices, send(): return lax.ppermute(value, ALL, pairs)  39.2 us
    pallas_call x3, Pallas kernels, products(): pl.pallas_call(functools.partial(units_kernel, pairs, index_pairs, len(co...  9.84 us
  transfers between devices with their start and end apart: 28, of which 18 were waited for; matrix products, arithmetic and copies ran while one was open for 6% of the time, Pallas kernels for 0%

profile of v9, /device:TPU:12, one launch (start us, length us, event | category | flops | bytes accessed | tf_op | source)
XLA Modules:
  0.0 163.6 jit_solution(9640036711182456049)
XLA Ops:
  0.0 5.9 %collective-permute-start = (bf16[2,512,512]{2,1,0:T(8,128)(2,1)}, bf16[2,512,512]{2,1,0:T(8,128)(2,1)}, u32[]{:S(2)}, u32[]{:S(2)}) collective-permute-start(bf16[2,512,512]{2,1,0:T(8,128)(2,1)} %source.1), channel_id=1, source_target_pairs={{1,0},{2,1},{3,2},{4,3},{5,4},{6,5},{7,6},{0,7},{9,8},{10,9},{11,1... | collective-permute-start | bytes 3145736 | tf_op jit(solution)/shard_map/ppermute | solution.py:38
  5.9 2.3 %collective-permute-start.2 = (bf16[2,512,512]{2,1,0:T(8,128)(2,1)}, bf16[2,512,512]{2,1,0:T(8,128)(2,1)S(1)}, u32[]{:S(2)}, u32[]{:S(2)}) collective-permute-start(bf16[2,512,512]{2,1,0:T(8,128)(2,1)} %source.1), channel_id=1, source_target_pairs={{8,0},{9,1},{10,2},{11,3},{12,4},{13,5},{14,6},{15,7},{0,8},{1,9},... | collective-permute-start | bytes 3145736 | tf_op jit(solution)/shard_map/ppermute | solution.py:38
  10.2 18.4 %collective-permute-done.refs_1_ = bf16[2,512,512]{2,1,0:T(8,128)(2,1)} collective-permute-done((bf16[2,512,512]{2,1,0:T(8,128)(2,1)}, bf16[2,512,512]{2,1,0:T(8,128)(2,1)}, u32[]{:S(2)}, u32[]{:S(2)}) %collective-permute-start) | collective-permute-done | bytes 1048608 | tf_op jit(solution)/shard_map/ppermute | solution.py:38
  28.6 3.3 %collective-permute-done.1.refs_2_.refs_1_ = bf16[2,512,512]{2,1,0:T(8,128)(2,1)S(1)} collective-permute-done((bf16[2,512,512]{2,1,0:T(8,128)(2,1)}, bf16[2,512,512]{2,1,0:T(8,128)(2,1)S(1)}, u32[]{:S(2)}, u32[]{:S(2)}) %collective-permute-start.1) | collective-permute-done | bytes 1048608 | tf_op jit(solution)/shard_map/ppermute | solution.py:38
  32.2 4.4 %shard_map.56 = (f32[4,256,512]{2,1,0:T(8,128)S(1)}, f32[4,256,512]{2,1,0:T(8,128)S(1)}) custom-call(s32[20]{0:T(128)S(1)} %get-tuple-element.52.table, bf16[2,512,512]{2,1,0:T(8,128)(2,1)S(1)} %shard_map.55.refs_0_, bf16[2,512,512]{2,1,0:T(8,128)(2,1)} %collective-permute-done.refs_1_, bf16[2,512,512]{2,1,0:T(8,128)(2,1)S(1)} %collective-permute-done.1.refs_2_.refs_1_, ...), custom_call_target="tpu_custom_call" | custom-call | tf_op jit(solution)/shard_map/pallas_call | solution.py:236
  36.7 2.4 %collective-permute-start.10 = (bf16[2,512,512]{2,1,0:T(8,128)(2,1)}, bf16[2,512,512]{2,1,0:T(8,128)(2,1)S(1)}, u32[]{:S(2)}, u32[]{:S(2)}) collective-permute-start(bf16[2,512,512]{2,1,0:T(8,128)(2,1)} %collective-permute-done.refs_1_), channel_id=1, source_target_pairs={{8,0},{9,1},{10,2},{11,3},{12,4},{13,5},{14,6},{15,7},{0,8},{1,9},... | collective-permute-start | bytes 3145736 | tf_op jit(solution)/shard_map/ppermute | solution.py:38
  39.1 2.9 %collective-permute-start.8 = (bf16[2,512,512]{2,1,0:T(8,128)(2,1)}, bf16[2,512,512]{2,1,0:T(8,128)(2,1)}, u32[]{:S(2)}, u32[]{:S(2)}) collective-permute-start(bf16[2,512,512]{2,1,0:T(8,128)(2,1)} %collective-permute-done.refs_1_), channel_id=1, source_target_pairs={{1,0},{2,1},{3,2},{4,3},{5,4},{6,5},{7,6},{0,7},{9,8},{10,9},{11,1... | collective-permute-start | bytes 3145736 | tf_op jit(solution)/shard_map/ppermute | solution.py:38
  44.6 5.7 %collective-permute-done.4 = f32[128,512]{1,0:T(8,128)S(1)} collective-permute-done((f32[128,512]{1,0:T(8,128)S(1)}, f32[128,512]{1,0:T(8,128)S(1)}, u32[]{:S(2)}, u32[]{:S(2)}) %collective-permute-start.4) | collective-permute-done | bytes 262176 | tf_op jit(solution)/shard_map/ppermute | solution.py:38
  52.8 10.6 %collective-permute-done.5 = f32[256,512]{1,0:T(8,128)S(1)} collective-permute-done((f32[256,512]{1,0:T(8,128)S(1)}, f32[256,512]{1,0:T(8,128)S(1)}, u32[]{:S(2)}, u32[]{:S(2)}) %collective-permute-start.5) | collective-permute-done | bytes 524320 | tf_op jit(solution)/shard_map/ppermute | solution.py:38
  65.7 2.5 %collective-permute-done.9.refs_3_.refs_0_ = bf16[2,512,512]{2,1,0:T(8,128)(2,1)S(1)} collective-permute-done((bf16[2,512,512]{2,1,0:T(8,128)(2,1)S(1)}, bf16[2,512,512]{2,1,0:T(8,128)(2,1)S(1)}, u32[]{:S(2)}, u32[]{:S(2)}) %collective-permute-start.9) | collective-permute-done | bytes 1048608 | tf_op jit(solution)/shard_map/ppermute | solution.py:38
  68.2 4.4 %shard_map.57 = (f32[4,256,512]{2,1,0:T(8,128)S(1)}, f32[4,256,512]{2,1,0:T(8,128)S(1)}) custom-call(s32[20]{0:T(128)S(1)} %get-tuple-element.53.table, bf16[2,512,512]{2,1,0:T(8,128)(2,1)S(1)} %shard_map.55.refs_0_, bf16[2,512,512]{2,1,0:T(8,128)(2,1)S(1)} %collective-permute-done.1.refs_2_.refs_1_, bf16[2,512,512]{2,1,0:T(8,128)(2,1)} %collective-permute-done.8.refs_2_, ...), custom_call_target="tpu_custom_call" | custom-call | tf_op jit(solution)/shard_map/pallas_call | solution.py:236
  72.7 1.3 collective-permute-start.16
  74.0 2.8 %collective-permute-done.11 = f32[4,256,512]{2,1,0:T(8,128)S(1)} collective-permute-done((f32[4,256,512]{2,1,0:T(8,128)S(1)}, f32[4,256,512]{2,1,0:T(8,128)S(1)}, u32[]{:S(2)}, u32[]{:S(2)}) %collective-permute-start.11) | collective-permute-done | bytes 2097184 | tf_op jit(solution)/shard_map/ppermute | solution.py:38
  77.9 1.6 collective-permute-start.12
  79.5 5.8 %collective-permute-done.13 = f32[128,512]{1,0:T(8,128)S(1)} collective-permute-done((f32[128,512]{1,0:T(8,128)S(1)}, f32[128,512]{1,0:T(8,128)S(1)}, u32[]{:S(2)}, u32[]{:S(2)}) %collective-permute-start.13) | collective-permute-done | bytes 262176 | tf_op jit(solution)/shard_map/ppermute | solution.py:38
  87.8 1.8 %collective-permute-start.14 = (f32[256,512]{1,0:T(8,128)}, f32[256,512]{1,0:T(8,128)}, u32[]{:S(2)}, u32[]{:S(2)}) collective-permute-start(f32[256,512]{1,0:T(8,128)} %pad_maximum_fusion.3), channel_id=1, source_target_pairs={{96,0},{97,1},{98,2},{99,3},{100,4},{101,5},{102,6},{103,7},{104,8... | collective-permute-start | bytes 1572872 | tf_op jit(solution)/shard_map/ppermute | solution.py:38
  90.5 10.5 %collective-permute-done.14 = f32[256,512]{1,0:T(8,128)} collective-permute-done((f32[256,512]{1,0:T(8,128)}, f32[256,512]{1,0:T(8,128)}, u32[]{:S(2)}, u32[]{:S(2)}) %collective-permute-start.14) | collective-permute-done | bytes 524320 | tf_op jit(solution)/shard_map/ppermute | solution.py:38
  101.0 3.0 %collective-permute-done.15 = f32[256,512]{1,0:T(8,128)} collective-permute-done((f32[256,512]{1,0:T(8,128)}, f32[256,512]{1,0:T(8,128)}, u32[]{:S(2)}, u32[]{:S(2)}) %collective-permute-start.15) | collective-permute-done | bytes 524320 | tf_op jit(solution)/shard_map/ppermute | solution.py:38
  104.0 2.1 %add_add_fusion.3 = f32[256,512]{1,0:T(8,128)} fusion(f32[256,512]{1,0:T(8,128)} %collective-permute-done.15, f32[256,512]{1,0:T(8,128)S(1)} %get-tuple-element.36, f32[256,512]{1,0:T(8,128)} %collective-permute-done.14), kind=kLoop, calls=%fused_computation.19 | loop fusion | flops 262144 | bytes 2097152 | tf_op jit(solution)/shard_map/add | solution.py:337
  107.2 1.4 collective-permute-start.18
  108.6 1.3 dynamic_slice.12
  110.7 2.5 %collective-permute-start.17 = (f32[256,512]{1,0:T(8,128)S(1)}, f32[256,512]{1,0:T(8,128)S(1)}, u32[]{:S(2)}, u32[]{:S(2)}) collective-permute-start(f32[256,512]{1,0:T(8,128)S(1)} %broadcast_select_fusion), channel_id=1, source_target_pairs={{128,0},{129,1},{130,2},{131,3},{132,4},{133,5},{134,6},{135,7},{1... | collective-permute-start | bytes 1572872 | tf_op jit(solution)/shard_map/ppermute | solution.py:38
  114.0 1.3 collective-permute-start.20
  116.0 9.6 %collective-permute-done.17 = f32[256,512]{1,0:T(8,128)S(1)} collective-permute-done((f32[256,512]{1,0:T(8,128)S(1)}, f32[256,512]{1,0:T(8,128)S(1)}, u32[]{:S(2)}, u32[]{:S(2)}) %collective-permute-start.17) | collective-permute-done | bytes 524320 | tf_op jit(solution)/shard_map/ppermute | solution.py:38
  127.8 3.0 %collective-permute-start.22 = (f32[256,512]{1,0:T(8,128)S(1)}, f32[256,512]{1,0:T(8,128)S(1)}, u32[]{:S(2)}, u32[]{:S(2)}) collective-permute-start(f32[256,512]{1,0:T(8,128)S(1)} %select_add_fusion), channel_id=1, source_target_pairs={{0,16},{128,151},{160,128},{176,0},{64,113},{192,150},{96,135},{22... | collective-permute-start | bytes 1572872 | tf_op jit(solution)/shard_map/ppermute | solution.py:38
  130.8 1.3 collective-permute-start.23
  132.1 1.3 collective-permute-start.24
  134.1 1.3 collective-permute-start.26
  135.4 5.8 %collective-permute-done.22 = f32[256,512]{1,0:T(8,128)S(1)} collective-permute-done((f32[256,512]{1,0:T(8,128)S(1)}, f32[256,512]{1,0:T(8,128)S(1)}, u32[]{:S(2)}, u32[]{:S(2)}) %collective-permute-start.22) | collective-permute-done | bytes 524320 | tf_op jit(solution)/shard_map/ppermute | solution.py:38
  141.2 1.3 collective-permute-start.27
  142.5 7.1 %collective-permute-done.23 = f32[256,512]{1,0:T(8,128)S(1)} collective-permute-done((f32[256,512]{1,0:T(8,128)S(1)}, f32[256,512]{1,0:T(8,128)S(1)}, u32[]{:S(2)}, u32[]{:S(2)}) %collective-permute-start.23) | collective-permute-done | bytes 524320 | tf_op jit(solution)/shard_map/ppermute | solution.py:38
  150.3 12.1 %collective-permute-done.26 = f32[256,512]{1,0:T(8,128)S(1)} collective-permute-done((f32[256,512]{1,0:T(8,128)S(1)}, f32[256,512]{1,0:T(8,128)S(1)}, u32[]{:S(2)}, u32[]{:S(2)}) %collective-permute-start.26) | collective-permute-done | bytes 524320 | tf_op jit(solution)/shard_map/ppermute | solution.py:38
  (62 shorter events, 22.3 us)
Async XLA Ops:
  0.0 28.6 %collective-permute-start = (bf16[2,512,512]{2,1,0:T(8,128)(2,1)}, bf16[2,512,512]{2,1,0:T(8,128)(2,1)}, u32[]{:S(2)}, u32[]{:S(2)}) collective-permute-start(bf16[2,512,512]{2,1,0:T(8,128)(2,1)} %source.1), channel_id=1, source_target_pairs={{1,0},{2,1},{3,2},{4,3},{5,4},{6,5},{7,6},{0,7},{9,8},{10,9},{11,1... | collective-permute-start | bytes 3145736 | tf_op jit(solution)/shard_map/ppermute | solution.py:38
  5.9 26.0 %collective-permute-start.1 = (bf16[2,512,512]{2,1,0:T(8,128)(2,1)}, bf16[2,512,512]{2,1,0:T(8,128)(2,1)S(1)}, u32[]{:S(2)}, u32[]{:S(2)}) collective-permute-start(bf16[2,512,512]{2,1,0:T(8,128)(2,1)} %source.1), channel_id=1, source_target_pairs={{7,0},{0,1},{1,2},{2,3},{3,4},{4,5},{5,6},{6,7},{15,8},{8,9},{9,10... | collective-permute-start | bytes 3145736 | tf_op jit(solution)/shard_map/ppermute | solution.py:38
  5.9 26.3 %collective-permute-start.2 = (bf16[2,512,512]{2,1,0:T(8,128)(2,1)}, bf16[2,512,512]{2,1,0:T(8,128)(2,1)S(1)}, u32[]{:S(2)}, u32[]{:S(2)}) collective-permute-start(bf16[2,512,512]{2,1,0:T(8,128)(2,1)} %source.1), channel_id=1, source_target_pairs={{8,0},{9,1},{10,2},{11,3},{12,4},{13,5},{14,6},{15,7},{0,8},{1,9},... | collective-permute-start | bytes 3145736 | tf_op jit(solution)/shard_map/ppermute | solution.py:38
  8.2 1.3 copy-start
  36.6 5.4 %collective-permute-start.3 = (f32[4,256,512]{2,1,0:T(8,128)S(1)}, f32[4,256,512]{2,1,0:T(8,128)S(1)}, u32[]{:S(2)}, u32[]{:S(2)}) collective-permute-start(f32[4,256,512]{2,1,0:T(8,128)S(1)} %get-tuple-element.29), channel_id=1, source_target_pairs={{16,0},{17,1},{18,2},{19,3},{20,4},{21,5},{22,6},{23,7},{24,8},{25... | collective-permute-start | bytes 6291464 | tf_op jit(solution)/shard_map/ppermute | solution.py:38
  36.7 29.0 %collective-permute-start.10 = (bf16[2,512,512]{2,1,0:T(8,128)(2,1)}, bf16[2,512,512]{2,1,0:T(8,128)(2,1)S(1)}, u32[]{:S(2)}, u32[]{:S(2)}) collective-permute-start(bf16[2,512,512]{2,1,0:T(8,128)(2,1)} %collective-permute-done.refs_1_), channel_id=1, source_target_pairs={{8,0},{9,1},{10,2},{11,3},{12,4},{13,5},{14,6},{15,7},{0,8},{1,9},... | collective-permute-start | bytes 3145736 | tf_op jit(solution)/shard_map/ppermute | solution.py:38
  39.1 26.6 %collective-permute-start.8 = (bf16[2,512,512]{2,1,0:T(8,128)(2,1)}, bf16[2,512,512]{2,1,0:T(8,128)(2,1)}, u32[]{:S(2)}, u32[]{:S(2)}) collective-permute-start(bf16[2,512,512]{2,1,0:T(8,128)(2,1)} %collective-permute-done.refs_1_), channel_id=1, source_target_pairs={{1,0},{2,1},{3,2},{4,3},{5,4},{6,5},{7,6},{0,7},{9,8},{10,9},{11,1... | collective-permute-start | bytes 3145736 | tf_op jit(solution)/shard_map/ppermute | solution.py:38
  42.1 26.1 %collective-permute-start.9 = (bf16[2,512,512]{2,1,0:T(8,128)(2,1)S(1)}, bf16[2,512,512]{2,1,0:T(8,128)(2,1)S(1)}, u32[]{:S(2)}, u32[]{:S(2)}) collective-permute-start(bf16[2,512,512]{2,1,0:T(8,128)(2,1)S(1)} %collective-permute-done.1.refs_2_.refs_1_), channel_id=1, source_target_pairs={{7,0},{0,1},{1,2},{2,3},{3,4},{4,5},{5,6},{6,7},{15,8},{8,9},{9,10... | collective-permute-start | bytes 3145736 | tf_op jit(solution)/shard_map/ppermute | solution.py:38
  42.1 8.2 %collective-permute-start.4 = (f32[128,512]{1,0:T(8,128)S(1)}, f32[128,512]{1,0:T(8,128)S(1)}, u32[]{:S(2)}, u32[]{:S(2)}) collective-permute-start(f32[128,512]{1,0:T(8,128)S(1)} %get-tuple-element.48), channel_id=1, source_target_pairs={{96,0},{97,1},{98,2},{99,3},{100,4},{101,5},{102,6},{103,7},{104,8... | collective-permute-start | bytes 786440 | tf_op jit(solution)/shard_map/ppermute | solution.py:38
  43.7 8.0 %collective-permute-start.6 = (f32[128,512]{1,0:T(8,128)S(1)}, f32[128,512]{1,0:T(8,128)S(1)}, u32[]{:S(2)}, u32[]{:S(2)}) collective-permute-start(f32[128,512]{1,0:T(8,128)S(1)} %get-tuple-element.49), channel_id=1, source_target_pairs={{32,0},{33,1},{34,2},{35,3},{36,4},{37,5},{38,6},{39,7},{40,8},{41... | collective-permute-start | bytes 786440 | tf_op jit(solution)/shard_map/ppermute | solution.py:38
  50.4 13.0 %collective-permute-start.5 = (f32[256,512]{1,0:T(8,128)S(1)}, f32[256,512]{1,0:T(8,128)S(1)}, u32[]{:S(2)}, u32[]{:S(2)}) collective-permute-start(f32[256,512]{1,0:T(8,128)S(1)} %pad_maximum_fusion.1), channel_id=1, source_target_pairs={{96,0},{97,1},{98,2},{99,3},{100,4},{101,5},{102,6},{103,7},{104,8... | collective-permute-start | bytes 1572872 | tf_op jit(solution)/shard_map/ppermute | solution.py:38
  51.7 12.9 %collective-permute-start.7 = (f32[256,512]{1,0:T(8,128)S(1)}, f32[256,512]{1,0:T(8,128)S(1)}, u32[]{:S(2)}, u32[]{:S(2)}) collective-permute-start(f32[256,512]{1,0:T(8,128)S(1)} %pad_maximum_fusion.2), channel_id=1, source_target_pairs={{32,0},{33,1},{34,2},{35,3},{36,4},{37,5},{38,6},{39,7},{40,8},{41... | collective-permute-start | bytes 1572872 | tf_op jit(solution)/shard_map/ppermute | solution.py:38
  72.6 4.2 %collective-permute-start.11 = (f32[4,256,512]{2,1,0:T(8,128)S(1)}, f32[4,256,512]{2,1,0:T(8,128)S(1)}, u32[]{:S(2)}, u32[]{:S(2)}) collective-permute-start(f32[4,256,512]{2,1,0:T(8,128)S(1)} %get-tuple-element.35), channel_id=1, source_target_pairs={{16,0},{17,1},{18,2},{19,3},{20,4},{21,5},{22,6},{23,7},{24,8},{25... | collective-permute-start | bytes 6291464 | tf_op jit(solution)/shard_map/ppermute | solution.py:38
  72.7 33.4 %collective-permute-start.16 = (bf16[2,512,512]{2,1,0:T(8,128)(2,1)}, bf16[2,512,512]{2,1,0:T(8,128)(2,1)S(1)}, u32[]{:S(2)}, u32[]{:S(2)}) collective-permute-start(bf16[2,512,512]{2,1,0:T(8,128)(2,1)} %collective-permute-done.8.refs_2_), channel_id=1, source_target_pairs={{8,0},{9,1},{10,2},{11,3},{12,4},{13,5},{14,6},{15,7},{0,8},{1,9},... | collective-permute-start | bytes 3145736 | tf_op jit(solution)/shard_map/ppermute | solution.py:38
  77.0 8.4 %collective-permute-start.13 = (f32[128,512]{1,0:T(8,128)S(1)}, f32[128,512]{1,0:T(8,128)S(1)}, u32[]{:S(2)}, u32[]{:S(2)}) collective-permute-start(f32[128,512]{1,0:T(8,128)S(1)} %get-tuple-element.46), channel_id=1, source_target_pairs={{32,0},{33,1},{34,2},{35,3},{36,4},{37,5},{38,6},{39,7},{40,8},{41... | collective-permute-start | bytes 786440 | tf_op jit(solution)/shard_map/ppermute | solution.py:38
  77.9 8.1 %collective-permute-start.12 = (f32[128,512]{1,0:T(8,128)S(1)}, f32[128,512]{1,0:T(8,128)S(1)}, u32[]{:S(2)}, u32[]{:S(2)}) collective-permute-start(f32[128,512]{1,0:T(8,128)S(1)} %get-tuple-element.47), channel_id=1, source_target_pairs={{96,0},{97,1},{98,2},{99,3},{100,4},{101,5},{102,6},{103,7},{104,8... | collective-permute-start | bytes 786440 | tf_op jit(solution)/shard_map/ppermute | solution.py:38
  87.8 13.3 %collective-permute-start.14 = (f32[256,512]{1,0:T(8,128)}, f32[256,512]{1,0:T(8,128)}, u32[]{:S(2)}, u32[]{:S(2)}) collective-permute-start(f32[256,512]{1,0:T(8,128)} %pad_maximum_fusion.3), channel_id=1, source_target_pairs={{96,0},{97,1},{98,2},{99,3},{100,4},{101,5},{102,6},{103,7},{104,8... | collective-permute-start | bytes 1572872 | tf_op jit(solution)/shard_map/ppermute | solution.py:38
  89.5 14.5 %collective-permute-start.15 = (f32[256,512]{1,0:T(8,128)}, f32[256,512]{1,0:T(8,128)}, u32[]{:S(2)}, u32[]{:S(2)}) collective-permute-start(f32[256,512]{1,0:T(8,128)} %pad_maximum_fusion.4), channel_id=1, source_target_pairs={{32,0},{33,1},{34,2},{35,3},{36,4},{37,5},{38,6},{39,7},{40,8},{41... | collective-permute-start | bytes 1572872 | tf_op jit(solution)/shard_map/ppermute | solution.py:38
  90.5 19.4 %copy-start.1 = (f32[256,512]{1,0:T(8,128)S(1)}, f32[256,512]{1,0:T(8,128)}, u32[]{:S(2)}) copy-start(f32[256,512]{1,0:T(8,128)} %fusion.3) | copy-start | bytes 1572868
  107.2 18.4 %copy-start.2 = (f32[256,512]{1,0:T(8,128)S(1)}, f32[256,512]{1,0:T(8,128)}, u32[]{:S(2)}) copy-start(f32[256,512]{1,0:T(8,128)} %add_add_fusion.3) | copy-start | bytes 1572868
  107.2 6.0 %collective-permute-start.18 = (f32[256,512]{1,0:T(8,128)S(1)}, f32[256,512]{1,0:T(8,128)S(1)}, u32[]{:S(2)}, u32[]{:S(2)}) collective-permute-start(f32[256,512]{1,0:T(8,128)S(1)} %bitcast.49), channel_id=1, source_target_pairs={{48,32},{80,64},{112,96},{16,0},{176,160},{208,192},{240,224},{144... | collective-permute-start | bytes 1572872 | tf_op jit(solution)/shard_map/ppermute | solution.py:38
  110.7 14.9 %collective-permute-start.17 = (f32[256,512]{1,0:T(8,128)S(1)}, f32[256,512]{1,0:T(8,128)S(1)}, u32[]{:S(2)}, u32[]{:S(2)}) collective-permute-start(f32[256,512]{1,0:T(8,128)S(1)} %broadcast_select_fusion), channel_id=1, source_target_pairs={{128,0},{129,1},{130,2},{131,3},{132,4},{133,5},{134,6},{135,7},{1... | collective-permute-start | bytes 1572872 | tf_op jit(solution)/shard_map/ppermute | solution.py:38
  113.3 13.1 %collective-permute-start.19 = (f32[256,512]{1,0:T(8,128)S(1)}, f32[256,512]{1,0:T(8,128)S(1)}, u32[]{:S(2)}, u32[]{:S(2)}) collective-permute-start(f32[256,512]{1,0:T(8,128)S(1)} %bitcast_add_fusion), channel_id=1, source_target_pairs={{2,66},{14,78},{19,83},{31,95},{36,100},{40,104},{53,117},{57,121}... | collective-permute-start | bytes 1572872 | tf_op jit(solution)/shard_map/ppermute | solution.py:38
  114.0 13.6 %collective-permute-start.20 = (f32[256,512]{1,0:T(8,128)S(1)}, f32[256,512]{1,0:T(8,128)S(1)}, u32[]{:S(2)}, u32[]{:S(2)}) collective-permute-start(f32[256,512]{1,0:T(8,128)S(1)} %bitcast_add_fusion), channel_id=1, source_target_pairs={{4,100},{8,104},{21,117},{25,121},{38,6},{42,10},{55,23},{59,27},{... | collective-permute-start | bytes 1572872 | tf_op jit(solution)/shard_map/ppermute | solution.py:38
  115.3 12.3 %collective-permute-start.21 = (f32[256,512]{1,0:T(8,128)S(1)}, f32[256,512]{1,0:T(8,128)S(1)}, u32[]{:S(2)}, u32[]{:S(2)}) collective-permute-start(f32[256,512]{1,0:T(8,128)S(1)} %bitcast_add_fusion), channel_id=1, source_target_pairs={{0,32},{12,44},{17,49},{29,61},{34,66},{46,78},{51,83},{63,95},{68... | collective-permute-start | bytes 1572872 | tf_op jit(solution)/shard_map/ppermute | solution.py:38
  127.8 13.4 %collective-permute-start.22 = (f32[256,512]{1,0:T(8,128)S(1)}, f32[256,512]{1,0:T(8,128)S(1)}, u32[]{:S(2)}, u32[]{:S(2)}) collective-permute-start(f32[256,512]{1,0:T(8,128)S(1)} %select_add_fusion), channel_id=1, source_target_pairs={{0,16},{128,151},{160,128},{176,0},{64,113},{192,150},{96,135},{22... | collective-permute-start | bytes 1572872 | tf_op jit(solution)/shard_map/ppermute | solution.py:38
  130.8 18.8 %collective-permute-start.23 = (f32[256,512]{1,0:T(8,128)S(1)}, f32[256,512]{1,0:T(8,128)S(1)}, u32[]{:S(2)}, u32[]{:S(2)}) collective-permute-start(f32[256,512]{1,0:T(8,128)S(1)} %add_add_fusion.2), channel_id=1, source_target_pairs={{32,166},{49,183},{66,192},{83,209},{100,226},{117,243},{6,132},{2... | collective-permute-start | bytes 1572872 | tf_op jit(solution)/shard_map/ppermute | solution.py:38
  132.1 18.0 %collective-permute-start.24 = (f32[256,512]{1,0:T(8,128)S(1)}, f32[256,512]{1,0:T(8,128)S(1)}, u32[]{:S(2)}, u32[]{:S(2)}) collective-permute-start(f32[256,512]{1,0:T(8,128)S(1)} %add_add_fusion.2), channel_id=1, source_target_pairs={{160,166},{177,183},{194,192},{211,209},{228,226},{245,243},{134,1... | collective-permute-start | bytes 1572872 | tf_op jit(solution)/shard_map/ppermute | solution.py:38
  133.4 16.8 %collective-permute-start.25 = (f32[256,512]{1,0:T(8,128)S(1)}, f32[256,512]{1,0:T(8,128)S(1)}, u32[]{:S(2)}, u32[]{:S(2)}) collective-permute-start(f32[256,512]{1,0:T(8,128)S(1)} %select_add_fusion), channel_id=1, source_target_pairs={{144,16},{16,150},{32,98},{48,0},{80,135},{208,114},{112,113},{240... | collective-permute-start | bytes 1572872 | tf_op jit(solution)/shard_map/ppermute | solution.py:38
  134.1 28.3 %collective-permute-start.26 = (f32[256,512]{1,0:T(8,128)S(1)}, f32[256,512]{1,0:T(8,128)S(1)}, u32[]{:S(2)}, u32[]{:S(2)}) collective-permute-start(f32[256,512]{1,0:T(8,128)S(1)} %add_add_fusion.2), channel_id=1, source_target_pairs={{104,226},{121,243},{10,132},{27,149},{44,166},{61,183},{78,192},{... | collective-permute-start | bytes 1572872 | tf_op jit(solution)/shard_map/ppermute | solution.py:38
  141.2 21.2 %collective-permute-start.27 = (f32[256,512]{1,0:T(8,128)S(1)}, f32[256,512]{1,0:T(8,128)S(1)}, u32[]{:S(2)}, u32[]{:S(2)}) collective-permute-start(f32[256,512]{1,0:T(8,128)S(1)} %add_add_fusion.2), channel_id=1, source_target_pairs={{232,226},{249,243},{138,132},{155,149},{172,166},{189,183},{206,1... | collective-permute-start | bytes 1572872 | tf_op jit(solution)/shard_map/ppermute | solution.py:38

commit v10 on v9

--- a/solution.py
+++ b/solution.py
@@ -168,7 +168,8 @@
     table_c = np.zeros((GROUPS, 4), np.int32)
     target_c = {}
     final = {half: [] for half in (0, 1)}
-    final_c = {(y, half): [] for y in (0, 1) for half in (0, 1)}
+    final_c = {half: [] for half in (0, 1)}
+    halves = np.zeros((16, GROUPS), np.int32)
     first = np.zeros((16, GROUPS), np.bool_)
     units, at, planes = spread()
     for h in range(2):
@@ -181,6 +182,7 @@
                     y = 1 - planes[own][place] if batch else planes[own][place]
                     final[half].append((device(y, x, core, own), col * GROUPS + row))
                     first[(y * NX + x) * 2 + core, own] = not batch
+                    halves[(y * NX + x) * 2 + core, own] = half
                     for aux in range(16):
                         entry, offset = tables[batch, aux, own, pair], (x - aux // 2) % NX
                         kept = aux % 2 == core
@@ -192,10 +194,15 @@
                             entry[1:] = offset, kept, half
             (((_, swap, _), row, col, half),) = units_of(PAIRS_C, h, z)
             table_c[own] = swap, 0, 1, half
-            target_c[own] = (1 - h, col // 2 % NX, col % 2)
-            for y in (0, 1):
-                final_c[y, half].append((device(y, *target_c[own][1:], own), col * GROUPS + row))
-    return tables.reshape(2, 16 * GROUPS, 20), table_c, target_c, first, final, final_c
+            y, x, core = min(
+                ((y, x, core) for y in (0, 1) for x in range(NX) for core in (0, 1)
+                 if halves[(y * NX + x) * 2 + core, own] != half),
+                key=lambda place: (min((place[1] - col // 2) % NX, (col // 2 - place[1]) % NX), place),
+            )
+            target_c[own] = (y, x, core)
+            final[half].append((device(y, x, core, own), col * GROUPS + row))
+            final_c[half].append((device(1 - y, x, core, own), col * GROUPS + row))
+    return tables.reshape(2, 16 * GROUPS, 20), table_c, target_c, first, halves, final, final_c
 
 
 def dot_t(a, b):
@@ -309,7 +316,7 @@
 
 
 def per_device(half_b):
-    local, codes_c, target_c, first, final, final_c = plan()
+    local, codes_c, target_c, first, halves, final, final_c = plan()
     aux, blk = lax.axis_index("aux"), lax.axis_index("blk")
     place = aux * GROUPS + blk
     table_a, table_b = jnp.asarray(local[0])[place], jnp.asarray(local[1])[place]
@@ -343,8 +350,9 @@
     part_c = one_x(one_core(part_c[0], target_c), target_c)
     done, part_c = together(done, part_c)
 
-    top = send(done, final[0]) + send(part_c, final_c[0, 0]) + send(part_c, final_c[1, 0])
-    bottom = send(done, final[1]) + send(part_c, final_c[0, 1]) + send(part_c, final_c[1, 1])
+    own_half = jnp.asarray(halves)[aux, blk]
+    top = send(jnp.where(own_half == 0, done, part_c), final[0]) + send(part_c, final_c[0])
+    bottom = send(jnp.where(own_half == 1, done, part_c), final[1]) + send(part_c, final_c[1])
     return jnp.concatenate([top, bottom], 0)
 
 

time: 167 us -> 163 us (0.976); the launches traced: 164 us -> 162 us
  waiting for transfers between devices: 101 us -> 98.1 us
    ppermute x28 -> x26, waiting for transfers between devices: 101 us -> 98.1 us  [send(): return lax.ppermute(value, ALL, pairs)]
    ppermute x28 -> x26, starting transfers between devices: 39.2 us -> 38.3 us  [send(): return lax.ppermute(value, ALL, pairs)]
  transfers between devices with their start and end apart: 28 -> 26, of which waited for: 18 -> 17; matrix products, arithmetic and copies ran while one was open for 6% -> 7% of each run, Pallas kernels for 0% -> 0%
where the time goes in v10:
time: 163 us; the launch traced here: 162 us
  waiting for transfers between devices  98.1 us (60%)
  starting transfers between devices  38.3 us (23%)
  Pallas kernels  9.91 us (6%)
  other arithmetic  8.93 us (5%)
  local copies, waits for them, and re-layouts  5.37 us (3%)
    ppermute x26, waiting for transfers between devices, send(): return lax.ppermute(value, ALL, pairs)  98.1 us
    ppermute x26, starting transfers between devices, send(): return lax.ppermute(value, ALL, pairs)  38.3 us
    pallas_call x3, Pallas kernels, products(): pl.pallas_call(functools.partial(units_kernel, pairs, index_pairs, len(co...  9.84 us
  transfers between devices with their start and end apart: 26, of which 17 were waited for; matrix products, arithmetic and copies ran while one was open for 7% of the time, Pallas kernels for 0%

profile of v10, /device:TPU:12, one launch (start us, length us, event | category | flops | bytes accessed | tf_op | source)
XLA Modules:
  0.0 162.2 jit_solution(15631860197603902530)
XLA Ops:
  0.0 5.9 %collective-permute-start = (bf16[2,512,512]{2,1,0:T(8,128)(2,1)}, bf16[2,512,512]{2,1,0:T(8,128)(2,1)}, u32[]{:S(2)}, u32[]{:S(2)}) collective-permute-start(bf16[2,512,512]{2,1,0:T(8,128)(2,1)} %source.1), channel_id=1, source_target_pairs={{1,0},{2,1},{3,2},{4,3},{5,4},{6,5},{7,6},{0,7},{9,8},{10,9},{11,1... | collective-permute-start | bytes 3145736 | tf_op jit(solution)/shard_map/ppermute | solution.py:38
  5.9 2.3 %collective-permute-start.2 = (bf16[2,512,512]{2,1,0:T(8,128)(2,1)}, bf16[2,512,512]{2,1,0:T(8,128)(2,1)S(1)}, u32[]{:S(2)}, u32[]{:S(2)}) collective-permute-start(bf16[2,512,512]{2,1,0:T(8,128)(2,1)} %source.1), channel_id=1, source_target_pairs={{8,0},{9,1},{10,2},{11,3},{12,4},{13,5},{14,6},{15,7},{0,8},{1,9},... | collective-permute-start | bytes 3145736 | tf_op jit(solution)/shard_map/ppermute | solution.py:38
  10.2 18.4 %collective-permute-done.refs_1_ = bf16[2,512,512]{2,1,0:T(8,128)(2,1)} collective-permute-done((bf16[2,512,512]{2,1,0:T(8,128)(2,1)}, bf16[2,512,512]{2,1,0:T(8,128)(2,1)}, u32[]{:S(2)}, u32[]{:S(2)}) %collective-permute-start) | collective-permute-done | bytes 1048608 | tf_op jit(solution)/shard_map/ppermute | solution.py:38
  28.6 3.3 %collective-permute-done.1.refs_2_.refs_1_ = bf16[2,512,512]{2,1,0:T(8,128)(2,1)S(1)} collective-permute-done((bf16[2,512,512]{2,1,0:T(8,128)(2,1)}, bf16[2,512,512]{2,1,0:T(8,128)(2,1)S(1)}, u32[]{:S(2)}, u32[]{:S(2)}) %collective-permute-start.1) | collective-permute-done | bytes 1048608 | tf_op jit(solution)/shard_map/ppermute | solution.py:38
  32.2 4.4 %shard_map.65 = (f32[4,256,512]{2,1,0:T(8,128)S(1)}, f32[4,256,512]{2,1,0:T(8,128)S(1)}) custom-call(s32[20]{0:T(128)S(1)} %get-tuple-element.54.table, bf16[2,512,512]{2,1,0:T(8,128)(2,1)S(1)} %shard_map.64.refs_0_, bf16[2,512,512]{2,1,0:T(8,128)(2,1)} %collective-permute-done.refs_1_, bf16[2,512,512]{2,1,0:T(8,128)(2,1)S(1)} %collective-permute-done.1.refs_2_.refs_1_, ...), custom_call_target="tpu_custom_call" | custom-call | tf_op jit(solution)/shard_map/pallas_call | solution.py:243
  36.7 2.4 %collective-permute-start.10 = (bf16[2,512,512]{2,1,0:T(8,128)(2,1)}, bf16[2,512,512]{2,1,0:T(8,128)(2,1)S(1)}, u32[]{:S(2)}, u32[]{:S(2)}) collective-permute-start(bf16[2,512,512]{2,1,0:T(8,128)(2,1)} %collective-permute-done.refs_1_), channel_id=1, source_target_pairs={{8,0},{9,1},{10,2},{11,3},{12,4},{13,5},{14,6},{15,7},{0,8},{1,9},... | collective-permute-start | bytes 3145736 | tf_op jit(solution)/shard_map/ppermute | solution.py:38
  39.1 2.9 %collective-permute-start.8 = (bf16[2,512,512]{2,1,0:T(8,128)(2,1)}, bf16[2,512,512]{2,1,0:T(8,128)(2,1)}, u32[]{:S(2)}, u32[]{:S(2)}) collective-permute-start(bf16[2,512,512]{2,1,0:T(8,128)(2,1)} %collective-permute-done.refs_1_), channel_id=1, source_target_pairs={{1,0},{2,1},{3,2},{4,3},{5,4},{6,5},{7,6},{0,7},{9,8},{10,9},{11,1... | collective-permute-start | bytes 3145736 | tf_op jit(solution)/shard_map/ppermute | solution.py:38
  44.6 5.7 %collective-permute-done.4 = f32[128,512]{1,0:T(8,128)S(1)} collective-permute-done((f32[128,512]{1,0:T(8,128)S(1)}, f32[128,512]{1,0:T(8,128)S(1)}, u32[]{:S(2)}, u32[]{:S(2)}) %collective-permute-start.4) | collective-permute-done | bytes 262176 | tf_op jit(solution)/shard_map/ppermute | solution.py:38
  52.8 10.6 %collective-permute-done.5 = f32[256,512]{1,0:T(8,128)S(1)} collective-permute-done((f32[256,512]{1,0:T(8,128)S(1)}, f32[256,512]{1,0:T(8,128)S(1)}, u32[]{:S(2)}, u32[]{:S(2)}) %collective-permute-start.5) | collective-permute-done | bytes 524320 | tf_op jit(solution)/shard_map/ppermute | solution.py:38
  65.7 2.5 %collective-permute-done.9.refs_3_.refs_0_ = bf16[2,512,512]{2,1,0:T(8,128)(2,1)S(1)} collective-permute-done((bf16[2,512,512]{2,1,0:T(8,128)(2,1)S(1)}, bf16[2,512,512]{2,1,0:T(8,128)(2,1)S(1)}, u32[]{:S(2)}, u32[]{:S(2)}) %collective-permute-start.9) | collective-permute-done | bytes 1048608 | tf_op jit(solution)/shard_map/ppermute | solution.py:38
  68.2 4.4 %shard_map.66 = (f32[4,256,512]{2,1,0:T(8,128)S(1)}, f32[4,256,512]{2,1,0:T(8,128)S(1)}) custom-call(s32[20]{0:T(128)S(1)} %get-tuple-element.55.table, bf16[2,512,512]{2,1,0:T(8,128)(2,1)S(1)} %shard_map.64.refs_0_, bf16[2,512,512]{2,1,0:T(8,128)(2,1)S(1)} %collective-permute-done.1.refs_2_.refs_1_, bf16[2,512,512]{2,1,0:T(8,128)(2,1)} %collective-permute-done.8.refs_2_, ...), custom_call_target="tpu_custom_call" | custom-call | tf_op jit(solution)/shard_map/pallas_call | solution.py:243
  72.7 1.3 collective-permute-start.16
  74.0 2.8 %collective-permute-done.11 = f32[4,256,512]{2,1,0:T(8,128)S(1)} collective-permute-done((f32[4,256,512]{2,1,0:T(8,128)S(1)}, f32[4,256,512]{2,1,0:T(8,128)S(1)}, u32[]{:S(2)}, u32[]{:S(2)}) %collective-permute-start.11) | collective-permute-done | bytes 2097184 | tf_op jit(solution)/shard_map/ppermute | solution.py:38
  77.9 1.6 collective-permute-start.12
  79.5 5.8 %collective-permute-done.13 = f32[128,512]{1,0:T(8,128)S(1)} collective-permute-done((f32[128,512]{1,0:T(8,128)S(1)}, f32[128,512]{1,0:T(8,128)S(1)}, u32[]{:S(2)}, u32[]{:S(2)}) %collective-permute-start.13) | collective-permute-done | bytes 262176 | tf_op jit(solution)/shard_map/ppermute | solution.py:38
  87.8 1.8 %collective-permute-start.14 = (f32[256,512]{1,0:T(8,128)}, f32[256,512]{1,0:T(8,128)}, u32[]{:S(2)}, u32[]{:S(2)}) collective-permute-start(f32[256,512]{1,0:T(8,128)} %pad_maximum_fusion.3), channel_id=1, source_target_pairs={{96,0},{97,1},{98,2},{99,3},{100,4},{101,5},{102,6},{103,7},{104,8... | collective-permute-start | bytes 1572872 | tf_op jit(solution)/shard_map/ppermute | solution.py:38
  90.5 10.5 %collective-permute-done.14 = f32[256,512]{1,0:T(8,128)} collective-permute-done((f32[256,512]{1,0:T(8,128)}, f32[256,512]{1,0:T(8,128)}, u32[]{:S(2)}, u32[]{:S(2)}) %collective-permute-start.14) | collective-permute-done | bytes 524320 | tf_op jit(solution)/shard_map/ppermute | solution.py:38
  101.1 3.0 %collective-permute-done.15 = f32[256,512]{1,0:T(8,128)} collective-permute-done((f32[256,512]{1,0:T(8,128)}, f32[256,512]{1,0:T(8,128)}, u32[]{:S(2)}, u32[]{:S(2)}) %collective-permute-start.15) | collective-permute-done | bytes 524320 | tf_op jit(solution)/shard_map/ppermute | solution.py:38
  104.0 2.1 %add_add_fusion.1 = f32[256,512]{1,0:T(8,128)} fusion(f32[256,512]{1,0:T(8,128)} %collective-permute-done.15, f32[256,512]{1,0:T(8,128)S(1)} %get-tuple-element.36, f32[256,512]{1,0:T(8,128)} %collective-permute-done.14), kind=kLoop, calls=%fused_computation.17 | loop fusion | flops 262144 | bytes 2097152 | tf_op jit(solution)/shard_map/add | solution.py:344
  107.2 1.4 collective-permute-start.18
  108.6 1.3 dynamic_slice.16
  110.7 2.5 %collective-permute-start.17 = (f32[256,512]{1,0:T(8,128)S(1)}, f32[256,512]{1,0:T(8,128)S(1)}, u32[]{:S(2)}, u32[]{:S(2)}) collective-permute-start(f32[256,512]{1,0:T(8,128)S(1)} %broadcast_select_fusion.1), channel_id=1, source_target_pairs={{128,0},{129,1},{130,2},{131,3},{132,4},{133,5},{134,6},{135,7},{1... | collective-permute-start | bytes 1572872 | tf_op jit(solution)/shard_map/ppermute | solution.py:38
  114.0 1.3 collective-permute-start.20
  116.0 1.3 dynamic_slice.15
  118.5 7.0 %collective-permute-done.17 = f32[256,512]{1,0:T(8,128)S(1)} collective-permute-done((f32[256,512]{1,0:T(8,128)S(1)}, f32[256,512]{1,0:T(8,128)S(1)}, u32[]{:S(2)}, u32[]{:S(2)}) %collective-permute-start.17) | collective-permute-done | bytes 524320 | tf_op jit(solution)/shard_map/ppermute | solution.py:38
  127.9 4.1 %collective-permute-start.22 = (f32[256,512]{1,0:T(8,128)S(1)}, f32[256,512]{1,0:T(8,128)S(1)}, u32[]{:S(2)}, u32[]{:S(2)}) collective-permute-start(f32[256,512]{1,0:T(8,128)S(1)} %get-tuple-element.52), channel_id=1, source_target_pairs={{0,16},{128,151},{160,128},{176,0},{64,113},{192,150},{96,135},{22... | collective-permute-start | bytes 1572872 | tf_op jit(solution)/shard_map/ppermute | solution.py:38
  132.0 1.3 collective-permute-start.23
  133.3 1.3 collective-permute-start.24
  134.6 1.3 collective-permute-start.25
  135.9 8.8 %collective-permute-done.22 = f32[256,512]{1,0:T(8,128)S(1)} collective-permute-done((f32[256,512]{1,0:T(8,128)S(1)}, f32[256,512]{1,0:T(8,128)S(1)}, u32[]{:S(2)}, u32[]{:S(2)}) %collective-permute-start.22) | collective-permute-done | bytes 524320 | tf_op jit(solution)/shard_map/ppermute | solution.py:38
  144.7 1.9 %collective-permute-done.23 = f32[256,512]{1,0:T(8,128)S(1)} collective-permute-done((f32[256,512]{1,0:T(8,128)S(1)}, f32[256,512]{1,0:T(8,128)S(1)}, u32[]{:S(2)}, u32[]{:S(2)}) %collective-permute-start.23) | collective-permute-done | bytes 524320 | tf_op jit(solution)/shard_map/ppermute | solution.py:38
  146.7 14.4 %collective-permute-done.24 = f32[256,512]{1,0:T(8,128)S(1)} collective-permute-done((f32[256,512]{1,0:T(8,128)S(1)}, f32[256,512]{1,0:T(8,128)S(1)}, u32[]{:S(2)}, u32[]{:S(2)}) %collective-permute-start.24) | collective-permute-done | bytes 524320 | tf_op jit(solution)/shard_map/ppermute | solution.py:38
  (60 shorter events, 21.0 us)
Async XLA Ops:
  0.0 28.6 %collective-permute-start = (bf16[2,512,512]{2,1,0:T(8,128)(2,1)}, bf16[2,512,512]{2,1,0:T(8,128)(2,1)}, u32[]{:S(2)}, u32[]{:S(2)}) collective-permute-start(bf16[2,512,512]{2,1,0:T(8,128)(2,1)} %source.1), channel_id=1, source_target_pairs={{1,0},{2,1},{3,2},{4,3},{5,4},{6,5},{7,6},{0,7},{9,8},{10,9},{11,1... | collective-permute-start | bytes 3145736 | tf_op jit(solution)/shard_map/ppermute | solution.py:38
  5.9 26.0 %collective-permute-start.1 = (bf16[2,512,512]{2,1,0:T(8,128)(2,1)}, bf16[2,512,512]{2,1,0:T(8,128)(2,1)S(1)}, u32[]{:S(2)}, u32[]{:S(2)}) collective-permute-start(bf16[2,512,512]{2,1,0:T(8,128)(2,1)} %source.1), channel_id=1, source_target_pairs={{7,0},{0,1},{1,2},{2,3},{3,4},{4,5},{5,6},{6,7},{15,8},{8,9},{9,10... | collective-permute-start | bytes 3145736 | tf_op jit(solution)/shard_map/ppermute | solution.py:38
  5.9 26.3 %collective-permute-start.2 = (bf16[2,512,512]{2,1,0:T(8,128)(2,1)}, bf16[2,512,512]{2,1,0:T(8,128)(2,1)S(1)}, u32[]{:S(2)}, u32[]{:S(2)}) collective-permute-start(bf16[2,512,512]{2,1,0:T(8,128)(2,1)} %source.1), channel_id=1, source_target_pairs={{8,0},{9,1},{10,2},{11,3},{12,4},{13,5},{14,6},{15,7},{0,8},{1,9},... | collective-permute-start | bytes 3145736 | tf_op jit(solution)/shard_map/ppermute | solution.py:38
  8.2 1.3 copy-start
  36.6 5.4 %collective-permute-start.3 = (f32[4,256,512]{2,1,0:T(8,128)S(1)}, f32[4,256,512]{2,1,0:T(8,128)S(1)}, u32[]{:S(2)}, u32[]{:S(2)}) collective-permute-start(f32[4,256,512]{2,1,0:T(8,128)S(1)} %get-tuple-element.29), channel_id=1, source_target_pairs={{16,0},{17,1},{18,2},{19,3},{20,4},{21,5},{22,6},{23,7},{24,8},{25... | collective-permute-start | bytes 6291464 | tf_op jit(solution)/shard_map/ppermute | solution.py:38
  36.7 29.0 %collective-permute-start.10 = (bf16[2,512,512]{2,1,0:T(8,128)(2,1)}, bf16[2,512,512]{2,1,0:T(8,128)(2,1)S(1)}, u32[]{:S(2)}, u32[]{:S(2)}) collective-permute-start(bf16[2,512,512]{2,1,0:T(8,128)(2,1)} %collective-permute-done.refs_1_), channel_id=1, source_target_pairs={{8,0},{9,1},{10,2},{11,3},{12,4},{13,5},{14,6},{15,7},{0,8},{1,9},... | collective-permute-start | bytes 3145736 | tf_op jit(solution)/shard_map/ppermute | solution.py:38
  39.1 26.6 %collective-permute-start.8 = (bf16[2,512,512]{2,1,0:T(8,128)(2,1)}, bf16[2,512,512]{2,1,0:T(8,128)(2,1)}, u32[]{:S(2)}, u32[]{:S(2)}) collective-permute-start(bf16[2,512,512]{2,1,0:T(8,128)(2,1)} %collective-permute-done.refs_1_), channel_id=1, source_target_pairs={{1,0},{2,1},{3,2},{4,3},{5,4},{6,5},{7,6},{0,7},{9,8},{10,9},{11,1... | collective-permute-start | bytes 3145736 | tf_op jit(solution)/shard_map/ppermute | solution.py:38
  42.1 26.1 %collective-permute-start.9 = (bf16[2,512,512]{2,1,0:T(8,128)(2,1)S(1)}, bf16[2,512,512]{2,1,0:T(8,128)(2,1)S(1)}, u32[]{:S(2)}, u32[]{:S(2)}) collective-permute-start(bf16[2,512,512]{2,1,0:T(8,128)(2,1)S(1)} %collective-permute-done.1.refs_2_.refs_1_), channel_id=1, source_target_pairs={{7,0},{0,1},{1,2},{2,3},{3,4},{4,5},{5,6},{6,7},{15,8},{8,9},{9,10... | collective-permute-start | bytes 3145736 | tf_op jit(solution)/shard_map/ppermute | solution.py:38
  42.1 8.2 %collective-permute-start.4 = (f32[128,512]{1,0:T(8,128)S(1)}, f32[128,512]{1,0:T(8,128)S(1)}, u32[]{:S(2)}, u32[]{:S(2)}) collective-permute-start(f32[128,512]{1,0:T(8,128)S(1)} %get-tuple-element.48), channel_id=1, source_target_pairs={{96,0},{97,1},{98,2},{99,3},{100,4},{101,5},{102,6},{103,7},{104,8... | collective-permute-start | bytes 786440 | tf_op jit(solution)/shard_map/ppermute | solution.py:38
  43.7 8.0 %collective-permute-start.6 = (f32[128,512]{1,0:T(8,128)S(1)}, f32[128,512]{1,0:T(8,128)S(1)}, u32[]{:S(2)}, u32[]{:S(2)}) collective-permute-start(f32[128,512]{1,0:T(8,128)S(1)} %get-tuple-element.49), channel_id=1, source_target_pairs={{32,0},{33,1},{34,2},{35,3},{36,4},{37,5},{38,6},{39,7},{40,8},{41... | collective-permute-start | bytes 786440 | tf_op jit(solution)/shard_map/ppermute | solution.py:38
  50.4 13.0 %collective-permute-start.5 = (f32[256,512]{1,0:T(8,128)S(1)}, f32[256,512]{1,0:T(8,128)S(1)}, u32[]{:S(2)}, u32[]{:S(2)}) collective-permute-start(f32[256,512]{1,0:T(8,128)S(1)} %pad_maximum_fusion.1), channel_id=1, source_target_pairs={{96,0},{97,1},{98,2},{99,3},{100,4},{101,5},{102,6},{103,7},{104,8... | collective-permute-start | bytes 1572872 | tf_op jit(solution)/shard_map/ppermute | solution.py:38
  51.7 12.9 %collective-permute-start.7 = (f32[256,512]{1,0:T(8,128)S(1)}, f32[256,512]{1,0:T(8,128)S(1)}, u32[]{:S(2)}, u32[]{:S(2)}) collective-permute-start(f32[256,512]{1,0:T(8,128)S(1)} %pad_maximum_fusion.2), channel_id=1, source_target_pairs={{32,0},{33,1},{34,2},{35,3},{36,4},{37,5},{38,6},{39,7},{40,8},{41... | collective-permute-start | bytes 1572872 | tf_op jit(solution)/shard_map/ppermute | solution.py:38
  72.6 4.2 %collective-permute-start.11 = (f32[4,256,512]{2,1,0:T(8,128)S(1)}, f32[4,256,512]{2,1,0:T(8,128)S(1)}, u32[]{:S(2)}, u32[]{:S(2)}) collective-permute-start(f32[4,256,512]{2,1,0:T(8,128)S(1)} %get-tuple-element.35), channel_id=1, source_target_pairs={{16,0},{17,1},{18,2},{19,3},{20,4},{21,5},{22,6},{23,7},{24,8},{25... | collective-permute-start | bytes 6291464 | tf_op jit(solution)/shard_map/ppermute | solution.py:38
  72.7 33.4 %collective-permute-start.16 = (bf16[2,512,512]{2,1,0:T(8,128)(2,1)}, bf16[2,512,512]{2,1,0:T(8,128)(2,1)S(1)}, u32[]{:S(2)}, u32[]{:S(2)}) collective-permute-start(bf16[2,512,512]{2,1,0:T(8,128)(2,1)} %collective-permute-done.8.refs_2_), channel_id=1, source_target_pairs={{8,0},{9,1},{10,2},{11,3},{12,4},{13,5},{14,6},{15,7},{0,8},{1,9},... | collective-permute-start | bytes 3145736 | tf_op jit(solution)/shard_map/ppermute | solution.py:38
  77.0 8.4 %collective-permute-start.13 = (f32[128,512]{1,0:T(8,128)S(1)}, f32[128,512]{1,0:T(8,128)S(1)}, u32[]{:S(2)}, u32[]{:S(2)}) collective-permute-start(f32[128,512]{1,0:T(8,128)S(1)} %get-tuple-element.46), channel_id=1, source_target_pairs={{32,0},{33,1},{34,2},{35,3},{36,4},{37,5},{38,6},{39,7},{40,8},{41... | collective-permute-start | bytes 786440 | tf_op jit(solution)/shard_map/ppermute | solution.py:38
  77.9 8.1 %collective-permute-start.12 = (f32[128,512]{1,0:T(8,128)S(1)}, f32[128,512]{1,0:T(8,128)S(1)}, u32[]{:S(2)}, u32[]{:S(2)}) collective-permute-start(f32[128,512]{1,0:T(8,128)S(1)} %get-tuple-element.47), channel_id=1, source_target_pairs={{96,0},{97,1},{98,2},{99,3},{100,4},{101,5},{102,6},{103,7},{104,8... | collective-permute-start | bytes 786440 | tf_op jit(solution)/shard_map/ppermute | solution.py:38
  87.8 13.3 %collective-permute-start.14 = (f32[256,512]{1,0:T(8,128)}, f32[256,512]{1,0:T(8,128)}, u32[]{:S(2)}, u32[]{:S(2)}) collective-permute-start(f32[256,512]{1,0:T(8,128)} %pad_maximum_fusion.3), channel_id=1, source_target_pairs={{96,0},{97,1},{98,2},{99,3},{100,4},{101,5},{102,6},{103,7},{104,8... | collective-permute-start | bytes 1572872 | tf_op jit(solution)/shard_map/ppermute | solution.py:38
  89.5 14.5 %collective-permute-start.15 = (f32[256,512]{1,0:T(8,128)}, f32[256,512]{1,0:T(8,128)}, u32[]{:S(2)}, u32[]{:S(2)}) collective-permute-start(f32[256,512]{1,0:T(8,128)} %pad_maximum_fusion.4), channel_id=1, source_target_pairs={{32,0},{33,1},{34,2},{35,3},{36,4},{37,5},{38,6},{39,7},{40,8},{41... | collective-permute-start | bytes 1572872 | tf_op jit(solution)/shard_map/ppermute | solution.py:38
  90.5 19.4 %copy-start.1 = (f32[256,512]{1,0:T(8,128)S(1)}, f32[256,512]{1,0:T(8,128)}, u32[]{:S(2)}) copy-start(f32[256,512]{1,0:T(8,128)} %fusion.3) | copy-start | bytes 1572868
  107.2 18.4 %copy-start.2 = (f32[256,512]{1,0:T(8,128)S(1)}, f32[256,512]{1,0:T(8,128)}, u32[]{:S(2)}) copy-start(f32[256,512]{1,0:T(8,128)} %add_add_fusion.1) | copy-start | bytes 1572868
  107.2 6.0 %collective-permute-start.18 = (f32[256,512]{1,0:T(8,128)S(1)}, f32[256,512]{1,0:T(8,128)S(1)}, u32[]{:S(2)}, u32[]{:S(2)}) collective-permute-start(f32[256,512]{1,0:T(8,128)S(1)} %bitcast.51), channel_id=1, source_target_pairs={{48,32},{80,64},{112,96},{16,0},{176,160},{208,192},{240,224},{144... | collective-permute-start | bytes 1572872 | tf_op jit(solution)/shard_map/ppermute | solution.py:38
  110.7 14.9 %collective-permute-start.17 = (f32[256,512]{1,0:T(8,128)S(1)}, f32[256,512]{1,0:T(8,128)S(1)}, u32[]{:S(2)}, u32[]{:S(2)}) collective-permute-start(f32[256,512]{1,0:T(8,128)S(1)} %broadcast_select_fusion.1), channel_id=1, source_target_pairs={{128,0},{129,1},{130,2},{131,3},{132,4},{133,5},{134,6},{135,7},{1... | collective-permute-start | bytes 1572872 | tf_op jit(solution)/shard_map/ppermute | solution.py:38
  113.3 13.1 %collective-permute-start.19 = (f32[256,512]{1,0:T(8,128)S(1)}, f32[256,512]{1,0:T(8,128)S(1)}, u32[]{:S(2)}, u32[]{:S(2)}) collective-permute-start(f32[256,512]{1,0:T(8,128)S(1)} %bitcast_add_fusion), channel_id=1, source_target_pairs={{14,78},{15,79},{18,82},{19,83},{40,104},{52,116},{53,117},{73,9},... | collective-permute-start | bytes 1572872 | tf_op jit(solution)/shard_map/ppermute | solution.py:38
  114.0 13.6 %collective-permute-start.20 = (f32[256,512]{1,0:T(8,128)S(1)}, f32[256,512]{1,0:T(8,128)S(1)}, u32[]{:S(2)}, u32[]{:S(2)}) collective-permute-start(f32[256,512]{1,0:T(8,128)S(1)} %bitcast_add_fusion), channel_id=1, source_target_pairs={{8,104},{20,116},{21,117},{41,9},{42,10},{43,11},{54,22},{55,23},{... | collective-permute-start | bytes 1572872 | tf_op jit(solution)/shard_map/ppermute | solution.py:38
  115.3 12.3 %collective-permute-start.21 = (f32[256,512]{1,0:T(8,128)S(1)}, f32[256,512]{1,0:T(8,128)S(1)}, u32[]{:S(2)}, u32[]{:S(2)}) collective-permute-start(f32[256,512]{1,0:T(8,128)S(1)} %bitcast_add_fusion), channel_id=1, source_target_pairs={{0,32},{12,44},{13,45},{17,49},{46,78},{47,79},{50,82},{51,83},{72... | collective-permute-start | bytes 1572872 | tf_op jit(solution)/shard_map/ppermute | solution.py:38
  127.9 16.8 %collective-permute-start.22 = (f32[256,512]{1,0:T(8,128)S(1)}, f32[256,512]{1,0:T(8,128)S(1)}, u32[]{:S(2)}, u32[]{:S(2)}) collective-permute-start(f32[256,512]{1,0:T(8,128)S(1)} %get-tuple-element.52), channel_id=1, source_target_pairs={{0,16},{128,151},{160,128},{176,0},{64,113},{192,150},{96,135},{22... | collective-permute-start | bytes 1572872 | tf_op jit(solution)/shard_map/ppermute | solution.py:38
  132.0 14.6 %collective-permute-start.23 = (f32[256,512]{1,0:T(8,128)S(1)}, f32[256,512]{1,0:T(8,128)S(1)}, u32[]{:S(2)}, u32[]{:S(2)}) collective-permute-start(f32[256,512]{1,0:T(8,128)S(1)} %add_add_fusion), channel_id=1, source_target_pairs={{160,166},{177,183},{210,192},{211,209},{116,226},{245,243},{22,13... | collective-permute-start | bytes 1572872 | tf_op jit(solution)/shard_map/ppermute | solution.py:38
  133.3 27.8 %collective-permute-start.24 = (f32[256,512]{1,0:T(8,128)S(1)}, f32[256,512]{1,0:T(8,128)S(1)}, u32[]{:S(2)}, u32[]{:S(2)}) collective-permute-start(f32[256,512]{1,0:T(8,128)S(1)} %get-tuple-element.53), channel_id=1, source_target_pairs={{144,16},{16,150},{32,98},{48,0},{80,135},{208,114},{112,113},{240... | collective-permute-start | bytes 1572872 | tf_op jit(solution)/shard_map/ppermute | solution.py:38
  134.6 26.5 %collective-permute-start.25 = (f32[256,512]{1,0:T(8,128)S(1)}, f32[256,512]{1,0:T(8,128)S(1)}, u32[]{:S(2)}, u32[]{:S(2)}) collective-permute-start(f32[256,512]{1,0:T(8,128)S(1)} %add_add_fusion), channel_id=1, source_target_pairs={{232,226},{137,243},{10,132},{139,149},{172,166},{173,183},{206,19... | collective-permute-start | bytes 1572872 | tf_op jit(solution)/shard_map/ppermute | solution.py:38

commit v11 on v10

--- a/solution.py
+++ b/solution.py
@@ -82,12 +82,11 @@
 
 def steps(a, b, n):
     ahead, back = (b - a) % n, (a - b) % n
-    share = 0.5 if ahead == back else 1.0
     found = []
     if ahead and ahead <= back:
-        found += [((a + i) % n, 1, share) for i in range(ahead)]
+        found += [((a + i) % n, 1, 1.0) for i in range(ahead)]
     if ahead and back <= ahead:
-        found += [((a - i) % n, -1, share) for i in range(back)]
+        found += [((a - i) % n, -1, 1.0) for i in range(back)]
     return found
 
 
@@ -294,6 +293,7 @@
 Y_SWAP = every(lambda y, x, c, h, z: (1 - y, x, c, block(h, z)))
 CORE_SWAP = every(lambda y, x, c, h, z: (y, x, 1 - c, block(h, z)))
 FROM_LEFT = every(lambda y, x, c, h, z: (y, x - 1, c, block(h, z)))
+FROM_FAR = every(lambda y, x, c, h, z: (y, x + 2, c, block(h, z)))
 FROM_RIGHT = every(lambda y, x, c, h, z: (y, x + 1, c, block(h, z)))
 FROM_UP = every(lambda y, x, c, h, z: (y, x, c, block(h, z + 1)))
 FROM_DOWN = every(lambda y, x, c, h, z: (y, x, c, block(h, z - 1)))
@@ -315,6 +315,12 @@
     return lax.optimization_barrier(values)
 
 
+def over_x(keep, got):
+    own, *others = together(*(keep[j] + got[j] for j in range(NX)))
+    right, far, left = (send(part, pairs) for part, pairs in zip(others, (FROM_LEFT, FROM_FAR, FROM_RIGHT)))
+    return own + far + (right + left)
+
+
 def per_device(half_b):
     local, codes_c, target_c, first, halves, final, final_c = plan()
     aux, blk = lax.axis_index("aux"), lax.axis_index("blk")
@@ -338,10 +344,7 @@
 
     held[Y2] = send(held[PP], FROM_OTHER)
     keep, given = products(table_b, [held[n] for n in HELD_B], HELD_B, PAIRS_B, (NX, NX))
-    own_b, right_b, left_b = near(keep, send(given, CORE_SWAP))
-    own_b, right_b, left_b = together(own_b, right_b, left_b)
-
-    total_b = own_b + send(right_b, FROM_LEFT) + send(left_b, FROM_RIGHT)
+    total_b = over_x(keep, send(given, CORE_SWAP))
     total_b, held[Y2] = together(total_b, held[Y2])
 
     has_first = jnp.asarray(first)[aux, blk]

time: 163 us -> 164 us (level)
    add x3 -> x2, other arithmetic: 2.56 us -> 3.73 us  [the longest x1 2.37 us: over_x(): return own + far + (right + left)]
    ppermute x26 -> x25, waiting for transfers between devices: 98.1 us -> 98.9 us  [send(): return lax.ppermute(value, ALL, pairs)]
    ppermute x26 -> x25, starting transfers between devices: 38.3 us -> 37.7 us  [send(): return lax.ppermute(value, ALL, pairs)]
  transfers between devices with their start and end apart: 26 -> 25, of which waited for: 17 -> 14; matrix products, arithmetic and copies ran while one was open for 7% -> 7% of each run, Pallas kernels for 0% -> 0%
where the time goes in v11:
time: 164 us; the launch traced here: 162 us
  waiting for transfers between devices  98.9 us (60%)
  starting transfers between devices  37.7 us (23%)
  Pallas kernels  9.91 us (6%)
  other arithmetic  8.23 us (5%)
  local copies, waits for them, and re-layouts  5.36 us (3%)
    ppermute x25, waiting for transfers between devices, send(): return lax.ppermute(value, ALL, pairs)  98.9 us
    ppermute x25, starting transfers between devices, send(): return lax.ppermute(value, ALL, pairs)  37.7 us
    pallas_call x3, Pallas kernels, products(): pl.pallas_call(functools.partial(units_kernel, pairs, index_pairs, len(co...  9.85 us
  transfers between devices with their start and end apart: 25, of which 14 were waited for; matrix products, arithmetic and copies ran while one was open for 7% of the time, Pallas kernels for 0%

profile of v11, /device:TPU:12, one launch (start us, length us, event | category | flops | bytes accessed | tf_op | source)
XLA Modules:
  0.0 161.7 jit_solution(3967823626288351083)
XLA Ops:
  0.0 5.9 %collective-permute-start = (bf16[2,512,512]{2,1,0:T(8,128)(2,1)}, bf16[2,512,512]{2,1,0:T(8,128)(2,1)}, u32[]{:S(2)}, u32[]{:S(2)}) collective-permute-start(bf16[2,512,512]{2,1,0:T(8,128)(2,1)} %source.1), channel_id=1, source_target_pairs={{1,0},{2,1},{3,2},{4,3},{5,4},{6,5},{7,6},{0,7},{9,8},{10,9},{11,1... | collective-permute-start | bytes 3145736 | tf_op jit(solution)/shard_map/ppermute | solution.py:38
  5.9 2.3 %collective-permute-start.2 = (bf16[2,512,512]{2,1,0:T(8,128)(2,1)}, bf16[2,512,512]{2,1,0:T(8,128)(2,1)S(1)}, u32[]{:S(2)}, u32[]{:S(2)}) collective-permute-start(bf16[2,512,512]{2,1,0:T(8,128)(2,1)} %source.1), channel_id=1, source_target_pairs={{8,0},{9,1},{10,2},{11,3},{12,4},{13,5},{14,6},{15,7},{0,8},{1,9},... | collective-permute-start | bytes 3145736 | tf_op jit(solution)/shard_map/ppermute | solution.py:38
  10.2 18.4 %collective-permute-done.refs_1_ = bf16[2,512,512]{2,1,0:T(8,128)(2,1)} collective-permute-done((bf16[2,512,512]{2,1,0:T(8,128)(2,1)}, bf16[2,512,512]{2,1,0:T(8,128)(2,1)}, u32[]{:S(2)}, u32[]{:S(2)}) %collective-permute-start) | collective-permute-done | bytes 1048608 | tf_op jit(solution)/shard_map/ppermute | solution.py:38
  28.6 3.3 %collective-permute-done.1.refs_2_.refs_1_ = bf16[2,512,512]{2,1,0:T(8,128)(2,1)S(1)} collective-permute-done((bf16[2,512,512]{2,1,0:T(8,128)(2,1)}, bf16[2,512,512]{2,1,0:T(8,128)(2,1)S(1)}, u32[]{:S(2)}, u32[]{:S(2)}) %collective-permute-start.1) | collective-permute-done | bytes 1048608 | tf_op jit(solution)/shard_map/ppermute | solution.py:38
  32.2 4.4 %shard_map.65 = (f32[4,256,512]{2,1,0:T(8,128)S(1)}, f32[4,256,512]{2,1,0:T(8,128)S(1)}) custom-call(s32[20]{0:T(128)S(1)} %get-tuple-element.55.table, bf16[2,512,512]{2,1,0:T(8,128)(2,1)S(1)} %shard_map.64.refs_0_, bf16[2,512,512]{2,1,0:T(8,128)(2,1)} %collective-permute-done.refs_1_, bf16[2,512,512]{2,1,0:T(8,128)(2,1)S(1)} %collective-permute-done.1.refs_2_.refs_1_, ...), custom_call_target="tpu_custom_call" | custom-call | tf_op jit(solution)/shard_map/pallas_call | solution.py:242
  36.7 2.4 %collective-permute-start.10 = (bf16[2,512,512]{2,1,0:T(8,128)(2,1)}, bf16[2,512,512]{2,1,0:T(8,128)(2,1)S(1)}, u32[]{:S(2)}, u32[]{:S(2)}) collective-permute-start(bf16[2,512,512]{2,1,0:T(8,128)(2,1)} %collective-permute-done.refs_1_), channel_id=1, source_target_pairs={{8,0},{9,1},{10,2},{11,3},{12,4},{13,5},{14,6},{15,7},{0,8},{1,9},... | collective-permute-start | bytes 3145736 | tf_op jit(solution)/shard_map/ppermute | solution.py:38
  39.1 2.9 %collective-permute-start.8 = (bf16[2,512,512]{2,1,0:T(8,128)(2,1)}, bf16[2,512,512]{2,1,0:T(8,128)(2,1)}, u32[]{:S(2)}, u32[]{:S(2)}) collective-permute-start(bf16[2,512,512]{2,1,0:T(8,128)(2,1)} %collective-permute-done.refs_1_), channel_id=1, source_target_pairs={{1,0},{2,1},{3,2},{4,3},{5,4},{6,5},{7,6},{0,7},{9,8},{10,9},{11,1... | collective-permute-start | bytes 3145736 | tf_op jit(solution)/shard_map/ppermute | solution.py:38
  42.1 1.3 collective-permute-start.4
  44.6 5.7 %collective-permute-done.4 = f32[128,512]{1,0:T(8,128)S(1)} collective-permute-done((f32[128,512]{1,0:T(8,128)S(1)}, f32[128,512]{1,0:T(8,128)S(1)}, u32[]{:S(2)}, u32[]{:S(2)}) %collective-permute-start.4) | collective-permute-done | bytes 262176 | tf_op jit(solution)/shard_map/ppermute | solution.py:38
  50.4 1.3 collective-permute-start.5
  52.8 10.6 %collective-permute-done.5 = f32[256,512]{1,0:T(8,128)S(1)} collective-permute-done((f32[256,512]{1,0:T(8,128)S(1)}, f32[256,512]{1,0:T(8,128)S(1)}, u32[]{:S(2)}, u32[]{:S(2)}) %collective-permute-start.5) | collective-permute-done | bytes 524320 | tf_op jit(solution)/shard_map/ppermute | solution.py:38
  65.7 2.5 %collective-permute-done.9.refs_3_.refs_0_ = bf16[2,512,512]{2,1,0:T(8,128)(2,1)S(1)} collective-permute-done((bf16[2,512,512]{2,1,0:T(8,128)(2,1)S(1)}, bf16[2,512,512]{2,1,0:T(8,128)(2,1)S(1)}, u32[]{:S(2)}, u32[]{:S(2)}) %collective-permute-start.9) | collective-permute-done | bytes 1048608 | tf_op jit(solution)/shard_map/ppermute | solution.py:38
  68.2 4.4 %shard_map.66 = (f32[4,256,512]{2,1,0:T(8,128)S(1)}, f32[4,256,512]{2,1,0:T(8,128)S(1)}) custom-call(s32[20]{0:T(128)S(1)} %get-tuple-element.56.table, bf16[2,512,512]{2,1,0:T(8,128)(2,1)S(1)} %shard_map.64.refs_0_, bf16[2,512,512]{2,1,0:T(8,128)(2,1)S(1)} %collective-permute-done.1.refs_2_.refs_1_, bf16[2,512,512]{2,1,0:T(8,128)(2,1)} %collective-permute-done.8.refs_2_, ...), custom_call_target="tpu_custom_call" | custom-call | tf_op jit(solution)/shard_map/pallas_call | solution.py:242
  72.7 1.3 collective-permute-start.15
  74.0 2.8 %collective-permute-done.11 = f32[4,256,512]{2,1,0:T(8,128)S(1)} collective-permute-done((f32[4,256,512]{2,1,0:T(8,128)S(1)}, f32[4,256,512]{2,1,0:T(8,128)S(1)}, u32[]{:S(2)}, u32[]{:S(2)}) %collective-permute-start.11) | collective-permute-done | bytes 2097184 | tf_op jit(solution)/shard_map/ppermute | solution.py:38
  76.9 1.4 fusion
  78.7 2.1 %collective-permute-start.13 = (f32[256,512]{1,0:T(8,128)}, f32[256,512]{1,0:T(8,128)}, u32[]{:S(2)}, u32[]{:S(2)}) collective-permute-start(f32[256,512]{1,0:T(8,128)} %get-tuple-element.39), channel_id=1, source_target_pairs={{96,0},{97,1},{98,2},{99,3},{100,4},{101,5},{102,6},{103,7},{104,8... | collective-permute-start | bytes 1572872 | tf_op jit(solution)/shard_map/ppermute | solution.py:38
  81.6 13.3 %collective-permute-done.12 = f32[256,512]{1,0:T(8,128)} collective-permute-done((f32[256,512]{1,0:T(8,128)}, f32[256,512]{1,0:T(8,128)}, u32[]{:S(2)}, u32[]{:S(2)}) %collective-permute-start.12) | collective-permute-done | bytes 524320 | tf_op jit(solution)/shard_map/ppermute | solution.py:38
  94.9 9.5 %collective-permute-done.13 = f32[256,512]{1,0:T(8,128)} collective-permute-done((f32[256,512]{1,0:T(8,128)}, f32[256,512]{1,0:T(8,128)}, u32[]{:S(2)}, u32[]{:S(2)}) %collective-permute-start.13) | collective-permute-done | bytes 524320 | tf_op jit(solution)/shard_map/ppermute | solution.py:38
  104.4 2.4 %add_add_fusion.1 = f32[256,512]{1,0:T(8,128)} fusion(f32[256,512]{1,0:T(8,128)} %collective-permute-done.13, f32[256,512]{1,0:T(8,128)} %collective-permute-done.14, f32[256,512]{1,0:T(8,128)S(1)} %get-tuple-element.37, f32[256,512]{1,0:T(8,128)} %collective-permute-done.12), kind=kLoop, calls=%fused_computation.19 | loop fusion | flops 393216 | bytes 2621440 | tf_op jit(solution)/shard_map/add | solution.py:321
  107.8 1.5 collective-permute-start.17
  109.3 1.3 dynamic_slice.16
  111.3 2.5 %collective-permute-start.16 = (f32[256,512]{1,0:T(8,128)S(1)}, f32[256,512]{1,0:T(8,128)S(1)}, u32[]{:S(2)}, u32[]{:S(2)}) collective-permute-start(f32[256,512]{1,0:T(8,128)S(1)} %broadcast_select_fusion.1), channel_id=1, source_target_pairs={{128,0},{129,1},{130,2},{131,3},{132,4},{133,5},{134,6},{135,7},{1... | collective-permute-start | bytes 1572872 | tf_op jit(solution)/shard_map/ppermute | solution.py:38
  115.9 1.3 dynamic_slice.15
  118.6 6.9 %collective-permute-done.16 = f32[256,512]{1,0:T(8,128)S(1)} collective-permute-done((f32[256,512]{1,0:T(8,128)S(1)}, f32[256,512]{1,0:T(8,128)S(1)}, u32[]{:S(2)}, u32[]{:S(2)}) %collective-permute-start.16) | collective-permute-done | bytes 524320 | tf_op jit(solution)/shard_map/ppermute | solution.py:38
  126.6 5.6 %collective-permute-start.21 = (f32[256,512]{1,0:T(8,128)S(1)}, f32[256,512]{1,0:T(8,128)S(1)}, u32[]{:S(2)}, u32[]{:S(2)}) collective-permute-start(f32[256,512]{1,0:T(8,128)S(1)} %get-tuple-element.53), channel_id=1, source_target_pairs={{128,128},{32,16},{160,114},{48,0},{64,113},{192,150},{96,135},{22... | collective-permute-start | bytes 1572872 | tf_op jit(solution)/shard_map/ppermute | solution.py:38
  132.2 1.3 collective-permute-start.22
  133.5 1.3 collective-permute-start.23
  134.8 1.3 collective-permute-start.24
  136.1 8.3 %collective-permute-done.21 = f32[256,512]{1,0:T(8,128)S(1)} collective-permute-done((f32[256,512]{1,0:T(8,128)S(1)}, f32[256,512]{1,0:T(8,128)S(1)}, u32[]{:S(2)}, u32[]{:S(2)}) %collective-permute-start.21) | collective-permute-done | bytes 524320 | tf_op jit(solution)/shard_map/ppermute | solution.py:38
  144.5 2.8 %collective-permute-done.22 = f32[256,512]{1,0:T(8,128)S(1)} collective-permute-done((f32[256,512]{1,0:T(8,128)S(1)}, f32[256,512]{1,0:T(8,128)S(1)}, u32[]{:S(2)}, u32[]{:S(2)}) %collective-permute-start.22) | collective-permute-done | bytes 524320 | tf_op jit(solution)/shard_map/ppermute | solution.py:38
  147.4 13.2 %collective-permute-done.23 = f32[256,512]{1,0:T(8,128)S(1)} collective-permute-done((f32[256,512]{1,0:T(8,128)S(1)}, f32[256,512]{1,0:T(8,128)S(1)}, u32[]{:S(2)}, u32[]{:S(2)}) %collective-permute-start.23) | collective-permute-done | bytes 524320 | tf_op jit(solution)/shard_map/ppermute | solution.py:38
  (51 shorter events, 14.7 us)
Async XLA Ops:
  0.0 28.6 %collective-permute-start = (bf16[2,512,512]{2,1,0:T(8,128)(2,1)}, bf16[2,512,512]{2,1,0:T(8,128)(2,1)}, u32[]{:S(2)}, u32[]{:S(2)}) collective-permute-start(bf16[2,512,512]{2,1,0:T(8,128)(2,1)} %source.1), channel_id=1, source_target_pairs={{1,0},{2,1},{3,2},{4,3},{5,4},{6,5},{7,6},{0,7},{9,8},{10,9},{11,1... | collective-permute-start | bytes 3145736 | tf_op jit(solution)/shard_map/ppermute | solution.py:38
  5.9 26.0 %collective-permute-start.1 = (bf16[2,512,512]{2,1,0:T(8,128)(2,1)}, bf16[2,512,512]{2,1,0:T(8,128)(2,1)S(1)}, u32[]{:S(2)}, u32[]{:S(2)}) collective-permute-start(bf16[2,512,512]{2,1,0:T(8,128)(2,1)} %source.1), channel_id=1, source_target_pairs={{7,0},{0,1},{1,2},{2,3},{3,4},{4,5},{5,6},{6,7},{15,8},{8,9},{9,10... | collective-permute-start | bytes 3145736 | tf_op jit(solution)/shard_map/ppermute | solution.py:38
  5.9 26.3 %collective-permute-start.2 = (bf16[2,512,512]{2,1,0:T(8,128)(2,1)}, bf16[2,512,512]{2,1,0:T(8,128)(2,1)S(1)}, u32[]{:S(2)}, u32[]{:S(2)}) collective-permute-start(bf16[2,512,512]{2,1,0:T(8,128)(2,1)} %source.1), channel_id=1, source_target_pairs={{8,0},{9,1},{10,2},{11,3},{12,4},{13,5},{14,6},{15,7},{0,8},{1,9},... | collective-permute-start | bytes 3145736 | tf_op jit(solution)/shard_map/ppermute | solution.py:38
  8.2 1.3 copy-start
  36.6 5.4 %collective-permute-start.3 = (f32[4,256,512]{2,1,0:T(8,128)S(1)}, f32[4,256,512]{2,1,0:T(8,128)S(1)}, u32[]{:S(2)}, u32[]{:S(2)}) collective-permute-start(f32[4,256,512]{2,1,0:T(8,128)S(1)} %get-tuple-element.30), channel_id=1, source_target_pairs={{16,0},{17,1},{18,2},{19,3},{20,4},{21,5},{22,6},{23,7},{24,8},{25... | collective-permute-start | bytes 6291464 | tf_op jit(solution)/shard_map/ppermute | solution.py:38
  36.7 29.0 %collective-permute-start.10 = (bf16[2,512,512]{2,1,0:T(8,128)(2,1)}, bf16[2,512,512]{2,1,0:T(8,128)(2,1)S(1)}, u32[]{:S(2)}, u32[]{:S(2)}) collective-permute-start(bf16[2,512,512]{2,1,0:T(8,128)(2,1)} %collective-permute-done.refs_1_), channel_id=1, source_target_pairs={{8,0},{9,1},{10,2},{11,3},{12,4},{13,5},{14,6},{15,7},{0,8},{1,9},... | collective-permute-start | bytes 3145736 | tf_op jit(solution)/shard_map/ppermute | solution.py:38
  39.1 26.6 %collective-permute-start.8 = (bf16[2,512,512]{2,1,0:T(8,128)(2,1)}, bf16[2,512,512]{2,1,0:T(8,128)(2,1)}, u32[]{:S(2)}, u32[]{:S(2)}) collective-permute-start(bf16[2,512,512]{2,1,0:T(8,128)(2,1)} %collective-permute-done.refs_1_), channel_id=1, source_target_pairs={{1,0},{2,1},{3,2},{4,3},{5,4},{6,5},{7,6},{0,7},{9,8},{10,9},{11,1... | collective-permute-start | bytes 3145736 | tf_op jit(solution)/shard_map/ppermute | solution.py:38
  42.1 26.1 %collective-permute-start.9 = (bf16[2,512,512]{2,1,0:T(8,128)(2,1)S(1)}, bf16[2,512,512]{2,1,0:T(8,128)(2,1)S(1)}, u32[]{:S(2)}, u32[]{:S(2)}) collective-permute-start(bf16[2,512,512]{2,1,0:T(8,128)(2,1)S(1)} %collective-permute-done.1.refs_2_.refs_1_), channel_id=1, source_target_pairs={{7,0},{0,1},{1,2},{2,3},{3,4},{4,5},{5,6},{6,7},{15,8},{8,9},{9,10... | collective-permute-start | bytes 3145736 | tf_op jit(solution)/shard_map/ppermute | solution.py:38
  42.1 8.2 %collective-permute-start.4 = (f32[128,512]{1,0:T(8,128)S(1)}, f32[128,512]{1,0:T(8,128)S(1)}, u32[]{:S(2)}, u32[]{:S(2)}) collective-permute-start(f32[128,512]{1,0:T(8,128)S(1)} %get-tuple-element.49), channel_id=1, source_target_pairs={{96,0},{97,1},{98,2},{99,3},{100,4},{101,5},{102,6},{103,7},{104,8... | collective-permute-start | bytes 786440 | tf_op jit(solution)/shard_map/ppermute | solution.py:38
  43.7 8.0 %collective-permute-start.6 = (f32[128,512]{1,0:T(8,128)S(1)}, f32[128,512]{1,0:T(8,128)S(1)}, u32[]{:S(2)}, u32[]{:S(2)}) collective-permute-start(f32[128,512]{1,0:T(8,128)S(1)} %get-tuple-element.50), channel_id=1, source_target_pairs={{32,0},{33,1},{34,2},{35,3},{36,4},{37,5},{38,6},{39,7},{40,8},{41... | collective-permute-start | bytes 786440 | tf_op jit(solution)/shard_map/ppermute | solution.py:38
  50.4 13.0 %collective-permute-start.5 = (f32[256,512]{1,0:T(8,128)S(1)}, f32[256,512]{1,0:T(8,128)S(1)}, u32[]{:S(2)}, u32[]{:S(2)}) collective-permute-start(f32[256,512]{1,0:T(8,128)S(1)} %pad_maximum_fusion.1), channel_id=1, source_target_pairs={{96,0},{97,1},{98,2},{99,3},{100,4},{101,5},{102,6},{103,7},{104,8... | collective-permute-start | bytes 1572872 | tf_op jit(solution)/shard_map/ppermute | solution.py:38
  51.7 12.9 %collective-permute-start.7 = (f32[256,512]{1,0:T(8,128)S(1)}, f32[256,512]{1,0:T(8,128)S(1)}, u32[]{:S(2)}, u32[]{:S(2)}) collective-permute-start(f32[256,512]{1,0:T(8,128)S(1)} %pad_maximum_fusion.2), channel_id=1, source_target_pairs={{32,0},{33,1},{34,2},{35,3},{36,4},{37,5},{38,6},{39,7},{40,8},{41... | collective-permute-start | bytes 1572872 | tf_op jit(solution)/shard_map/ppermute | solution.py:38
  72.6 4.2 %collective-permute-start.11 = (f32[4,256,512]{2,1,0:T(8,128)S(1)}, f32[4,256,512]{2,1,0:T(8,128)S(1)}, u32[]{:S(2)}, u32[]{:S(2)}) collective-permute-start(f32[4,256,512]{2,1,0:T(8,128)S(1)} %get-tuple-element.36), channel_id=1, source_target_pairs={{16,0},{17,1},{18,2},{19,3},{20,4},{21,5},{22,6},{23,7},{24,8},{25... | collective-permute-start | bytes 6291464 | tf_op jit(solution)/shard_map/ppermute | solution.py:38
  72.7 34.0 %collective-permute-start.15 = (bf16[2,512,512]{2,1,0:T(8,128)(2,1)}, bf16[2,512,512]{2,1,0:T(8,128)(2,1)S(1)}, u32[]{:S(2)}, u32[]{:S(2)}) collective-permute-start(bf16[2,512,512]{2,1,0:T(8,128)(2,1)} %collective-permute-done.8.refs_2_), channel_id=1, source_target_pairs={{8,0},{9,1},{10,2},{11,3},{12,4},{13,5},{14,6},{15,7},{0,8},{1,9},... | collective-permute-start | bytes 3145736 | tf_op jit(solution)/shard_map/ppermute | solution.py:38
  78.2 16.6 %collective-permute-start.12 = (f32[256,512]{1,0:T(8,128)}, f32[256,512]{1,0:T(8,128)}, u32[]{:S(2)}, u32[]{:S(2)}) collective-permute-start(f32[256,512]{1,0:T(8,128)} %get-tuple-element.38), channel_id=1, source_target_pairs={{64,0},{65,1},{66,2},{67,3},{68,4},{69,5},{70,6},{71,7},{72,8},{73... | collective-permute-start | bytes 1572872 | tf_op jit(solution)/shard_map/ppermute | solution.py:38
  78.7 25.6 %collective-permute-start.13 = (f32[256,512]{1,0:T(8,128)}, f32[256,512]{1,0:T(8,128)}, u32[]{:S(2)}, u32[]{:S(2)}) collective-permute-start(f32[256,512]{1,0:T(8,128)} %get-tuple-element.39), channel_id=1, source_target_pairs={{96,0},{97,1},{98,2},{99,3},{100,4},{101,5},{102,6},{103,7},{104,8... | collective-permute-start | bytes 1572872 | tf_op jit(solution)/shard_map/ppermute | solution.py:38
  80.8 23.6 %collective-permute-start.14 = (f32[256,512]{1,0:T(8,128)}, f32[256,512]{1,0:T(8,128)}, u32[]{:S(2)}, u32[]{:S(2)}) collective-permute-start(f32[256,512]{1,0:T(8,128)} %get-tuple-element.40), channel_id=1, source_target_pairs={{32,0},{33,1},{34,2},{35,3},{36,4},{37,5},{38,6},{39,7},{40,8},{41... | collective-permute-start | bytes 1572872 | tf_op jit(solution)/shard_map/ppermute | solution.py:38
  81.6 29.0 %copy-start.1 = (f32[256,512]{1,0:T(8,128)S(1)}, f32[256,512]{1,0:T(8,128)}, u32[]{:S(2)}) copy-start(f32[256,512]{1,0:T(8,128)} %fusion.6) | copy-start | bytes 1572868
  107.8 17.7 %copy-start.2 = (f32[256,512]{1,0:T(8,128)S(1)}, f32[256,512]{1,0:T(8,128)}, u32[]{:S(2)}) copy-start(f32[256,512]{1,0:T(8,128)} %add_add_fusion.1) | copy-start | bytes 1572868
  107.8 5.9 %collective-permute-start.17 = (f32[256,512]{1,0:T(8,128)S(1)}, f32[256,512]{1,0:T(8,128)S(1)}, u32[]{:S(2)}, u32[]{:S(2)}) collective-permute-start(f32[256,512]{1,0:T(8,128)S(1)} %bitcast.41), channel_id=1, source_target_pairs={{32,48},{64,80},{96,112},{0,16},{160,176},{192,208},{224,240},{128... | collective-permute-start | bytes 1572872 | tf_op jit(solution)/shard_map/ppermute | solution.py:38
  111.3 14.2 %collective-permute-start.16 = (f32[256,512]{1,0:T(8,128)S(1)}, f32[256,512]{1,0:T(8,128)S(1)}, u32[]{:S(2)}, u32[]{:S(2)}) collective-permute-start(f32[256,512]{1,0:T(8,128)S(1)} %broadcast_select_fusion.1), channel_id=1, source_target_pairs={{128,0},{129,1},{130,2},{131,3},{132,4},{133,5},{134,6},{135,7},{1... | collective-permute-start | bytes 1572872 | tf_op jit(solution)/shard_map/ppermute | solution.py:38
  113.8 12.4 %collective-permute-start.18 = (f32[256,512]{1,0:T(8,128)S(1)}, f32[256,512]{1,0:T(8,128)S(1)}, u32[]{:S(2)}, u32[]{:S(2)}) collective-permute-start(f32[256,512]{1,0:T(8,128)S(1)} %bitcast_add_fusion), channel_id=1, source_target_pairs={{14,78},{18,82},{19,83},{31,95},{40,104},{41,105},{52,116},{53,117... | collective-permute-start | bytes 1572872 | tf_op jit(solution)/shard_map/ppermute | solution.py:38
  114.5 11.7 %collective-permute-start.19 = (f32[256,512]{1,0:T(8,128)S(1)}, f32[256,512]{1,0:T(8,128)S(1)}, u32[]{:S(2)}, u32[]{:S(2)}) collective-permute-start(f32[256,512]{1,0:T(8,128)S(1)} %bitcast_add_fusion), channel_id=1, source_target_pairs={{8,104},{9,105},{20,116},{21,117},{42,10},{43,11},{54,22},{55,23},... | collective-permute-start | bytes 1572872 | tf_op jit(solution)/shard_map/ppermute | solution.py:38
  115.2 11.1 %collective-permute-start.20 = (f32[256,512]{1,0:T(8,128)S(1)}, f32[256,512]{1,0:T(8,128)S(1)}, u32[]{:S(2)}, u32[]{:S(2)}) collective-permute-start(f32[256,512]{1,0:T(8,128)S(1)} %bitcast_add_fusion), channel_id=1, source_target_pairs={{12,44},{13,45},{16,48},{17,49},{46,78},{50,82},{51,83},{63,95},{7... | collective-permute-start | bytes 1572872 | tf_op jit(solution)/shard_map/ppermute | solution.py:38
  126.6 17.9 %collective-permute-start.21 = (f32[256,512]{1,0:T(8,128)S(1)}, f32[256,512]{1,0:T(8,128)S(1)}, u32[]{:S(2)}, u32[]{:S(2)}) collective-permute-start(f32[256,512]{1,0:T(8,128)S(1)} %get-tuple-element.53), channel_id=1, source_target_pairs={{128,128},{32,16},{160,114},{48,0},{64,113},{192,150},{96,135},{22... | collective-permute-start | bytes 1572872 | tf_op jit(solution)/shard_map/ppermute | solution.py:38
  132.2 15.1 %collective-permute-start.22 = (f32[256,512]{1,0:T(8,128)S(1)}, f32[256,512]{1,0:T(8,128)S(1)}, u32[]{:S(2)}, u32[]{:S(2)}) collective-permute-start(f32[256,512]{1,0:T(8,128)S(1)} %add_add_fusion), channel_id=1, source_target_pairs={{48,166},{177,183},{82,192},{211,209},{244,226},{117,243},{150,132... | collective-permute-start | bytes 1572872 | tf_op jit(solution)/shard_map/ppermute | solution.py:38
  133.5 27.1 %collective-permute-start.23 = (f32[256,512]{1,0:T(8,128)S(1)}, f32[256,512]{1,0:T(8,128)S(1)}, u32[]{:S(2)}, u32[]{:S(2)}) collective-permute-start(f32[256,512]{1,0:T(8,128)S(1)} %get-tuple-element.54), channel_id=1, source_target_pairs={{0,98},{144,135},{16,151},{176,0},{208,113},{80,114},{112,16},{240... | collective-permute-start | bytes 1572872 | tf_op jit(solution)/shard_map/ppermute | solution.py:38
  134.8 25.8 %collective-permute-start.24 = (f32[256,512]{1,0:T(8,128)S(1)}, f32[256,512]{1,0:T(8,128)S(1)}, u32[]{:S(2)}, u32[]{:S(2)}) collective-permute-start(f32[256,512]{1,0:T(8,128)S(1)} %add_add_fusion), channel_id=1, source_target_pairs={{104,226},{233,243},{138,132},{139,149},{172,166},{173,183},{206,1... | collective-permute-start | bytes 1572872 | tf_op jit(solution)/shard_map/ppermute | solution.py:38

commit v12 on v11

--- a/solution.py
+++ b/solution.py
@@ -311,14 +311,12 @@
     return keep[0] + got[0], right, left
 
 
+def split(value):
+    return [value[j] for j in range(NX)]
+
+
 def together(*values):
     return lax.optimization_barrier(values)
-
-
-def over_x(keep, got):
-    own, *others = together(*(keep[j] + got[j] for j in range(NX)))
-    right, far, left = (send(part, pairs) for part, pairs in zip(others, (FROM_LEFT, FROM_FAR, FROM_RIGHT)))
-    return own + far + (right + left)
 
 
 def per_device(half_b):
@@ -344,13 +342,16 @@
 
     held[Y2] = send(held[PP], FROM_OTHER)
     keep, given = products(table_b, [held[n] for n in HELD_B], HELD_B, PAIRS_B, (NX, NX))
-    total_b = over_x(keep, send(given, CORE_SWAP))
-    total_b, held[Y2] = together(total_b, held[Y2])
+    own, *others = together(*(k + g for k, g in zip(split(keep), split(send(given, CORE_SWAP)))))
+    right, far, left = (send(part, pairs) for part, pairs in zip(others, (FROM_LEFT, FROM_FAR, FROM_RIGHT)))
+    held[Y2], right = together(held[Y2], right)
+    (part_c,) = products(table_c, [held[n] for n in HELD_C], HELD_C, PAIRS_C, (1,))
+    part_c = one_core(part_c[0], target_c)
+    total_b, part_c = together((own + right) + (far + left), part_c)
 
     has_first = jnp.asarray(first)[aux, blk]
     done = jnp.where(has_first, total_a, total_b) + send(jnp.where(has_first, total_b, total_a), Y_SWAP)
-    (part_c,) = products(table_c, [held[n] for n in HELD_C], HELD_C, PAIRS_C, (1,))
-    part_c = one_x(one_core(part_c[0], target_c), target_c)
+    part_c = one_x(part_c, target_c)
     done, part_c = together(done, part_c)
 
     own_half = jnp.asarray(halves)[aux, blk]

time: 164 us -> 159 us (0.970)
  waiting for transfers between devices: 98.9 us -> 93.9 us
  local copies, waits for them, and re-layouts: 5.36 us -> 7.44 us
    ppermute x25, waiting for transfers between devices: 98.9 us -> 93.9 us  [send(): return lax.ppermute(value, ALL, pairs)]
    unnamed x6 -> x8, local copies, waits for them, and re-layouts: 1.27 us -> 3.46 us
  transfers between devices with their start and end apart: 25 -> 25, of which waited for: 14 -> 13; matrix products, arithmetic and copies ran while one was open for 7% -> 6% of each run, Pallas kernels for 0% -> 1%
where the time goes in v12:
time: 159 us; the launch traced here: 157 us
  waiting for transfers between devices  93.9 us (59%)
  starting transfers between devices  36.7 us (23%)
  Pallas kernels  9.91 us (6%)
  other arithmetic  7.61 us (5%)
  local copies, waits for them, and re-layouts  7.44 us (5%)
    ppermute x25, waiting for transfers between devices, send(): return lax.ppermute(value, ALL, pairs)  93.9 us
    ppermute x25, starting transfers between devices, send(): return lax.ppermute(value, ALL, pairs)  36.7 us
    pallas_call x3, Pallas kernels, products(): pl.pallas_call(functools.partial(units_kernel, pairs, index_pairs, len(co...  9.84 us
    unnamed x8, local copies, waits for them, and re-layouts  3.46 us
  transfers between devices with their start and end apart: 25, of which 13 were waited for; matrix products, arithmetic and copies ran while one was open for 6% of the time, Pallas kernels for 1%

profile of v12, /device:TPU:12, one launch (start us, length us, event | category | flops | bytes accessed | tf_op | source)
XLA Modules:
  0.0 157.0 jit_solution(9419442000411372942)
XLA Ops:
  0.0 5.9 %collective-permute-start = (bf16[2,512,512]{2,1,0:T(8,128)(2,1)}, bf16[2,512,512]{2,1,0:T(8,128)(2,1)}, u32[]{:S(2)}, u32[]{:S(2)}) collective-permute-start(bf16[2,512,512]{2,1,0:T(8,128)(2,1)} %source.1), channel_id=1, source_target_pairs={{1,0},{2,1},{3,2},{4,3},{5,4},{6,5},{7,6},{0,7},{9,8},{10,9},{11,1... | collective-permute-start | bytes 3145736 | tf_op jit(solution)/shard_map/ppermute | solution.py:38
  5.9 2.3 %collective-permute-start.2 = (bf16[2,512,512]{2,1,0:T(8,128)(2,1)}, bf16[2,512,512]{2,1,0:T(8,128)(2,1)S(1)}, u32[]{:S(2)}, u32[]{:S(2)}) collective-permute-start(bf16[2,512,512]{2,1,0:T(8,128)(2,1)} %source.1), channel_id=1, source_target_pairs={{8,0},{9,1},{10,2},{11,3},{12,4},{13,5},{14,6},{15,7},{0,8},{1,9},... | collective-permute-start | bytes 3145736 | tf_op jit(solution)/shard_map/ppermute | solution.py:38
  8.2 1.3 copy-done
  10.2 18.4 %collective-permute-done.refs_1_ = bf16[2,512,512]{2,1,0:T(8,128)(2,1)} collective-permute-done((bf16[2,512,512]{2,1,0:T(8,128)(2,1)}, bf16[2,512,512]{2,1,0:T(8,128)(2,1)}, u32[]{:S(2)}, u32[]{:S(2)}) %collective-permute-start) | collective-permute-done | bytes 1048608 | tf_op jit(solution)/shard_map/ppermute | solution.py:38
  28.6 3.3 %collective-permute-done.1.refs_2_.refs_1_ = bf16[2,512,512]{2,1,0:T(8,128)(2,1)S(1)} collective-permute-done((bf16[2,512,512]{2,1,0:T(8,128)(2,1)}, bf16[2,512,512]{2,1,0:T(8,128)(2,1)S(1)}, u32[]{:S(2)}, u32[]{:S(2)}) %collective-permute-start.1) | collective-permute-done | bytes 1048608 | tf_op jit(solution)/shard_map/ppermute | solution.py:38
  32.2 4.4 %shard_map.65 = (f32[4,256,512]{2,1,0:T(8,128)S(1)}, f32[4,256,512]{2,1,0:T(8,128)S(1)}) custom-call(s32[20]{0:T(128)S(1)} %get-tuple-element.59.table, bf16[2,512,512]{2,1,0:T(8,128)(2,1)S(1)} %shard_map.64.refs_0_, bf16[2,512,512]{2,1,0:T(8,128)(2,1)} %collective-permute-done.refs_1_, bf16[2,512,512]{2,1,0:T(8,128)(2,1)S(1)} %collective-permute-done.1.refs_2_.refs_1_, ...), custom_call_target="tpu_custom_call" | custom-call | tf_op jit(solution)/shard_map/pallas_call | solution.py:242
  36.7 2.4 %collective-permute-start.10 = (bf16[2,512,512]{2,1,0:T(8,128)(2,1)}, bf16[2,512,512]{2,1,0:T(8,128)(2,1)S(1)}, u32[]{:S(2)}, u32[]{:S(2)}) collective-permute-start(bf16[2,512,512]{2,1,0:T(8,128)(2,1)} %collective-permute-done.refs_1_), channel_id=1, source_target_pairs={{8,0},{9,1},{10,2},{11,3},{12,4},{13,5},{14,6},{15,7},{0,8},{1,9},... | collective-permute-start | bytes 3145736 | tf_op jit(solution)/shard_map/ppermute | solution.py:38
  39.1 2.9 %collective-permute-start.8 = (bf16[2,512,512]{2,1,0:T(8,128)(2,1)}, bf16[2,512,512]{2,1,0:T(8,128)(2,1)}, u32[]{:S(2)}, u32[]{:S(2)}) collective-permute-start(bf16[2,512,512]{2,1,0:T(8,128)(2,1)} %collective-permute-done.refs_1_), channel_id=1, source_target_pairs={{1,0},{2,1},{3,2},{4,3},{5,4},{6,5},{7,6},{0,7},{9,8},{10,9},{11,1... | collective-permute-start | bytes 3145736 | tf_op jit(solution)/shard_map/ppermute | solution.py:38
  42.1 1.3 collective-permute-start.4
  44.6 5.7 %collective-permute-done.4 = f32[128,512]{1,0:T(8,128)S(1)} collective-permute-done((f32[128,512]{1,0:T(8,128)S(1)}, f32[128,512]{1,0:T(8,128)S(1)}, u32[]{:S(2)}, u32[]{:S(2)}) %collective-permute-start.4) | collective-permute-done | bytes 262176 | tf_op jit(solution)/shard_map/ppermute | solution.py:38
  50.4 1.3 collective-permute-start.5
  52.8 10.6 %collective-permute-done.5 = f32[256,512]{1,0:T(8,128)S(1)} collective-permute-done((f32[256,512]{1,0:T(8,128)S(1)}, f32[256,512]{1,0:T(8,128)S(1)}, u32[]{:S(2)}, u32[]{:S(2)}) %collective-permute-start.5) | collective-permute-done | bytes 524320 | tf_op jit(solution)/shard_map/ppermute | solution.py:38
  63.4 1.3 collective-permute-done.7
  65.7 2.5 %collective-permute-done.9.refs_3_.refs_0_ = bf16[2,512,512]{2,1,0:T(8,128)(2,1)S(1)} collective-permute-done((bf16[2,512,512]{2,1,0:T(8,128)(2,1)S(1)}, bf16[2,512,512]{2,1,0:T(8,128)(2,1)S(1)}, u32[]{:S(2)}, u32[]{:S(2)}) %collective-permute-start.9) | collective-permute-done | bytes 1048608 | tf_op jit(solution)/shard_map/ppermute | solution.py:38
  68.2 4.4 %shard_map.66 = (f32[4,256,512]{2,1,0:T(8,128)S(1)}, f32[4,256,512]{2,1,0:T(8,128)S(1)}) custom-call(s32[20]{0:T(128)S(1)} %get-tuple-element.60.table, bf16[2,512,512]{2,1,0:T(8,128)(2,1)S(1)} %shard_map.64.refs_0_, bf16[2,512,512]{2,1,0:T(8,128)(2,1)S(1)} %collective-permute-done.1.refs_2_.refs_1_, bf16[2,512,512]{2,1,0:T(8,128)(2,1)} %collective-permute-done.8.refs_2_, ...), custom_call_target="tpu_custom_call" | custom-call | tf_op jit(solution)/shard_map/pallas_call | solution.py:242
  72.7 1.3 collective-permute-start.12
  74.0 2.8 %collective-permute-done.11 = f32[4,256,512]{2,1,0:T(8,128)S(1)} collective-permute-done((f32[4,256,512]{2,1,0:T(8,128)S(1)}, f32[4,256,512]{2,1,0:T(8,128)S(1)}, u32[]{:S(2)}, u32[]{:S(2)}) %collective-permute-start.11) | collective-permute-done | bytes 2097184 | tf_op jit(solution)/shard_map/ppermute | solution.py:38
  76.9 1.4 fusion
  82.1 18.0 %collective-permute-done.12.refs_1_ = bf16[2,512,512]{2,1,0:T(8,128)(2,1)S(1)} collective-permute-done((bf16[2,512,512]{2,1,0:T(8,128)(2,1)}, bf16[2,512,512]{2,1,0:T(8,128)(2,1)S(1)}, u32[]{:S(2)}, u32[]{:S(2)}) %collective-permute-start.12) | collective-permute-done | bytes 1048608 | tf_op jit(solution)/shard_map/ppermute | solution.py:38
  103.2 1.7 %collective-permute-start.16 = (f32[256,512]{1,0:T(8,128)S(1)}, f32[256,512]{1,0:T(8,128)S(1)}, u32[]{:S(2)}, u32[]{:S(2)}) collective-permute-start(f32[256,512]{1,0:T(8,128)S(1)} %bitcast.41), channel_id=1, source_target_pairs={{32,48},{64,80},{96,112},{0,16},{160,176},{192,208},{224,240},{128... | collective-permute-start | bytes 1572872 | tf_op jit(solution)/shard_map/ppermute | solution.py:38
  104.9 1.3 dynamic_slice.16
  106.2 1.6 %add_add_fusion.1 = f32[256,512]{1,0:T(8,128)S(1)} fusion(f32[256,512]{1,0:T(8,128)} %collective-permute-done.14, f32[256,512]{1,0:T(8,128)} %collective-permute-done.15, f32[256,512]{1,0:T(8,128)S(1)} %get-tuple-element.39, f32[256,512]{1,0:T(8,128)} %collective-permute-done.13), kind=kLoop, calls=%fused_computation.19 | loop fusion | flops 393216 | bytes 2621440 | tf_op jit(solution)/shard_map/add | solution.py:350
  108.7 1.3 collective-permute-start.17
  112.1 1.3 dynamic_slice.15
  114.5 7.5 %collective-permute-done.17 = f32[256,512]{1,0:T(8,128)S(1)} collective-permute-done((f32[256,512]{1,0:T(8,128)S(1)}, f32[256,512]{1,0:T(8,128)S(1)}, u32[]{:S(2)}, u32[]{:S(2)}) %collective-permute-start.17) | collective-permute-done | bytes 524320 | tf_op jit(solution)/shard_map/ppermute | solution.py:38
  123.2 5.1 %collective-permute-start.21 = (f32[256,512]{1,0:T(8,128)S(1)}, f32[256,512]{1,0:T(8,128)S(1)}, u32[]{:S(2)}, u32[]{:S(2)}) collective-permute-start(f32[256,512]{1,0:T(8,128)S(1)} %get-tuple-element.57), channel_id=1, source_target_pairs={{128,128},{32,16},{160,114},{48,0},{64,113},{192,150},{96,135},{22... | collective-permute-start | bytes 1572872 | tf_op jit(solution)/shard_map/ppermute | solution.py:38
  128.3 1.3 collective-permute-start.22
  129.6 1.3 collective-permute-start.23
  130.9 1.3 collective-permute-start.24
  132.2 8.2 %collective-permute-done.21 = f32[256,512]{1,0:T(8,128)S(1)} collective-permute-done((f32[256,512]{1,0:T(8,128)S(1)}, f32[256,512]{1,0:T(8,128)S(1)}, u32[]{:S(2)}, u32[]{:S(2)}) %collective-permute-start.21) | collective-permute-done | bytes 524320 | tf_op jit(solution)/shard_map/ppermute | solution.py:38
  140.4 4.4 %collective-permute-done.22 = f32[256,512]{1,0:T(8,128)S(1)} collective-permute-done((f32[256,512]{1,0:T(8,128)S(1)}, f32[256,512]{1,0:T(8,128)S(1)}, u32[]{:S(2)}, u32[]{:S(2)}) %collective-permute-start.22) | collective-permute-done | bytes 524320 | tf_op jit(solution)/shard_map/ppermute | solution.py:38
  144.8 11.1 %collective-permute-done.23 = f32[256,512]{1,0:T(8,128)S(1)} collective-permute-done((f32[256,512]{1,0:T(8,128)S(1)}, f32[256,512]{1,0:T(8,128)S(1)}, u32[]{:S(2)}, u32[]{:S(2)}) %collective-permute-start.23) | collective-permute-done | bytes 524320 | tf_op jit(solution)/shard_map/ppermute | solution.py:38
  (53 shorter events, 17.0 us)
Async XLA Ops:
  0.0 28.6 %collective-permute-start = (bf16[2,512,512]{2,1,0:T(8,128)(2,1)}, bf16[2,512,512]{2,1,0:T(8,128)(2,1)}, u32[]{:S(2)}, u32[]{:S(2)}) collective-permute-start(bf16[2,512,512]{2,1,0:T(8,128)(2,1)} %source.1), channel_id=1, source_target_pairs={{1,0},{2,1},{3,2},{4,3},{5,4},{6,5},{7,6},{0,7},{9,8},{10,9},{11,1... | collective-permute-start | bytes 3145736 | tf_op jit(solution)/shard_map/ppermute | solution.py:38
  5.9 26.0 %collective-permute-start.1 = (bf16[2,512,512]{2,1,0:T(8,128)(2,1)}, bf16[2,512,512]{2,1,0:T(8,128)(2,1)S(1)}, u32[]{:S(2)}, u32[]{:S(2)}) collective-permute-start(bf16[2,512,512]{2,1,0:T(8,128)(2,1)} %source.1), channel_id=1, source_target_pairs={{7,0},{0,1},{1,2},{2,3},{3,4},{4,5},{5,6},{6,7},{15,8},{8,9},{9,10... | collective-permute-start | bytes 3145736 | tf_op jit(solution)/shard_map/ppermute | solution.py:38
  5.9 26.3 %collective-permute-start.2 = (bf16[2,512,512]{2,1,0:T(8,128)(2,1)}, bf16[2,512,512]{2,1,0:T(8,128)(2,1)S(1)}, u32[]{:S(2)}, u32[]{:S(2)}) collective-permute-start(bf16[2,512,512]{2,1,0:T(8,128)(2,1)} %source.1), channel_id=1, source_target_pairs={{8,0},{9,1},{10,2},{11,3},{12,4},{13,5},{14,6},{15,7},{0,8},{1,9},... | collective-permute-start | bytes 3145736 | tf_op jit(solution)/shard_map/ppermute | solution.py:38
  8.2 1.3 copy-start
  36.6 5.4 %collective-permute-start.3 = (f32[4,256,512]{2,1,0:T(8,128)S(1)}, f32[4,256,512]{2,1,0:T(8,128)S(1)}, u32[]{:S(2)}, u32[]{:S(2)}) collective-permute-start(f32[4,256,512]{2,1,0:T(8,128)S(1)} %get-tuple-element.32), channel_id=1, source_target_pairs={{16,0},{17,1},{18,2},{19,3},{20,4},{21,5},{22,6},{23,7},{24,8},{25... | collective-permute-start | bytes 6291464 | tf_op jit(solution)/shard_map/ppermute | solution.py:38
  36.7 29.0 %collective-permute-start.10 = (bf16[2,512,512]{2,1,0:T(8,128)(2,1)}, bf16[2,512,512]{2,1,0:T(8,128)(2,1)S(1)}, u32[]{:S(2)}, u32[]{:S(2)}) collective-permute-start(bf16[2,512,512]{2,1,0:T(8,128)(2,1)} %collective-permute-done.refs_1_), channel_id=1, source_target_pairs={{8,0},{9,1},{10,2},{11,3},{12,4},{13,5},{14,6},{15,7},{0,8},{1,9},... | collective-permute-start | bytes 3145736 | tf_op jit(solution)/shard_map/ppermute | solution.py:38
  39.1 26.6 %collective-permute-start.8 = (bf16[2,512,512]{2,1,0:T(8,128)(2,1)}, bf16[2,512,512]{2,1,0:T(8,128)(2,1)}, u32[]{:S(2)}, u32[]{:S(2)}) collective-permute-start(bf16[2,512,512]{2,1,0:T(8,128)(2,1)} %collective-permute-done.refs_1_), channel_id=1, source_target_pairs={{1,0},{2,1},{3,2},{4,3},{5,4},{6,5},{7,6},{0,7},{9,8},{10,9},{11,1... | collective-permute-start | bytes 3145736 | tf_op jit(solution)/shard_map/ppermute | solution.py:38
  42.1 26.1 %collective-permute-start.9 = (bf16[2,512,512]{2,1,0:T(8,128)(2,1)S(1)}, bf16[2,512,512]{2,1,0:T(8,128)(2,1)S(1)}, u32[]{:S(2)}, u32[]{:S(2)}) collective-permute-start(bf16[2,512,512]{2,1,0:T(8,128)(2,1)S(1)} %collective-permute-done.1.refs_2_.refs_1_), channel_id=1, source_target_pairs={{7,0},{0,1},{1,2},{2,3},{3,4},{4,5},{5,6},{6,7},{15,8},{8,9},{9,10... | collective-permute-start | bytes 3145736 | tf_op jit(solution)/shard_map/ppermute | solution.py:38
  42.1 8.2 %collective-permute-start.4 = (f32[128,512]{1,0:T(8,128)S(1)}, f32[128,512]{1,0:T(8,128)S(1)}, u32[]{:S(2)}, u32[]{:S(2)}) collective-permute-start(f32[128,512]{1,0:T(8,128)S(1)} %get-tuple-element.53), channel_id=1, source_target_pairs={{96,0},{97,1},{98,2},{99,3},{100,4},{101,5},{102,6},{103,7},{104,8... | collective-permute-start | bytes 786440 | tf_op jit(solution)/shard_map/ppermute | solution.py:38
  43.7 8.0 %collective-permute-start.6 = (f32[128,512]{1,0:T(8,128)S(1)}, f32[128,512]{1,0:T(8,128)S(1)}, u32[]{:S(2)}, u32[]{:S(2)}) collective-permute-start(f32[128,512]{1,0:T(8,128)S(1)} %get-tuple-element.54), channel_id=1, source_target_pairs={{32,0},{33,1},{34,2},{35,3},{36,4},{37,5},{38,6},{39,7},{40,8},{41... | collective-permute-start | bytes 786440 | tf_op jit(solution)/shard_map/ppermute | solution.py:38
  50.4 13.0 %collective-permute-start.5 = (f32[256,512]{1,0:T(8,128)S(1)}, f32[256,512]{1,0:T(8,128)S(1)}, u32[]{:S(2)}, u32[]{:S(2)}) collective-permute-start(f32[256,512]{1,0:T(8,128)S(1)} %pad_maximum_fusion.1), channel_id=1, source_target_pairs={{96,0},{97,1},{98,2},{99,3},{100,4},{101,5},{102,6},{103,7},{104,8... | collective-permute-start | bytes 1572872 | tf_op jit(solution)/shard_map/ppermute | solution.py:38
  51.7 12.9 %collective-permute-start.7 = (f32[256,512]{1,0:T(8,128)S(1)}, f32[256,512]{1,0:T(8,128)S(1)}, u32[]{:S(2)}, u32[]{:S(2)}) collective-permute-start(f32[256,512]{1,0:T(8,128)S(1)} %pad_maximum_fusion.2), channel_id=1, source_target_pairs={{32,0},{33,1},{34,2},{35,3},{36,4},{37,5},{38,6},{39,7},{40,8},{41... | collective-permute-start | bytes 1572872 | tf_op jit(solution)/shard_map/ppermute | solution.py:38
  72.6 4.2 %collective-permute-start.11 = (f32[4,256,512]{2,1,0:T(8,128)S(1)}, f32[4,256,512]{2,1,0:T(8,128)S(1)}, u32[]{:S(2)}, u32[]{:S(2)}) collective-permute-start(f32[4,256,512]{2,1,0:T(8,128)S(1)} %get-tuple-element.38), channel_id=1, source_target_pairs={{16,0},{17,1},{18,2},{19,3},{20,4},{21,5},{22,6},{23,7},{24,8},{25... | collective-permute-start | bytes 6291464 | tf_op jit(solution)/shard_map/ppermute | solution.py:38
  72.7 27.3 %collective-permute-start.12 = (bf16[2,512,512]{2,1,0:T(8,128)(2,1)}, bf16[2,512,512]{2,1,0:T(8,128)(2,1)S(1)}, u32[]{:S(2)}, u32[]{:S(2)}) collective-permute-start(bf16[2,512,512]{2,1,0:T(8,128)(2,1)} %collective-permute-done.8.refs_2_), channel_id=1, source_target_pairs={{8,0},{9,1},{10,2},{11,3},{12,4},{13,5},{14,6},{15,7},{0,8},{1,9},... | collective-permute-start | bytes 3145736 | tf_op jit(solution)/shard_map/ppermute | solution.py:38
  78.2 22.8 %collective-permute-start.13 = (f32[256,512]{1,0:T(8,128)}, f32[256,512]{1,0:T(8,128)}, u32[]{:S(2)}, u32[]{:S(2)}) collective-permute-start(f32[256,512]{1,0:T(8,128)} %get-tuple-element.40), channel_id=1, source_target_pairs={{96,0},{97,1},{98,2},{99,3},{100,4},{101,5},{102,6},{103,7},{104,8... | collective-permute-start | bytes 1572872 | tf_op jit(solution)/shard_map/ppermute | solution.py:38
  79.4 26.8 %collective-permute-start.14 = (f32[256,512]{1,0:T(8,128)}, f32[256,512]{1,0:T(8,128)}, u32[]{:S(2)}, u32[]{:S(2)}) collective-permute-start(f32[256,512]{1,0:T(8,128)} %get-tuple-element.42), channel_id=1, source_target_pairs={{64,0},{65,1},{66,2},{67,3},{68,4},{69,5},{70,6},{71,7},{72,8},{73... | collective-permute-start | bytes 1572872 | tf_op jit(solution)/shard_map/ppermute | solution.py:38
  80.2 26.0 %collective-permute-start.15 = (f32[256,512]{1,0:T(8,128)}, f32[256,512]{1,0:T(8,128)}, u32[]{:S(2)}, u32[]{:S(2)}) collective-permute-start(f32[256,512]{1,0:T(8,128)} %get-tuple-element.43), channel_id=1, source_target_pairs={{32,0},{33,1},{34,2},{35,3},{36,4},{37,5},{38,6},{39,7},{40,8},{41... | collective-permute-start | bytes 1572872 | tf_op jit(solution)/shard_map/ppermute | solution.py:38
  100.0 1.0 copy-start.1
  101.0 1.2 copy-start.2
  103.2 4.6 %collective-permute-start.16 = (f32[256,512]{1,0:T(8,128)S(1)}, f32[256,512]{1,0:T(8,128)S(1)}, u32[]{:S(2)}, u32[]{:S(2)}) collective-permute-start(f32[256,512]{1,0:T(8,128)S(1)} %bitcast.41), channel_id=1, source_target_pairs={{32,48},{64,80},{96,112},{0,16},{160,176},{192,208},{224,240},{128... | collective-permute-start | bytes 1572872 | tf_op jit(solution)/shard_map/ppermute | solution.py:38
  106.2 1.8 %copy-start.3 = (f32[256,512]{1,0:T(8,128)S(1)}, f32[256,512]{1,0:T(8,128)}, u32[]{:S(2)}) copy-start(f32[256,512]{1,0:T(8,128)} %fusion.6) | copy-start | bytes 1572868
  108.7 13.3 %collective-permute-start.17 = (f32[256,512]{1,0:T(8,128)S(1)}, f32[256,512]{1,0:T(8,128)S(1)}, u32[]{:S(2)}, u32[]{:S(2)}) collective-permute-start(f32[256,512]{1,0:T(8,128)S(1)} %broadcast_select_fusion.1), channel_id=1, source_target_pairs={{128,0},{129,1},{130,2},{131,3},{132,4},{133,5},{134,6},{135,7},{1... | collective-permute-start | bytes 1572872 | tf_op jit(solution)/shard_map/ppermute | solution.py:38
  110.0 12.7 %collective-permute-start.18 = (f32[256,512]{1,0:T(8,128)S(1)}, f32[256,512]{1,0:T(8,128)S(1)}, u32[]{:S(2)}, u32[]{:S(2)}) collective-permute-start(f32[256,512]{1,0:T(8,128)S(1)} %bitcast_add_fusion), channel_id=1, source_target_pairs={{14,78},{18,82},{19,83},{31,95},{40,104},{41,105},{52,116},{53,117... | collective-permute-start | bytes 1572872 | tf_op jit(solution)/shard_map/ppermute | solution.py:38
  110.7 12.1 %collective-permute-start.19 = (f32[256,512]{1,0:T(8,128)S(1)}, f32[256,512]{1,0:T(8,128)S(1)}, u32[]{:S(2)}, u32[]{:S(2)}) collective-permute-start(f32[256,512]{1,0:T(8,128)S(1)} %bitcast_add_fusion), channel_id=1, source_target_pairs={{8,104},{9,105},{20,116},{21,117},{42,10},{43,11},{54,22},{55,23},... | collective-permute-start | bytes 1572872 | tf_op jit(solution)/shard_map/ppermute | solution.py:38
  111.4 11.4 %collective-permute-start.20 = (f32[256,512]{1,0:T(8,128)S(1)}, f32[256,512]{1,0:T(8,128)S(1)}, u32[]{:S(2)}, u32[]{:S(2)}) collective-permute-start(f32[256,512]{1,0:T(8,128)S(1)} %bitcast_add_fusion), channel_id=1, source_target_pairs={{12,44},{13,45},{16,48},{17,49},{46,78},{50,82},{51,83},{63,95},{7... | collective-permute-start | bytes 1572872 | tf_op jit(solution)/shard_map/ppermute | solution.py:38
  123.2 17.2 %collective-permute-start.21 = (f32[256,512]{1,0:T(8,128)S(1)}, f32[256,512]{1,0:T(8,128)S(1)}, u32[]{:S(2)}, u32[]{:S(2)}) collective-permute-start(f32[256,512]{1,0:T(8,128)S(1)} %get-tuple-element.57), channel_id=1, source_target_pairs={{128,128},{32,16},{160,114},{48,0},{64,113},{192,150},{96,135},{22... | collective-permute-start | bytes 1572872 | tf_op jit(solution)/shard_map/ppermute | solution.py:38
  128.3 16.5 %collective-permute-start.22 = (f32[256,512]{1,0:T(8,128)S(1)}, f32[256,512]{1,0:T(8,128)S(1)}, u32[]{:S(2)}, u32[]{:S(2)}) collective-permute-start(f32[256,512]{1,0:T(8,128)S(1)} %add_add_fusion), channel_id=1, source_target_pairs={{48,166},{177,183},{82,192},{211,209},{244,226},{117,243},{150,132... | collective-permute-start | bytes 1572872 | tf_op jit(solution)/shard_map/ppermute | solution.py:38
  129.6 26.3 %collective-permute-start.23 = (f32[256,512]{1,0:T(8,128)S(1)}, f32[256,512]{1,0:T(8,128)S(1)}, u32[]{:S(2)}, u32[]{:S(2)}) collective-permute-start(f32[256,512]{1,0:T(8,128)S(1)} %get-tuple-element.58), channel_id=1, source_target_pairs={{0,98},{144,135},{16,151},{176,0},{208,113},{80,114},{112,16},{240... | collective-permute-start | bytes 1572872 | tf_op jit(solution)/shard_map/ppermute | solution.py:38
  130.9 25.0 %collective-permute-start.24 = (f32[256,512]{1,0:T(8,128)S(1)}, f32[256,512]{1,0:T(8,128)S(1)}, u32[]{:S(2)}, u32[]{:S(2)}) collective-permute-start(f32[256,512]{1,0:T(8,128)S(1)} %add_add_fusion), channel_id=1, source_target_pairs={{104,226},{233,243},{138,132},{139,149},{172,166},{173,183},{206,1... | collective-permute-start | bytes 1572872 | tf_op jit(solution)/shard_map/ppermute | solution.py:38

commit v13 on v12

--- a/solution.py
+++ b/solution.py
@@ -132,9 +132,8 @@
                 for link, share in on(own, batch, place, at[own][batch][place], planes[own][place]):
                     load[link] += share
         for unit in units_of(PAIRS_C, h, z):
-            for y in (0, 1):
-                for link, share in links(own, unit[2] % 8, y, unit):
-                    load[link] += share
+            for link, share in links(own, unit[2] % 8, 1 - h, unit):
+                load[link] += share
     for _ in range(trials):
         own, batch, u, v = draw.randrange(GROUPS), draw.randrange(2), draw.randrange(8), draw.randrange(8)
         if (u - v) % 2:
@@ -167,7 +166,6 @@
     table_c = np.zeros((GROUPS, 4), np.int32)
     target_c = {}
     final = {half: [] for half in (0, 1)}
-    final_c = {half: [] for half in (0, 1)}
     halves = np.zeros((16, GROUPS), np.int32)
     first = np.zeros((16, GROUPS), np.bool_)
     units, at, planes = spread()
@@ -200,8 +198,7 @@
             )
             target_c[own] = (y, x, core)
             final[half].append((device(y, x, core, own), col * GROUPS + row))
-            final_c[half].append((device(1 - y, x, core, own), col * GROUPS + row))
-    return tables.reshape(2, 16 * GROUPS, 20), table_c, target_c, first, halves, final, final_c
+    return tables.reshape(2, 16 * GROUPS, 20), table_c, target_c, first, halves, final
 
 
 def dot_t(a, b):
@@ -290,6 +287,11 @@
     return value + parts[0] + (parts[1] + parts[2])
 
 
+def one_y(value, targets):
+    pairs = [(device(1 - y, x, c, b), device(y, x, c, b)) for b, (y, x, c) in targets.items()]
+    return value + send(value, pairs)
+
+
 Y_SWAP = every(lambda y, x, c, h, z: (1 - y, x, c, block(h, z)))
 CORE_SWAP = every(lambda y, x, c, h, z: (y, x, 1 - c, block(h, z)))
 FROM_LEFT = every(lambda y, x, c, h, z: (y, x - 1, c, block(h, z)))
@@ -320,7 +322,7 @@
 
 
 def per_device(half_b):
-    local, codes_c, target_c, first, halves, final, final_c = plan()
+    local, codes_c, target_c, first, halves, final = plan()
     aux, blk = lax.axis_index("aux"), lax.axis_index("blk")
     place = aux * GROUPS + blk
     table_a, table_b = jnp.asarray(local[0])[place], jnp.asarray(local[1])[place]
@@ -351,12 +353,12 @@
 
     has_first = jnp.asarray(first)[aux, blk]
     done = jnp.where(has_first, total_a, total_b) + send(jnp.where(has_first, total_b, total_a), Y_SWAP)
-    part_c = one_x(part_c, target_c)
+    part_c = one_y(one_x(part_c, target_c), target_c)
     done, part_c = together(done, part_c)
 
     own_half = jnp.asarray(halves)[aux, blk]
-    top = send(jnp.where(own_half == 0, done, part_c), final[0]) + send(part_c, final_c[0])
-    bottom = send(jnp.where(own_half == 1, done, part_c), final[1]) + send(part_c, final_c[1])
+    top = send(jnp.where(own_half == 0, done, part_c), final[0])
+    bottom = send(jnp.where(own_half == 1, done, part_c), final[1])
     return jnp.concatenate([top, bottom], 0)
 
 

time: 159 us -> 163 us (1.025)
  waiting for transfers between devices: 93.9 us -> 98.1 us
  starting transfers between devices: 36.7 us -> 40.1 us
  local copies, waits for them, and re-layouts: 7.44 us -> 5.26 us
    ppermute x25 -> x24, waiting for transfers between devices: 93.9 us -> 98.1 us  [send(): return lax.ppermute(value, ALL, pairs)]
    ppermute x25 -> x24, starting transfers between devices: 36.7 us -> 40.1 us  [send(): return lax.ppermute(value, ALL, pairs)]
    unnamed x8 -> x4, local copies, waits for them, and re-layouts: 3.46 us -> 1.26 us
  transfers between devices with their start and end apart: 25 -> 24, of which waited for: 13 -> 14; matrix products, arithmetic and copies ran while one was open for 6% -> 6% of each run, Pallas kernels for 1% -> 1%
where the time goes in v13:
time: 163 us; the launch traced here: 162 us
  waiting for transfers between devices  98.1 us (60%)
  starting transfers between devices  40.1 us (25%)
  Pallas kernels  9.91 us (6%)
  other arithmetic  7.47 us (5%)
  local copies, waits for them, and re-layouts  5.26 us (3%)
    ppermute x24, waiting for transfers between devices, send(): return lax.ppermute(value, ALL, pairs)  98.1 us
    ppermute x24, starting transfers between devices, send(): return lax.ppermute(value, ALL, pairs)  40.1 us
    pallas_call x3, Pallas kernels, products(): pl.pallas_call(functools.partial(units_kernel, pairs, index_pairs, len(co...  9.85 us
  transfers between devices with their start and end apart: 24, of which 14 were waited for; matrix products, arithmetic and copies ran while one was open for 6% of the time, Pallas kernels for 1%

profile of v13, /device:TPU:12, one launch (start us, length us, event | category | flops | bytes accessed | tf_op | source)
XLA Modules:
  0.0 162.2 jit_solution(14762617996682696755)
XLA Ops:
  0.0 5.9 %collective-permute-start = (bf16[2,512,512]{2,1,0:T(8,128)(2,1)}, bf16[2,512,512]{2,1,0:T(8,128)(2,1)}, u32[]{:S(2)}, u32[]{:S(2)}) collective-permute-start(bf16[2,512,512]{2,1,0:T(8,128)(2,1)} %source.1), channel_id=1, source_target_pairs={{1,0},{2,1},{3,2},{4,3},{5,4},{6,5},{7,6},{0,7},{9,8},{10,9},{11,1... | collective-permute-start | bytes 3145736 | tf_op jit(solution)/shard_map/ppermute | solution.py:38
  5.9 2.3 %collective-permute-start.2 = (bf16[2,512,512]{2,1,0:T(8,128)(2,1)}, bf16[2,512,512]{2,1,0:T(8,128)(2,1)S(1)}, u32[]{:S(2)}, u32[]{:S(2)}) collective-permute-start(bf16[2,512,512]{2,1,0:T(8,128)(2,1)} %source.1), channel_id=1, source_target_pairs={{8,0},{9,1},{10,2},{11,3},{12,4},{13,5},{14,6},{15,7},{0,8},{1,9},... | collective-permute-start | bytes 3145736 | tf_op jit(solution)/shard_map/ppermute | solution.py:38
  8.2 1.3 copy-done
  10.2 18.4 %collective-permute-done.refs_1_ = bf16[2,512,512]{2,1,0:T(8,128)(2,1)} collective-permute-done((bf16[2,512,512]{2,1,0:T(8,128)(2,1)}, bf16[2,512,512]{2,1,0:T(8,128)(2,1)}, u32[]{:S(2)}, u32[]{:S(2)}) %collective-permute-start) | collective-permute-done | bytes 1048608 | tf_op jit(solution)/shard_map/ppermute | solution.py:38
  28.6 3.3 %collective-permute-done.1.refs_2_.refs_1_ = bf16[2,512,512]{2,1,0:T(8,128)(2,1)S(1)} collective-permute-done((bf16[2,512,512]{2,1,0:T(8,128)(2,1)}, bf16[2,512,512]{2,1,0:T(8,128)(2,1)S(1)}, u32[]{:S(2)}, u32[]{:S(2)}) %collective-permute-start.1) | collective-permute-done | bytes 1048608 | tf_op jit(solution)/shard_map/ppermute | solution.py:38
  32.2 4.4 %shard_map.65 = (f32[4,256,512]{2,1,0:T(8,128)S(1)}, f32[4,256,512]{2,1,0:T(8,128)S(1)}) custom-call(s32[20]{0:T(128)S(1)} %get-tuple-element.59.table, bf16[2,512,512]{2,1,0:T(8,128)(2,1)S(1)} %shard_map.64.refs_0_, bf16[2,512,512]{2,1,0:T(8,128)(2,1)} %collective-permute-done.refs_1_, bf16[2,512,512]{2,1,0:T(8,128)(2,1)S(1)} %collective-permute-done.1.refs_2_.refs_1_, ...), custom_call_target="tpu_custom_call" | custom-call | tf_op jit(solution)/shard_map/pallas_call | solution.py:239
  36.7 2.4 %collective-permute-start.10 = (bf16[2,512,512]{2,1,0:T(8,128)(2,1)}, bf16[2,512,512]{2,1,0:T(8,128)(2,1)S(1)}, u32[]{:S(2)}, u32[]{:S(2)}) collective-permute-start(bf16[2,512,512]{2,1,0:T(8,128)(2,1)} %collective-permute-done.refs_1_), channel_id=1, source_target_pairs={{8,0},{9,1},{10,2},{11,3},{12,4},{13,5},{14,6},{15,7},{0,8},{1,9},... | collective-permute-start | bytes 3145736 | tf_op jit(solution)/shard_map/ppermute | solution.py:38
  39.1 2.9 %collective-permute-start.8 = (bf16[2,512,512]{2,1,0:T(8,128)(2,1)}, bf16[2,512,512]{2,1,0:T(8,128)(2,1)}, u32[]{:S(2)}, u32[]{:S(2)}) collective-permute-start(bf16[2,512,512]{2,1,0:T(8,128)(2,1)} %collective-permute-done.refs_1_), channel_id=1, source_target_pairs={{1,0},{2,1},{3,2},{4,3},{5,4},{6,5},{7,6},{0,7},{9,8},{10,9},{11,1... | collective-permute-start | bytes 3145736 | tf_op jit(solution)/shard_map/ppermute | solution.py:38
  42.1 1.3 collective-permute-start.4
  44.6 5.7 %collective-permute-done.4 = f32[128,512]{1,0:T(8,128)S(1)} collective-permute-done((f32[128,512]{1,0:T(8,128)S(1)}, f32[128,512]{1,0:T(8,128)S(1)}, u32[]{:S(2)}, u32[]{:S(2)}) %collective-permute-start.4) | collective-permute-done | bytes 262176 | tf_op jit(solution)/shard_map/ppermute | solution.py:38
  50.4 1.3 collective-permute-start.5
  52.8 10.6 %collective-permute-done.5 = f32[256,512]{1,0:T(8,128)S(1)} collective-permute-done((f32[256,512]{1,0:T(8,128)S(1)}, f32[256,512]{1,0:T(8,128)S(1)}, u32[]{:S(2)}, u32[]{:S(2)}) %collective-permute-start.5) | collective-permute-done | bytes 524320 | tf_op jit(solution)/shard_map/ppermute | solution.py:38
  63.4 1.3 collective-permute-done.7
  65.7 2.5 %collective-permute-done.9.refs_3_.refs_0_ = bf16[2,512,512]{2,1,0:T(8,128)(2,1)S(1)} collective-permute-done((bf16[2,512,512]{2,1,0:T(8,128)(2,1)S(1)}, bf16[2,512,512]{2,1,0:T(8,128)(2,1)S(1)}, u32[]{:S(2)}, u32[]{:S(2)}) %collective-permute-start.9) | collective-permute-done | bytes 1048608 | tf_op jit(solution)/shard_map/ppermute | solution.py:38
  68.2 4.4 %shard_map.66 = (f32[4,256,512]{2,1,0:T(8,128)S(1)}, f32[4,256,512]{2,1,0:T(8,128)S(1)}) custom-call(s32[20]{0:T(128)S(1)} %get-tuple-element.60.table, bf16[2,512,512]{2,1,0:T(8,128)(2,1)S(1)} %shard_map.64.refs_0_, bf16[2,512,512]{2,1,0:T(8,128)(2,1)S(1)} %collective-permute-done.1.refs_2_.refs_1_, bf16[2,512,512]{2,1,0:T(8,128)(2,1)} %collective-permute-done.8.refs_2_, ...), custom_call_target="tpu_custom_call" | custom-call | tf_op jit(solution)/shard_map/pallas_call | solution.py:239
  72.7 1.3 collective-permute-start.12
  74.0 2.8 %collective-permute-done.11 = f32[4,256,512]{2,1,0:T(8,128)S(1)} collective-permute-done((f32[4,256,512]{2,1,0:T(8,128)S(1)}, f32[4,256,512]{2,1,0:T(8,128)S(1)}, u32[]{:S(2)}, u32[]{:S(2)}) %collective-permute-start.11) | collective-permute-done | bytes 2097184 | tf_op jit(solution)/shard_map/ppermute | solution.py:38
  76.9 1.4 fusion
  78.2 1.2 collective-permute-start.13
  80.2 1.1 collective-permute-start.15
  82.1 17.9 %collective-permute-done.12.refs_1_ = bf16[2,512,512]{2,1,0:T(8,128)(2,1)S(1)} collective-permute-done((bf16[2,512,512]{2,1,0:T(8,128)(2,1)}, bf16[2,512,512]{2,1,0:T(8,128)(2,1)S(1)}, u32[]{:S(2)}, u32[]{:S(2)}) %collective-permute-start.12) | collective-permute-done | bytes 1048608 | tf_op jit(solution)/shard_map/ppermute | solution.py:38
  101.1 1.8 %collective-permute-start.16 = (f32[256,512]{1,0:T(8,128)S(1)}, f32[256,512]{1,0:T(8,128)S(1)}, u32[]{:S(2)}, u32[]{:S(2)}) collective-permute-start(f32[256,512]{1,0:T(8,128)S(1)} %bitcast.41), channel_id=1, source_target_pairs={{32,48},{64,80},{96,112},{0,16},{160,176},{192,208},{224,240},{128... | collective-permute-start | bytes 1572872 | tf_op jit(solution)/shard_map/ppermute | solution.py:38
  103.8 1.8 %collective-permute-done.15 = f32[256,512]{1,0:T(8,128)} collective-permute-done((f32[256,512]{1,0:T(8,128)}, f32[256,512]{1,0:T(8,128)}, u32[]{:S(2)}, u32[]{:S(2)}) %collective-permute-start.15) | collective-permute-done | bytes 524320 | tf_op jit(solution)/shard_map/ppermute | solution.py:38
  105.6 1.6 add_add_fusion.1
  109.4 1.3 dynamic_slice.16
  111.4 1.4 collective-permute-start.17
  113.8 1.3 dynamic_slice.15
  116.2 9.5 %collective-permute-done.17 = f32[256,512]{1,0:T(8,128)S(1)} collective-permute-done((f32[256,512]{1,0:T(8,128)S(1)}, f32[256,512]{1,0:T(8,128)S(1)}, u32[]{:S(2)}, u32[]{:S(2)}) %collective-permute-start.17) | collective-permute-done | bytes 524320 | tf_op jit(solution)/shard_map/ppermute | solution.py:38
  126.8 10.1 %collective-permute-start.22 = (f32[256,512]{1,0:T(8,128)S(1)}, f32[256,512]{1,0:T(8,128)S(1)}, u32[]{:S(2)}, u32[]{:S(2)}) collective-permute-start(f32[256,512]{1,0:T(8,128)S(1)} %get-tuple-element.57), channel_id=1, source_target_pairs={{128,128},{32,16},{160,114},{64,113},{192,151},{224,135},{96,150},... | collective-permute-start | bytes 1572872 | tf_op jit(solution)/shard_map/ppermute | solution.py:38
  136.8 1.3 collective-permute-start.23
  138.1 10.9 %collective-permute-done.22 = f32[256,512]{1,0:T(8,128)S(1)} collective-permute-done((f32[256,512]{1,0:T(8,128)S(1)}, f32[256,512]{1,0:T(8,128)S(1)}, u32[]{:S(2)}, u32[]{:S(2)}) %collective-permute-start.22) | collective-permute-done | bytes 524320 | tf_op jit(solution)/shard_map/ppermute | solution.py:38
  149.0 12.1 %collective-permute-done.23 = f32[256,512]{1,0:T(8,128)S(1)} collective-permute-done((f32[256,512]{1,0:T(8,128)S(1)}, f32[256,512]{1,0:T(8,128)S(1)}, u32[]{:S(2)}, u32[]{:S(2)}) %collective-permute-start.23) | collective-permute-done | bytes 524320 | tf_op jit(solution)/shard_map/ppermute | solution.py:38
  (46 shorter events, 14.0 us)
Async XLA Ops:
  0.0 28.6 %collective-permute-start = (bf16[2,512,512]{2,1,0:T(8,128)(2,1)}, bf16[2,512,512]{2,1,0:T(8,128)(2,1)}, u32[]{:S(2)}, u32[]{:S(2)}) collective-permute-start(bf16[2,512,512]{2,1,0:T(8,128)(2,1)} %source.1), channel_id=1, source_target_pairs={{1,0},{2,1},{3,2},{4,3},{5,4},{6,5},{7,6},{0,7},{9,8},{10,9},{11,1... | collective-permute-start | bytes 3145736 | tf_op jit(solution)/shard_map/ppermute | solution.py:38
  5.9 26.0 %collective-permute-start.1 = (bf16[2,512,512]{2,1,0:T(8,128)(2,1)}, bf16[2,512,512]{2,1,0:T(8,128)(2,1)S(1)}, u32[]{:S(2)}, u32[]{:S(2)}) collective-permute-start(bf16[2,512,512]{2,1,0:T(8,128)(2,1)} %source.1), channel_id=1, source_target_pairs={{7,0},{0,1},{1,2},{2,3},{3,4},{4,5},{5,6},{6,7},{15,8},{8,9},{9,10... | collective-permute-start | bytes 3145736 | tf_op jit(solution)/shard_map/ppermute | solution.py:38
  5.9 26.3 %collective-permute-start.2 = (bf16[2,512,512]{2,1,0:T(8,128)(2,1)}, bf16[2,512,512]{2,1,0:T(8,128)(2,1)S(1)}, u32[]{:S(2)}, u32[]{:S(2)}) collective-permute-start(bf16[2,512,512]{2,1,0:T(8,128)(2,1)} %source.1), channel_id=1, source_target_pairs={{8,0},{9,1},{10,2},{11,3},{12,4},{13,5},{14,6},{15,7},{0,8},{1,9},... | collective-permute-start | bytes 3145736 | tf_op jit(solution)/shard_map/ppermute | solution.py:38
  8.2 1.3 copy-start
  36.6 5.4 %collective-permute-start.3 = (f32[4,256,512]{2,1,0:T(8,128)S(1)}, f32[4,256,512]{2,1,0:T(8,128)S(1)}, u32[]{:S(2)}, u32[]{:S(2)}) collective-permute-start(f32[4,256,512]{2,1,0:T(8,128)S(1)} %get-tuple-element.32), channel_id=1, source_target_pairs={{16,0},{17,1},{18,2},{19,3},{20,4},{21,5},{22,6},{23,7},{24,8},{25... | collective-permute-start | bytes 6291464 | tf_op jit(solution)/shard_map/ppermute | solution.py:38
  36.7 29.0 %collective-permute-start.10 = (bf16[2,512,512]{2,1,0:T(8,128)(2,1)}, bf16[2,512,512]{2,1,0:T(8,128)(2,1)S(1)}, u32[]{:S(2)}, u32[]{:S(2)}) collective-permute-start(bf16[2,512,512]{2,1,0:T(8,128)(2,1)} %collective-permute-done.refs_1_), channel_id=1, source_target_pairs={{8,0},{9,1},{10,2},{11,3},{12,4},{13,5},{14,6},{15,7},{0,8},{1,9},... | collective-permute-start | bytes 3145736 | tf_op jit(solution)/shard_map/ppermute | solution.py:38
  39.1 26.6 %collective-permute-start.8 = (bf16[2,512,512]{2,1,0:T(8,128)(2,1)}, bf16[2,512,512]{2,1,0:T(8,128)(2,1)}, u32[]{:S(2)}, u32[]{:S(2)}) collective-permute-start(bf16[2,512,512]{2,1,0:T(8,128)(2,1)} %collective-permute-done.refs_1_), channel_id=1, source_target_pairs={{1,0},{2,1},{3,2},{4,3},{5,4},{6,5},{7,6},{0,7},{9,8},{10,9},{11,1... | collective-permute-start | bytes 3145736 | tf_op jit(solution)/shard_map/ppermute | solution.py:38
  42.1 26.1 %collective-permute-start.9 = (bf16[2,512,512]{2,1,0:T(8,128)(2,1)S(1)}, bf16[2,512,512]{2,1,0:T(8,128)(2,1)S(1)}, u32[]{:S(2)}, u32[]{:S(2)}) collective-permute-start(bf16[2,512,512]{2,1,0:T(8,128)(2,1)S(1)} %collective-permute-done.1.refs_2_.refs_1_), channel_id=1, source_target_pairs={{7,0},{0,1},{1,2},{2,3},{3,4},{4,5},{5,6},{6,7},{15,8},{8,9},{9,10... | collective-permute-start | bytes 3145736 | tf_op jit(solution)/shard_map/ppermute | solution.py:38
  42.1 8.2 %collective-permute-start.4 = (f32[128,512]{1,0:T(8,128)S(1)}, f32[128,512]{1,0:T(8,128)S(1)}, u32[]{:S(2)}, u32[]{:S(2)}) collective-permute-start(f32[128,512]{1,0:T(8,128)S(1)} %get-tuple-element.53), channel_id=1, source_target_pairs={{96,0},{97,1},{98,2},{99,3},{100,4},{101,5},{102,6},{103,7},{104,8... | collective-permute-start | bytes 786440 | tf_op jit(solution)/shard_map/ppermute | solution.py:38
  43.7 8.0 %collective-permute-start.6 = (f32[128,512]{1,0:T(8,128)S(1)}, f32[128,512]{1,0:T(8,128)S(1)}, u32[]{:S(2)}, u32[]{:S(2)}) collective-permute-start(f32[128,512]{1,0:T(8,128)S(1)} %get-tuple-element.54), channel_id=1, source_target_pairs={{32,0},{33,1},{34,2},{35,3},{36,4},{37,5},{38,6},{39,7},{40,8},{41... | collective-permute-start | bytes 786440 | tf_op jit(solution)/shard_map/ppermute | solution.py:38
  50.4 13.0 %collective-permute-start.5 = (f32[256,512]{1,0:T(8,128)S(1)}, f32[256,512]{1,0:T(8,128)S(1)}, u32[]{:S(2)}, u32[]{:S(2)}) collective-permute-start(f32[256,512]{1,0:T(8,128)S(1)} %pad_maximum_fusion.1), channel_id=1, source_target_pairs={{96,0},{97,1},{98,2},{99,3},{100,4},{101,5},{102,6},{103,7},{104,8... | collective-permute-start | bytes 1572872 | tf_op jit(solution)/shard_map/ppermute | solution.py:38
  51.7 12.9 %collective-permute-start.7 = (f32[256,512]{1,0:T(8,128)S(1)}, f32[256,512]{1,0:T(8,128)S(1)}, u32[]{:S(2)}, u32[]{:S(2)}) collective-permute-start(f32[256,512]{1,0:T(8,128)S(1)} %pad_maximum_fusion.2), channel_id=1, source_target_pairs={{32,0},{33,1},{34,2},{35,3},{36,4},{37,5},{38,6},{39,7},{40,8},{41... | collective-permute-start | bytes 1572872 | tf_op jit(solution)/shard_map/ppermute | solution.py:38
  72.6 4.2 %collective-permute-start.11 = (f32[4,256,512]{2,1,0:T(8,128)S(1)}, f32[4,256,512]{2,1,0:T(8,128)S(1)}, u32[]{:S(2)}, u32[]{:S(2)}) collective-permute-start(f32[4,256,512]{2,1,0:T(8,128)S(1)} %get-tuple-element.38), channel_id=1, source_target_pairs={{16,0},{17,1},{18,2},{19,3},{20,4},{21,5},{22,6},{23,7},{24,8},{25... | collective-permute-start | bytes 6291464 | tf_op jit(solution)/shard_map/ppermute | solution.py:38
  72.7 27.3 %collective-permute-start.12 = (bf16[2,512,512]{2,1,0:T(8,128)(2,1)}, bf16[2,512,512]{2,1,0:T(8,128)(2,1)S(1)}, u32[]{:S(2)}, u32[]{:S(2)}) collective-permute-start(bf16[2,512,512]{2,1,0:T(8,128)(2,1)} %collective-permute-done.8.refs_2_), channel_id=1, source_target_pairs={{8,0},{9,1},{10,2},{11,3},{12,4},{13,5},{14,6},{15,7},{0,8},{1,9},... | collective-permute-start | bytes 3145736 | tf_op jit(solution)/shard_map/ppermute | solution.py:38
  78.2 21.8 %collective-permute-start.13 = (f32[256,512]{1,0:T(8,128)}, f32[256,512]{1,0:T(8,128)}, u32[]{:S(2)}, u32[]{:S(2)}) collective-permute-start(f32[256,512]{1,0:T(8,128)} %get-tuple-element.40), channel_id=1, source_target_pairs={{96,0},{97,1},{98,2},{99,3},{100,4},{101,5},{102,6},{103,7},{104,8... | collective-permute-start | bytes 1572872 | tf_op jit(solution)/shard_map/ppermute | solution.py:38
  79.4 24.3 %collective-permute-start.14 = (f32[256,512]{1,0:T(8,128)}, f32[256,512]{1,0:T(8,128)}, u32[]{:S(2)}, u32[]{:S(2)}) collective-permute-start(f32[256,512]{1,0:T(8,128)} %get-tuple-element.42), channel_id=1, source_target_pairs={{64,0},{65,1},{66,2},{67,3},{68,4},{69,5},{70,6},{71,7},{72,8},{73... | collective-permute-start | bytes 1572872 | tf_op jit(solution)/shard_map/ppermute | solution.py:38
  80.2 25.4 %collective-permute-start.15 = (f32[256,512]{1,0:T(8,128)}, f32[256,512]{1,0:T(8,128)}, u32[]{:S(2)}, u32[]{:S(2)}) collective-permute-start(f32[256,512]{1,0:T(8,128)} %get-tuple-element.43), channel_id=1, source_target_pairs={{32,0},{33,1},{34,2},{35,3},{36,4},{37,5},{38,6},{39,7},{40,8},{41... | collective-permute-start | bytes 1572872 | tf_op jit(solution)/shard_map/ppermute | solution.py:38
  101.0 9.6 %copy-start.1 = (f32[256,512]{1,0:T(8,128)S(1)}, f32[256,512]{1,0:T(8,128)}, u32[]{:S(2)}) copy-start(f32[256,512]{1,0:T(8,128)} %fusion.6) | copy-start | bytes 1572868
  101.1 6.1 %collective-permute-start.16 = (f32[256,512]{1,0:T(8,128)S(1)}, f32[256,512]{1,0:T(8,128)S(1)}, u32[]{:S(2)}, u32[]{:S(2)}) collective-permute-start(f32[256,512]{1,0:T(8,128)S(1)} %bitcast.41), channel_id=1, source_target_pairs={{32,48},{64,80},{96,112},{0,16},{160,176},{192,208},{224,240},{128... | collective-permute-start | bytes 1572872 | tf_op jit(solution)/shard_map/ppermute | solution.py:38
  107.3 5.5 %collective-permute-start.18 = (f32[256,512]{1,0:T(8,128)S(1)}, f32[256,512]{1,0:T(8,128)S(1)}, u32[]{:S(2)}, u32[]{:S(2)}) collective-permute-start(f32[256,512]{1,0:T(8,128)S(1)} %bitcast_add_fusion), channel_id=1, source_target_pairs={{14,78},{15,79},{18,82},{19,83},{40,104},{41,105},{52,116},{53,117... | collective-permute-start | bytes 1572872 | tf_op jit(solution)/shard_map/ppermute | solution.py:38
  108.0 4.9 %collective-permute-start.19 = (f32[256,512]{1,0:T(8,128)S(1)}, f32[256,512]{1,0:T(8,128)S(1)}, u32[]{:S(2)}, u32[]{:S(2)}) collective-permute-start(f32[256,512]{1,0:T(8,128)S(1)} %bitcast_add_fusion), channel_id=1, source_target_pairs={{8,104},{9,105},{20,116},{21,117},{42,10},{54,22},{55,23},{59,27},... | collective-permute-start | bytes 1572872 | tf_op jit(solution)/shard_map/ppermute | solution.py:38
  108.7 4.2 %collective-permute-start.20 = (f32[256,512]{1,0:T(8,128)S(1)}, f32[256,512]{1,0:T(8,128)S(1)}, u32[]{:S(2)}, u32[]{:S(2)}) collective-permute-start(f32[256,512]{1,0:T(8,128)S(1)} %bitcast_add_fusion), channel_id=1, source_target_pairs={{12,44},{13,45},{16,48},{17,49},{46,78},{47,79},{50,82},{51,83},{7... | collective-permute-start | bytes 1572872 | tf_op jit(solution)/shard_map/ppermute | solution.py:38
  111.4 14.3 %collective-permute-start.17 = (f32[256,512]{1,0:T(8,128)S(1)}, f32[256,512]{1,0:T(8,128)S(1)}, u32[]{:S(2)}, u32[]{:S(2)}) collective-permute-start(f32[256,512]{1,0:T(8,128)S(1)} %broadcast_select_fusion.1), channel_id=1, source_target_pairs={{128,0},{129,1},{130,2},{131,3},{132,4},{133,5},{134,6},{135,7},{1... | collective-permute-start | bytes 1572872 | tf_op jit(solution)/shard_map/ppermute | solution.py:38
  113.1 13.5 %collective-permute-start.21 = (f32[256,512]{1,0:T(8,128)S(1)}, f32[256,512]{1,0:T(8,128)S(1)}, u32[]{:S(2)}, u32[]{:S(2)}) collective-permute-start(f32[256,512]{1,0:T(8,128)S(1)} %add_add_fusion), channel_id=1, source_target_pairs={{176,48},{177,49},{210,82},{211,83},{244,116},{245,117},{150,22},{... | collective-permute-start | bytes 1572872 | tf_op jit(solution)/shard_map/ppermute | solution.py:38
  126.8 22.3 %collective-permute-start.22 = (f32[256,512]{1,0:T(8,128)S(1)}, f32[256,512]{1,0:T(8,128)S(1)}, u32[]{:S(2)}, u32[]{:S(2)}) collective-permute-start(f32[256,512]{1,0:T(8,128)S(1)} %get-tuple-element.57), channel_id=1, source_target_pairs={{128,128},{32,16},{160,114},{64,113},{192,151},{224,135},{96,150},... | collective-permute-start | bytes 1572872 | tf_op jit(solution)/shard_map/ppermute | solution.py:38
  136.8 24.3 %collective-permute-start.23 = (f32[256,512]{1,0:T(8,128)S(1)}, f32[256,512]{1,0:T(8,128)S(1)}, u32[]{:S(2)}, u32[]{:S(2)}) collective-permute-start(f32[256,512]{1,0:T(8,128)S(1)} %get-tuple-element.58), channel_id=1, source_target_pairs={{0,98},{144,135},{16,0},{176,16},{48,151},{80,113},{208,150},{112,... | collective-permute-start | bytes 1572872 | tf_op jit(solution)/shard_map/ppermute | solution.py:38

commit v14 on v12

--- a/solution.py
+++ b/solution.py
@@ -216,8 +216,8 @@
     return total
 
 
-def units_kernel(pairs, index_pairs, spare, table, *refs):
-    held, outs = refs[: len(refs) - spare], refs[len(refs) - spare :]
+def units_kernel(pairs, index_pairs, kept, table, *refs):
+    held, out = refs[:-1], refs[-1]
     for at, ((first, second), (_, _, halves)) in enumerate(zip(index_pairs, pairs)):
         swap, one, two, half = (table[4 * at + i] for i in range(4))
         for turned in range(1 if first == second else 2):
@@ -226,25 +226,23 @@
 
                 @pl.when(swap == turned)
                 def _():
-                    outs[1][two] = half_product(rows, cols, 1 - half)
-                    outs[0][one] = half_product(rows, cols, half)
+                    out[one if kept else two] = half_product(rows, cols, half if kept else 1 - half)
 
             else:
-                for mine in range(2 - len(outs), 2):
-
-                    @pl.when((swap == turned) & (two == mine))
-                    def _():
-                        outs[1 - mine][one] = half_product(rows, cols, half)
-
-
-def products(table, held, names, pairs, counts):
+
+                @pl.when((swap == turned) & (two == kept))
+                def _():
+                    out[one] = half_product(rows, cols, half)
+
+
+def products(table, held, names, pairs, kept, count=NX):
     index_pairs = tuple((names.index(a), names.index(b)) for a, b, _ in pairs)
     return pl.pallas_call(
-        functools.partial(units_kernel, pairs, index_pairs, len(counts)),
-        out_shape=[pltpu.VMEM((count, 256, 512), jnp.float32) for count in counts],
+        functools.partial(units_kernel, pairs, index_pairs, kept),
+        out_shape=pltpu.VMEM((count, 256, 512), jnp.float32),
         in_specs=[pl.BlockSpec(memory_space=pltpu.SMEM)]
         + [pl.BlockSpec(memory_space=pltpu.VMEM)] * len(held),
-        out_specs=[pl.BlockSpec(memory_space=pltpu.VMEM)] * len(counts),
+        out_specs=pl.BlockSpec(memory_space=pltpu.VMEM),
         compiler_params=pltpu.CompilerParams(vmem_limit_bytes=VMEM_LIMIT),
     )(table, *held)
 
@@ -335,17 +333,17 @@
     held[PP] = send(held[PZ], FROM_UP)
     held[MM] = send(held[MZ], FROM_DOWN)
     held[Y1] = send(held[PZ], FROM_OTHER)
-    keep, given = products(table_a, [held[n] for n in HELD_A], HELD_A, PAIRS_A, (NX, NX))
+    given, keep = (products(table_a, [held[n] for n in HELD_A], HELD_A, PAIRS_A, kept) for kept in (0, 1))
     own_a, right_a, left_a = near(keep, send(given, CORE_SWAP))
     total_a = own_a + send(right_a, FROM_LEFT) + send(left_a, FROM_RIGHT)
     total_a, held[PP], held[MM], held[Y1] = together(total_a, held[PP], held[MM], held[Y1])
 
     held[Y2] = send(held[PP], FROM_OTHER)
-    keep, given = products(table_b, [held[n] for n in HELD_B], HELD_B, PAIRS_B, (NX, NX))
+    given, keep = (products(table_b, [held[n] for n in HELD_B], HELD_B, PAIRS_B, kept) for kept in (0, 1))
     own, *others = together(*(k + g for k, g in zip(split(keep), split(send(given, CORE_SWAP)))))
     right, far, left = (send(part, pairs) for part, pairs in zip(others, (FROM_LEFT, FROM_FAR, FROM_RIGHT)))
     held[Y2], right = together(held[Y2], right)
-    (part_c,) = products(table_c, [held[n] for n in HELD_C], HELD_C, PAIRS_C, (1,))
+    part_c = products(table_c, [held[n] for n in HELD_C], HELD_C, PAIRS_C, 1, 1)
     part_c = one_core(part_c[0], target_c)
     total_b, part_c = together((own + right) + (far + left), part_c)
 

time: 159 us -> 160 us (level); the launches traced: 157 us -> 160 us
  waiting for transfers between devices: 93.9 us -> 88.3 us
  starting transfers between devices: 36.7 us -> 41.6 us
  Pallas kernels: 9.91 us -> 14.3 us
    ppermute x25, waiting for transfers between devices: 93.9 us -> 88.3 us  [send(): return lax.ppermute(value, ALL, pairs)]
    ppermute x25, starting transfers between devices: 36.7 us -> 41.6 us  [send(): return lax.ppermute(value, ALL, pairs)]
    pallas_call x3 -> x5, Pallas kernels: 9.84 us -> 14.2 us  [products(): pl.pallas_call(functools.partial(units_kernel, pairs, index_pairs, kept),...]
    unnamed x8 -> x6, local copies, waits for them, and re-layouts: 3.46 us -> 1.27 us
  transfers between devices with their start and end apart: 25 -> 25, of which waited for: 13 -> 13; matrix products, arithmetic and copies ran while one was open for 6% -> 6% of each run, Pallas kernels for 1% -> 5%
where the time goes in v14:
time: 160 us
  waiting for transfers between devices  88.3 us (55%)
  starting transfers between devices  41.6 us (26%)
  Pallas kernels  14.3 us (9%)
  other arithmetic  7.82 us (5%)
  local copies, waits for them, and re-layouts  6.02 us (4%)
  between operations  1.61 us (1%)
    ppermute x25, waiting for transfers between devices, send(): return lax.ppermute(value, ALL, pairs)  88.3 us
    ppermute x25, starting transfers between devices, send(): return lax.ppermute(value, ALL, pairs)  41.6 us
    pallas_call x5, Pallas kernels, products(): pl.pallas_call(functools.partial(units_kernel, pairs, index_pairs, kept),...  14.2 us
  transfers between devices with their start and end apart: 25, of which 13 were waited for; matrix products, arithmetic and copies ran while one was open for 6% of the time, Pallas kernels for 5%

profile of v14, /device:TPU:12, one launch (start us, length us, event | category | flops | bytes accessed | tf_op | source)
XLA Modules:
  0.0 159.7 jit_solution(17784745727315471750)
XLA Ops:
  0.0 5.9 %collective-permute-start = (bf16[2,512,512]{2,1,0:T(8,128)(2,1)}, bf16[2,512,512]{2,1,0:T(8,128)(2,1)S(1)}, u32[]{:S(2)}, u32[]{:S(2)}) collective-permute-start(bf16[2,512,512]{2,1,0:T(8,128)(2,1)} %source.1), channel_id=1, source_target_pairs={{1,0},{2,1},{3,2},{4,3},{5,4},{6,5},{7,6},{0,7},{9,8},{10,9},{11,1... | collective-permute-start | bytes 3145736 | tf_op jit(solution)/shard_map/ppermute | solution.py:38
  5.9 2.3 %collective-permute-start.2 = (bf16[2,512,512]{2,1,0:T(8,128)(2,1)}, bf16[2,512,512]{2,1,0:T(8,128)(2,1)}, u32[]{:S(2)}, u32[]{:S(2)}) collective-permute-start(bf16[2,512,512]{2,1,0:T(8,128)(2,1)} %source.1), channel_id=1, source_target_pairs={{8,0},{9,1},{10,2},{11,3},{12,4},{13,5},{14,6},{15,7},{0,8},{1,9},... | collective-permute-start | bytes 3145736 | tf_op jit(solution)/shard_map/ppermute | solution.py:38
  10.2 18.4 %collective-permute-done.refs_1_ = bf16[2,512,512]{2,1,0:T(8,128)(2,1)S(1)} collective-permute-done((bf16[2,512,512]{2,1,0:T(8,128)(2,1)}, bf16[2,512,512]{2,1,0:T(8,128)(2,1)S(1)}, u32[]{:S(2)}, u32[]{:S(2)}) %collective-permute-start) | collective-permute-done | bytes 1048608 | tf_op jit(solution)/shard_map/ppermute | solution.py:38
  28.6 3.3 %collective-permute-done.1.refs_2_.refs_1_ = bf16[2,512,512]{2,1,0:T(8,128)(2,1)S(1)} collective-permute-done((bf16[2,512,512]{2,1,0:T(8,128)(2,1)}, bf16[2,512,512]{2,1,0:T(8,128)(2,1)S(1)}, u32[]{:S(2)}, u32[]{:S(2)}) %collective-permute-start.1) | collective-permute-done | bytes 1048608 | tf_op jit(solution)/shard_map/ppermute | solution.py:38
  32.3 3.1 %shard_map.66 = f32[4,256,512]{2,1,0:T(8,128)S(1)} custom-call(s32[20]{0:T(128)S(1)} %fusion.11.table, bf16[2,512,512]{2,1,0:T(8,128)(2,1)S(1)} %shard_map.64.refs_0_, bf16[2,512,512]{2,1,0:T(8,128)(2,1)S(1)} %collective-permute-done.refs_1_, bf16[2,512,512]{2,1,0:T(8,128)(2,1)S(1)} %collective-permute-done.1.refs_2_.refs_1_, ...), custom_call_target="tpu_custom_call" | custom-call | tf_op jit(solution)/shard_map/pallas_call | solution.py:240
  35.5 3.1 %shard_map.65 = f32[4,256,512]{2,1,0:T(8,128)S(1)} custom-call(s32[20]{0:T(128)S(1)} %fusion.11.table, bf16[2,512,512]{2,1,0:T(8,128)(2,1)S(1)} %shard_map.64.refs_0_, bf16[2,512,512]{2,1,0:T(8,128)(2,1)S(1)} %collective-permute-done.refs_1_, bf16[2,512,512]{2,1,0:T(8,128)(2,1)S(1)} %collective-permute-done.1.refs_2_.refs_1_, ...), custom_call_target="tpu_custom_call" | custom-call | tf_op jit(solution)/shard_map/pallas_call | solution.py:240
  38.8 2.4 %collective-permute-start.10 = (bf16[2,512,512]{2,1,0:T(8,128)(2,1)}, bf16[2,512,512]{2,1,0:T(8,128)(2,1)S(1)}, u32[]{:S(2)}, u32[]{:S(2)}) collective-permute-start(bf16[2,512,512]{2,1,0:T(8,128)(2,1)} %copy-done), channel_id=1, source_target_pairs={{8,0},{9,1},{10,2},{11,3},{12,4},{13,5},{14,6},{15,7},{0,8},{1,9},... | collective-permute-start | bytes 3145736 | tf_op jit(solution)/shard_map/ppermute | solution.py:38
  41.2 3.1 %collective-permute-start.8 = (bf16[2,512,512]{2,1,0:T(8,128)(2,1)}, bf16[2,512,512]{2,1,0:T(8,128)(2,1)}, u32[]{:S(2)}, u32[]{:S(2)}) collective-permute-start(bf16[2,512,512]{2,1,0:T(8,128)(2,1)} %copy-done), channel_id=1, source_target_pairs={{1,0},{2,1},{3,2},{4,3},{5,4},{6,5},{7,6},{0,7},{9,8},{10,9},{11,1... | collective-permute-start | bytes 3145736 | tf_op jit(solution)/shard_map/ppermute | solution.py:38
  44.4 1.3 collective-permute-start.4
  46.8 5.6 %collective-permute-done.4 = f32[128,512]{1,0:T(8,128)S(1)} collective-permute-done((f32[128,512]{1,0:T(8,128)S(1)}, f32[128,512]{1,0:T(8,128)S(1)}, u32[]{:S(2)}, u32[]{:S(2)}) %collective-permute-start.4) | collective-permute-done | bytes 262176 | tf_op jit(solution)/shard_map/ppermute | solution.py:38
  52.5 1.5 collective-permute-start.5
  55.6 9.9 %collective-permute-done.5 = f32[256,512]{1,0:T(8,128)S(1)} collective-permute-done((f32[256,512]{1,0:T(8,128)S(1)}, f32[256,512]{1,0:T(8,128)S(1)}, u32[]{:S(2)}, u32[]{:S(2)}) %collective-permute-start.5) | collective-permute-done | bytes 524320 | tf_op jit(solution)/shard_map/ppermute | solution.py:38
  67.7 3.1 %shard_map.68 = f32[4,256,512]{2,1,0:T(8,128)S(1)} custom-call(s32[20]{0:T(128)S(1)} %fusion.12.table, bf16[2,512,512]{2,1,0:T(8,128)(2,1)S(1)} %shard_map.64.refs_0_, bf16[2,512,512]{2,1,0:T(8,128)(2,1)S(1)} %collective-permute-done.1.refs_2_.refs_1_, bf16[2,512,512]{2,1,0:T(8,128)(2,1)} %collective-permute-done.8.refs_2_, ...), custom_call_target="tpu_custom_call" | custom-call | tf_op jit(solution)/shard_map/pallas_call | solution.py:240
  70.9 1.3 collective-permute-start.12
  72.2 3.2 %shard_map.67 = f32[4,256,512]{2,1,0:T(8,128)S(1)} custom-call(s32[20]{0:T(128)S(1)} %fusion.12.table, bf16[2,512,512]{2,1,0:T(8,128)(2,1)S(1)} %shard_map.64.refs_0_, bf16[2,512,512]{2,1,0:T(8,128)(2,1)S(1)} %collective-permute-done.1.refs_2_.refs_1_, bf16[2,512,512]{2,1,0:T(8,128)(2,1)} %collective-permute-done.8.refs_2_, ...), custom_call_target="tpu_custom_call" | custom-call | tf_op jit(solution)/shard_map/pallas_call | solution.py:240
  75.4 1.4 fusion
  76.8 2.8 %collective-permute-start.13 = (f32[256,512]{1,0:T(8,128)S(1)}, f32[256,512]{1,0:T(8,128)}, u32[]{:S(2)}, u32[]{:S(2)}) collective-permute-start(f32[256,512]{1,0:T(8,128)S(1)} %get-tuple-element.32), channel_id=1, source_target_pairs={{96,0},{97,1},{98,2},{99,3},{100,4},{101,5},{102,6},{103,7},{104,8... | collective-permute-start | bytes 1572872 | tf_op jit(solution)/shard_map/ppermute | solution.py:38
  79.6 1.6 collective-permute-start.15
  81.9 16.5 %collective-permute-done.12.refs_1_ = bf16[2,512,512]{2,1,0:T(8,128)(2,1)} collective-permute-done((bf16[2,512,512]{2,1,0:T(8,128)(2,1)}, bf16[2,512,512]{2,1,0:T(8,128)(2,1)}, u32[]{:S(2)}, u32[]{:S(2)}) %collective-permute-start.12) | collective-permute-done | bytes 1048608 | tf_op jit(solution)/shard_map/ppermute | solution.py:38
  98.3 1.7 %shard_map.69 = f32[1,256,512]{2,1,0:T(8,128)S(1)} custom-call(s32[4]{0:T(128)S(1)} %fusion.13.table, bf16[2,512,512]{2,1,0:T(8,128)(2,1)S(1)} %collective-permute-done.9.refs_3_.refs_0_, bf16[2,512,512]{2,1,0:T(8,128)(2,1)} %collective-permute-done.12.refs_1_), custom_call_target="tpu_custom_call" | custom-call | tf_op jit(solution)/shard_map/pallas_call | solution.py:240
  100.0 1.6 collective-permute-start.16
  101.6 1.4 dynamic_slice.16
  104.2 1.7 %add_add_fusion.1 = f32[256,512]{1,0:T(8,128)S(1)} fusion(f32[256,512]{1,0:T(8,128)} %collective-permute-done.14, f32[256,512]{1,0:T(8,128)} %collective-permute-done.15, f32[256,512]{1,0:T(8,128)} %get-tuple-element.31, f32[256,512]{1,0:T(8,128)} %collective-permute-done.13), kind=kLoop, calls=%fused_computation.19 | loop fusion | flops 393216 | bytes 2621440 | tf_op jit(solution)/shard_map/add | solution.py:348
  110.0 1.3 dynamic_slice.15
  112.5 7.2 %collective-permute-done.17 = f32[256,512]{1,0:T(8,128)S(1)} collective-permute-done((f32[256,512]{1,0:T(8,128)S(1)}, f32[256,512]{1,0:T(8,128)S(1)}, u32[]{:S(2)}, u32[]{:S(2)}) %collective-permute-start.17) | collective-permute-done | bytes 524320 | tf_op jit(solution)/shard_map/ppermute | solution.py:38
  120.9 8.9 %collective-permute-start.21 = (f32[256,512]{1,0:T(8,128)S(1)}, f32[256,512]{1,0:T(8,128)S(1)}, u32[]{:S(2)}, u32[]{:S(2)}) collective-permute-start(f32[256,512]{1,0:T(8,128)S(1)} %get-tuple-element.49), channel_id=1, source_target_pairs={{128,128},{32,16},{160,114},{48,0},{64,113},{192,150},{96,135},{22... | collective-permute-start | bytes 1572872 | tf_op jit(solution)/shard_map/ppermute | solution.py:38
  129.8 1.3 collective-permute-start.22
  131.1 1.3 collective-permute-start.23
  132.4 1.3 collective-permute-start.24
  133.7 8.0 %collective-permute-done.21 = f32[256,512]{1,0:T(8,128)S(1)} collective-permute-done((f32[256,512]{1,0:T(8,128)S(1)}, f32[256,512]{1,0:T(8,128)S(1)}, u32[]{:S(2)}, u32[]{:S(2)}) %collective-permute-start.21) | collective-permute-done | bytes 524320 | tf_op jit(solution)/shard_map/ppermute | solution.py:38
  141.7 2.0 %collective-permute-done.22 = f32[256,512]{1,0:T(8,128)S(1)} collective-permute-done((f32[256,512]{1,0:T(8,128)S(1)}, f32[256,512]{1,0:T(8,128)S(1)}, u32[]{:S(2)}, u32[]{:S(2)}) %collective-permute-start.22) | collective-permute-done | bytes 524320 | tf_op jit(solution)/shard_map/ppermute | solution.py:38
  143.8 14.0 %collective-permute-done.23 = f32[256,512]{1,0:T(8,128)S(1)} collective-permute-done((f32[256,512]{1,0:T(8,128)S(1)}, f32[256,512]{1,0:T(8,128)S(1)}, u32[]{:S(2)}, u32[]{:S(2)}) %collective-permute-start.23) | collective-permute-done | bytes 524320 | tf_op jit(solution)/shard_map/ppermute | solution.py:38
  (54 shorter events, 16.9 us)
Async XLA Ops:
  0.0 28.6 %collective-permute-start = (bf16[2,512,512]{2,1,0:T(8,128)(2,1)}, bf16[2,512,512]{2,1,0:T(8,128)(2,1)S(1)}, u32[]{:S(2)}, u32[]{:S(2)}) collective-permute-start(bf16[2,512,512]{2,1,0:T(8,128)(2,1)} %source.1), channel_id=1, source_target_pairs={{1,0},{2,1},{3,2},{4,3},{5,4},{6,5},{7,6},{0,7},{9,8},{10,9},{11,1... | collective-permute-start | bytes 3145736 | tf_op jit(solution)/shard_map/ppermute | solution.py:38
  5.9 26.0 %collective-permute-start.1 = (bf16[2,512,512]{2,1,0:T(8,128)(2,1)}, bf16[2,512,512]{2,1,0:T(8,128)(2,1)S(1)}, u32[]{:S(2)}, u32[]{:S(2)}) collective-permute-start(bf16[2,512,512]{2,1,0:T(8,128)(2,1)} %source.1), channel_id=1, source_target_pairs={{7,0},{0,1},{1,2},{2,3},{3,4},{4,5},{5,6},{6,7},{15,8},{8,9},{9,10... | collective-permute-start | bytes 3145736 | tf_op jit(solution)/shard_map/ppermute | solution.py:38
  5.9 26.4 %collective-permute-start.2 = (bf16[2,512,512]{2,1,0:T(8,128)(2,1)}, bf16[2,512,512]{2,1,0:T(8,128)(2,1)}, u32[]{:S(2)}, u32[]{:S(2)}) collective-permute-start(bf16[2,512,512]{2,1,0:T(8,128)(2,1)} %source.1), channel_id=1, source_target_pairs={{8,0},{9,1},{10,2},{11,3},{12,4},{13,5},{14,6},{15,7},{0,8},{1,9},... | collective-permute-start | bytes 3145736 | tf_op jit(solution)/shard_map/ppermute | solution.py:38
  8.2 1.3 copy-start.1
  28.6 6.9 %copy-start = (bf16[2,512,512]{2,1,0:T(8,128)(2,1)}, bf16[2,512,512]{2,1,0:T(8,128)(2,1)S(1)}, u32[]{:S(2)}) copy-start(bf16[2,512,512]{2,1,0:T(8,128)(2,1)S(1)} %collective-permute-done.refs_1_) | copy-start | bytes 3145732
  35.4 8.9 %collective-permute-start.3 = (f32[4,256,512]{2,1,0:T(8,128)S(1)}, f32[4,256,512]{2,1,0:T(8,128)S(1)}, u32[]{:S(2)}, u32[]{:S(2)}) collective-permute-start(f32[4,256,512]{2,1,0:T(8,128)S(1)} %shard_map.66), channel_id=1, source_target_pairs={{16,0},{17,1},{18,2},{19,3},{20,4},{21,5},{22,6},{23,7},{24,8},{25... | collective-permute-start | bytes 6291464 | tf_op jit(solution)/shard_map/ppermute | solution.py:38
  38.7 29.0 %collective-permute-start.9 = (bf16[2,512,512]{2,1,0:T(8,128)(2,1)S(1)}, bf16[2,512,512]{2,1,0:T(8,128)(2,1)S(1)}, u32[]{:S(2)}, u32[]{:S(2)}) collective-permute-start(bf16[2,512,512]{2,1,0:T(8,128)(2,1)S(1)} %collective-permute-done.1.refs_2_.refs_1_), channel_id=1, source_target_pairs={{7,0},{0,1},{1,2},{2,3},{3,4},{4,5},{5,6},{6,7},{15,8},{8,9},{9,10... | collective-permute-start | bytes 3145736 | tf_op jit(solution)/shard_map/ppermute | solution.py:38
  38.8 28.9 %collective-permute-start.10 = (bf16[2,512,512]{2,1,0:T(8,128)(2,1)}, bf16[2,512,512]{2,1,0:T(8,128)(2,1)S(1)}, u32[]{:S(2)}, u32[]{:S(2)}) collective-permute-start(bf16[2,512,512]{2,1,0:T(8,128)(2,1)} %copy-done), channel_id=1, source_target_pairs={{8,0},{9,1},{10,2},{11,3},{12,4},{13,5},{14,6},{15,7},{0,8},{1,9},... | collective-permute-start | bytes 3145736 | tf_op jit(solution)/shard_map/ppermute | solution.py:38
  41.2 26.5 %collective-permute-start.8 = (bf16[2,512,512]{2,1,0:T(8,128)(2,1)}, bf16[2,512,512]{2,1,0:T(8,128)(2,1)}, u32[]{:S(2)}, u32[]{:S(2)}) collective-permute-start(bf16[2,512,512]{2,1,0:T(8,128)(2,1)} %copy-done), channel_id=1, source_target_pairs={{1,0},{2,1},{3,2},{4,3},{5,4},{6,5},{7,6},{0,7},{9,8},{10,9},{11,1... | collective-permute-start | bytes 3145736 | tf_op jit(solution)/shard_map/ppermute | solution.py:38
  44.4 8.0 %collective-permute-start.4 = (f32[128,512]{1,0:T(8,128)S(1)}, f32[128,512]{1,0:T(8,128)S(1)}, u32[]{:S(2)}, u32[]{:S(2)}) collective-permute-start(f32[128,512]{1,0:T(8,128)S(1)} %get-tuple-element.45), channel_id=1, source_target_pairs={{96,0},{97,1},{98,2},{99,3},{100,4},{101,5},{102,6},{103,7},{104,8... | collective-permute-start | bytes 786440 | tf_op jit(solution)/shard_map/ppermute | solution.py:38
  45.9 8.1 %collective-permute-start.6 = (f32[128,512]{1,0:T(8,128)S(1)}, f32[128,512]{1,0:T(8,128)S(1)}, u32[]{:S(2)}, u32[]{:S(2)}) collective-permute-start(f32[128,512]{1,0:T(8,128)S(1)} %get-tuple-element.46), channel_id=1, source_target_pairs={{32,0},{33,1},{34,2},{35,3},{36,4},{37,5},{38,6},{39,7},{40,8},{41... | collective-permute-start | bytes 786440 | tf_op jit(solution)/shard_map/ppermute | solution.py:38
  52.5 13.1 %collective-permute-start.5 = (f32[256,512]{1,0:T(8,128)S(1)}, f32[256,512]{1,0:T(8,128)S(1)}, u32[]{:S(2)}, u32[]{:S(2)}) collective-permute-start(f32[256,512]{1,0:T(8,128)S(1)} %pad_maximum_fusion.1), channel_id=1, source_target_pairs={{96,0},{97,1},{98,2},{99,3},{100,4},{101,5},{102,6},{103,7},{104,8... | collective-permute-start | bytes 1572872 | tf_op jit(solution)/shard_map/ppermute | solution.py:38
  54.0 12.6 %collective-permute-start.7 = (f32[256,512]{1,0:T(8,128)S(1)}, f32[256,512]{1,0:T(8,128)S(1)}, u32[]{:S(2)}, u32[]{:S(2)}) collective-permute-start(f32[256,512]{1,0:T(8,128)S(1)} %pad_maximum_fusion.2), channel_id=1, source_target_pairs={{32,0},{33,1},{34,2},{35,3},{36,4},{37,5},{38,6},{39,7},{40,8},{41... | collective-permute-start | bytes 1572872 | tf_op jit(solution)/shard_map/ppermute | solution.py:38
  70.8 4.6 %collective-permute-start.11 = (f32[4,256,512]{2,1,0:T(8,128)S(1)}, f32[4,256,512]{2,1,0:T(8,128)S(1)}, u32[]{:S(2)}, u32[]{:S(2)}) collective-permute-start(f32[4,256,512]{2,1,0:T(8,128)S(1)} %shard_map.68), channel_id=1, source_target_pairs={{16,0},{17,1},{18,2},{19,3},{20,4},{21,5},{22,6},{23,7},{24,8},{25... | collective-permute-start | bytes 6291464 | tf_op jit(solution)/shard_map/ppermute | solution.py:38
  70.9 27.4 %collective-permute-start.12 = (bf16[2,512,512]{2,1,0:T(8,128)(2,1)}, bf16[2,512,512]{2,1,0:T(8,128)(2,1)}, u32[]{:S(2)}, u32[]{:S(2)}) collective-permute-start(bf16[2,512,512]{2,1,0:T(8,128)(2,1)} %collective-permute-done.8.refs_2_), channel_id=1, source_target_pairs={{8,0},{9,1},{10,2},{11,3},{12,4},{13,5},{14,6},{15,7},{0,8},{1,9},... | collective-permute-start | bytes 3145736 | tf_op jit(solution)/shard_map/ppermute | solution.py:38
  76.8 21.5 %collective-permute-start.13 = (f32[256,512]{1,0:T(8,128)S(1)}, f32[256,512]{1,0:T(8,128)}, u32[]{:S(2)}, u32[]{:S(2)}) collective-permute-start(f32[256,512]{1,0:T(8,128)S(1)} %get-tuple-element.32), channel_id=1, source_target_pairs={{96,0},{97,1},{98,2},{99,3},{100,4},{101,5},{102,6},{103,7},{104,8... | collective-permute-start | bytes 1572872 | tf_op jit(solution)/shard_map/ppermute | solution.py:38
  79.6 23.4 %collective-permute-start.14 = (f32[256,512]{1,0:T(8,128)}, f32[256,512]{1,0:T(8,128)}, u32[]{:S(2)}, u32[]{:S(2)}) collective-permute-start(f32[256,512]{1,0:T(8,128)} %get-tuple-element.34), channel_id=1, source_target_pairs={{64,0},{65,1},{66,2},{67,3},{68,4},{69,5},{70,6},{71,7},{72,8},{73... | collective-permute-start | bytes 1572872 | tf_op jit(solution)/shard_map/ppermute | solution.py:38
  79.6 24.6 %collective-permute-start.15 = (f32[256,512]{1,0:T(8,128)}, f32[256,512]{1,0:T(8,128)}, u32[]{:S(2)}, u32[]{:S(2)}) collective-permute-start(f32[256,512]{1,0:T(8,128)} %get-tuple-element.35), channel_id=1, source_target_pairs={{32,0},{33,1},{34,2},{35,3},{36,4},{37,5},{38,6},{39,7},{40,8},{41... | collective-permute-start | bytes 1572872 | tf_op jit(solution)/shard_map/ppermute | solution.py:38
  100.0 5.9 %collective-permute-start.16 = (f32[256,512]{1,0:T(8,128)S(1)}, f32[256,512]{1,0:T(8,128)S(1)}, u32[]{:S(2)}, u32[]{:S(2)}) collective-permute-start(f32[256,512]{1,0:T(8,128)S(1)} %bitcast.41), channel_id=1, source_target_pairs={{32,48},{64,80},{96,112},{0,16},{160,176},{192,208},{224,240},{128... | collective-permute-start | bytes 1572872 | tf_op jit(solution)/shard_map/ppermute | solution.py:38
  103.0 3.0 %copy-start.2 = (f32[256,512]{1,0:T(8,128)S(1)}, f32[256,512]{1,0:T(8,128)}, u32[]{:S(2)}) copy-start(f32[256,512]{1,0:T(8,128)} %fusion.6) | copy-start | bytes 1572868
  106.8 12.9 %collective-permute-start.17 = (f32[256,512]{1,0:T(8,128)S(1)}, f32[256,512]{1,0:T(8,128)S(1)}, u32[]{:S(2)}, u32[]{:S(2)}) collective-permute-start(f32[256,512]{1,0:T(8,128)S(1)} %broadcast_select_fusion.1), channel_id=1, source_target_pairs={{128,0},{129,1},{130,2},{131,3},{132,4},{133,5},{134,6},{135,7},{1... | collective-permute-start | bytes 1572872 | tf_op jit(solution)/shard_map/ppermute | solution.py:38
  107.9 12.7 %collective-permute-start.18 = (f32[256,512]{1,0:T(8,128)S(1)}, f32[256,512]{1,0:T(8,128)S(1)}, u32[]{:S(2)}, u32[]{:S(2)}) collective-permute-start(f32[256,512]{1,0:T(8,128)S(1)} %bitcast_add_fusion), channel_id=1, source_target_pairs={{14,78},{18,82},{19,83},{31,95},{40,104},{41,105},{52,116},{53,117... | collective-permute-start | bytes 1572872 | tf_op jit(solution)/shard_map/ppermute | solution.py:38
  108.6 12.0 %collective-permute-start.19 = (f32[256,512]{1,0:T(8,128)S(1)}, f32[256,512]{1,0:T(8,128)S(1)}, u32[]{:S(2)}, u32[]{:S(2)}) collective-permute-start(f32[256,512]{1,0:T(8,128)S(1)} %bitcast_add_fusion), channel_id=1, source_target_pairs={{8,104},{9,105},{20,116},{21,117},{42,10},{43,11},{54,22},{55,23},... | collective-permute-start | bytes 1572872 | tf_op jit(solution)/shard_map/ppermute | solution.py:38
  109.3 11.3 %collective-permute-start.20 = (f32[256,512]{1,0:T(8,128)S(1)}, f32[256,512]{1,0:T(8,128)S(1)}, u32[]{:S(2)}, u32[]{:S(2)}) collective-permute-start(f32[256,512]{1,0:T(8,128)S(1)} %bitcast_add_fusion), channel_id=1, source_target_pairs={{12,44},{13,45},{16,48},{17,49},{46,78},{50,82},{51,83},{63,95},{7... | collective-permute-start | bytes 1572872 | tf_op jit(solution)/shard_map/ppermute | solution.py:38
  120.9 20.8 %collective-permute-start.21 = (f32[256,512]{1,0:T(8,128)S(1)}, f32[256,512]{1,0:T(8,128)S(1)}, u32[]{:S(2)}, u32[]{:S(2)}) collective-permute-start(f32[256,512]{1,0:T(8,128)S(1)} %get-tuple-element.49), channel_id=1, source_target_pairs={{128,128},{32,16},{160,114},{48,0},{64,113},{192,150},{96,135},{22... | collective-permute-start | bytes 1572872 | tf_op jit(solution)/shard_map/ppermute | solution.py:38
  129.8 13.9 %collective-permute-start.22 = (f32[256,512]{1,0:T(8,128)S(1)}, f32[256,512]{1,0:T(8,128)S(1)}, u32[]{:S(2)}, u32[]{:S(2)}) collective-permute-start(f32[256,512]{1,0:T(8,128)S(1)} %add_add_fusion), channel_id=1, source_target_pairs={{48,166},{177,183},{82,192},{211,209},{244,226},{117,243},{150,132... | collective-permute-start | bytes 1572872 | tf_op jit(solution)/shard_map/ppermute | solution.py:38
  131.1 26.7 %collective-permute-start.23 = (f32[256,512]{1,0:T(8,128)S(1)}, f32[256,512]{1,0:T(8,128)S(1)}, u32[]{:S(2)}, u32[]{:S(2)}) collective-permute-start(f32[256,512]{1,0:T(8,128)S(1)} %get-tuple-element.50), channel_id=1, source_target_pairs={{0,98},{144,135},{16,151},{176,0},{208,113},{80,114},{112,16},{240... | collective-permute-start | bytes 1572872 | tf_op jit(solution)/shard_map/ppermute | solution.py:38
  132.4 26.2 %collective-permute-start.24 = (f32[256,512]{1,0:T(8,128)S(1)}, f32[256,512]{1,0:T(8,128)S(1)}, u32[]{:S(2)}, u32[]{:S(2)}) collective-permute-start(f32[256,512]{1,0:T(8,128)S(1)} %add_add_fusion), channel_id=1, source_target_pairs={{104,226},{233,243},{138,132},{139,149},{172,166},{173,183},{206,1... | collective-permute-start | bytes 1572872 | tf_op jit(solution)/shard_map/ppermute | solution.py:38

commit v15 on v12

--- a/solution.py
+++ b/solution.py
@@ -134,7 +134,7 @@
         for unit in units_of(PAIRS_C, h, z):
             for y in (0, 1):
                 for link, share in links(own, unit[2] % 8, y, unit):
-                    load[link] += share
+                    load[link] += 3 * share
     for _ in range(trials):
         own, batch, u, v = draw.randrange(GROUPS), draw.randrange(2), draw.randrange(8), draw.randrange(8)
         if (u - v) % 2:

time: 159 us -> 159 us (level)
  no operation moved by 1% of the time
where the time goes in v15:
time: 159 us; the launch traced here: 158 us
  waiting for transfers between devices  94.1 us (59%)
  starting transfers between devices  38 us (24%)
  Pallas kernels  9.91 us (6%)
  other arithmetic  7.61 us (5%)
  local copies, waits for them, and re-layouts  7.44 us (5%)
    ppermute x25, waiting for transfers between devices, send(): return lax.ppermute(value, ALL, pairs)  94.1 us
    ppermute x25, starting transfers between devices, send(): return lax.ppermute(value, ALL, pairs)  38 us
    pallas_call x3, Pallas kernels, products(): pl.pallas_call(functools.partial(units_kernel, pairs, index_pairs, len(co...  9.84 us
    unnamed x8, local copies, waits for them, and re-layouts  3.46 us
  transfers between devices with their start and end apart: 25, of which 13 were waited for; matrix products, arithmetic and copies ran while one was open for 6% of the time, Pallas kernels for 1%

profile of v15, /device:TPU:12, one launch (start us, length us, event | category | flops | bytes accessed | tf_op | source)
XLA Modules:
  0.0 158.4 jit_solution(675476330489970746)
XLA Ops:
  0.0 5.9 %collective-permute-start = (bf16[2,512,512]{2,1,0:T(8,128)(2,1)}, bf16[2,512,512]{2,1,0:T(8,128)(2,1)}, u32[]{:S(2)}, u32[]{:S(2)}) collective-permute-start(bf16[2,512,512]{2,1,0:T(8,128)(2,1)} %source.1), channel_id=1, source_target_pairs={{1,0},{2,1},{3,2},{4,3},{5,4},{6,5},{7,6},{0,7},{9,8},{10,9},{11,1... | collective-permute-start | bytes 3145736 | tf_op jit(solution)/shard_map/ppermute | solution.py:38
  5.9 2.3 %collective-permute-start.2 = (bf16[2,512,512]{2,1,0:T(8,128)(2,1)}, bf16[2,512,512]{2,1,0:T(8,128)(2,1)S(1)}, u32[]{:S(2)}, u32[]{:S(2)}) collective-permute-start(bf16[2,512,512]{2,1,0:T(8,128)(2,1)} %source.1), channel_id=1, source_target_pairs={{8,0},{9,1},{10,2},{11,3},{12,4},{13,5},{14,6},{15,7},{0,8},{1,9},... | collective-permute-start | bytes 3145736 | tf_op jit(solution)/shard_map/ppermute | solution.py:38
  8.2 1.3 copy-done
  10.2 18.4 %collective-permute-done.refs_1_ = bf16[2,512,512]{2,1,0:T(8,128)(2,1)} collective-permute-done((bf16[2,512,512]{2,1,0:T(8,128)(2,1)}, bf16[2,512,512]{2,1,0:T(8,128)(2,1)}, u32[]{:S(2)}, u32[]{:S(2)}) %collective-permute-start) | collective-permute-done | bytes 1048608 | tf_op jit(solution)/shard_map/ppermute | solution.py:38
  28.6 3.3 %collective-permute-done.1.refs_2_.refs_1_ = bf16[2,512,512]{2,1,0:T(8,128)(2,1)S(1)} collective-permute-done((bf16[2,512,512]{2,1,0:T(8,128)(2,1)}, bf16[2,512,512]{2,1,0:T(8,128)(2,1)S(1)}, u32[]{:S(2)}, u32[]{:S(2)}) %collective-permute-start.1) | collective-permute-done | bytes 1048608 | tf_op jit(solution)/shard_map/ppermute | solution.py:38
  32.2 4.4 %shard_map.65 = (f32[4,256,512]{2,1,0:T(8,128)S(1)}, f32[4,256,512]{2,1,0:T(8,128)S(1)}) custom-call(s32[20]{0:T(128)S(1)} %get-tuple-element.59.table, bf16[2,512,512]{2,1,0:T(8,128)(2,1)S(1)} %shard_map.64.refs_0_, bf16[2,512,512]{2,1,0:T(8,128)(2,1)} %collective-permute-done.refs_1_, bf16[2,512,512]{2,1,0:T(8,128)(2,1)S(1)} %collective-permute-done.1.refs_2_.refs_1_, ...), custom_call_target="tpu_custom_call" | custom-call | tf_op jit(solution)/shard_map/pallas_call | solution.py:242
  36.7 2.4 %collective-permute-start.10 = (bf16[2,512,512]{2,1,0:T(8,128)(2,1)}, bf16[2,512,512]{2,1,0:T(8,128)(2,1)S(1)}, u32[]{:S(2)}, u32[]{:S(2)}) collective-permute-start(bf16[2,512,512]{2,1,0:T(8,128)(2,1)} %collective-permute-done.refs_1_), channel_id=1, source_target_pairs={{8,0},{9,1},{10,2},{11,3},{12,4},{13,5},{14,6},{15,7},{0,8},{1,9},... | collective-permute-start | bytes 3145736 | tf_op jit(solution)/shard_map/ppermute | solution.py:38
  39.1 2.9 %collective-permute-start.8 = (bf16[2,512,512]{2,1,0:T(8,128)(2,1)}, bf16[2,512,512]{2,1,0:T(8,128)(2,1)}, u32[]{:S(2)}, u32[]{:S(2)}) collective-permute-start(bf16[2,512,512]{2,1,0:T(8,128)(2,1)} %collective-permute-done.refs_1_), channel_id=1, source_target_pairs={{1,0},{2,1},{3,2},{4,3},{5,4},{6,5},{7,6},{0,7},{9,8},{10,9},{11,1... | collective-permute-start | bytes 3145736 | tf_op jit(solution)/shard_map/ppermute | solution.py:38
  42.1 1.3 collective-permute-start.4
  44.6 5.7 %collective-permute-done.4 = f32[128,512]{1,0:T(8,128)S(1)} collective-permute-done((f32[128,512]{1,0:T(8,128)S(1)}, f32[128,512]{1,0:T(8,128)S(1)}, u32[]{:S(2)}, u32[]{:S(2)}) %collective-permute-start.4) | collective-permute-done | bytes 262176 | tf_op jit(solution)/shard_map/ppermute | solution.py:38
  50.4 1.3 collective-permute-start.5
  52.8 10.6 %collective-permute-done.5 = f32[256,512]{1,0:T(8,128)S(1)} collective-permute-done((f32[256,512]{1,0:T(8,128)S(1)}, f32[256,512]{1,0:T(8,128)S(1)}, u32[]{:S(2)}, u32[]{:S(2)}) %collective-permute-start.5) | collective-permute-done | bytes 524320 | tf_op jit(solution)/shard_map/ppermute | solution.py:38
  63.4 1.3 collective-permute-done.7
  65.7 2.5 %collective-permute-done.9.refs_3_.refs_0_ = bf16[2,512,512]{2,1,0:T(8,128)(2,1)S(1)} collective-permute-done((bf16[2,512,512]{2,1,0:T(8,128)(2,1)S(1)}, bf16[2,512,512]{2,1,0:T(8,128)(2,1)S(1)}, u32[]{:S(2)}, u32[]{:S(2)}) %collective-permute-start.9) | collective-permute-done | bytes 1048608 | tf_op jit(solution)/shard_map/ppermute | solution.py:38
  68.2 4.4 %shard_map.66 = (f32[4,256,512]{2,1,0:T(8,128)S(1)}, f32[4,256,512]{2,1,0:T(8,128)S(1)}) custom-call(s32[20]{0:T(128)S(1)} %get-tuple-element.60.table, bf16[2,512,512]{2,1,0:T(8,128)(2,1)S(1)} %shard_map.64.refs_0_, bf16[2,512,512]{2,1,0:T(8,128)(2,1)S(1)} %collective-permute-done.1.refs_2_.refs_1_, bf16[2,512,512]{2,1,0:T(8,128)(2,1)} %collective-permute-done.8.refs_2_, ...), custom_call_target="tpu_custom_call" | custom-call | tf_op jit(solution)/shard_map/pallas_call | solution.py:242
  72.7 1.3 collective-permute-start.12
  74.0 2.8 %collective-permute-done.11 = f32[4,256,512]{2,1,0:T(8,128)S(1)} collective-permute-done((f32[4,256,512]{2,1,0:T(8,128)S(1)}, f32[4,256,512]{2,1,0:T(8,128)S(1)}, u32[]{:S(2)}, u32[]{:S(2)}) %collective-permute-start.11) | collective-permute-done | bytes 2097184 | tf_op jit(solution)/shard_map/ppermute | solution.py:38
  76.9 1.4 fusion
  82.1 18.0 %collective-permute-done.12.refs_1_ = bf16[2,512,512]{2,1,0:T(8,128)(2,1)S(1)} collective-permute-done((bf16[2,512,512]{2,1,0:T(8,128)(2,1)}, bf16[2,512,512]{2,1,0:T(8,128)(2,1)S(1)}, u32[]{:S(2)}, u32[]{:S(2)}) %collective-permute-start.12) | collective-permute-done | bytes 1048608 | tf_op jit(solution)/shard_map/ppermute | solution.py:38
  103.2 1.7 %collective-permute-start.16 = (f32[256,512]{1,0:T(8,128)S(1)}, f32[256,512]{1,0:T(8,128)S(1)}, u32[]{:S(2)}, u32[]{:S(2)}) collective-permute-start(f32[256,512]{1,0:T(8,128)S(1)} %bitcast.41), channel_id=1, source_target_pairs={{32,48},{64,80},{96,112},{0,16},{160,176},{192,208},{224,240},{128... | collective-permute-start | bytes 1572872 | tf_op jit(solution)/shard_map/ppermute | solution.py:38
  104.9 1.3 dynamic_slice.16
  106.2 1.6 %add_add_fusion.1 = f32[256,512]{1,0:T(8,128)S(1)} fusion(f32[256,512]{1,0:T(8,128)} %collective-permute-done.14, f32[256,512]{1,0:T(8,128)} %collective-permute-done.15, f32[256,512]{1,0:T(8,128)S(1)} %get-tuple-element.39, f32[256,512]{1,0:T(8,128)} %collective-permute-done.13), kind=kLoop, calls=%fused_computation.19 | loop fusion | flops 393216 | bytes 2621440 | tf_op jit(solution)/shard_map/add | solution.py:350
  108.7 1.3 collective-permute-start.17
  112.1 1.3 dynamic_slice.15
  114.5 7.5 %collective-permute-done.17 = f32[256,512]{1,0:T(8,128)S(1)} collective-permute-done((f32[256,512]{1,0:T(8,128)S(1)}, f32[256,512]{1,0:T(8,128)S(1)}, u32[]{:S(2)}, u32[]{:S(2)}) %collective-permute-start.17) | collective-permute-done | bytes 524320 | tf_op jit(solution)/shard_map/ppermute | solution.py:38
  123.2 6.4 %collective-permute-start.21 = (f32[256,512]{1,0:T(8,128)S(1)}, f32[256,512]{1,0:T(8,128)S(1)}, u32[]{:S(2)}, u32[]{:S(2)}) collective-permute-start(f32[256,512]{1,0:T(8,128)S(1)} %get-tuple-element.57), channel_id=1, source_target_pairs={{0,16},{160,128},{32,114},{64,113},{192,151},{96,135},{224,150},{2... | collective-permute-start | bytes 1572872 | tf_op jit(solution)/shard_map/ppermute | solution.py:38
  129.5 1.3 collective-permute-start.22
  130.8 1.3 collective-permute-start.23
  132.1 1.3 collective-permute-start.24
  133.4 6.7 %collective-permute-done.21 = f32[256,512]{1,0:T(8,128)S(1)} collective-permute-done((f32[256,512]{1,0:T(8,128)S(1)}, f32[256,512]{1,0:T(8,128)S(1)}, u32[]{:S(2)}, u32[]{:S(2)}) %collective-permute-start.21) | collective-permute-done | bytes 524320 | tf_op jit(solution)/shard_map/ppermute | solution.py:38
  140.1 4.6 %collective-permute-done.22 = f32[256,512]{1,0:T(8,128)S(1)} collective-permute-done((f32[256,512]{1,0:T(8,128)S(1)}, f32[256,512]{1,0:T(8,128)S(1)}, u32[]{:S(2)}, u32[]{:S(2)}) %collective-permute-start.22) | collective-permute-done | bytes 524320 | tf_op jit(solution)/shard_map/ppermute | solution.py:38
  144.8 12.5 %collective-permute-done.23 = f32[256,512]{1,0:T(8,128)S(1)} collective-permute-done((f32[256,512]{1,0:T(8,128)S(1)}, f32[256,512]{1,0:T(8,128)S(1)}, u32[]{:S(2)}, u32[]{:S(2)}) %collective-permute-start.23) | collective-permute-done | bytes 524320 | tf_op jit(solution)/shard_map/ppermute | solution.py:38
  (53 shorter events, 17.0 us)
Async XLA Ops:
  0.0 28.6 %collective-permute-start = (bf16[2,512,512]{2,1,0:T(8,128)(2,1)}, bf16[2,512,512]{2,1,0:T(8,128)(2,1)}, u32[]{:S(2)}, u32[]{:S(2)}) collective-permute-start(bf16[2,512,512]{2,1,0:T(8,128)(2,1)} %source.1), channel_id=1, source_target_pairs={{1,0},{2,1},{3,2},{4,3},{5,4},{6,5},{7,6},{0,7},{9,8},{10,9},{11,1... | collective-permute-start | bytes 3145736 | tf_op jit(solution)/shard_map/ppermute | solution.py:38
  5.9 26.0 %collective-permute-start.1 = (bf16[2,512,512]{2,1,0:T(8,128)(2,1)}, bf16[2,512,512]{2,1,0:T(8,128)(2,1)S(1)}, u32[]{:S(2)}, u32[]{:S(2)}) collective-permute-start(bf16[2,512,512]{2,1,0:T(8,128)(2,1)} %source.1), channel_id=1, source_target_pairs={{7,0},{0,1},{1,2},{2,3},{3,4},{4,5},{5,6},{6,7},{15,8},{8,9},{9,10... | collective-permute-start | bytes 3145736 | tf_op jit(solution)/shard_map/ppermute | solution.py:38
  5.9 26.3 %collective-permute-start.2 = (bf16[2,512,512]{2,1,0:T(8,128)(2,1)}, bf16[2,512,512]{2,1,0:T(8,128)(2,1)S(1)}, u32[]{:S(2)}, u32[]{:S(2)}) collective-permute-start(bf16[2,512,512]{2,1,0:T(8,128)(2,1)} %source.1), channel_id=1, source_target_pairs={{8,0},{9,1},{10,2},{11,3},{12,4},{13,5},{14,6},{15,7},{0,8},{1,9},... | collective-permute-start | bytes 3145736 | tf_op jit(solution)/shard_map/ppermute | solution.py:38
  8.2 1.3 copy-start
  36.6 5.4 %collective-permute-start.3 = (f32[4,256,512]{2,1,0:T(8,128)S(1)}, f32[4,256,512]{2,1,0:T(8,128)S(1)}, u32[]{:S(2)}, u32[]{:S(2)}) collective-permute-start(f32[4,256,512]{2,1,0:T(8,128)S(1)} %get-tuple-element.32), channel_id=1, source_target_pairs={{16,0},{17,1},{18,2},{19,3},{20,4},{21,5},{22,6},{23,7},{24,8},{25... | collective-permute-start | bytes 6291464 | tf_op jit(solution)/shard_map/ppermute | solution.py:38
  36.7 29.0 %collective-permute-start.10 = (bf16[2,512,512]{2,1,0:T(8,128)(2,1)}, bf16[2,512,512]{2,1,0:T(8,128)(2,1)S(1)}, u32[]{:S(2)}, u32[]{:S(2)}) collective-permute-start(bf16[2,512,512]{2,1,0:T(8,128)(2,1)} %collective-permute-done.refs_1_), channel_id=1, source_target_pairs={{8,0},{9,1},{10,2},{11,3},{12,4},{13,5},{14,6},{15,7},{0,8},{1,9},... | collective-permute-start | bytes 3145736 | tf_op jit(solution)/shard_map/ppermute | solution.py:38
  39.1 26.6 %collective-permute-start.8 = (bf16[2,512,512]{2,1,0:T(8,128)(2,1)}, bf16[2,512,512]{2,1,0:T(8,128)(2,1)}, u32[]{:S(2)}, u32[]{:S(2)}) collective-permute-start(bf16[2,512,512]{2,1,0:T(8,128)(2,1)} %collective-permute-done.refs_1_), channel_id=1, source_target_pairs={{1,0},{2,1},{3,2},{4,3},{5,4},{6,5},{7,6},{0,7},{9,8},{10,9},{11,1... | collective-permute-start | bytes 3145736 | tf_op jit(solution)/shard_map/ppermute | solution.py:38
  42.1 26.1 %collective-permute-start.9 = (bf16[2,512,512]{2,1,0:T(8,128)(2,1)S(1)}, bf16[2,512,512]{2,1,0:T(8,128)(2,1)S(1)}, u32[]{:S(2)}, u32[]{:S(2)}) collective-permute-start(bf16[2,512,512]{2,1,0:T(8,128)(2,1)S(1)} %collective-permute-done.1.refs_2_.refs_1_), channel_id=1, source_target_pairs={{7,0},{0,1},{1,2},{2,3},{3,4},{4,5},{5,6},{6,7},{15,8},{8,9},{9,10... | collective-permute-start | bytes 3145736 | tf_op jit(solution)/shard_map/ppermute | solution.py:38
  42.1 8.2 %collective-permute-start.4 = (f32[128,512]{1,0:T(8,128)S(1)}, f32[128,512]{1,0:T(8,128)S(1)}, u32[]{:S(2)}, u32[]{:S(2)}) collective-permute-start(f32[128,512]{1,0:T(8,128)S(1)} %get-tuple-element.53), channel_id=1, source_target_pairs={{96,0},{97,1},{98,2},{99,3},{100,4},{101,5},{102,6},{103,7},{104,8... | collective-permute-start | bytes 786440 | tf_op jit(solution)/shard_map/ppermute | solution.py:38
  43.7 8.0 %collective-permute-start.6 = (f32[128,512]{1,0:T(8,128)S(1)}, f32[128,512]{1,0:T(8,128)S(1)}, u32[]{:S(2)}, u32[]{:S(2)}) collective-permute-start(f32[128,512]{1,0:T(8,128)S(1)} %get-tuple-element.54), channel_id=1, source_target_pairs={{32,0},{33,1},{34,2},{35,3},{36,4},{37,5},{38,6},{39,7},{40,8},{41... | collective-permute-start | bytes 786440 | tf_op jit(solution)/shard_map/ppermute | solution.py:38
  50.4 13.0 %collective-permute-start.5 = (f32[256,512]{1,0:T(8,128)S(1)}, f32[256,512]{1,0:T(8,128)S(1)}, u32[]{:S(2)}, u32[]{:S(2)}) collective-permute-start(f32[256,512]{1,0:T(8,128)S(1)} %pad_maximum_fusion.1), channel_id=1, source_target_pairs={{96,0},{97,1},{98,2},{99,3},{100,4},{101,5},{102,6},{103,7},{104,8... | collective-permute-start | bytes 1572872 | tf_op jit(solution)/shard_map/ppermute | solution.py:38
  51.7 12.9 %collective-permute-start.7 = (f32[256,512]{1,0:T(8,128)S(1)}, f32[256,512]{1,0:T(8,128)S(1)}, u32[]{:S(2)}, u32[]{:S(2)}) collective-permute-start(f32[256,512]{1,0:T(8,128)S(1)} %pad_maximum_fusion.2), channel_id=1, source_target_pairs={{32,0},{33,1},{34,2},{35,3},{36,4},{37,5},{38,6},{39,7},{40,8},{41... | collective-permute-start | bytes 1572872 | tf_op jit(solution)/shard_map/ppermute | solution.py:38
  72.6 4.2 %collective-permute-start.11 = (f32[4,256,512]{2,1,0:T(8,128)S(1)}, f32[4,256,512]{2,1,0:T(8,128)S(1)}, u32[]{:S(2)}, u32[]{:S(2)}) collective-permute-start(f32[4,256,512]{2,1,0:T(8,128)S(1)} %get-tuple-element.38), channel_id=1, source_target_pairs={{16,0},{17,1},{18,2},{19,3},{20,4},{21,5},{22,6},{23,7},{24,8},{25... | collective-permute-start | bytes 6291464 | tf_op jit(solution)/shard_map/ppermute | solution.py:38
  72.7 27.3 %collective-permute-start.12 = (bf16[2,512,512]{2,1,0:T(8,128)(2,1)}, bf16[2,512,512]{2,1,0:T(8,128)(2,1)S(1)}, u32[]{:S(2)}, u32[]{:S(2)}) collective-permute-start(bf16[2,512,512]{2,1,0:T(8,128)(2,1)} %collective-permute-done.8.refs_2_), channel_id=1, source_target_pairs={{8,0},{9,1},{10,2},{11,3},{12,4},{13,5},{14,6},{15,7},{0,8},{1,9},... | collective-permute-start | bytes 3145736 | tf_op jit(solution)/shard_map/ppermute | solution.py:38
  78.2 22.8 %collective-permute-start.13 = (f32[256,512]{1,0:T(8,128)}, f32[256,512]{1,0:T(8,128)}, u32[]{:S(2)}, u32[]{:S(2)}) collective-permute-start(f32[256,512]{1,0:T(8,128)} %get-tuple-element.40), channel_id=1, source_target_pairs={{96,0},{97,1},{98,2},{99,3},{100,4},{101,5},{102,6},{103,7},{104,8... | collective-permute-start | bytes 1572872 | tf_op jit(solution)/shard_map/ppermute | solution.py:38
  79.4 26.8 %collective-permute-start.14 = (f32[256,512]{1,0:T(8,128)}, f32[256,512]{1,0:T(8,128)}, u32[]{:S(2)}, u32[]{:S(2)}) collective-permute-start(f32[256,512]{1,0:T(8,128)} %get-tuple-element.42), channel_id=1, source_target_pairs={{64,0},{65,1},{66,2},{67,3},{68,4},{69,5},{70,6},{71,7},{72,8},{73... | collective-permute-start | bytes 1572872 | tf_op jit(solution)/shard_map/ppermute | solution.py:38
  80.2 26.0 %collective-permute-start.15 = (f32[256,512]{1,0:T(8,128)}, f32[256,512]{1,0:T(8,128)}, u32[]{:S(2)}, u32[]{:S(2)}) collective-permute-start(f32[256,512]{1,0:T(8,128)} %get-tuple-element.43), channel_id=1, source_target_pairs={{32,0},{33,1},{34,2},{35,3},{36,4},{37,5},{38,6},{39,7},{40,8},{41... | collective-permute-start | bytes 1572872 | tf_op jit(solution)/shard_map/ppermute | solution.py:38
  100.0 1.0 copy-start.1
  101.0 1.2 copy-start.2
  103.2 4.6 %collective-permute-start.16 = (f32[256,512]{1,0:T(8,128)S(1)}, f32[256,512]{1,0:T(8,128)S(1)}, u32[]{:S(2)}, u32[]{:S(2)}) collective-permute-start(f32[256,512]{1,0:T(8,128)S(1)} %bitcast.41), channel_id=1, source_target_pairs={{32,48},{64,80},{96,112},{0,16},{160,176},{192,208},{224,240},{128... | collective-permute-start | bytes 1572872 | tf_op jit(solution)/shard_map/ppermute | solution.py:38
  106.2 1.8 %copy-start.3 = (f32[256,512]{1,0:T(8,128)S(1)}, f32[256,512]{1,0:T(8,128)}, u32[]{:S(2)}) copy-start(f32[256,512]{1,0:T(8,128)} %fusion.6) | copy-start | bytes 1572868
  108.7 13.3 %collective-permute-start.17 = (f32[256,512]{1,0:T(8,128)S(1)}, f32[256,512]{1,0:T(8,128)S(1)}, u32[]{:S(2)}, u32[]{:S(2)}) collective-permute-start(f32[256,512]{1,0:T(8,128)S(1)} %broadcast_select_fusion.1), channel_id=1, source_target_pairs={{128,0},{129,1},{130,2},{131,3},{132,4},{133,5},{134,6},{135,7},{1... | collective-permute-start | bytes 1572872 | tf_op jit(solution)/shard_map/ppermute | solution.py:38
  110.0 12.7 %collective-permute-start.18 = (f32[256,512]{1,0:T(8,128)S(1)}, f32[256,512]{1,0:T(8,128)S(1)}, u32[]{:S(2)}, u32[]{:S(2)}) collective-permute-start(f32[256,512]{1,0:T(8,128)S(1)} %bitcast_add_fusion), channel_id=1, source_target_pairs={{14,78},{15,79},{18,82},{19,83},{40,104},{41,105},{52,116},{53,117... | collective-permute-start | bytes 1572872 | tf_op jit(solution)/shard_map/ppermute | solution.py:38
  110.7 12.1 %collective-permute-start.19 = (f32[256,512]{1,0:T(8,128)S(1)}, f32[256,512]{1,0:T(8,128)S(1)}, u32[]{:S(2)}, u32[]{:S(2)}) collective-permute-start(f32[256,512]{1,0:T(8,128)S(1)} %bitcast_add_fusion), channel_id=1, source_target_pairs={{8,104},{9,105},{20,116},{21,117},{42,10},{43,11},{54,22},{55,23},... | collective-permute-start | bytes 1572872 | tf_op jit(solution)/shard_map/ppermute | solution.py:38
  111.4 11.4 %collective-permute-start.20 = (f32[256,512]{1,0:T(8,128)S(1)}, f32[256,512]{1,0:T(8,128)S(1)}, u32[]{:S(2)}, u32[]{:S(2)}) collective-permute-start(f32[256,512]{1,0:T(8,128)S(1)} %bitcast_add_fusion), channel_id=1, source_target_pairs={{12,44},{13,45},{16,48},{17,49},{46,78},{47,79},{50,82},{51,83},{7... | collective-permute-start | bytes 1572872 | tf_op jit(solution)/shard_map/ppermute | solution.py:38
  123.2 17.0 %collective-permute-start.21 = (f32[256,512]{1,0:T(8,128)S(1)}, f32[256,512]{1,0:T(8,128)S(1)}, u32[]{:S(2)}, u32[]{:S(2)}) collective-permute-start(f32[256,512]{1,0:T(8,128)S(1)} %get-tuple-element.57), channel_id=1, source_target_pairs={{0,16},{160,128},{32,114},{64,113},{192,151},{96,135},{224,150},{2... | collective-permute-start | bytes 1572872 | tf_op jit(solution)/shard_map/ppermute | solution.py:38
  129.5 15.2 %collective-permute-start.22 = (f32[256,512]{1,0:T(8,128)S(1)}, f32[256,512]{1,0:T(8,128)S(1)}, u32[]{:S(2)}, u32[]{:S(2)}) collective-permute-start(f32[256,512]{1,0:T(8,128)S(1)} %add_add_fusion), channel_id=1, source_target_pairs={{176,166},{177,183},{82,192},{83,209},{116,226},{117,243},{150,132... | collective-permute-start | bytes 1572872 | tf_op jit(solution)/shard_map/ppermute | solution.py:38
  130.8 26.5 %collective-permute-start.23 = (f32[256,512]{1,0:T(8,128)S(1)}, f32[256,512]{1,0:T(8,128)S(1)}, u32[]{:S(2)}, u32[]{:S(2)}) collective-permute-start(f32[256,512]{1,0:T(8,128)S(1)} %get-tuple-element.58), channel_id=1, source_target_pairs={{128,98},{16,135},{144,151},{48,16},{176,0},{208,113},{80,150},{11... | collective-permute-start | bytes 1572872 | tf_op jit(solution)/shard_map/ppermute | solution.py:38
  132.1 25.2 %collective-permute-start.24 = (f32[256,512]{1,0:T(8,128)S(1)}, f32[256,512]{1,0:T(8,128)S(1)}, u32[]{:S(2)}, u32[]{:S(2)}) collective-permute-start(f32[256,512]{1,0:T(8,128)S(1)} %add_add_fusion), channel_id=1, source_target_pairs={{232,226},{233,243},{138,132},{139,149},{172,166},{173,183},{206,1... | collective-permute-start | bytes 1572872 | tf_op jit(solution)/shard_map/ppermute | solution.py:38
